TPU v7x, 32 devices: a whole 2x2x4 slice. The times are simulated.
32 devices in a mesh: head: 8 (over z, y), ctx: 4 (over x, core).
Axes of the slice: x: 2, y: 2, z: 4, core: 2. Of those that a mesh axis runs over, the one named last changes fastest.
Arguments:
- latent: bfloat16 [4, 16, 512], P('ctx', 'head'), may hold values from -6 to 6
- gain: float32 [512], replicated, may hold values from 0.1 to 1.9
- cotangent: bfloat16 [4, 16, 64, 256], P('ctx', None, 'head'), may hold values from -1 to 1
- weight: bfloat16 [512, 64, 256], P('ctx', 'head'), may hold values from -0.25 to 0.25
Outputs:
- latent_gradient: float32 [4, 16, 512], P('ctx', 'head')
- weight_grad: float32 [512, 64, 256], P('ctx', 'head')
All inputs are finite; a program needn't handle non-finite values.
Results may differ from a plain program's by a relative error of at most 0.0029.
Values may be sent and summed in bfloat16 or wider, within the bound.
No kernel may reach another device: no remote copies, remote signals or barrier semaphores. Data moves between devices by JAX's collectives and lax.ppermute only.
A program may use at most 64 MiB of HBM per device.

v0:
```python
import jax
import jax.numpy as jnp
from jax import lax
from jax.sharding import PartitionSpec as P


def per_device(latent, gain, cotangent, weight):
    width = latent.shape[2]
    gathered = lax.all_gather(latent, "head", axis=1, tiled=True)[0]
    raw_latent = gathered.astype(jnp.float32)
    root_mean_square = lax.rsqrt(jnp.mean(raw_latent * raw_latent, axis=1, keepdims=True) + 1e-06)
    latent_hat = raw_latent * root_mean_square
    normed_latent = (latent_hat * gain).astype(jnp.bfloat16)
    shard_rows = gathered.shape[0]
    flat = cotangent[0].reshape(shard_rows, -1)
    whole_weight = lax.all_gather(weight, "ctx", axis=0, tiled=True).reshape(width, -1)
    weight_grad = lax.psum_scatter(
        lax.dot_general(
            normed_latent, flat, (((0,), (0,)), ((), ())), preferred_element_type=jnp.float32
        ),
        "ctx",
        scatter_dimension=0,
        tiled=True,
    ).reshape(weight.shape)
    grad_rows = lax.psum_scatter(
        lax.dot_general(
            flat, whole_weight, (((1,), (1,)), ((), ())), preferred_element_type=jnp.float32
        ),
        "head",
        scatter_dimension=0,
        tiled=True,
    )
    own_raw = latent[0].astype(jnp.float32)
    own_rms = lax.rsqrt(jnp.mean(own_raw * own_raw, axis=1, keepdims=True) + 1e-06)
    own_hat = own_raw * own_rms
    scaled_latent = grad_rows * gain
    inner_product = jnp.mean(scaled_latent * own_hat, axis=1, keepdims=True)
    latent_gradient = own_rms * (scaled_latent - own_hat * inner_product)
    return (latent_gradient[None], weight_grad)


def solution(mesh):
    return jax.shard_map(
        per_device,
        mesh=mesh,
        in_specs=(
            P("ctx", "head", None),
            P(),
            P("ctx", None, "head", None),
            P("ctx", "head", None),
        ),
        out_specs=(P("ctx", "head", None), P("ctx", "head", None)),
        check_vma=False,
    )
```

profile of v0, /device:TPU:0, one launch (start us, length us, event | category | flops | bytes accessed | tf_op | source)
XLA Modules:
  0.0 100.2 jit_solution(14318562812304246688)
XLA Ops:
  7.2 0.0 all-gather.2.cloned.1.call-start
  7.2 0.7 all-gather.2.cloned.1.call-update
  7.9 0.0 reduce-scatter.2.cloned.1.call-start
  7.9 0.7 copy.7
  8.6 0.9 copy.9
  9.5 32.2 %all_gather.7 = bf16[1,16,512]{2,0,1:T(2,128)(2,1)S(1)} all-gather(bf16[1,2,512]{2,0,1:T(2,128)(2,1)S(1)} %copy.7), channel_id=1, replica_groups=mesh['head'=8,'ctx'=4] {'head'}, dimensions={1}, use_global_device_ids=true | all-gather | bytes 18432 | tf_op jit(solution)/shard_map/all_gather | solution.py:9
  41.7 0.1 fusion
  41.8 3.4 %fusion.4 = f32[512,2048]{1,0:T(8,128)} fusion(bf16[16,2048]{1,0:T(8,128)(2,1)S(1)} %bitcast.25, f32[512]{0:T(512)} %param.5, f32[16]{0:T(128)S(1)} %add_rsqrt_fusion, bf16[1,16,512]{2,0,1:T(2,128)(2,1)S(1)} %all_gather.7), kind=kOutput, calls=%fused_computation.6 | convolution fusion | flops 33587200 | bytes 4278336 | tf_op jit(solution)/shard_map/dot_general | solution.py:18
  45.2 0.0 copy-start.2
  45.2 0.0 copy-start
  45.2 0.0 reduce-scatter.2.cloned.1.call-update
  45.3 0.6 copy-done.2
  45.9 0.6 dynamic-slice
  47.1 0.0 copy-done
  47.1 0.1 fusion.15
  47.3 0.0 all-gather.2.cloned.1.call-done
  47.3 2.3 %copy.10 = bf16[64,8,8,256]{3,1,2,0:T(8,128)(2,1)S(1)} copy(bf16[64,8,8,256]{3,2,1,0:T(8,128)(2,1)} %bitcast.22) | data formatting | bytes 4194304
  49.6 0.0 copy-start.1
  49.6 0.6 fusion.16
  50.2 37.1 %all-reduce = f32[16,512]{1,0:T(8,128)S(1)} all-reduce(f32[16,512]{1,0:T(8,128)S(1)} %fusion.16), channel_id=2, replica_groups=mesh['head'=8,'ctx'=4] {'head'}, use_global_device_ids=true, to_apply=%region_1.0.clone | all-reduce | flops 8192 | bytes 65536
  87.3 0.0 copy-done.1
  87.3 0.2 fusion.11
  87.5 0.7 fusion.14
  88.2 2.7 %reduce-scatter.2.cloned.1.call-done = f32[128,2048]{1,0:T(8,128)} async-done(((f32[512,2048]{1,0:T(8,128)}), f32[128,2048]{1,0:T(8,128)}) %reduce-scatter.2.cloned.1.call-update) | async-done | bytes 1048592 | tf_op jit(solution)/shard_map/reduce_scatter | solution.py:17
  90.8 2.5 %copy.11 = f32[16,8,8,256]{3,2,1,0:T(8,128)} copy(f32[16,8,8,256]{3,1,2,0:T(8,128)} %bitcast.23) | data formatting | bytes 2097152
  (3 shorter events, 0.0 us)
Async XLA Ops:
  7.2 40.1 %all-gather.2.cloned.1.call-start = ((), (), s32[]{:S(2)}) async-start(), calls=%async_computation.1 | async-start | bytes 2621440 | tf_op jit(solution)/shard_map/all_gather | solution.py:16
  7.9 82.9 %reduce-scatter.2.cloned.1.call-start = ((), (), s32[]{:S(2)}) async-start(), calls=%async_computation.2 | async-start | bytes 5242880 | tf_op jit(solution)/shard_map/reduce_scatter | solution.py:17
  45.2 0.7 copy-start.2
  45.2 1.9 %copy-start = (bf16[1,2,512]{2,1,0:T(2,128)(2,1)S(1)}, bf16[1,2,512]{2,1,0:T(2,128)(2,1)}, u32[]{:S(2)}) copy-start(bf16[1,2,512]{2,1,0:T(2,128)(2,1)} %param.4) | copy-start | bytes 6148
  49.6 37.7 %copy-start.1 = (f32[512]{0:T(512)S(1)}, f32[512]{0:T(512)}, u32[]{:S(2)}) copy-start(f32[512]{0:T(512)} %param.5) | copy-start | bytes 6148
Sparse Core Ops, SparseCore 0:
  9.6 25.2 all-gather.1
  45.4 45.4 reduce-scatter.1
where the time goes:
time: 101 us; the launch traced here: 100 us
  blocking collectives  69.3 us (69%)
  between operations  14.7 us (15%)
  local copies, waits for them, and re-layouts  7.56 us (7%)
  matrix products  4.06 us (4%)
  waiting for transfers between devices  3.4 us (3%)
  other arithmetic  1.11 us (1%)
    unnamed x1, blocking collectives  37.1 us
    all_gather x1, blocking collectives, per_device(): gathered = lax.all_gather(latent, 'head', axis=1, tiled=True)[0]  32.2 us
    unnamed x11, local copies, waits for them, and re-layouts  7.56 us
    dot_general x1, matrix products, per_device(): lax.dot_general(normed_latent, flat, (((0,), (0,)), ((), ())), preferred_...  3.42 us
    reduce_scatter x1, waiting for transfers between devices, per_device(): lax.psum_scatter(lax.dot_general(normed_latent, flat, (((0,), (0,)), ((),...  2.69 us
  transfers between devices with their start and end apart: 2, of which 1 were waited for; matrix products, arithmetic and copies ran while one was open for 10% of the time, Pallas kernels for 0%

commit v1 on v0

v1 whole, which is shorter than its diff:
```python
import functools

import jax
import jax.numpy as jnp
from jax import lax
from jax.experimental import pallas as pl
from jax.experimental.pallas import tpu as pltpu
from jax.sharding import PartitionSpec as P


F32 = jnp.float32
BF16 = jnp.bfloat16


def iota(shape, axis):
    return lax.broadcasted_iota(jnp.int32, shape, axis)


def one_hot(condition):
    return jnp.where(condition, 1.0, 0.0).astype(BF16)


def matmul(a, b, a_axis=1, b_axis=0):
    return lax.dot_general(a, b, (((a_axis,), (b_axis,)), ((), ())), preferred_element_type=F32)


def reverse_bits(value, count):
    out = 0
    for bit in range(count):
        out = out | (((value >> bit) & 1) << (count - 1 - bit))
    return out


def weight_kernel(heads, own_ref, other_ref, out_ref):
    core = lax.axis_index("ctx") & 1
    rows = own_ref.shape[0] // heads
    group = min(rows, max(256 // heads, 1))
    size = group * heads
    to, at = iota((size, size), 0), iota((size, size), 1)
    order = one_hot(at == (to % group) * heads + to // group)
    for ref, place in ((own_ref, core), (other_ref, 1 - core)):
        for start in range(0, rows, group):
            moved = matmul(order, ref[pl.ds(start * heads, size), :]).astype(BF16)
            first = pl.multiple_of(place * rows + start, group)
            for h in range(heads):
                out_ref[h, pl.ds(first, group), :] = moved[h * group : (h + 1) * group, :]


def partial_kernel(head_count, heads, owned, *refs):
    shard_refs, weight_ref, out_ref = refs[:-2], refs[-2], refs[-1]
    shards = len(shard_refs)
    me = lax.axis_index("head")
    bits = head_count.bit_length() - 1
    rows = head_count * owned
    stacked = jnp.concatenate([ref[...] for ref in shard_refs], axis=0)
    size = shards * rows * heads
    to, at = iota((size, size), 0), iota((size, size), 1)
    i, j = to % owned, (to // owned) % shards
    position = (to // (owned * shards)) % head_count
    token = (reverse_bits(position, bits) ^ me) * owned + i
    order = one_hot(at == (j * rows + token) * heads + to // (rows * shards))
    moved = matmul(order, stacked).astype(BF16)
    part = rows * shards
    total = matmul(moved[:part], weight_ref[0], 1, 1)
    for h in range(1, heads):
        total += matmul(moved[h * part : (h + 1) * part], weight_ref[h], 1, 1)
    out_ref[...] = total


def norm_kernel(columns, latent_ref, gain_ref, *out_refs):
    column = lax.axis_index("ctx") >> 1
    raw = latent_ref[...].astype(F32)
    rms = lax.rsqrt(jnp.mean(raw * raw, axis=1, keepdims=True) + 1e-06)
    normed = ((raw * rms) * gain_ref[...]).astype(BF16).astype(F32)
    width = normed.shape[1] // columns
    for j, ref in enumerate(out_refs):
        block = normed[:, :width]
        for b in range(1, columns):
            block = jnp.where((column ^ j) == b, normed[:, b * width : (b + 1) * width], block)
        ref[...] = block


def weight_grad_kernel(head_count, heads, owned, columns, normed_ref, *refs):
    shard_refs, out_ref, scratch_ref = refs[:-2], refs[-2], refs[-1]
    me = lax.axis_index("head")
    core = lax.axis_index("ctx") & 1
    rows = out_ref.shape[0] // heads
    tokens = head_count * owned
    normed = normed_ref[...].astype(BF16)
    size = columns * tokens * heads
    at, to = iota((normed.shape[0], size), 0), iota((normed.shape[0], size), 1)
    token, j = (to // heads) % tokens, to // (heads * tokens)
    cots = []
    for side in range(2):
        place = (((token // owned) ^ me) * 2 + (core ^ side)) * columns + j
        spread = one_hot(at == place * owned + token % owned)
        scratch_ref[side] = matmul(normed, spread, 0, 0)
        cots.append(jnp.concatenate([r[...] for r in shard_refs[side * columns : (side + 1) * columns]], axis=0))
    group = min(rows, max(256 // heads, 1))
    keep = (iota((1, heads, size), 2) % heads) == iota((1, heads, size), 1)
    for start in range(0, rows, group):
        total = None
        for side in range(2):
            block = scratch_ref[side, pl.ds(pl.multiple_of(core * rows + start, group), group), :]
            left = jnp.where(keep, block[:, None, :], 0.0).reshape(group * heads, size).astype(BF16)
            part = matmul(left, cots[side])
            total = part if total is None else total + part
        out_ref[start * heads : (start + group) * heads, :] = total


def latent_kernel(columns, latent_ref, gain_ref, *refs):
    block_refs, out_ref = refs[:-1], refs[-1]
    column = lax.axis_index("ctx") >> 1
    raw = latent_ref[...].astype(F32)
    rms = lax.rsqrt(jnp.mean(raw * raw, axis=1, keepdims=True) + 1e-06)
    hat = raw * rms
    blocks = []
    for b in range(columns):
        block = block_refs[0][...]
        for j in range(1, columns):
            block = jnp.where((column ^ j) == b, block_refs[j][...], block)
        blocks.append(block)
    scaled = jnp.concatenate(blocks, axis=1) * gain_ref[...]
    inner = jnp.mean(scaled * hat, axis=1, keepdims=True)
    out_ref[...] = rms * (scaled - hat * inner)


def per_device(head_count, ctx_count, latent, gain, cotangent, weight):
    columns = ctx_count // 2
    owned, width = latent.shape[1:]
    _, tokens, heads, channels = cotangent.shape
    rows = weight.shape[0]
    params = pltpu.CompilerParams(vmem_limit_bytes=48 * 1024 * 1024)

    def ctx_swap(value, mask):
        return lax.ppermute(value, "ctx", [(i, i ^ mask) for i in range(ctx_count)])

    def head_swap(value, mask):
        return lax.ppermute(value, "head", [(i, i ^ mask) for i in range(head_count)])

    def call(kernel, out, *args, scratch=(), flops=0):
        moved = sum(a.size * a.dtype.itemsize for a in args)
        return pl.pallas_call(
            kernel,
            out_shape=out,
            scratch_shapes=scratch,
            compiler_params=params,
            cost_estimate=pl.CostEstimate(flops=flops, bytes_accessed=moved, transcendentals=0),
        )(*args)

    flat = cotangent.reshape(tokens * heads, channels)
    shards = [flat]
    mask = 2
    while mask < ctx_count:
        shards += [ctx_swap(s, mask) for s in shards]
        mask *= 2
    weight_flat = weight.reshape(rows * heads, channels)
    weight_other = ctx_swap(weight_flat, 1)
    chip_weight = call(
        functools.partial(weight_kernel, heads),
        jax.ShapeDtypeStruct((heads, 2 * rows, channels), BF16),
        weight_flat,
        weight_other,
    )
    gain_row = gain.reshape(1, width)

    block = jax.ShapeDtypeStruct((owned, 2 * rows), F32)
    normed = list(call(functools.partial(norm_kernel, columns), [block] * columns, latent[0], gain_row))
    mask = 2
    while mask < ctx_count:
        for j in range(columns):
            if j & (mask >> 1):
                normed[j] = ctx_swap(normed[j], mask)
        mask *= 2
    mine = jnp.concatenate(normed, axis=0)
    theirs = ctx_swap(mine, 1)
    core = lax.axis_index("ctx") & 1
    normed = jnp.where(core == 0, jnp.concatenate([mine, theirs]), jnp.concatenate([theirs, mine]))

    sums = call(
        functools.partial(partial_kernel, head_count, heads, owned),
        jax.ShapeDtypeStruct((head_count * columns * owned, 2 * rows), F32),
        *shards,
        chip_weight,
    )
    mask = 1
    while mask < head_count:
        half = sums.shape[0] // 2
        got = head_swap(jnp.concatenate([sums[half:], normed], axis=0), mask)
        sums = sums[:half] + got[:half]
        normed = jnp.concatenate([normed, got[half:]], axis=0)
        mask *= 2

    blocks = [sums[j * owned : (j + 1) * owned] for j in range(columns)]
    mask = 2
    while mask < ctx_count:
        for j in range(columns):
            if j & (mask >> 1):
                blocks[j] = ctx_swap(blocks[j], mask)
        mask *= 2

    others = [ctx_swap(s, 1) for s in shards]
    weight_grad = call(
        functools.partial(weight_grad_kernel, head_count, heads, owned, columns),
        jax.ShapeDtypeStruct((rows * heads, channels), F32),
        normed,
        *shards,
        *others,
        scratch=[pltpu.VMEM((2, 2 * rows, columns * tokens * heads), F32)],
        flops=2 * rows * heads * channels * ctx_count * tokens * heads,
    )
    latent_gradient = call(
        functools.partial(latent_kernel, columns),
        jax.ShapeDtypeStruct((owned, width), F32),
        latent[0],
        gain_row,
        *blocks,
    )
    return latent_gradient[None], weight_grad.reshape(weight.shape)


def solution(mesh):
    return jax.shard_map(
        functools.partial(per_device, mesh.shape["head"], mesh.shape["ctx"]),
        mesh=mesh,
        in_specs=(
            P("ctx", "head", None),
            P(),
            P("ctx", None, "head", None),
            P("ctx", "head", None),
        ),
        out_specs=(P("ctx", "head", None), P("ctx", "head", None)),
        check_vma=False,
    )
```

time: 101 us -> 28.9 us (0.29)
  blocking collectives: 69.3 us -> 0 us
  starting transfers between devices: 0.08 us -> 14.5 us
  between operations: 14.7 us -> 0.75 us
  local copies, waits for them, and re-layouts: 7.56 us -> 1.25 us
  waiting for transfers between devices: 3.4 us -> 8.67 us
  matrix products: 4.06 us -> 0 us
  Pallas kernels: 0 us -> 3.42 us
  other arithmetic: 1.11 us -> 0.06 us
    unnamed x1 -> x0, blocking collectives: 37.1 us -> none
    all_gather x1 -> x0, blocking collectives: 32.2 us -> none  [per_device(): gathered = lax.all_gather(latent, 'head', axis=1, tiled=True)[0]]
    ppermute x0 -> x10, starting transfers between devices: none -> 14.5 us  [the longest x7 7.82 us: ctx_swap(): return lax.ppermute(value, 'ctx', [(i, i ^ mask) for i in range(ctx_count)])]
    ppermute x0 -> x10, waiting for transfers between devices: none -> 8.67 us  [the longest x3 5.52 us: head_swap(): lax.ppermute(value, 'head', [(i, i ^ mask) for i in range(head_count)])]
    unnamed x11 -> x8, local copies, waits for them, and re-layouts: 7.56 us -> 1.2 us
    dot_general x2 -> x0, matrix products: 4.06 us -> none  [the longest x1 3.42 us: per_device(): lax.dot_general(normed_latent, flat, (((0,), (0,)), ((), ())), preferred_...]
    pallas_call x0 -> x5, Pallas kernels: none -> 3.42 us  [call(): pl.pallas_call(kernel, out_shape=out, scratch_shapes=scratch, compiler_pa...]
    reduce_scatter x1 -> x0, waiting for transfers between devices: 2.69 us -> none  [per_device(): lax.psum_scatter(lax.dot_general(normed_latent, flat, (((0,), (0,)), ((),...]
  transfers between devices with their start and end apart: 2 -> 10, of which waited for: 1 -> 6; matrix products, arithmetic and copies ran while one was open for 10% -> 0% of each run, Pallas kernels for 0% -> 8%
where the time goes in v1:
time: 28.9 us; the launch traced here: 28.7 us
  starting transfers between devices  14.5 us (50%)
  waiting for transfers between devices  8.67 us (30%)
  Pallas kernels  3.42 us (12%)
  local copies, waits for them, and re-layouts  1.25 us (4%)
  between operations  0.75 us (3%)
    ppermute x7, starting transfers between devices, ctx_swap(): return lax.ppermute(value, 'ctx', [(i, i ^ mask) for i in range(ctx_count)])  7.82 us
    ppermute x3, starting transfers between devices, head_swap(): lax.ppermute(value, 'head', [(i, i ^ mask) for i in range(head_count)])  6.71 us
    ppermute x3, waiting for transfers between devices, head_swap(): lax.ppermute(value, 'head', [(i, i ^ mask) for i in range(head_count)])  5.52 us
    pallas_call x5, Pallas kernels, call(): pl.pallas_call(kernel, out_shape=out, scratch_shapes=scratch, compiler_pa...  3.42 us
    ppermute x7, waiting for transfers between devices, ctx_swap(): return lax.ppermute(value, 'ctx', [(i, i ^ mask) for i in range(ctx_count)])  3.14 us
    unnamed x8, local copies, waits for them, and re-layouts  1.2 us
  transfers between devices with their start and end apart: 10, of which 6 were waited for; matrix products, arithmetic and copies ran while one was open for 0% of the time, Pallas kernels for 8%

profile of v1, /device:TPU:0, one launch (start us, length us, event | category | flops | bytes accessed | tf_op | source)
XLA Modules:
  0.0 28.7 jit_solution(6861557725130687069)
XLA Ops:
  0.6 0.0 copy-start.3
  0.6 0.0 copy-start.2
  0.6 0.5 %collective-permute-start.1 = (bf16[1024,256]{1,0:T(8,128)(2,1)}, bf16[1024,256]{1,0:T(8,128)(2,1)S(1)}, u32[]{:S(2)}, u32[]{:S(2)}) collective-permute-start(bf16[1024,256]{1,0:T(8,128)(2,1)} %bitcast.6), channel_id=1, source_target_pairs={{0,1},{1,0},{2,3},{3,2},{4,5},{5,4},{6,7},{7,6},{8,9},{9,8},{10,11... | collective-permute-start | bytes 1572872 | tf_op jit(solution)/shard_map/ppermute | solution.py:136
  1.2 0.1 copy-done.3
  1.3 0.0 copy-done.2
  1.3 0.1 shard_map.61
  1.4 3.0 %collective-permute-start.2 = (f32[2,256]{1,0:T(2,128)S(1)}, f32[2,256]{1,0:T(2,128)S(1)}, u32[]{:S(2)}, u32[]{:S(2)}) collective-permute-start(f32[2,256]{1,0:T(2,128)S(1)} %get-tuple-element.5), channel_id=1, source_target_pairs={{0,2},{1,3},{2,0},{3,1},{4,6},{5,7},{6,4},{7,5},{8,10},{9,11},{10,... | collective-permute-start | bytes 6152 | tf_op jit(solution)/shard_map/ppermute | solution.py:136
  4.4 1.6 %collective-permute-done.2 = f32[2,256]{1,0:T(2,128)S(1)} collective-permute-done((f32[2,256]{1,0:T(2,128)S(1)}, f32[2,256]{1,0:T(2,128)S(1)}, u32[]{:S(2)}, u32[]{:S(2)}) %collective-permute-start.2) | collective-permute-done | bytes 2080 | tf_op jit(solution)/shard_map/ppermute | solution.py:136
  6.0 0.0 collective-permute-start.3
  6.0 2.1 %collective-permute-start = (bf16[128,256]{1,0:T(8,128)(2,1)}, bf16[128,256]{1,0:T(8,128)(2,1)S(1)}, u32[]{:S(2)}, u32[]{:S(2)}) collective-permute-start(bf16[128,256]{1,0:T(8,128)(2,1)} %bitcast.8), channel_id=1, source_target_pairs={{0,2},{1,3},{2,0},{3,1},{4,6},{5,7},{6,4},{7,5},{8,10},{9,11},{10,... | collective-permute-start | bytes 196616 | tf_op jit(solution)/shard_map/ppermute | solution.py:136
  8.1 0.0 collective-permute-done.3
  8.1 0.0 collective-permute-done.1.other_ref
  8.1 0.0 copy-start
  8.1 1.0 %copy-done = bf16[128,8,256]{2,1,0:T(8,128)(2,1)S(1)} copy-done((bf16[128,8,256]{2,1,0:T(8,128)(2,1)S(1)}, bf16[128,8,256]{2,1,0:T(8,128)(2,1)}, u32[]{:S(2)}) %copy-start) | copy-done | bytes 524312
  9.1 0.0 copy-start.1
  9.1 0.4 %shard_map.59.refs_2_ = bf16[8,256,256]{2,1,0:T(8,128)(2,1)S(1)} custom-call(bf16[1024,256]{1,0:T(8,128)(2,1)S(1)} %bitcast.7, bf16[1024,256]{1,0:T(8,128)(2,1)S(1)} %collective-permute-done.1.other_ref), custom_call_target="tpu_custom_call" | custom-call | bytes 1048576 | tf_op jit(solution)/shard_map/pallas_call | solution.py:143
  9.6 1.4 %collective-permute-done.refs_1_ = bf16[128,256]{1,0:T(8,128)(2,1)S(1)} collective-permute-done((bf16[128,256]{1,0:T(8,128)(2,1)}, bf16[128,256]{1,0:T(8,128)(2,1)S(1)}, u32[]{:S(2)}, u32[]{:S(2)}) %collective-permute-start) | collective-permute-done | bytes 65568 | tf_op jit(solution)/shard_map/ppermute | solution.py:136
  11.0 0.0 copy-done.1
  11.0 0.5 %shard_map.60 = f32[32,256]{1,0:T(8,128)S(1)} custom-call(bf16[128,256]{1,0:T(8,128)(2,1)S(1)} %bitcast.9, bf16[128,256]{1,0:T(8,128)(2,1)S(1)} %collective-permute-done.refs_1_, bf16[8,256,256]{2,1,0:T(8,128)(2,1)S(1)} %shard_map.59.refs_2_), custom_call_target="tpu_custom_call" | custom-call | bytes 1179648 | tf_op jit(solution)/shard_map/pallas_call | solution.py:143
  11.5 1.8 %collective-permute-start.4 = (f32[24,256]{1,0:T(8,128)S(1)}, f32[24,256]{1,0:T(8,128)S(1)}, u32[]{:S(2)}, u32[]{:S(2)}) collective-permute-start(f32[24,256]{1,0:T(8,128)S(1)} %pad_maximum_fusion.2), channel_id=1, source_target_pairs={{0,4},{4,0},{8,12},{12,8},{16,20},{20,16},{24,28},{28,24},{1,5},{5... | collective-permute-start | bytes 73736 | tf_op jit(solution)/shard_map/ppermute | solution.py:139
  13.3 2.1 %collective-permute-done.4 = f32[24,256]{1,0:T(8,128)S(1)} collective-permute-done((f32[24,256]{1,0:T(8,128)S(1)}, f32[24,256]{1,0:T(8,128)S(1)}, u32[]{:S(2)}, u32[]{:S(2)}) %collective-permute-start.4) | collective-permute-done | bytes 24608 | tf_op jit(solution)/shard_map/ppermute | solution.py:139
  15.4 1.9 %collective-permute-start.5 = (f32[24,256]{1,0:T(8,128)S(1)}, f32[24,256]{1,0:T(8,128)S(1)}, u32[]{:S(2)}, u32[]{:S(2)}) collective-permute-start(f32[24,256]{1,0:T(8,128)S(1)} %pad_maximum_fusion.3), channel_id=1, source_target_pairs={{0,8},{4,12},{8,0},{12,4},{16,24},{20,28},{24,16},{28,20},{1,9},{5... | collective-permute-start | bytes 73736 | tf_op jit(solution)/shard_map/ppermute | solution.py:139
  17.3 2.0 %collective-permute-done.5 = f32[24,256]{1,0:T(8,128)S(1)} collective-permute-done((f32[24,256]{1,0:T(8,128)S(1)}, f32[24,256]{1,0:T(8,128)S(1)}, u32[]{:S(2)}, u32[]{:S(2)}) %collective-permute-start.5) | collective-permute-done | bytes 24608 | tf_op jit(solution)/shard_map/ppermute | solution.py:139
  19.3 3.0 %collective-permute-start.6 = (f32[36,256]{1,0:T(8,128)S(1)}, f32[36,256]{1,0:T(8,128)S(1)}, u32[]{:S(2)}, u32[]{:S(2)}) collective-permute-start(f32[36,256]{1,0:T(8,128)S(1)} %pad_maximum_fusion.1), channel_id=1, source_target_pairs={{0,16},{4,20},{8,24},{12,28},{16,0},{20,4},{24,8},{28,12},{1,17},{... | collective-permute-start | bytes 110600 | tf_op jit(solution)/shard_map/ppermute | solution.py:139
  22.3 0.0 collective-permute-start.8
  22.3 0.5 %collective-permute-start.9 = (bf16[128,256]{1,0:T(8,128)(2,1)S(1)}, bf16[128,256]{1,0:T(8,128)(2,1)S(1)}, u32[]{:S(2)}, u32[]{:S(2)}) collective-permute-start(bf16[128,256]{1,0:T(8,128)(2,1)S(1)} %collective-permute-done.refs_1_), channel_id=1, source_target_pairs={{0,1},{1,0},{2,3},{3,2},{4,5},{5,4},{6,7},{7,6},{8,9},{9,8},{10,11... | collective-permute-start | bytes 196616 | tf_op jit(solution)/shard_map/ppermute | solution.py:136
  22.8 1.5 %collective-permute-done.6 = f32[36,256]{1,0:T(8,128)S(1)} collective-permute-done((f32[36,256]{1,0:T(8,128)S(1)}, f32[36,256]{1,0:T(8,128)S(1)}, u32[]{:S(2)}, u32[]{:S(2)}) %collective-permute-start.6) | collective-permute-done | bytes 36896 | tf_op jit(solution)/shard_map/ppermute | solution.py:139
  24.3 1.7 %collective-permute-start.7 = (f32[2,256]{1,0:T(2,128)S(1)}, f32[2,256]{1,0:T(2,128)S(1)}, u32[]{:S(2)}, u32[]{:S(2)}) collective-permute-start(f32[2,256]{1,0:T(2,128)S(1)} %get-tuple-element.6), channel_id=1, source_target_pairs={{0,2},{1,3},{2,0},{3,1},{4,6},{5,7},{6,4},{7,5},{8,10},{9,11},{10,... | collective-permute-start | bytes 6152 | tf_op jit(solution)/shard_map/ppermute | solution.py:136
  26.1 0.0 collective-permute-done.8.refs_2_
  26.1 0.0 collective-permute-done.9.refs_3_
  26.1 1.6 %shard_map.63 = f32[1024,256]{1,0:T(8,128)} custom-call(f32[64,256]{1,0:T(8,128)S(1)} %pad_maximum_fusion.normed_ref, bf16[128,256]{1,0:T(8,128)(2,1)S(1)} %bitcast.11, bf16[128,256]{1,0:T(8,128)(2,1)S(1)} %collective-permute-done.refs_1_, bf16[128,256]{1,0:T(8,128)(2,1)S(1)} %collective-permute-done.8.refs_2_, ...), custom_call_target="tpu_custom_call" | custom-call | flops 268435456 | bytes 327680 | tf_op jit(solution)/shard_map/pallas_call | solution.py:143
  27.7 0.2 collective-permute-done.7.refs_1_
  27.9 0.8 %shard_map.62 = f32[2,512]{1,0:T(2,128)} custom-call(bf16[2,512]{1,0:T(2,128)(2,1)S(1)} %bitcast.13, f32[1,512]{1,0:T(1,128)S(1)} %bitcast.15, f32[2,256]{1,0:T(2,128)S(1)} %get-tuple-element.7.refs_0_, f32[2,256]{1,0:T(2,128)S(1)} %collective-permute-done.7.refs_1_), custom_call_target="tpu_custom_call" | custom-call | bytes 8192 | tf_op jit(solution)/shard_map/pallas_call | solution.py:143
  (16 shorter events, 0.1 us)
Async XLA Ops:
  0.6 0.7 %copy-start.3 = (f32[512]{0:T(512)S(1)}, f32[512]{0:T(512)}, u32[]{:S(2)}) copy-start(f32[512]{0:T(512)} %param.5) | copy-start | bytes 6148
  0.6 0.7 %copy-start.2 = (bf16[1,2,512]{2,1,0:T(2,128)(2,1)S(1)}, bf16[1,2,512]{2,1,0:T(2,128)(2,1)}, u32[]{:S(2)}) copy-start(bf16[1,2,512]{2,1,0:T(2,128)(2,1)} %param.4) | copy-start | bytes 6148
  0.6 7.4 %collective-permute-start.1 = (bf16[1024,256]{1,0:T(8,128)(2,1)}, bf16[1024,256]{1,0:T(8,128)(2,1)S(1)}, u32[]{:S(2)}, u32[]{:S(2)}) collective-permute-start(bf16[1024,256]{1,0:T(8,128)(2,1)} %bitcast.6), channel_id=1, source_target_pairs={{0,1},{1,0},{2,3},{3,2},{4,5},{5,4},{6,7},{7,6},{8,9},{9,8},{10,11... | collective-permute-start | bytes 1572872 | tf_op jit(solution)/shard_map/ppermute | solution.py:136
  1.4 4.5 %collective-permute-start.2 = (f32[2,256]{1,0:T(2,128)S(1)}, f32[2,256]{1,0:T(2,128)S(1)}, u32[]{:S(2)}, u32[]{:S(2)}) collective-permute-start(f32[2,256]{1,0:T(2,128)S(1)} %get-tuple-element.5), channel_id=1, source_target_pairs={{0,2},{1,3},{2,0},{3,1},{4,6},{5,7},{6,4},{7,5},{8,10},{9,11},{10,... | collective-permute-start | bytes 6152 | tf_op jit(solution)/shard_map/ppermute | solution.py:136
  6.0 2.1 %collective-permute-start.3 = (f32[4,256]{1,0:T(4,128)S(1)}, f32[4,256]{1,0:T(4,128)S(1)}, u32[]{:S(2)}, u32[]{:S(2)}) collective-permute-start(f32[4,256]{1,0:T(4,128)S(1)} %pad_maximum_fusion.4), channel_id=1, source_target_pairs={{0,1},{1,0},{2,3},{3,2},{4,5},{5,4},{6,7},{7,6},{8,9},{9,8},{10,11... | collective-permute-start | bytes 12296 | tf_op jit(solution)/shard_map/ppermute | solution.py:136
  6.0 5.0 %collective-permute-start = (bf16[128,256]{1,0:T(8,128)(2,1)}, bf16[128,256]{1,0:T(8,128)(2,1)S(1)}, u32[]{:S(2)}, u32[]{:S(2)}) collective-permute-start(bf16[128,256]{1,0:T(8,128)(2,1)} %bitcast.8), channel_id=1, source_target_pairs={{0,2},{1,3},{2,0},{3,1},{4,6},{5,7},{6,4},{7,5},{8,10},{9,11},{10,... | collective-permute-start | bytes 196616 | tf_op jit(solution)/shard_map/ppermute | solution.py:136
  8.1 1.0 %copy-start = (bf16[128,8,256]{2,1,0:T(8,128)(2,1)S(1)}, bf16[128,8,256]{2,1,0:T(8,128)(2,1)}, u32[]{:S(2)}) copy-start(bf16[128,8,256]{2,1,0:T(8,128)(2,1)} %param.7) | copy-start | bytes 1572868
  9.1 1.8 %copy-start.1 = (bf16[1,16,8,256]{3,2,1,0:T(8,128)(2,1)S(1)}, bf16[1,16,8,256]{3,2,1,0:T(8,128)(2,1)}, u32[]{:S(2)}) copy-start(bf16[1,16,8,256]{3,2,1,0:T(8,128)(2,1)} %param.6) | copy-start | bytes 196612
  11.5 3.9 %collective-permute-start.4 = (f32[24,256]{1,0:T(8,128)S(1)}, f32[24,256]{1,0:T(8,128)S(1)}, u32[]{:S(2)}, u32[]{:S(2)}) collective-permute-start(f32[24,256]{1,0:T(8,128)S(1)} %pad_maximum_fusion.2), channel_id=1, source_target_pairs={{0,4},{4,0},{8,12},{12,8},{16,20},{20,16},{24,28},{28,24},{1,5},{5... | collective-permute-start | bytes 73736 | tf_op jit(solution)/shard_map/ppermute | solution.py:139
  15.4 3.9 %collective-permute-start.5 = (f32[24,256]{1,0:T(8,128)S(1)}, f32[24,256]{1,0:T(8,128)S(1)}, u32[]{:S(2)}, u32[]{:S(2)}) collective-permute-start(f32[24,256]{1,0:T(8,128)S(1)} %pad_maximum_fusion.3), channel_id=1, source_target_pairs={{0,8},{4,12},{8,0},{12,4},{16,24},{20,28},{24,16},{28,20},{1,9},{5... | collective-permute-start | bytes 73736 | tf_op jit(solution)/shard_map/ppermute | solution.py:139
  19.3 5.0 %collective-permute-start.6 = (f32[36,256]{1,0:T(8,128)S(1)}, f32[36,256]{1,0:T(8,128)S(1)}, u32[]{:S(2)}, u32[]{:S(2)}) collective-permute-start(f32[36,256]{1,0:T(8,128)S(1)} %pad_maximum_fusion.1), channel_id=1, source_target_pairs={{0,16},{4,20},{8,24},{12,28},{16,0},{20,4},{24,8},{28,12},{1,17},{... | collective-permute-start | bytes 110600 | tf_op jit(solution)/shard_map/ppermute | solution.py:139
  22.3 3.8 %collective-permute-start.8 = (bf16[128,256]{1,0:T(8,128)(2,1)S(1)}, bf16[128,256]{1,0:T(8,128)(2,1)S(1)}, u32[]{:S(2)}, u32[]{:S(2)}) collective-permute-start(bf16[128,256]{1,0:T(8,128)(2,1)S(1)} %bitcast.10), channel_id=1, source_target_pairs={{0,1},{1,0},{2,3},{3,2},{4,5},{5,4},{6,7},{7,6},{8,9},{9,8},{10,11... | collective-permute-start | bytes 196616 | tf_op jit(solution)/shard_map/ppermute | solution.py:136
  22.3 3.8 %collective-permute-start.9 = (bf16[128,256]{1,0:T(8,128)(2,1)S(1)}, bf16[128,256]{1,0:T(8,128)(2,1)S(1)}, u32[]{:S(2)}, u32[]{:S(2)}) collective-permute-start(bf16[128,256]{1,0:T(8,128)(2,1)S(1)} %collective-permute-done.refs_1_), channel_id=1, source_target_pairs={{0,1},{1,0},{2,3},{3,2},{4,5},{5,4},{6,7},{7,6},{8,9},{9,8},{10,11... | collective-permute-start | bytes 196616 | tf_op jit(solution)/shard_map/ppermute | solution.py:136
  24.3 3.6 %collective-permute-start.7 = (f32[2,256]{1,0:T(2,128)S(1)}, f32[2,256]{1,0:T(2,128)S(1)}, u32[]{:S(2)}, u32[]{:S(2)}) collective-permute-start(f32[2,256]{1,0:T(2,128)S(1)} %get-tuple-element.6), channel_id=1, source_target_pairs={{0,2},{1,3},{2,0},{3,1},{4,6},{5,7},{6,4},{7,5},{8,10},{9,11},{10,... | collective-permute-start | bytes 6152 | tf_op jit(solution)/shard_map/ppermute | solution.py:136

commit v2 on v1

--- a/solution.py
+++ b/solution.py
@@ -28,6 +28,13 @@
     out = 0
     for bit in range(count):
         out = out | (((value >> bit) & 1) << (count - 1 - bit))
+    return out
+
+
+def parity(value, count):
+    out = value & 1
+    for bit in range(1, count):
+        out = out ^ ((value >> bit) & 1)
     return out
 
 
@@ -46,13 +53,14 @@
                 out_ref[h, pl.ds(first, group), :] = moved[h * group : (h + 1) * group, :]
 
 
-def partial_kernel(head_count, heads, owned, *refs):
+def partial_kernel(head_count, heads, owned, own_ref, other_ref, *refs):
     shard_refs, weight_ref, out_ref = refs[:-2], refs[-2], refs[-1]
-    shards = len(shard_refs)
+    shards = len(shard_refs) + 1
     me = lax.axis_index("head")
     bits = head_count.bit_length() - 1
     rows = head_count * owned
-    stacked = jnp.concatenate([ref[...] for ref in shard_refs], axis=0)
+    first = jnp.where(parity(me, bits) == 0, own_ref[...], other_ref[...])
+    stacked = jnp.concatenate([first] + [ref[...] for ref in shard_refs], axis=0)
     size = shards * rows * heads
     to, at = iota((size, size), 0), iota((size, size), 1)
     i, j = to % owned, (to // owned) % shards
@@ -67,9 +75,10 @@
     out_ref[...] = total
 
 
-def norm_kernel(columns, latent_ref, gain_ref, *out_refs):
-    column = lax.axis_index("ctx") >> 1
-    raw = latent_ref[...].astype(F32)
+def norm_kernel(columns, own_ref, other_ref, gain_ref, *out_refs):
+    core, column = lax.axis_index("ctx") & 1, lax.axis_index("ctx") >> 1
+    own, other = own_ref[...].astype(F32), other_ref[...].astype(F32)
+    raw = jnp.concatenate([jnp.where(core == 0, own, other), jnp.where(core == 0, other, own)], axis=0)
     rms = lax.rsqrt(jnp.mean(raw * raw, axis=1, keepdims=True) + 1e-06)
     normed = ((raw * rms) * gain_ref[...]).astype(BF16).astype(F32)
     width = normed.shape[1] // columns
@@ -84,6 +93,7 @@
     shard_refs, out_ref, scratch_ref = refs[:-2], refs[-2], refs[-1]
     me = lax.axis_index("head")
     core = lax.axis_index("ctx") & 1
+    role = core ^ parity(me, head_count.bit_length() - 1)
     rows = out_ref.shape[0] // heads
     tokens = head_count * owned
     normed = normed_ref[...].astype(BF16)
@@ -92,7 +102,7 @@
     token, j = (to // heads) % tokens, to // (heads * tokens)
     cots = []
     for side in range(2):
-        place = (((token // owned) ^ me) * 2 + (core ^ side)) * columns + j
+        place = (((token // owned) ^ me) * columns + j) * 2 + (jnp.where(j == 0, core, role) ^ side)
         spread = one_hot(at == place * owned + token % owned)
         scratch_ref[side] = matmul(normed, spread, 0, 0)
         cots.append(jnp.concatenate([r[...] for r in shard_refs[side * columns : (side + 1) * columns]], axis=0))
@@ -101,24 +111,28 @@
     for start in range(0, rows, group):
         total = None
         for side in range(2):
-            block = scratch_ref[side, pl.ds(pl.multiple_of(core * rows + start, group), group), :]
+            block = scratch_ref[side, start : start + group, :]
             left = jnp.where(keep, block[:, None, :], 0.0).reshape(group * heads, size).astype(BF16)
             part = matmul(left, cots[side])
             total = part if total is None else total + part
         out_ref[start * heads : (start + group) * heads, :] = total
 
 
-def latent_kernel(columns, latent_ref, gain_ref, *refs):
-    block_refs, out_ref = refs[:-1], refs[-1]
+def latent_kernel(head_count, columns, latent_ref, gain_ref, *refs):
+    block_refs, other_refs, out_ref = refs[:columns], refs[columns:-1], refs[-1]
     column = lax.axis_index("ctx") >> 1
+    odd = parity(lax.axis_index("head"), head_count.bit_length() - 1)
     raw = latent_ref[...].astype(F32)
     rms = lax.rsqrt(jnp.mean(raw * raw, axis=1, keepdims=True) + 1e-06)
     hat = raw * rms
+    relative = [ref[...] for ref in block_refs]
+    for j, ref in enumerate(other_refs):
+        relative[2 * j] = jnp.where(odd == 0, relative[2 * j], ref[...])
     blocks = []
     for b in range(columns):
-        block = block_refs[0][...]
+        block = relative[0]
         for j in range(1, columns):
-            block = jnp.where((column ^ j) == b, block_refs[j][...], block)
+            block = jnp.where((column ^ j) == b, relative[j], block)
         blocks.append(block)
     scaled = jnp.concatenate(blocks, axis=1) * gain_ref[...]
     inner = jnp.mean(scaled * hat, axis=1, keepdims=True)
@@ -130,13 +144,26 @@
     owned, width = latent.shape[1:]
     _, tokens, heads, channels = cotangent.shape
     rows = weight.shape[0]
+    bits = head_count.bit_length() - 1
     params = pltpu.CompilerParams(vmem_limit_bytes=48 * 1024 * 1024)
 
+    def swap(value, partner):
+        pairs = [
+            (h * ctx_count + c, p * ctx_count + q)
+            for h in range(head_count)
+            for c in range(ctx_count)
+            for p, q in [partner(h, c)]
+        ]
+        return lax.ppermute(value, ("head", "ctx"), pairs)
+
     def ctx_swap(value, mask):
-        return lax.ppermute(value, "ctx", [(i, i ^ mask) for i in range(ctx_count)])
+        return swap(value, lambda h, c: (h, c ^ mask))
+
+    def role_swap(value, mask):
+        return swap(value, lambda h, c: (h, c ^ mask ^ parity(h, bits)))
 
     def head_swap(value, mask):
-        return lax.ppermute(value, "head", [(i, i ^ mask) for i in range(head_count)])
+        return swap(value, lambda h, c: (h ^ mask, c ^ 1))
 
     def call(kernel, out, *args, scratch=(), flops=0):
         moved = sum(a.size * a.dtype.itemsize for a in args)
@@ -148,12 +175,17 @@
             cost_estimate=pl.CostEstimate(flops=flops, bytes_accessed=moved, transcendentals=0),
         )(*args)
 
-    flat = cotangent.reshape(tokens * heads, channels)
-    shards = [flat]
-    mask = 2
-    while mask < ctx_count:
-        shards += [ctx_swap(s, mask) for s in shards]
-        mask *= 2
+    own = cotangent.reshape(tokens * heads, channels)
+    far = [role_swap(own, 2)]
+    other = ctx_swap(own, 1)
+    if columns > 2:
+        first = jnp.where(parity(lax.axis_index("head"), bits) == 0, own, other)
+        shards = [first] + far
+        mask = 4
+        while mask < ctx_count:
+            shards += [ctx_swap(s, mask) for s in shards]
+            mask *= 2
+        far = shards[1:]
     weight_flat = weight.reshape(rows * heads, channels)
     weight_other = ctx_swap(weight_flat, 1)
     chip_weight = call(
@@ -164,57 +196,72 @@
     )
     gain_row = gain.reshape(1, width)
 
-    block = jax.ShapeDtypeStruct((owned, 2 * rows), F32)
-    normed = list(call(functools.partial(norm_kernel, columns), [block] * columns, latent[0], gain_row))
+    latent_other = ctx_swap(latent[0], 1)
+    latent_own, latent_other, chip_weight = lax.optimization_barrier((latent[0], latent_other, chip_weight))
+    block = jax.ShapeDtypeStruct((2 * owned, 2 * rows), F32)
+    normed = list(call(functools.partial(norm_kernel, columns), [block] * columns, latent_own, latent_other, gain_row))
     mask = 2
     while mask < ctx_count:
         for j in range(columns):
             if j & (mask >> 1):
-                normed[j] = ctx_swap(normed[j], mask)
+                normed[j] = ctx_swap(normed[j], mask | 1)
         mask *= 2
-    mine = jnp.concatenate(normed, axis=0)
-    theirs = ctx_swap(mine, 1)
-    core = lax.axis_index("ctx") & 1
-    normed = jnp.where(core == 0, jnp.concatenate([mine, theirs]), jnp.concatenate([theirs, mine]))
+    normed = jnp.concatenate(normed, axis=0)
 
     sums = call(
         functools.partial(partial_kernel, head_count, heads, owned),
         jax.ShapeDtypeStruct((head_count * columns * owned, 2 * rows), F32),
-        *shards,
+        own,
+        other,
+        *far,
         chip_weight,
     )
+    core = lax.axis_index("ctx") & 1
     mask = 1
     while mask < head_count:
         half = sums.shape[0] // 2
-        got = head_swap(jnp.concatenate([sums[half:], normed], axis=0), mask)
+        if 2 * mask < head_count:
+            got = head_swap(jnp.concatenate([sums[half:], normed], axis=0), mask)
+            normed = jnp.concatenate([normed, got[half:]], axis=0)
+        else:
+            keep = jnp.where(core == 0, normed[:, :rows], normed[:, rows:])
+            send = jnp.where(core == 0, normed[:, rows:], normed[:, :rows])
+            count = send.shape[0] // 2
+            send = jnp.concatenate([send[:count], send[count:]], axis=1)
+            got = head_swap(jnp.concatenate([sums[half:], send], axis=0), mask)
+            normed = jnp.concatenate([keep, got[half:, :rows], got[half:, rows:]], axis=0)
         sums = sums[:half] + got[:half]
-        normed = jnp.concatenate([normed, got[half:]], axis=0)
         mask *= 2
 
     blocks = [sums[j * owned : (j + 1) * owned] for j in range(columns)]
-    mask = 2
-    while mask < ctx_count:
+    mask = ctx_count // 2
+    while mask > 2:
         for j in range(columns):
             if j & (mask >> 1):
                 blocks[j] = ctx_swap(blocks[j], mask)
-        mask *= 2
-
-    others = [ctx_swap(s, 1) for s in shards]
+        mask //= 2
+    kept = [ctx_swap(blocks[j], 1) for j in range(0, columns, 2)]
+    for j in range(1, columns, 2):
+        blocks[j] = role_swap(blocks[j], 2)
+
     weight_grad = call(
         functools.partial(weight_grad_kernel, head_count, heads, owned, columns),
         jax.ShapeDtypeStruct((rows * heads, channels), F32),
         normed,
-        *shards,
-        *others,
-        scratch=[pltpu.VMEM((2, 2 * rows, columns * tokens * heads), F32)],
+        own,
+        *far,
+        other,
+        *[ctx_swap(s, 1) for s in far],
+        scratch=[pltpu.VMEM((2, rows, columns * tokens * heads), F32)],
         flops=2 * rows * heads * channels * ctx_count * tokens * heads,
     )
     latent_gradient = call(
-        functools.partial(latent_kernel, columns),
+        functools.partial(latent_kernel, head_count, columns),
         jax.ShapeDtypeStruct((owned, width), F32),
         latent[0],
         gain_row,
         *blocks,
+        *kept,
     )
     return latent_gradient[None], weight_grad.reshape(weight.shape)
 

time: 28.9 us -> 24.6 us (0.85)
  starting transfers between devices: 14.5 us -> 11.9 us
  waiting for transfers between devices: 8.67 us -> 6.93 us
    ppermute x10 -> x11, starting transfers between devices: 14.5 us -> 11.9 us  [swap(): return lax.ppermute(value, ('head', 'ctx'), pairs)]
    ppermute x10 -> x11, waiting for transfers between devices: 8.67 us -> 6.93 us  [swap(): return lax.ppermute(value, ('head', 'ctx'), pairs)]
  transfers between devices with their start and end apart: 10 -> 11, of which waited for: 6 -> 5; matrix products, arithmetic and copies ran while one was open for 0% -> 0% of each run, Pallas kernels for 8% -> 11%
where the time goes in v2:
time: 24.6 us; the launch traced here: 24.4 us
  starting transfers between devices  11.9 us (48%)
  waiting for transfers between devices  6.93 us (28%)
  Pallas kernels  3.4 us (14%)
  local copies, waits for them, and re-layouts  1.32 us (5%)
  between operations  0.75 us (3%)
    ppermute x11, starting transfers between devices, swap(): return lax.ppermute(value, ('head', 'ctx'), pairs)  11.9 us
    ppermute x11, waiting for transfers between devices, swap(): return lax.ppermute(value, ('head', 'ctx'), pairs)  6.93 us
    pallas_call x5, Pallas kernels, call(): pl.pallas_call(kernel, out_shape=out, scratch_shapes=scratch, compiler_pa...  3.4 us
    unnamed x8, local copies, waits for them, and re-layouts  1.27 us
  transfers between devices with their start and end apart: 11, of which 5 were waited for; matrix products, arithmetic and copies ran while one was open for 0% of the time, Pallas kernels for 11%

profile of v2, /device:TPU:0, one launch (start us, length us, event | category | flops | bytes accessed | tf_op | source)
XLA Modules:
  0.0 24.4 jit_solution(8427681064383577236)
XLA Ops:
  0.6 0.0 copy-start.2
  0.6 0.5 %collective-permute-start.3 = (bf16[1024,256]{1,0:T(8,128)(2,1)}, bf16[1024,256]{1,0:T(8,128)(2,1)S(1)}, u32[]{:S(2)}, u32[]{:S(2)}) collective-permute-start(bf16[1024,256]{1,0:T(8,128)(2,1)} %bitcast.6), channel_id=1, source_target_pairs={{0,1},{1,0},{2,3},{3,2},{4,5},{5,4},{6,7},{7,6},{8,9},{9,8},{10,11... | collective-permute-start | bytes 1572872 | tf_op jit(solution)/shard_map/ppermute | solution.py:157
  1.2 2.6 %collective-permute-start.1 = (bf16[128,256]{1,0:T(8,128)(2,1)}, bf16[128,256]{1,0:T(8,128)(2,1)S(1)}, u32[]{:S(2)}, u32[]{:S(2)}) collective-permute-start(bf16[128,256]{1,0:T(8,128)(2,1)} %bitcast.8), channel_id=1, source_target_pairs={{0,2},{1,3},{2,0},{3,1},{4,7},{5,6},{6,5},{7,4},{8,11},{9,10},{10,... | collective-permute-start | bytes 196616 | tf_op jit(solution)/shard_map/ppermute | solution.py:157
  3.7 0.2 collective-permute-start
  3.9 0.0 copy-done.2
  3.9 0.3 %collective-permute-start.2 = (bf16[2,512]{1,0:T(2,128)(2,1)S(1)}, bf16[2,512]{1,0:T(2,128)(2,1)S(1)}, u32[]{:S(2)}, u32[]{:S(2)}) collective-permute-start(bf16[2,512]{1,0:T(2,128)(2,1)S(1)} %bitcast.12), channel_id=1, source_target_pairs={{0,1},{1,0},{2,3},{3,2},{4,5},{5,4},{6,7},{7,6},{8,9},{9,8},{10,11... | collective-permute-start | bytes 6152 | tf_op jit(solution)/shard_map/ppermute | solution.py:157
  4.2 0.0 collective-permute-done.3.other_ref
  4.2 0.0 copy-start
  4.2 1.0 %copy-done = bf16[128,8,256]{2,1,0:T(8,128)(2,1)S(1)} copy-done((bf16[128,8,256]{2,1,0:T(8,128)(2,1)S(1)}, bf16[128,8,256]{2,1,0:T(8,128)(2,1)}, u32[]{:S(2)}) %copy-start) | copy-done | bytes 524312
  5.3 0.0 copy-start.3
  5.3 0.0 copy-start.1
  5.3 0.4 %shard_map.59.refs_1_ = bf16[8,256,256]{2,1,0:T(8,128)(2,1)S(1)} custom-call(bf16[1024,256]{1,0:T(8,128)(2,1)S(1)} %bitcast.7, bf16[1024,256]{1,0:T(8,128)(2,1)S(1)} %collective-permute-done.3.other_ref), custom_call_target="tpu_custom_call" | custom-call | bytes 1048576 | tf_op jit(solution)/shard_map/pallas_call | solution.py:170
  5.7 0.0 collective-permute-done.2.other_ref
  5.7 0.2 copy-done.3
  6.0 0.1 shard_map.61
  6.1 1.3 %collective-permute-start.4 = (f32[4,256]{1,0:T(4,128)S(1)}, f32[4,256]{1,0:T(4,128)S(1)}, u32[]{:S(2)}, u32[]{:S(2)}) collective-permute-start(f32[4,256]{1,0:T(4,128)S(1)} %get-tuple-element.11), channel_id=1, source_target_pairs={{0,3},{1,2},{2,1},{3,0},{4,7},{5,6},{6,5},{7,4},{8,11},{9,10},{10,... | collective-permute-start | bytes 12296 | tf_op jit(solution)/shard_map/ppermute | solution.py:157
  7.3 0.0 collective-permute-done.1.refs_0_.refs_1_
  7.3 0.0 collective-permute-done.other_ref.refs_2_
  7.3 0.0 copy-done.1
  7.3 0.5 %shard_map.60 = f32[32,256]{1,0:T(8,128)S(1)} custom-call(bf16[128,256]{1,0:T(8,128)(2,1)S(1)} %bitcast.10, bf16[128,256]{1,0:T(8,128)(2,1)S(1)} %collective-permute-done.other_ref.refs_2_, bf16[128,256]{1,0:T(8,128)(2,1)S(1)} %collective-permute-done.1.refs_0_.refs_1_, bf16[8,256,256]{2,1,0:T(8,128)(2,1)S(1)} %shard_map.59.refs_1_), custom_call_target="tpu_custom_call" | custom-call | bytes 1245184 | tf_op jit(solution)/shard_map/pallas_call | solution.py:170
  7.9 1.2 %collective-permute-done.4 = f32[4,256]{1,0:T(4,128)S(1)} collective-permute-done((f32[4,256]{1,0:T(4,128)S(1)}, f32[4,256]{1,0:T(4,128)S(1)}, u32[]{:S(2)}, u32[]{:S(2)}) %collective-permute-start.4) | collective-permute-done | bytes 4128 | tf_op jit(solution)/shard_map/ppermute | solution.py:157
  9.1 1.3 %collective-permute-start.5 = (f32[24,256]{1,0:T(8,128)S(1)}, f32[24,256]{1,0:T(8,128)S(1)}, u32[]{:S(2)}, u32[]{:S(2)}) collective-permute-start(f32[24,256]{1,0:T(8,128)S(1)} %pad_maximum_fusion.2), channel_id=1, source_target_pairs={{0,5},{1,4},{2,7},{3,6},{4,1},{5,0},{6,3},{7,2},{8,13},{9,12},{10,... | collective-permute-start | bytes 73736 | tf_op jit(solution)/shard_map/ppermute | solution.py:157
  10.4 2.0 %collective-permute-done.5 = f32[24,256]{1,0:T(8,128)S(1)} collective-permute-done((f32[24,256]{1,0:T(8,128)S(1)}, f32[24,256]{1,0:T(8,128)S(1)}, u32[]{:S(2)}, u32[]{:S(2)}) %collective-permute-start.5) | collective-permute-done | bytes 24608 | tf_op jit(solution)/shard_map/ppermute | solution.py:157
  12.4 1.4 %collective-permute-start.6 = (f32[24,256]{1,0:T(8,128)S(1)}, f32[24,256]{1,0:T(8,128)S(1)}, u32[]{:S(2)}, u32[]{:S(2)}) collective-permute-start(f32[24,256]{1,0:T(8,128)S(1)} %pad_maximum_fusion.3), channel_id=1, source_target_pairs={{0,9},{1,8},{2,11},{3,10},{4,13},{5,12},{6,15},{7,14},{8,1},{9,0},... | collective-permute-start | bytes 73736 | tf_op jit(solution)/shard_map/ppermute | solution.py:157
  13.8 1.9 %collective-permute-done.6 = f32[24,256]{1,0:T(8,128)S(1)} collective-permute-done((f32[24,256]{1,0:T(8,128)S(1)}, f32[24,256]{1,0:T(8,128)S(1)}, u32[]{:S(2)}, u32[]{:S(2)}) %collective-permute-start.6) | collective-permute-done | bytes 24608 | tf_op jit(solution)/shard_map/ppermute | solution.py:157
  15.8 2.4 %collective-permute-start.7 = (f32[20,256]{1,0:T(8,128)S(1)}, f32[20,256]{1,0:T(8,128)S(1)}, u32[]{:S(2)}, u32[]{:S(2)}) collective-permute-start(f32[20,256]{1,0:T(8,128)S(1)} %maximum_maximum_fusion), channel_id=1, source_target_pairs={{0,17},{1,16},{2,19},{3,18},{4,21},{5,20},{6,23},{7,22},{8,25},{9,... | collective-permute-start | bytes 61448 | tf_op jit(solution)/shard_map/ppermute | solution.py:157
  18.2 0.4 %collective-permute-start.10 = (bf16[128,256]{1,0:T(8,128)(2,1)S(1)}, bf16[128,256]{1,0:T(8,128)(2,1)S(1)}, u32[]{:S(2)}, u32[]{:S(2)}) collective-permute-start(bf16[128,256]{1,0:T(8,128)(2,1)S(1)} %collective-permute-done.1.refs_0_.refs_1_), channel_id=1, source_target_pairs={{0,1},{1,0},{2,3},{3,2},{4,5},{5,4},{6,7},{7,6},{8,9},{9,8},{10,11... | collective-permute-start | bytes 196616 | tf_op jit(solution)/shard_map/ppermute | solution.py:157
  18.6 1.4 %collective-permute-done.7 = f32[20,256]{1,0:T(8,128)S(1)} collective-permute-done((f32[20,256]{1,0:T(8,128)S(1)}, f32[20,256]{1,0:T(8,128)S(1)}, u32[]{:S(2)}, u32[]{:S(2)}) %collective-permute-start.7) | collective-permute-done | bytes 20512 | tf_op jit(solution)/shard_map/ppermute | solution.py:157
  20.0 1.5 %collective-permute-start.8 = (f32[2,256]{1,0:T(2,128)S(1)}, f32[2,256]{1,0:T(2,128)S(1)}, u32[]{:S(2)}, u32[]{:S(2)}) collective-permute-start(f32[2,256]{1,0:T(2,128)S(1)} %get-tuple-element.18), channel_id=1, source_target_pairs={{0,2},{1,3},{2,0},{3,1},{4,7},{5,6},{6,5},{7,4},{8,11},{9,10},{10,... | collective-permute-start | bytes 6152 | tf_op jit(solution)/shard_map/ppermute | solution.py:157
  21.5 0.0 collective-permute-start.9
  21.6 0.0 collective-permute-done.10.refs_3_
  21.6 1.6 %shard_map.63 = f32[1024,256]{1,0:T(8,128)} custom-call(f32[64,128]{1,0:T(8,128)S(1)} %pad_maximum_fusion.1.normed_ref, bf16[128,256]{1,0:T(8,128)(2,1)S(1)} %bitcast.11, bf16[128,256]{1,0:T(8,128)(2,1)S(1)} %collective-permute-done.1.refs_0_.refs_1_, bf16[128,256]{1,0:T(8,128)(2,1)S(1)} %collective-permute-done.other_ref.refs_2_, ...), custom_call_target="tpu_custom_call" | custom-call | flops 268435456 | bytes 294912 | tf_op jit(solution)/shard_map/pallas_call | solution.py:170
  23.1 0.4 %collective-permute-done.8.refs_1_ = f32[2,256]{1,0:T(2,128)S(1)} collective-permute-done((f32[2,256]{1,0:T(2,128)S(1)}, f32[2,256]{1,0:T(2,128)S(1)}, u32[]{:S(2)}, u32[]{:S(2)}) %collective-permute-start.8) | collective-permute-done | bytes 2080 | tf_op jit(solution)/shard_map/ppermute | solution.py:157
  23.6 0.0 collective-permute-done.9.refs_2_
  23.6 0.8 %shard_map.62 = f32[2,512]{1,0:T(2,128)} custom-call(bf16[2,512]{1,0:T(2,128)(2,1)S(1)} %bitcast.14, f32[1,512]{1,0:T(1,128)S(1)} %bitcast.16, f32[2,256]{1,0:T(2,128)S(1)} %get-tuple-element.19.refs_0_, f32[2,256]{1,0:T(2,128)S(1)} %collective-permute-done.8.refs_1_, f32[2,256]{1,0:T(2,128)S(1)} %collective-permute-done.9.refs_2_), custom_call_target="tpu_custom_call" | custom-call | bytes 10240 | tf_op jit(solution)/shard_map/pallas_call | solution.py:170
  (17 shorter events, 0.1 us)
Async XLA Ops:
  0.6 3.3 %copy-start.2 = (bf16[1,2,512]{2,1,0:T(2,128)(2,1)S(1)}, bf16[1,2,512]{2,1,0:T(2,128)(2,1)}, u32[]{:S(2)}) copy-start(bf16[1,2,512]{2,1,0:T(2,128)(2,1)} %param.4) | copy-start | bytes 6148
  0.6 3.6 %collective-permute-start.3 = (bf16[1024,256]{1,0:T(8,128)(2,1)}, bf16[1024,256]{1,0:T(8,128)(2,1)S(1)}, u32[]{:S(2)}, u32[]{:S(2)}) collective-permute-start(bf16[1024,256]{1,0:T(8,128)(2,1)} %bitcast.6), channel_id=1, source_target_pairs={{0,1},{1,0},{2,3},{3,2},{4,5},{5,4},{6,7},{7,6},{8,9},{9,8},{10,11... | collective-permute-start | bytes 1572872 | tf_op jit(solution)/shard_map/ppermute | solution.py:157
  1.2 6.2 %collective-permute-start.1 = (bf16[128,256]{1,0:T(8,128)(2,1)}, bf16[128,256]{1,0:T(8,128)(2,1)S(1)}, u32[]{:S(2)}, u32[]{:S(2)}) collective-permute-start(bf16[128,256]{1,0:T(8,128)(2,1)} %bitcast.8), channel_id=1, source_target_pairs={{0,2},{1,3},{2,0},{3,1},{4,7},{5,6},{6,5},{7,4},{8,11},{9,10},{10,... | collective-permute-start | bytes 196616 | tf_op jit(solution)/shard_map/ppermute | solution.py:157
  3.7 3.6 %collective-permute-start = (bf16[128,256]{1,0:T(8,128)(2,1)}, bf16[128,256]{1,0:T(8,128)(2,1)S(1)}, u32[]{:S(2)}, u32[]{:S(2)}) collective-permute-start(bf16[128,256]{1,0:T(8,128)(2,1)} %bitcast.9), channel_id=1, source_target_pairs={{0,1},{1,0},{2,3},{3,2},{4,5},{5,4},{6,7},{7,6},{8,9},{9,8},{10,11... | collective-permute-start | bytes 196616 | tf_op jit(solution)/shard_map/ppermute | solution.py:157
  3.9 1.8 %collective-permute-start.2 = (bf16[2,512]{1,0:T(2,128)(2,1)S(1)}, bf16[2,512]{1,0:T(2,128)(2,1)S(1)}, u32[]{:S(2)}, u32[]{:S(2)}) collective-permute-start(bf16[2,512]{1,0:T(2,128)(2,1)S(1)} %bitcast.12), channel_id=1, source_target_pairs={{0,1},{1,0},{2,3},{3,2},{4,5},{5,4},{6,7},{7,6},{8,9},{9,8},{10,11... | collective-permute-start | bytes 6152 | tf_op jit(solution)/shard_map/ppermute | solution.py:157
  4.2 1.0 %copy-start = (bf16[128,8,256]{2,1,0:T(8,128)(2,1)S(1)}, bf16[128,8,256]{2,1,0:T(8,128)(2,1)}, u32[]{:S(2)}) copy-start(bf16[128,8,256]{2,1,0:T(8,128)(2,1)} %param.7) | copy-start | bytes 1572868
  5.3 0.7 %copy-start.3 = (f32[512]{0:T(512)S(1)}, f32[512]{0:T(512)}, u32[]{:S(2)}) copy-start(f32[512]{0:T(512)} %param.5) | copy-start | bytes 6148
  5.3 2.1 %copy-start.1 = (bf16[1,16,8,256]{3,2,1,0:T(8,128)(2,1)S(1)}, bf16[1,16,8,256]{3,2,1,0:T(8,128)(2,1)}, u32[]{:S(2)}) copy-start(bf16[1,16,8,256]{3,2,1,0:T(8,128)(2,1)} %param.6) | copy-start | bytes 196612
  6.1 3.0 %collective-permute-start.4 = (f32[4,256]{1,0:T(4,128)S(1)}, f32[4,256]{1,0:T(4,128)S(1)}, u32[]{:S(2)}, u32[]{:S(2)}) collective-permute-start(f32[4,256]{1,0:T(4,128)S(1)} %get-tuple-element.11), channel_id=1, source_target_pairs={{0,3},{1,2},{2,1},{3,0},{4,7},{5,6},{6,5},{7,4},{8,11},{9,10},{10,... | collective-permute-start | bytes 12296 | tf_op jit(solution)/shard_map/ppermute | solution.py:157
  9.1 3.3 %collective-permute-start.5 = (f32[24,256]{1,0:T(8,128)S(1)}, f32[24,256]{1,0:T(8,128)S(1)}, u32[]{:S(2)}, u32[]{:S(2)}) collective-permute-start(f32[24,256]{1,0:T(8,128)S(1)} %pad_maximum_fusion.2), channel_id=1, source_target_pairs={{0,5},{1,4},{2,7},{3,6},{4,1},{5,0},{6,3},{7,2},{8,13},{9,12},{10,... | collective-permute-start | bytes 73736 | tf_op jit(solution)/shard_map/ppermute | solution.py:157
  12.4 3.3 %collective-permute-start.6 = (f32[24,256]{1,0:T(8,128)S(1)}, f32[24,256]{1,0:T(8,128)S(1)}, u32[]{:S(2)}, u32[]{:S(2)}) collective-permute-start(f32[24,256]{1,0:T(8,128)S(1)} %pad_maximum_fusion.3), channel_id=1, source_target_pairs={{0,9},{1,8},{2,11},{3,10},{4,13},{5,12},{6,15},{7,14},{8,1},{9,0},... | collective-permute-start | bytes 73736 | tf_op jit(solution)/shard_map/ppermute | solution.py:157
  15.8 4.2 %collective-permute-start.7 = (f32[20,256]{1,0:T(8,128)S(1)}, f32[20,256]{1,0:T(8,128)S(1)}, u32[]{:S(2)}, u32[]{:S(2)}) collective-permute-start(f32[20,256]{1,0:T(8,128)S(1)} %maximum_maximum_fusion), channel_id=1, source_target_pairs={{0,17},{1,16},{2,19},{3,18},{4,21},{5,20},{6,23},{7,22},{8,25},{9,... | collective-permute-start | bytes 61448 | tf_op jit(solution)/shard_map/ppermute | solution.py:157
  18.2 3.4 %collective-permute-start.10 = (bf16[128,256]{1,0:T(8,128)(2,1)S(1)}, bf16[128,256]{1,0:T(8,128)(2,1)S(1)}, u32[]{:S(2)}, u32[]{:S(2)}) collective-permute-start(bf16[128,256]{1,0:T(8,128)(2,1)S(1)} %collective-permute-done.1.refs_0_.refs_1_), channel_id=1, source_target_pairs={{0,1},{1,0},{2,3},{3,2},{4,5},{5,4},{6,7},{7,6},{8,9},{9,8},{10,11... | collective-permute-start | bytes 196616 | tf_op jit(solution)/shard_map/ppermute | solution.py:157
  20.0 3.6 %collective-permute-start.8 = (f32[2,256]{1,0:T(2,128)S(1)}, f32[2,256]{1,0:T(2,128)S(1)}, u32[]{:S(2)}, u32[]{:S(2)}) collective-permute-start(f32[2,256]{1,0:T(2,128)S(1)} %get-tuple-element.18), channel_id=1, source_target_pairs={{0,2},{1,3},{2,0},{3,1},{4,7},{5,6},{6,5},{7,4},{8,11},{9,10},{10,... | collective-permute-start | bytes 6152 | tf_op jit(solution)/shard_map/ppermute | solution.py:157
  21.5 2.1 %collective-permute-start.9 = (f32[2,256]{1,0:T(2,128)S(1)}, f32[2,256]{1,0:T(2,128)S(1)}, u32[]{:S(2)}, u32[]{:S(2)}) collective-permute-start(f32[2,256]{1,0:T(2,128)S(1)} %get-tuple-element.19.refs_0_), channel_id=1, source_target_pairs={{0,1},{1,0},{2,3},{3,2},{4,5},{5,4},{6,7},{7,6},{8,9},{9,8},{10,11... | collective-permute-start | bytes 6152 | tf_op jit(solution)/shard_map/ppermute | solution.py:157

commit v3 on v2

--- a/solution.py
+++ b/solution.py
@@ -186,20 +186,21 @@
             shards += [ctx_swap(s, mask) for s in shards]
             mask *= 2
         far = shards[1:]
+    latent_other = ctx_swap(latent[0], 1)
+    gain_row = gain.reshape(1, width)
+    block = jax.ShapeDtypeStruct((2 * owned, 2 * rows), F32)
+    normed = list(call(functools.partial(norm_kernel, columns), [block] * columns, latent[0], latent_other, gain_row))
+
     weight_flat = weight.reshape(rows * heads, channels)
     weight_other = ctx_swap(weight_flat, 1)
+    weight_flat, weight_other, *normed = lax.optimization_barrier((weight_flat, weight_other, *normed))
     chip_weight = call(
         functools.partial(weight_kernel, heads),
         jax.ShapeDtypeStruct((heads, 2 * rows, channels), BF16),
         weight_flat,
         weight_other,
     )
-    gain_row = gain.reshape(1, width)
-
-    latent_other = ctx_swap(latent[0], 1)
-    latent_own, latent_other, chip_weight = lax.optimization_barrier((latent[0], latent_other, chip_weight))
-    block = jax.ShapeDtypeStruct((2 * owned, 2 * rows), F32)
-    normed = list(call(functools.partial(norm_kernel, columns), [block] * columns, latent_own, latent_other, gain_row))
+
     mask = 2
     while mask < ctx_count:
         for j in range(columns):

time: 24.6 us -> 23.8 us (0.967)
  starting transfers between devices: 11.9 us -> 11.3 us
  waiting for transfers between devices: 6.93 us -> 6.55 us
    ppermute x11, starting transfers between devices: 11.9 us -> 11.3 us  [swap(): return lax.ppermute(value, ('head', 'ctx'), pairs)]
    ppermute x11, waiting for transfers between devices: 6.93 us -> 6.55 us  [swap(): return lax.ppermute(value, ('head', 'ctx'), pairs)]
  transfers between devices with their start and end apart: 11 -> 11, of which waited for: 5 -> 6; matrix products, arithmetic and copies ran while one was open for 0% -> 0% of each run, Pallas kernels for 11% -> 11%
where the time goes in v3:
time: 23.8 us; the launch traced here: 23.5 us
  starting transfers between devices  11.3 us (47%)
  waiting for transfers between devices  6.55 us (28%)
  Pallas kernels  3.39 us (14%)
  local copies, waits for them, and re-layouts  1.47 us (6%)
  between operations  0.75 us (3%)
    ppermute x11, starting transfers between devices, swap(): return lax.ppermute(value, ('head', 'ctx'), pairs)  11.3 us
    ppermute x11, waiting for transfers between devices, swap(): return lax.ppermute(value, ('head', 'ctx'), pairs)  6.55 us
    pallas_call x5, Pallas kernels, call(): pl.pallas_call(kernel, out_shape=out, scratch_shapes=scratch, compiler_pa...  3.39 us
    unnamed x8, local copies, waits for them, and re-layouts  1.42 us
  transfers between devices with their start and end apart: 11, of which 6 were waited for; matrix products, arithmetic and copies ran while one was open for 0% of the time, Pallas kernels for 11%

profile of v3, /device:TPU:0, one launch (start us, length us, event | category | flops | bytes accessed | tf_op | source)
XLA Modules:
  0.0 23.5 jit_solution(813928039895936853)
XLA Ops:
  0.6 0.0 copy-start.2
  0.6 0.5 %collective-permute-start.2 = (bf16[1024,256]{1,0:T(8,128)(2,1)}, bf16[1024,256]{1,0:T(8,128)(2,1)S(1)}, u32[]{:S(2)}, u32[]{:S(2)}) collective-permute-start(bf16[1024,256]{1,0:T(8,128)(2,1)} %bitcast.6), channel_id=1, source_target_pairs={{0,1},{1,0},{2,3},{3,2},{4,5},{5,4},{6,7},{7,6},{8,9},{9,8},{10,11... | collective-permute-start | bytes 1572872 | tf_op jit(solution)/shard_map/ppermute | solution.py:157
  1.2 0.0 copy-start.3
  1.2 2.6 %collective-permute-start.1 = (bf16[128,256]{1,0:T(8,128)(2,1)}, bf16[128,256]{1,0:T(8,128)(2,1)S(1)}, u32[]{:S(2)}, u32[]{:S(2)}) collective-permute-start(bf16[128,256]{1,0:T(8,128)(2,1)} %bitcast.8), channel_id=1, source_target_pairs={{0,2},{1,3},{2,0},{3,1},{4,7},{5,6},{6,5},{7,4},{8,11},{9,10},{10,... | collective-permute-start | bytes 196616 | tf_op jit(solution)/shard_map/ppermute | solution.py:157
  3.7 0.2 collective-permute-start
  3.9 0.0 copy-done.2
  3.9 0.4 %collective-permute-start.3 = (bf16[2,512]{1,0:T(2,128)(2,1)S(1)}, bf16[2,512]{1,0:T(2,128)(2,1)S(1)}, u32[]{:S(2)}, u32[]{:S(2)}) collective-permute-start(bf16[2,512]{1,0:T(2,128)(2,1)S(1)} %bitcast.12), channel_id=1, source_target_pairs={{0,1},{1,0},{2,3},{3,2},{4,5},{5,4},{6,7},{7,6},{8,9},{9,8},{10,11... | collective-permute-start | bytes 6152 | tf_op jit(solution)/shard_map/ppermute | solution.py:157
  4.2 0.8 %collective-permute-done.3.other_ref = bf16[2,512]{1,0:T(2,128)(2,1)S(1)} collective-permute-done((bf16[2,512]{1,0:T(2,128)(2,1)S(1)}, bf16[2,512]{1,0:T(2,128)(2,1)S(1)}, u32[]{:S(2)}, u32[]{:S(2)}) %collective-permute-start.3) | collective-permute-done | bytes 2080 | tf_op jit(solution)/shard_map/ppermute | solution.py:157
  5.1 0.0 copy-done.3
  5.1 0.1 shard_map.59
  5.2 0.0 collective-permute-done.2.other_ref
  5.2 0.3 %collective-permute-start.4 = (f32[4,256]{1,0:T(4,128)S(1)}, f32[4,256]{1,0:T(4,128)S(1)}, u32[]{:S(2)}, u32[]{:S(2)}) collective-permute-start(f32[4,256]{1,0:T(4,128)S(1)} %get-tuple-element.13), channel_id=1, source_target_pairs={{0,3},{1,2},{2,1},{3,0},{4,7},{5,6},{6,5},{7,4},{8,11},{9,10},{10,... | collective-permute-start | bytes 12296 | tf_op jit(solution)/shard_map/ppermute | solution.py:157
  5.5 0.0 copy-start
  5.5 1.0 %copy-done = bf16[128,8,256]{2,1,0:T(8,128)(2,1)S(1)} copy-done((bf16[128,8,256]{2,1,0:T(8,128)(2,1)S(1)}, bf16[128,8,256]{2,1,0:T(8,128)(2,1)}, u32[]{:S(2)}) %copy-start) | copy-done | bytes 524312
  6.5 0.0 copy-start.1
  6.6 0.4 %shard_map.60.refs_1_ = bf16[8,256,256]{2,1,0:T(8,128)(2,1)S(1)} custom-call(bf16[1024,256]{1,0:T(8,128)(2,1)S(1)} %bitcast.7, bf16[1024,256]{1,0:T(8,128)(2,1)S(1)} %collective-permute-done.2.other_ref), custom_call_target="tpu_custom_call" | custom-call | bytes 1048576 | tf_op jit(solution)/shard_map/pallas_call | solution.py:170
  7.0 0.0 collective-permute-done.1.refs_0_.refs_1_
  7.0 0.0 collective-permute-done.other_ref.refs_2_
  7.0 0.4 %copy-done.1 = bf16[1,16,8,256]{3,2,1,0:T(8,128)(2,1)S(1)} copy-done((bf16[1,16,8,256]{3,2,1,0:T(8,128)(2,1)S(1)}, bf16[1,16,8,256]{3,2,1,0:T(8,128)(2,1)}, u32[]{:S(2)}) %copy-start.1) | copy-done | bytes 65560
  7.4 0.5 %shard_map.61 = f32[32,256]{1,0:T(8,128)S(1)} custom-call(bf16[128,256]{1,0:T(8,128)(2,1)S(1)} %bitcast.10, bf16[128,256]{1,0:T(8,128)(2,1)S(1)} %collective-permute-done.other_ref.refs_2_, bf16[128,256]{1,0:T(8,128)(2,1)S(1)} %collective-permute-done.1.refs_0_.refs_1_, bf16[8,256,256]{2,1,0:T(8,128)(2,1)S(1)} %shard_map.60.refs_1_), custom_call_target="tpu_custom_call" | custom-call | bytes 1245184 | tf_op jit(solution)/shard_map/pallas_call | solution.py:170
  7.9 0.3 %collective-permute-done.4 = f32[4,256]{1,0:T(4,128)S(1)} collective-permute-done((f32[4,256]{1,0:T(4,128)S(1)}, f32[4,256]{1,0:T(4,128)S(1)}, u32[]{:S(2)}, u32[]{:S(2)}) %collective-permute-start.4) | collective-permute-done | bytes 4128 | tf_op jit(solution)/shard_map/ppermute | solution.py:157
  8.3 1.5 %collective-permute-start.5 = (f32[24,256]{1,0:T(8,128)S(1)}, f32[24,256]{1,0:T(8,128)S(1)}, u32[]{:S(2)}, u32[]{:S(2)}) collective-permute-start(f32[24,256]{1,0:T(8,128)S(1)} %pad_maximum_fusion.2), channel_id=1, source_target_pairs={{0,5},{1,4},{2,7},{3,6},{4,1},{5,0},{6,3},{7,2},{8,13},{9,12},{10,... | collective-permute-start | bytes 73736 | tf_op jit(solution)/shard_map/ppermute | solution.py:157
  9.8 1.8 %collective-permute-done.5 = f32[24,256]{1,0:T(8,128)S(1)} collective-permute-done((f32[24,256]{1,0:T(8,128)S(1)}, f32[24,256]{1,0:T(8,128)S(1)}, u32[]{:S(2)}, u32[]{:S(2)}) %collective-permute-start.5) | collective-permute-done | bytes 24608 | tf_op jit(solution)/shard_map/ppermute | solution.py:157
  11.6 1.6 %collective-permute-start.6 = (f32[24,256]{1,0:T(8,128)S(1)}, f32[24,256]{1,0:T(8,128)S(1)}, u32[]{:S(2)}, u32[]{:S(2)}) collective-permute-start(f32[24,256]{1,0:T(8,128)S(1)} %pad_maximum_fusion.3), channel_id=1, source_target_pairs={{0,9},{1,8},{2,11},{3,10},{4,13},{5,12},{6,15},{7,14},{8,1},{9,0},... | collective-permute-start | bytes 73736 | tf_op jit(solution)/shard_map/ppermute | solution.py:157
  13.2 1.7 %collective-permute-done.6 = f32[24,256]{1,0:T(8,128)S(1)} collective-permute-done((f32[24,256]{1,0:T(8,128)S(1)}, f32[24,256]{1,0:T(8,128)S(1)}, u32[]{:S(2)}, u32[]{:S(2)}) %collective-permute-start.6) | collective-permute-done | bytes 24608 | tf_op jit(solution)/shard_map/ppermute | solution.py:157
  14.9 2.6 %collective-permute-start.7 = (f32[20,256]{1,0:T(8,128)S(1)}, f32[20,256]{1,0:T(8,128)S(1)}, u32[]{:S(2)}, u32[]{:S(2)}) collective-permute-start(f32[20,256]{1,0:T(8,128)S(1)} %maximum_maximum_fusion), channel_id=1, source_target_pairs={{0,17},{1,16},{2,19},{3,18},{4,21},{5,20},{6,23},{7,22},{8,25},{9,... | collective-permute-start | bytes 61448 | tf_op jit(solution)/shard_map/ppermute | solution.py:157
  17.6 0.2 collective-permute-start.10
  17.8 1.4 %collective-permute-done.7 = f32[20,256]{1,0:T(8,128)S(1)} collective-permute-done((f32[20,256]{1,0:T(8,128)S(1)}, f32[20,256]{1,0:T(8,128)S(1)}, u32[]{:S(2)}, u32[]{:S(2)}) %collective-permute-start.7) | collective-permute-done | bytes 20512 | tf_op jit(solution)/shard_map/ppermute | solution.py:157
  19.2 1.4 %collective-permute-start.8 = (f32[2,256]{1,0:T(2,128)S(1)}, f32[2,256]{1,0:T(2,128)S(1)}, u32[]{:S(2)}, u32[]{:S(2)}) collective-permute-start(f32[2,256]{1,0:T(2,128)S(1)} %get-tuple-element.20), channel_id=1, source_target_pairs={{0,2},{1,3},{2,0},{3,1},{4,7},{5,6},{6,5},{7,4},{8,11},{9,10},{10,... | collective-permute-start | bytes 6152 | tf_op jit(solution)/shard_map/ppermute | solution.py:157
  20.6 0.0 collective-permute-start.9
  20.6 0.0 collective-permute-done.10.refs_3_
  20.6 1.6 %shard_map.63 = f32[1024,256]{1,0:T(8,128)} custom-call(f32[64,128]{1,0:T(8,128)S(1)} %pad_maximum_fusion.1.normed_ref, bf16[128,256]{1,0:T(8,128)(2,1)S(1)} %bitcast.11, bf16[128,256]{1,0:T(8,128)(2,1)S(1)} %collective-permute-done.1.refs_0_.refs_1_, bf16[128,256]{1,0:T(8,128)(2,1)S(1)} %collective-permute-done.other_ref.refs_2_, ...), custom_call_target="tpu_custom_call" | custom-call | flops 268435456 | bytes 294912 | tf_op jit(solution)/shard_map/pallas_call | solution.py:170
  22.2 0.5 %collective-permute-done.8.refs_1_ = f32[2,256]{1,0:T(2,128)S(1)} collective-permute-done((f32[2,256]{1,0:T(2,128)S(1)}, f32[2,256]{1,0:T(2,128)S(1)}, u32[]{:S(2)}, u32[]{:S(2)}) %collective-permute-start.8) | collective-permute-done | bytes 2080 | tf_op jit(solution)/shard_map/ppermute | solution.py:157
  22.8 0.0 collective-permute-done.9.refs_2_
  22.8 0.8 %shard_map.62 = f32[2,512]{1,0:T(2,128)} custom-call(bf16[2,512]{1,0:T(2,128)(2,1)S(1)} %bitcast.14, f32[1,512]{1,0:T(1,128)S(1)} %bitcast.16, f32[2,256]{1,0:T(2,128)S(1)} %get-tuple-element.21.refs_0_, f32[2,256]{1,0:T(2,128)S(1)} %collective-permute-done.8.refs_1_, f32[2,256]{1,0:T(2,128)S(1)} %collective-permute-done.9.refs_2_), custom_call_target="tpu_custom_call" | custom-call | bytes 10240 | tf_op jit(solution)/shard_map/pallas_call | solution.py:170
  (17 shorter events, 0.1 us)
Async XLA Ops:
  0.6 3.3 %copy-start.2 = (bf16[1,2,512]{2,1,0:T(2,128)(2,1)S(1)}, bf16[1,2,512]{2,1,0:T(2,128)(2,1)}, u32[]{:S(2)}) copy-start(bf16[1,2,512]{2,1,0:T(2,128)(2,1)} %param.4) | copy-start | bytes 6148
  0.6 4.5 %collective-permute-start.2 = (bf16[1024,256]{1,0:T(8,128)(2,1)}, bf16[1024,256]{1,0:T(8,128)(2,1)S(1)}, u32[]{:S(2)}, u32[]{:S(2)}) collective-permute-start(bf16[1024,256]{1,0:T(8,128)(2,1)} %bitcast.6), channel_id=1, source_target_pairs={{0,1},{1,0},{2,3},{3,2},{4,5},{5,4},{6,7},{7,6},{8,9},{9,8},{10,11... | collective-permute-start | bytes 1572872 | tf_op jit(solution)/shard_map/ppermute | solution.py:157
  1.2 3.9 %copy-start.3 = (f32[512]{0:T(512)S(1)}, f32[512]{0:T(512)}, u32[]{:S(2)}) copy-start(f32[512]{0:T(512)} %param.5) | copy-start | bytes 6148
  1.2 5.8 %collective-permute-start.1 = (bf16[128,256]{1,0:T(8,128)(2,1)}, bf16[128,256]{1,0:T(8,128)(2,1)S(1)}, u32[]{:S(2)}, u32[]{:S(2)}) collective-permute-start(bf16[128,256]{1,0:T(8,128)(2,1)} %bitcast.8), channel_id=1, source_target_pairs={{0,2},{1,3},{2,0},{3,1},{4,7},{5,6},{6,5},{7,4},{8,11},{9,10},{10,... | collective-permute-start | bytes 196616 | tf_op jit(solution)/shard_map/ppermute | solution.py:157
  3.7 3.3 %collective-permute-start = (bf16[128,256]{1,0:T(8,128)(2,1)}, bf16[128,256]{1,0:T(8,128)(2,1)S(1)}, u32[]{:S(2)}, u32[]{:S(2)}) collective-permute-start(bf16[128,256]{1,0:T(8,128)(2,1)} %bitcast.9), channel_id=1, source_target_pairs={{0,1},{1,0},{2,3},{3,2},{4,5},{5,4},{6,7},{7,6},{8,9},{9,8},{10,11... | collective-permute-start | bytes 196616 | tf_op jit(solution)/shard_map/ppermute | solution.py:157
  3.9 1.2 %collective-permute-start.3 = (bf16[2,512]{1,0:T(2,128)(2,1)S(1)}, bf16[2,512]{1,0:T(2,128)(2,1)S(1)}, u32[]{:S(2)}, u32[]{:S(2)}) collective-permute-start(bf16[2,512]{1,0:T(2,128)(2,1)S(1)} %bitcast.12), channel_id=1, source_target_pairs={{0,1},{1,0},{2,3},{3,2},{4,5},{5,4},{6,7},{7,6},{8,9},{9,8},{10,11... | collective-permute-start | bytes 6152 | tf_op jit(solution)/shard_map/ppermute | solution.py:157
  5.2 3.1 %collective-permute-start.4 = (f32[4,256]{1,0:T(4,128)S(1)}, f32[4,256]{1,0:T(4,128)S(1)}, u32[]{:S(2)}, u32[]{:S(2)}) collective-permute-start(f32[4,256]{1,0:T(4,128)S(1)} %get-tuple-element.13), channel_id=1, source_target_pairs={{0,3},{1,2},{2,1},{3,0},{4,7},{5,6},{6,5},{7,4},{8,11},{9,10},{10,... | collective-permute-start | bytes 12296 | tf_op jit(solution)/shard_map/ppermute | solution.py:157
  5.5 1.0 %copy-start = (bf16[128,8,256]{2,1,0:T(8,128)(2,1)S(1)}, bf16[128,8,256]{2,1,0:T(8,128)(2,1)}, u32[]{:S(2)}) copy-start(bf16[128,8,256]{2,1,0:T(8,128)(2,1)} %param.7) | copy-start | bytes 1572868
  6.5 0.8 %copy-start.1 = (bf16[1,16,8,256]{3,2,1,0:T(8,128)(2,1)S(1)}, bf16[1,16,8,256]{3,2,1,0:T(8,128)(2,1)}, u32[]{:S(2)}) copy-start(bf16[1,16,8,256]{3,2,1,0:T(8,128)(2,1)} %param.6) | copy-start | bytes 196612
  8.3 3.3 %collective-permute-start.5 = (f32[24,256]{1,0:T(8,128)S(1)}, f32[24,256]{1,0:T(8,128)S(1)}, u32[]{:S(2)}, u32[]{:S(2)}) collective-permute-start(f32[24,256]{1,0:T(8,128)S(1)} %pad_maximum_fusion.2), channel_id=1, source_target_pairs={{0,5},{1,4},{2,7},{3,6},{4,1},{5,0},{6,3},{7,2},{8,13},{9,12},{10,... | collective-permute-start | bytes 73736 | tf_op jit(solution)/shard_map/ppermute | solution.py:157
  11.6 3.3 %collective-permute-start.6 = (f32[24,256]{1,0:T(8,128)S(1)}, f32[24,256]{1,0:T(8,128)S(1)}, u32[]{:S(2)}, u32[]{:S(2)}) collective-permute-start(f32[24,256]{1,0:T(8,128)S(1)} %pad_maximum_fusion.3), channel_id=1, source_target_pairs={{0,9},{1,8},{2,11},{3,10},{4,13},{5,12},{6,15},{7,14},{8,1},{9,0},... | collective-permute-start | bytes 73736 | tf_op jit(solution)/shard_map/ppermute | solution.py:157
  14.9 4.2 %collective-permute-start.7 = (f32[20,256]{1,0:T(8,128)S(1)}, f32[20,256]{1,0:T(8,128)S(1)}, u32[]{:S(2)}, u32[]{:S(2)}) collective-permute-start(f32[20,256]{1,0:T(8,128)S(1)} %maximum_maximum_fusion), channel_id=1, source_target_pairs={{0,17},{1,16},{2,19},{3,18},{4,21},{5,20},{6,23},{7,22},{8,25},{9,... | collective-permute-start | bytes 61448 | tf_op jit(solution)/shard_map/ppermute | solution.py:157
  17.6 3.0 %collective-permute-start.10 = (bf16[128,256]{1,0:T(8,128)(2,1)S(1)}, bf16[128,256]{1,0:T(8,128)(2,1)S(1)}, u32[]{:S(2)}, u32[]{:S(2)}) collective-permute-start(bf16[128,256]{1,0:T(8,128)(2,1)S(1)} %collective-permute-done.1.refs_0_.refs_1_), channel_id=1, source_target_pairs={{0,1},{1,0},{2,3},{3,2},{4,5},{5,4},{6,7},{7,6},{8,9},{9,8},{10,11... | collective-permute-start | bytes 196616 | tf_op jit(solution)/shard_map/ppermute | solution.py:157
  19.2 3.6 %collective-permute-start.8 = (f32[2,256]{1,0:T(2,128)S(1)}, f32[2,256]{1,0:T(2,128)S(1)}, u32[]{:S(2)}, u32[]{:S(2)}) collective-permute-start(f32[2,256]{1,0:T(2,128)S(1)} %get-tuple-element.20), channel_id=1, source_target_pairs={{0,2},{1,3},{2,0},{3,1},{4,7},{5,6},{6,5},{7,4},{8,11},{9,10},{10,... | collective-permute-start | bytes 6152 | tf_op jit(solution)/shard_map/ppermute | solution.py:157
  20.6 2.2 %collective-permute-start.9 = (f32[2,256]{1,0:T(2,128)S(1)}, f32[2,256]{1,0:T(2,128)S(1)}, u32[]{:S(2)}, u32[]{:S(2)}) collective-permute-start(f32[2,256]{1,0:T(2,128)S(1)} %get-tuple-element.21.refs_0_), channel_id=1, source_target_pairs={{0,1},{1,0},{2,3},{3,2},{4,5},{5,4},{6,7},{7,6},{8,9},{9,8},{10,11... | collective-permute-start | bytes 6152 | tf_op jit(solution)/shard_map/ppermute | solution.py:157

commit v4 on v3

--- a/solution.py
+++ b/solution.py
@@ -11,18 +11,14 @@
 F32 = jnp.float32
 BF16 = jnp.bfloat16
 
-
 def iota(shape, axis):
     return lax.broadcasted_iota(jnp.int32, shape, axis)
 
-
 def one_hot(condition):
     return jnp.where(condition, 1.0, 0.0).astype(BF16)
 
-
 def matmul(a, b, a_axis=1, b_axis=0):
     return lax.dot_general(a, b, (((a_axis,), (b_axis,)), ((), ())), preferred_element_type=F32)
-
 
 def reverse_bits(value, count):
     out = 0
@@ -30,50 +26,69 @@
         out = out | (((value >> bit) & 1) << (count - 1 - bit))
     return out
 
-
-def parity(value, count):
+def odd_head(value, count):
     out = value & 1
     for bit in range(1, count):
         out = out ^ ((value >> bit) & 1)
     return out
 
-
-def weight_kernel(heads, own_ref, other_ref, out_ref):
-    core = lax.axis_index("ctx") & 1
-    rows = own_ref.shape[0] // heads
+def row_order(rows, heads):
     group = min(rows, max(256 // heads, 1))
     size = group * heads
     to, at = iota((size, size), 0), iota((size, size), 1)
-    order = one_hot(at == (to % group) * heads + to // group)
-    for ref, place in ((own_ref, core), (other_ref, 1 - core)):
-        for start in range(0, rows, group):
-            moved = matmul(order, ref[pl.ds(start * heads, size), :]).astype(BF16)
-            first = pl.multiple_of(place * rows + start, group)
-            for h in range(heads):
-                out_ref[h, pl.ds(first, group), :] = moved[h * group : (h + 1) * group, :]
-
-
-def partial_kernel(head_count, heads, owned, own_ref, other_ref, *refs):
-    shard_refs, weight_ref, out_ref = refs[:-2], refs[-2], refs[-1]
-    shards = len(shard_refs) + 1
+    return group, one_hot(at == (to % group) * heads + to // group)
+
+def own_kernel(head_count, heads, owned, shards, weight_hbm, own_hbm, out_ref, own_ref, order_ref, weight_ref, sems):
     me = lax.axis_index("head")
     bits = head_count.bit_length() - 1
-    rows = head_count * owned
-    first = jnp.where(parity(me, bits) == 0, own_ref[...], other_ref[...])
-    stacked = jnp.concatenate([first] + [ref[...] for ref in shard_refs], axis=0)
-    size = shards * rows * heads
+    rows = out_ref.shape[1]
+    pieces = sems.shape[0] - 1
+    span = rows * heads // pieces
+    copies = [
+        pltpu.make_async_copy(weight_hbm.at[pl.ds(n * span, span)], weight_ref.at[pl.ds(n * span, span)], sems.at[n])
+        for n in range(pieces)
+    ]
+    copies.append(pltpu.make_async_copy(own_hbm, own_ref, sems.at[pieces]))
+    for copy in copies:
+        copy.start()
+    tokens = head_count * owned
+    size = shards * tokens * heads
     to, at = iota((size, size), 0), iota((size, size), 1)
     i, j = to % owned, (to // owned) % shards
     position = (to // (owned * shards)) % head_count
     token = (reverse_bits(position, bits) ^ me) * owned + i
-    order = one_hot(at == (j * rows + token) * heads + to // (rows * shards))
-    moved = matmul(order, stacked).astype(BF16)
-    part = rows * shards
-    total = matmul(moved[:part], weight_ref[0], 1, 1)
+    order_ref[...] = one_hot(at == (j * tokens + token) * heads + to // (tokens * shards))
+    group, order = row_order(rows, heads)
+    for n in range(pieces):
+        copies[n].wait()
+        for start in range(n * span // heads, (n + 1) * span // heads, group):
+            moved = matmul(order, weight_ref[pl.ds(start * heads, group * heads), :]).astype(BF16)
+            for h in range(heads):
+                out_ref[h, pl.ds(start, group), :] = moved[h * group : (h + 1) * group, :]
+    copies[pieces].wait()
+
+def other_kernel(heads, weight_ref, out_ref):
+    rows = out_ref.shape[1]
+    group, order = row_order(rows, heads)
+    for start in range(0, rows, group):
+        moved = matmul(order, weight_ref[pl.ds(start * heads, group * heads), :]).astype(BF16)
+        for h in range(heads):
+            out_ref[h, pl.ds(start, group), :] = moved[h * group : (h + 1) * group, :]
+
+def partial_kernel(head_count, order_ref, own_weight_ref, other_weight_ref, own_ref, other_ref, *refs):
+    shard_refs, out_ref = refs[:-1], refs[-1]
+    odd = odd_head(lax.axis_index("head"), head_count.bit_length() - 1) == 1
+    first = jnp.where(odd, other_ref[...], own_ref[...])
+    stacked = jnp.concatenate([first] + [ref[...] for ref in shard_refs], axis=0)
+    moved = matmul(order_ref[...], stacked).astype(BF16)
+    heads, part = own_weight_ref.shape[0], out_ref.shape[0]
+    own = matmul(moved[:part], own_weight_ref[0], 1, 1)
+    other = matmul(moved[:part], other_weight_ref[0], 1, 1)
     for h in range(1, heads):
-        total += matmul(moved[h * part : (h + 1) * part], weight_ref[h], 1, 1)
-    out_ref[...] = total
-
+        own += matmul(moved[h * part : (h + 1) * part], own_weight_ref[h], 1, 1)
+        other += matmul(moved[h * part : (h + 1) * part], other_weight_ref[h], 1, 1)
+    core = lax.axis_index("ctx") & 1
+    out_ref[...] = jnp.concatenate([jnp.where(core == 0, own, other), jnp.where(core == 0, other, own)], axis=1)
 
 def norm_kernel(columns, own_ref, other_ref, gain_ref, *out_refs):
     core, column = lax.axis_index("ctx") & 1, lax.axis_index("ctx") >> 1
@@ -88,12 +103,11 @@
             block = jnp.where((column ^ j) == b, normed[:, b * width : (b + 1) * width], block)
         ref[...] = block
 
-
 def weight_grad_kernel(head_count, heads, owned, columns, normed_ref, *refs):
     shard_refs, out_ref, scratch_ref = refs[:-2], refs[-2], refs[-1]
     me = lax.axis_index("head")
     core = lax.axis_index("ctx") & 1
-    role = core ^ parity(me, head_count.bit_length() - 1)
+    role = core ^ odd_head(me, head_count.bit_length() - 1)
     rows = out_ref.shape[0] // heads
     tokens = head_count * owned
     normed = normed_ref[...].astype(BF16)
@@ -117,11 +131,10 @@
             total = part if total is None else total + part
         out_ref[start * heads : (start + group) * heads, :] = total
 
-
 def latent_kernel(head_count, columns, latent_ref, gain_ref, *refs):
     block_refs, other_refs, out_ref = refs[:columns], refs[columns:-1], refs[-1]
     column = lax.axis_index("ctx") >> 1
-    odd = parity(lax.axis_index("head"), head_count.bit_length() - 1)
+    odd = odd_head(lax.axis_index("head"), head_count.bit_length() - 1)
     raw = latent_ref[...].astype(F32)
     rms = lax.rsqrt(jnp.mean(raw * raw, axis=1, keepdims=True) + 1e-06)
     hat = raw * rms
@@ -138,7 +151,6 @@
     inner = jnp.mean(scaled * hat, axis=1, keepdims=True)
     out_ref[...] = rms * (scaled - hat * inner)
 
-
 def per_device(head_count, ctx_count, latent, gain, cotangent, weight):
     columns = ctx_count // 2
     owned, width = latent.shape[1:]
@@ -160,47 +172,56 @@
         return swap(value, lambda h, c: (h, c ^ mask))
 
     def role_swap(value, mask):
-        return swap(value, lambda h, c: (h, c ^ mask ^ parity(h, bits)))
+        return swap(value, lambda h, c: (h, c ^ mask ^ odd_head(h, bits)))
 
     def head_swap(value, mask):
         return swap(value, lambda h, c: (h ^ mask, c ^ 1))
 
-    def call(kernel, out, *args, scratch=(), flops=0):
+    def call(kernel, out, *args, scratch=(), flops=0, raw=0):
         moved = sum(a.size * a.dtype.itemsize for a in args)
         return pl.pallas_call(
             kernel,
             out_shape=out,
+            in_specs=[pl.BlockSpec(memory_space=pltpu.HBM if n < raw else pltpu.VMEM) for n in range(len(args))],
             scratch_shapes=scratch,
             compiler_params=params,
             cost_estimate=pl.CostEstimate(flops=flops, bytes_accessed=moved, transcendentals=0),
-        )(*args)
+        )(*[pltpu.with_memory_space_constraint(a, pltpu.HBM) if n < raw else a for n, a in enumerate(args)])
 
     own = cotangent.reshape(tokens * heads, channels)
     far = [role_swap(own, 2)]
     other = ctx_swap(own, 1)
+    weight_flat = weight.reshape(rows * heads, channels)
+    latent_other = ctx_swap(latent[0], 1)
+    weight_other = ctx_swap(weight_flat, 1)
+    gain_row = gain.reshape(1, width)
+
+    ordered = jax.ShapeDtypeStruct((heads, rows, channels), BF16)
+    size = columns * tokens * heads
+    pieces = 4 if rows % 4 == 0 and rows // 4 * heads >= 256 else 1
+    own_weight, own_copy, order = call(
+        functools.partial(own_kernel, head_count, heads, owned, columns),
+        [ordered, jax.ShapeDtypeStruct(own.shape, BF16), jax.ShapeDtypeStruct((size, size), BF16)],
+        weight_flat,
+        own,
+        scratch=[
+            pltpu.VMEM(weight_flat.shape, BF16),
+            pltpu.SemaphoreType.DMA((pieces + 1,)),
+        ],
+        raw=2,
+    )
     if columns > 2:
-        first = jnp.where(parity(lax.axis_index("head"), bits) == 0, own, other)
-        shards = [first] + far
+        mine = jnp.where(odd_head(lax.axis_index("head"), bits) == 1, other, own_copy)
         mask = 4
         while mask < ctx_count:
-            shards += [ctx_swap(s, mask) for s in shards]
+            far += [ctx_swap(s, mask) for s in [mine] + far]
             mask *= 2
-        far = shards[1:]
-    latent_other = ctx_swap(latent[0], 1)
-    gain_row = gain.reshape(1, width)
+
     block = jax.ShapeDtypeStruct((2 * owned, 2 * rows), F32)
+
     normed = list(call(functools.partial(norm_kernel, columns), [block] * columns, latent[0], latent_other, gain_row))
-
-    weight_flat = weight.reshape(rows * heads, channels)
-    weight_other = ctx_swap(weight_flat, 1)
-    weight_flat, weight_other, *normed = lax.optimization_barrier((weight_flat, weight_other, *normed))
-    chip_weight = call(
-        functools.partial(weight_kernel, heads),
-        jax.ShapeDtypeStruct((heads, 2 * rows, channels), BF16),
-        weight_flat,
-        weight_other,
-    )
-
+    weight_other, *normed = lax.optimization_barrier((weight_other, *normed))
+    other_weight = call(functools.partial(other_kernel, heads), ordered, weight_other)
     mask = 2
     while mask < ctx_count:
         for j in range(columns):
@@ -210,12 +231,14 @@
     normed = jnp.concatenate(normed, axis=0)
 
     sums = call(
-        functools.partial(partial_kernel, head_count, heads, owned),
+        functools.partial(partial_kernel, head_count),
         jax.ShapeDtypeStruct((head_count * columns * owned, 2 * rows), F32),
-        own,
+        order,
+        own_weight,
+        other_weight,
+        own_copy,
         other,
         *far,
-        chip_weight,
     )
     core = lax.axis_index("ctx") & 1
     mask = 1
@@ -249,7 +272,7 @@
         functools.partial(weight_grad_kernel, head_count, heads, owned, columns),
         jax.ShapeDtypeStruct((rows * heads, channels), F32),
         normed,
-        own,
+        own_copy,
         *far,
         other,
         *[ctx_swap(s, 1) for s in far],
@@ -265,7 +288,6 @@
         *kept,
     )
     return latent_gradient[None], weight_grad.reshape(weight.shape)
-
 
 def solution(mesh):
     return jax.shard_map(

time: 23.8 us -> 23.8 us (level)
  Pallas kernels: 3.39 us -> 5.14 us
  local copies, waits for them, and re-layouts: 1.47 us -> 0.04 us
  waiting for transfers between devices: 6.55 us -> 5.81 us
  starting transfers between devices: 11.3 us -> 11.8 us
    pallas_call x5 -> x6, Pallas kernels: 3.39 us -> 5.14 us  [call(): pl.pallas_call(kernel, out_shape=out, in_specs=[pl.BlockSpec(memory_space...]
    unnamed x8 -> x4, local copies, waits for them, and re-layouts: 1.42 us -> 0.01 us
    ppermute x11, waiting for transfers between devices: 6.55 us -> 5.81 us  [swap(): return lax.ppermute(value, ('head', 'ctx'), pairs)]
    ppermute x11, starting transfers between devices: 11.3 us -> 11.8 us  [swap(): return lax.ppermute(value, ('head', 'ctx'), pairs)]
  transfers between devices with their start and end apart: 11 -> 11, of which waited for: 6 -> 5; matrix products, arithmetic and copies ran while one was open for 0% -> 0% of each run, Pallas kernels for 11% -> 18%
where the time goes in v4:
time: 23.8 us; the launch traced here: 23.6 us
  starting transfers between devices  11.8 us (50%)
  waiting for transfers between devices  5.81 us (24%)
  Pallas kernels  5.14 us (22%)
  between operations  0.74 us (3%)
    ppermute x11, starting transfers between devices, swap(): return lax.ppermute(value, ('head', 'ctx'), pairs)  11.8 us
    ppermute x11, waiting for transfers between devices, swap(): return lax.ppermute(value, ('head', 'ctx'), pairs)  5.81 us
    pallas_call x6, Pallas kernels, call(): pl.pallas_call(kernel, out_shape=out, in_specs=[pl.BlockSpec(memory_space...  5.14 us
  transfers between devices with their start and end apart: 11, of which 5 were waited for; matrix products, arithmetic and copies ran while one was open for 0% of the time, Pallas kernels for 18%

profile of v4, /device:TPU:0, one launch (start us, length us, event | category | flops | bytes accessed | tf_op | source)
XLA Modules:
  0.0 23.6 jit_solution(16979817240252368145)
XLA Ops:
  0.6 0.0 copy-start
  0.6 0.5 %collective-permute-start = (bf16[1024,256]{1,0:T(8,128)(2,1)}, bf16[1024,256]{1,0:T(8,128)(2,1)S(1)}, u32[]{:S(2)}, u32[]{:S(2)}) collective-permute-start(bf16[1024,256]{1,0:T(8,128)(2,1)} %bitcast.12), channel_id=1, source_target_pairs={{0,1},{1,0},{2,3},{3,2},{4,5},{5,4},{6,7},{7,6},{8,9},{9,8},{10,11... | collective-permute-start | bytes 1572872 | tf_op jit(solution)/shard_map/ppermute | solution.py:169
  1.2 0.0 copy-start.1
  1.2 2.6 %collective-permute-start.3 = (bf16[128,256]{1,0:T(8,128)(2,1)}, bf16[128,256]{1,0:T(8,128)(2,1)S(1)}, u32[]{:S(2)}, u32[]{:S(2)}) collective-permute-start(bf16[128,256]{1,0:T(8,128)(2,1)} %bitcast.14), channel_id=1, source_target_pairs={{0,2},{1,3},{2,0},{3,1},{4,7},{5,6},{6,5},{7,4},{8,11},{9,10},{10,... | collective-permute-start | bytes 196616 | tf_op jit(solution)/shard_map/ppermute | solution.py:169
  3.7 0.2 collective-permute-start.2
  3.9 0.0 copy-done
  3.9 0.4 %collective-permute-start.1 = (bf16[2,512]{1,0:T(2,128)(2,1)S(1)}, bf16[2,512]{1,0:T(2,128)(2,1)S(1)}, u32[]{:S(2)}, u32[]{:S(2)}) collective-permute-start(bf16[2,512]{1,0:T(2,128)(2,1)S(1)} %bitcast.6), channel_id=1, source_target_pairs={{0,1},{1,0},{2,3},{3,2},{4,5},{5,4},{6,7},{7,6},{8,9},{9,8},{10,11... | collective-permute-start | bytes 6152 | tf_op jit(solution)/shard_map/ppermute | solution.py:169
  4.2 0.8 %collective-permute-done.1.other_ref = bf16[2,512]{1,0:T(2,128)(2,1)S(1)} collective-permute-done((bf16[2,512]{1,0:T(2,128)(2,1)S(1)}, bf16[2,512]{1,0:T(2,128)(2,1)S(1)}, u32[]{:S(2)}, u32[]{:S(2)}) %collective-permute-start.1) | collective-permute-done | bytes 2080 | tf_op jit(solution)/shard_map/ppermute | solution.py:169
  5.1 0.0 copy-done.1
  5.1 0.1 shard_map.60
  5.2 0.0 collective-permute-done.weight_ref
  5.2 0.3 %collective-permute-start.4 = (f32[4,256]{1,0:T(4,128)S(1)}, f32[4,256]{1,0:T(4,128)S(1)}, u32[]{:S(2)}, u32[]{:S(2)}) collective-permute-start(f32[4,256]{1,0:T(4,128)S(1)} %get-tuple-element.17), channel_id=1, source_target_pairs={{0,3},{1,2},{2,1},{3,0},{4,7},{5,6},{6,5},{7,4},{8,11},{9,10},{10,... | collective-permute-start | bytes 12296 | tf_op jit(solution)/shard_map/ppermute | solution.py:169
  5.5 1.8 %shard_map.59 = (bf16[8,128,256]{2,1,0:T(8,128)(2,1)S(1)}, bf16[128,256]{1,0:T(8,128)(2,1)S(1)}, bf16[256,256]{1,0:T(8,128)(2,1)S(1)}) custom-call(bf16[1024,256]{1,0:T(8,128)(2,1)} %bitcast.13, bf16[128,256]{1,0:T(8,128)(2,1)} %bitcast.16), custom_call_target="tpu_custom_call" | custom-call | bytes 589824 | tf_op jit(solution)/shard_map/pallas_call | solution.py:182
  7.3 0.3 %shard_map.61.other_weight_ref = bf16[8,128,256]{2,1,0:T(8,128)(2,1)S(1)} custom-call(bf16[1024,256]{1,0:T(8,128)(2,1)S(1)} %collective-permute-done.weight_ref), custom_call_target="tpu_custom_call" | custom-call | bytes 524288 | tf_op jit(solution)/shard_map/pallas_call | solution.py:182
  7.6 0.0 collective-permute-done.3.refs_0_.refs_1_
  7.7 0.0 collective-permute-done.2.other_ref.refs_2_
  7.7 0.6 %shard_map.62 = f32[32,256]{1,0:T(8,128)S(1)} custom-call(bf16[256,256]{1,0:T(8,128)(2,1)S(1)} %get-tuple-element.10.order_ref, bf16[8,128,256]{2,1,0:T(8,128)(2,1)S(1)} %get-tuple-element.11.own_weight_ref, bf16[8,128,256]{2,1,0:T(8,128)(2,1)S(1)} %shard_map.61.other_weight_ref, bf16[128,256]{1,0:T(8,128)(2,1)S(1)} %get-tuple-element.15.own_ref.refs_0_, ...), custom_call_target="tpu_custom_call" | custom-call | bytes 1376256 | tf_op jit(solution)/shard_map/pallas_call | solution.py:182
  8.2 0.0 collective-permute-done.4
  8.3 1.6 %collective-permute-start.5 = (f32[24,256]{1,0:T(8,128)S(1)}, f32[24,256]{1,0:T(8,128)S(1)}, u32[]{:S(2)}, u32[]{:S(2)}) collective-permute-start(f32[24,256]{1,0:T(8,128)S(1)} %pad_maximum_fusion.2), channel_id=1, source_target_pairs={{0,5},{1,4},{2,7},{3,6},{4,1},{5,0},{6,3},{7,2},{8,13},{9,12},{10,... | collective-permute-start | bytes 73736 | tf_op jit(solution)/shard_map/ppermute | solution.py:169
  9.9 1.7 %collective-permute-done.5 = f32[24,256]{1,0:T(8,128)S(1)} collective-permute-done((f32[24,256]{1,0:T(8,128)S(1)}, f32[24,256]{1,0:T(8,128)S(1)}, u32[]{:S(2)}, u32[]{:S(2)}) %collective-permute-start.5) | collective-permute-done | bytes 24608 | tf_op jit(solution)/shard_map/ppermute | solution.py:169
  11.6 1.6 %collective-permute-start.6 = (f32[24,256]{1,0:T(8,128)S(1)}, f32[24,256]{1,0:T(8,128)S(1)}, u32[]{:S(2)}, u32[]{:S(2)}) collective-permute-start(f32[24,256]{1,0:T(8,128)S(1)} %pad_maximum_fusion.3), channel_id=1, source_target_pairs={{0,9},{1,8},{2,11},{3,10},{4,13},{5,12},{6,15},{7,14},{8,1},{9,0},... | collective-permute-start | bytes 73736 | tf_op jit(solution)/shard_map/ppermute | solution.py:169
  13.3 1.7 %collective-permute-done.6 = f32[24,256]{1,0:T(8,128)S(1)} collective-permute-done((f32[24,256]{1,0:T(8,128)S(1)}, f32[24,256]{1,0:T(8,128)S(1)}, u32[]{:S(2)}, u32[]{:S(2)}) %collective-permute-start.6) | collective-permute-done | bytes 24608 | tf_op jit(solution)/shard_map/ppermute | solution.py:169
  15.0 2.6 %collective-permute-start.7 = (f32[20,256]{1,0:T(8,128)S(1)}, f32[20,256]{1,0:T(8,128)S(1)}, u32[]{:S(2)}, u32[]{:S(2)}) collective-permute-start(f32[20,256]{1,0:T(8,128)S(1)} %maximum_maximum_fusion), channel_id=1, source_target_pairs={{0,17},{1,16},{2,19},{3,18},{4,21},{5,20},{6,23},{7,22},{8,25},{9,... | collective-permute-start | bytes 61448 | tf_op jit(solution)/shard_map/ppermute | solution.py:169
  17.7 0.3 %collective-permute-start.10 = (bf16[128,256]{1,0:T(8,128)(2,1)S(1)}, bf16[128,256]{1,0:T(8,128)(2,1)S(1)}, u32[]{:S(2)}, u32[]{:S(2)}) collective-permute-start(bf16[128,256]{1,0:T(8,128)(2,1)S(1)} %collective-permute-done.3.refs_0_.refs_1_), channel_id=1, source_target_pairs={{0,1},{1,0},{2,3},{3,2},{4,5},{5,4},{6,7},{7,6},{8,9},{9,8},{10,11... | collective-permute-start | bytes 196616 | tf_op jit(solution)/shard_map/ppermute | solution.py:169
  18.0 1.2 %collective-permute-done.7 = f32[20,256]{1,0:T(8,128)S(1)} collective-permute-done((f32[20,256]{1,0:T(8,128)S(1)}, f32[20,256]{1,0:T(8,128)S(1)}, u32[]{:S(2)}, u32[]{:S(2)}) %collective-permute-start.7) | collective-permute-done | bytes 20512 | tf_op jit(solution)/shard_map/ppermute | solution.py:169
  19.3 1.7 %collective-permute-start.8 = (f32[2,256]{1,0:T(2,128)S(1)}, f32[2,256]{1,0:T(2,128)S(1)}, u32[]{:S(2)}, u32[]{:S(2)}) collective-permute-start(f32[2,256]{1,0:T(2,128)S(1)} %get-tuple-element.24), channel_id=1, source_target_pairs={{0,2},{1,3},{2,0},{3,1},{4,7},{5,6},{6,5},{7,4},{8,11},{9,10},{10,... | collective-permute-start | bytes 6152 | tf_op jit(solution)/shard_map/ppermute | solution.py:169
  20.9 0.0 collective-permute-start.9
  21.0 0.0 collective-permute-done.10.refs_3_
  21.0 1.6 %shard_map.64 = f32[1024,256]{1,0:T(8,128)} custom-call(f32[64,128]{1,0:T(8,128)S(1)} %pad_maximum_fusion.1.normed_ref, bf16[128,256]{1,0:T(8,128)(2,1)S(1)} %get-tuple-element.15.own_ref.refs_0_, bf16[128,256]{1,0:T(8,128)(2,1)S(1)} %collective-permute-done.3.refs_0_.refs_1_, bf16[128,256]{1,0:T(8,128)(2,1)S(1)} %collective-permute-done.2.other_ref.refs_2_, ...), custom_call_target="tpu_custom_call" | custom-call | flops 268435456 | bytes 294912 | tf_op jit(solution)/shard_map/pallas_call | solution.py:182
  22.6 0.3 %collective-permute-done.8.refs_1_ = f32[2,256]{1,0:T(2,128)S(1)} collective-permute-done((f32[2,256]{1,0:T(2,128)S(1)}, f32[2,256]{1,0:T(2,128)S(1)}, u32[]{:S(2)}, u32[]{:S(2)}) %collective-permute-start.8) | collective-permute-done | bytes 2080 | tf_op jit(solution)/shard_map/ppermute | solution.py:169
  22.9 0.0 collective-permute-done.9.refs_2_
  22.9 0.8 %shard_map.63 = f32[2,512]{1,0:T(2,128)} custom-call(bf16[2,512]{1,0:T(2,128)(2,1)S(1)} %bitcast.8, f32[1,512]{1,0:T(1,128)S(1)} %bitcast.10, f32[2,256]{1,0:T(2,128)S(1)} %get-tuple-element.25.refs_0_, f32[2,256]{1,0:T(2,128)S(1)} %collective-permute-done.8.refs_1_, f32[2,256]{1,0:T(2,128)S(1)} %collective-permute-done.9.refs_2_), custom_call_target="tpu_custom_call" | custom-call | bytes 10240 | tf_op jit(solution)/shard_map/pallas_call | solution.py:182
  (17 shorter events, 0.1 us)
Async XLA Ops:
  0.6 3.3 %copy-start = (bf16[1,2,512]{2,1,0:T(2,128)(2,1)S(1)}, bf16[1,2,512]{2,1,0:T(2,128)(2,1)}, u32[]{:S(2)}) copy-start(bf16[1,2,512]{2,1,0:T(2,128)(2,1)} %param.4) | copy-start | bytes 6148
  0.6 4.5 %collective-permute-start = (bf16[1024,256]{1,0:T(8,128)(2,1)}, bf16[1024,256]{1,0:T(8,128)(2,1)S(1)}, u32[]{:S(2)}, u32[]{:S(2)}) collective-permute-start(bf16[1024,256]{1,0:T(8,128)(2,1)} %bitcast.12), channel_id=1, source_target_pairs={{0,1},{1,0},{2,3},{3,2},{4,5},{5,4},{6,7},{7,6},{8,9},{9,8},{10,11... | collective-permute-start | bytes 1572872 | tf_op jit(solution)/shard_map/ppermute | solution.py:169
  1.2 3.9 %copy-start.1 = (f32[512]{0:T(512)S(1)}, f32[512]{0:T(512)}, u32[]{:S(2)}) copy-start(f32[512]{0:T(512)} %param.5) | copy-start | bytes 6148
  1.2 6.5 %collective-permute-start.3 = (bf16[128,256]{1,0:T(8,128)(2,1)}, bf16[128,256]{1,0:T(8,128)(2,1)S(1)}, u32[]{:S(2)}, u32[]{:S(2)}) collective-permute-start(bf16[128,256]{1,0:T(8,128)(2,1)} %bitcast.14), channel_id=1, source_target_pairs={{0,2},{1,3},{2,0},{3,1},{4,7},{5,6},{6,5},{7,4},{8,11},{9,10},{10,... | collective-permute-start | bytes 196616 | tf_op jit(solution)/shard_map/ppermute | solution.py:169
  3.7 3.9 %collective-permute-start.2 = (bf16[128,256]{1,0:T(8,128)(2,1)}, bf16[128,256]{1,0:T(8,128)(2,1)S(1)}, u32[]{:S(2)}, u32[]{:S(2)}) collective-permute-start(bf16[128,256]{1,0:T(8,128)(2,1)} %bitcast.15), channel_id=1, source_target_pairs={{0,1},{1,0},{2,3},{3,2},{4,5},{5,4},{6,7},{7,6},{8,9},{9,8},{10,11... | collective-permute-start | bytes 196616 | tf_op jit(solution)/shard_map/ppermute | solution.py:169
  3.9 1.2 %collective-permute-start.1 = (bf16[2,512]{1,0:T(2,128)(2,1)S(1)}, bf16[2,512]{1,0:T(2,128)(2,1)S(1)}, u32[]{:S(2)}, u32[]{:S(2)}) collective-permute-start(bf16[2,512]{1,0:T(2,128)(2,1)S(1)} %bitcast.6), channel_id=1, source_target_pairs={{0,1},{1,0},{2,3},{3,2},{4,5},{5,4},{6,7},{7,6},{8,9},{9,8},{10,11... | collective-permute-start | bytes 6152 | tf_op jit(solution)/shard_map/ppermute | solution.py:169
  5.2 3.1 %collective-permute-start.4 = (f32[4,256]{1,0:T(4,128)S(1)}, f32[4,256]{1,0:T(4,128)S(1)}, u32[]{:S(2)}, u32[]{:S(2)}) collective-permute-start(f32[4,256]{1,0:T(4,128)S(1)} %get-tuple-element.17), channel_id=1, source_target_pairs={{0,3},{1,2},{2,1},{3,0},{4,7},{5,6},{6,5},{7,4},{8,11},{9,10},{10,... | collective-permute-start | bytes 12296 | tf_op jit(solution)/shard_map/ppermute | solution.py:169
  8.3 3.3 %collective-permute-start.5 = (f32[24,256]{1,0:T(8,128)S(1)}, f32[24,256]{1,0:T(8,128)S(1)}, u32[]{:S(2)}, u32[]{:S(2)}) collective-permute-start(f32[24,256]{1,0:T(8,128)S(1)} %pad_maximum_fusion.2), channel_id=1, source_target_pairs={{0,5},{1,4},{2,7},{3,6},{4,1},{5,0},{6,3},{7,2},{8,13},{9,12},{10,... | collective-permute-start | bytes 73736 | tf_op jit(solution)/shard_map/ppermute | solution.py:169
  11.6 3.3 %collective-permute-start.6 = (f32[24,256]{1,0:T(8,128)S(1)}, f32[24,256]{1,0:T(8,128)S(1)}, u32[]{:S(2)}, u32[]{:S(2)}) collective-permute-start(f32[24,256]{1,0:T(8,128)S(1)} %pad_maximum_fusion.3), channel_id=1, source_target_pairs={{0,9},{1,8},{2,11},{3,10},{4,13},{5,12},{6,15},{7,14},{8,1},{9,0},... | collective-permute-start | bytes 73736 | tf_op jit(solution)/shard_map/ppermute | solution.py:169
  15.0 4.2 %collective-permute-start.7 = (f32[20,256]{1,0:T(8,128)S(1)}, f32[20,256]{1,0:T(8,128)S(1)}, u32[]{:S(2)}, u32[]{:S(2)}) collective-permute-start(f32[20,256]{1,0:T(8,128)S(1)} %maximum_maximum_fusion), channel_id=1, source_target_pairs={{0,17},{1,16},{2,19},{3,18},{4,21},{5,20},{6,23},{7,22},{8,25},{9,... | collective-permute-start | bytes 61448 | tf_op jit(solution)/shard_map/ppermute | solution.py:169
  17.7 3.3 %collective-permute-start.10 = (bf16[128,256]{1,0:T(8,128)(2,1)S(1)}, bf16[128,256]{1,0:T(8,128)(2,1)S(1)}, u32[]{:S(2)}, u32[]{:S(2)}) collective-permute-start(bf16[128,256]{1,0:T(8,128)(2,1)S(1)} %collective-permute-done.3.refs_0_.refs_1_), channel_id=1, source_target_pairs={{0,1},{1,0},{2,3},{3,2},{4,5},{5,4},{6,7},{7,6},{8,9},{9,8},{10,11... | collective-permute-start | bytes 196616 | tf_op jit(solution)/shard_map/ppermute | solution.py:169
  19.3 3.6 %collective-permute-start.8 = (f32[2,256]{1,0:T(2,128)S(1)}, f32[2,256]{1,0:T(2,128)S(1)}, u32[]{:S(2)}, u32[]{:S(2)}) collective-permute-start(f32[2,256]{1,0:T(2,128)S(1)} %get-tuple-element.24), channel_id=1, source_target_pairs={{0,2},{1,3},{2,0},{3,1},{4,7},{5,6},{6,5},{7,4},{8,11},{9,10},{10,... | collective-permute-start | bytes 6152 | tf_op jit(solution)/shard_map/ppermute | solution.py:169
  20.9 1.9 %collective-permute-start.9 = (f32[2,256]{1,0:T(2,128)S(1)}, f32[2,256]{1,0:T(2,128)S(1)}, u32[]{:S(2)}, u32[]{:S(2)}) collective-permute-start(f32[2,256]{1,0:T(2,128)S(1)} %get-tuple-element.25.refs_0_), channel_id=1, source_target_pairs={{0,1},{1,0},{2,3},{3,2},{4,5},{5,4},{6,7},{7,6},{8,9},{9,8},{10,11... | collective-permute-start | bytes 6152 | tf_op jit(solution)/shard_map/ppermute | solution.py:169

commit v5 on v3

--- a/solution.py
+++ b/solution.py
@@ -189,7 +189,7 @@
     latent_other = ctx_swap(latent[0], 1)
     gain_row = gain.reshape(1, width)
     block = jax.ShapeDtypeStruct((2 * owned, 2 * rows), F32)
-    normed = list(call(functools.partial(norm_kernel, columns), [block] * columns, latent[0], latent_other, gain_row))
+    normed = list(call(functools.partial(norm_kernel, columns), [block] * columns, latent[0], latent_other, gain_row, flops=4 * 10**8))
 
     weight_flat = weight.reshape(rows * heads, channels)
     weight_other = ctx_swap(weight_flat, 1)

time: 23.8 us -> 23.7 us (level)
  waiting for transfers between devices: 6.55 us -> 7.96 us
  local copies, waits for them, and re-layouts: 1.47 us -> 0.66 us
  starting transfers between devices: 11.3 us -> 10.7 us
    ppermute x11, waiting for transfers between devices: 6.55 us -> 7.96 us  [swap(): return lax.ppermute(value, ('head', 'ctx'), pairs)]
    unnamed x8, local copies, waits for them, and re-layouts: 1.42 us -> 0.62 us
    ppermute x11, starting transfers between devices: 11.3 us -> 10.7 us  [swap(): return lax.ppermute(value, ('head', 'ctx'), pairs)]
  transfers between devices with their start and end apart: 11 -> 11, of which waited for: 6 -> 7; matrix products, arithmetic and copies ran while one was open for 0% -> 0% of each run, Pallas kernels for 11% -> 11%
where the time goes in v5:
time: 23.7 us; the launch traced here: 23.6 us
  starting transfers between devices  10.7 us (45%)
  waiting for transfers between devices  7.96 us (34%)
  Pallas kernels  3.4 us (14%)
  between operations  0.74 us (3%)
  local copies, waits for them, and re-layouts  0.66 us (3%)
    ppermute x11, starting transfers between devices, swap(): return lax.ppermute(value, ('head', 'ctx'), pairs)  10.7 us
    ppermute x11, waiting for transfers between devices, swap(): return lax.ppermute(value, ('head', 'ctx'), pairs)  7.96 us
    pallas_call x5, Pallas kernels, call(): pl.pallas_call(kernel, out_shape=out, scratch_shapes=scratch, compiler_pa...  3.4 us
    unnamed x8, local copies, waits for them, and re-layouts  0.62 us
  transfers between devices with their start and end apart: 11, of which 7 were waited for; matrix products, arithmetic and copies ran while one was open for 0% of the time, Pallas kernels for 11%

profile of v5, /device:TPU:0, one launch (start us, length us, event | category | flops | bytes accessed | tf_op | source)
XLA Modules:
  0.0 23.6 jit_solution(12425876758363946579)
XLA Ops:
  0.6 0.0 copy-start.2
  0.6 0.5 %collective-permute-start.2 = (bf16[1024,256]{1,0:T(8,128)(2,1)}, bf16[1024,256]{1,0:T(8,128)(2,1)S(1)}, u32[]{:S(2)}, u32[]{:S(2)}) collective-permute-start(bf16[1024,256]{1,0:T(8,128)(2,1)} %bitcast.6), channel_id=1, source_target_pairs={{0,1},{1,0},{2,3},{3,2},{4,5},{5,4},{6,7},{7,6},{8,9},{9,8},{10,11... | collective-permute-start | bytes 1572872 | tf_op jit(solution)/shard_map/ppermute | solution.py:157
  1.2 0.0 copy-start.3
  1.2 2.6 %collective-permute-start.1 = (bf16[128,256]{1,0:T(8,128)(2,1)}, bf16[128,256]{1,0:T(8,128)(2,1)S(1)}, u32[]{:S(2)}, u32[]{:S(2)}) collective-permute-start(bf16[128,256]{1,0:T(8,128)(2,1)} %bitcast.8), channel_id=1, source_target_pairs={{0,2},{1,3},{2,0},{3,1},{4,7},{5,6},{6,5},{7,4},{8,11},{9,10},{10,... | collective-permute-start | bytes 196616 | tf_op jit(solution)/shard_map/ppermute | solution.py:157
  3.7 0.2 collective-permute-start
  3.9 0.0 copy-done.2
  3.9 0.4 %collective-permute-start.3 = (bf16[2,512]{1,0:T(2,128)(2,1)S(1)}, bf16[2,512]{1,0:T(2,128)(2,1)S(1)}, u32[]{:S(2)}, u32[]{:S(2)}) collective-permute-start(bf16[2,512]{1,0:T(2,128)(2,1)S(1)} %bitcast.12), channel_id=1, source_target_pairs={{0,1},{1,0},{2,3},{3,2},{4,5},{5,4},{6,7},{7,6},{8,9},{9,8},{10,11... | collective-permute-start | bytes 6152 | tf_op jit(solution)/shard_map/ppermute | solution.py:157
  4.2 0.8 %collective-permute-done.3.other_ref = bf16[2,512]{1,0:T(2,128)(2,1)S(1)} collective-permute-done((bf16[2,512]{1,0:T(2,128)(2,1)S(1)}, bf16[2,512]{1,0:T(2,128)(2,1)S(1)}, u32[]{:S(2)}, u32[]{:S(2)}) %collective-permute-start.3) | collective-permute-done | bytes 2080 | tf_op jit(solution)/shard_map/ppermute | solution.py:157
  5.1 0.0 copy-done.3
  5.1 0.0 copy-start
  5.1 0.1 shard_map.59
  5.2 0.0 collective-permute-done.2.other_ref
  5.2 0.0 copy-start.1
  5.2 0.3 %collective-permute-start.4 = (f32[4,256]{1,0:T(4,128)S(1)}, f32[4,256]{1,0:T(4,128)S(1)}, u32[]{:S(2)}, u32[]{:S(2)}) collective-permute-start(f32[4,256]{1,0:T(4,128)S(1)} %get-tuple-element.13), channel_id=1, source_target_pairs={{0,3},{1,2},{2,1},{3,0},{4,7},{5,6},{6,5},{7,4},{8,11},{9,10},{10,... | collective-permute-start | bytes 12296 | tf_op jit(solution)/shard_map/ppermute | solution.py:157
  5.5 0.6 %copy-done = bf16[128,8,256]{2,1,0:T(8,128)(2,1)S(1)} copy-done((bf16[128,8,256]{2,1,0:T(8,128)(2,1)S(1)}, bf16[128,8,256]{2,1,0:T(8,128)(2,1)}, u32[]{:S(2)}) %copy-start) | copy-done | bytes 524312
  6.1 0.4 %shard_map.60.refs_1_ = bf16[8,256,256]{2,1,0:T(8,128)(2,1)S(1)} custom-call(bf16[1024,256]{1,0:T(8,128)(2,1)S(1)} %bitcast.7, bf16[1024,256]{1,0:T(8,128)(2,1)S(1)} %collective-permute-done.2.other_ref), custom_call_target="tpu_custom_call" | custom-call | bytes 1048576 | tf_op jit(solution)/shard_map/pallas_call | solution.py:170
  6.6 0.1 collective-permute-done.1.refs_0_.refs_1_
  6.6 0.0 collective-permute-done.other_ref.refs_2_
  6.6 0.0 copy-done.1
  6.6 0.5 %shard_map.61 = f32[32,256]{1,0:T(8,128)S(1)} custom-call(bf16[128,256]{1,0:T(8,128)(2,1)S(1)} %bitcast.10, bf16[128,256]{1,0:T(8,128)(2,1)S(1)} %collective-permute-done.other_ref.refs_2_, bf16[128,256]{1,0:T(8,128)(2,1)S(1)} %collective-permute-done.1.refs_0_.refs_1_, bf16[8,256,256]{2,1,0:T(8,128)(2,1)S(1)} %shard_map.60.refs_1_), custom_call_target="tpu_custom_call" | custom-call | bytes 1245184 | tf_op jit(solution)/shard_map/pallas_call | solution.py:170
  7.2 1.1 %collective-permute-done.4 = f32[4,256]{1,0:T(4,128)S(1)} collective-permute-done((f32[4,256]{1,0:T(4,128)S(1)}, f32[4,256]{1,0:T(4,128)S(1)}, u32[]{:S(2)}, u32[]{:S(2)}) %collective-permute-start.4) | collective-permute-done | bytes 4128 | tf_op jit(solution)/shard_map/ppermute | solution.py:157
  8.3 1.5 %collective-permute-start.5 = (f32[24,256]{1,0:T(8,128)S(1)}, f32[24,256]{1,0:T(8,128)S(1)}, u32[]{:S(2)}, u32[]{:S(2)}) collective-permute-start(f32[24,256]{1,0:T(8,128)S(1)} %pad_maximum_fusion.2), channel_id=1, source_target_pairs={{0,5},{1,4},{2,7},{3,6},{4,1},{5,0},{6,3},{7,2},{8,13},{9,12},{10,... | collective-permute-start | bytes 73736 | tf_op jit(solution)/shard_map/ppermute | solution.py:157
  9.8 1.7 %collective-permute-done.5 = f32[24,256]{1,0:T(8,128)S(1)} collective-permute-done((f32[24,256]{1,0:T(8,128)S(1)}, f32[24,256]{1,0:T(8,128)S(1)}, u32[]{:S(2)}, u32[]{:S(2)}) %collective-permute-start.5) | collective-permute-done | bytes 24608 | tf_op jit(solution)/shard_map/ppermute | solution.py:157
  11.6 1.6 %collective-permute-start.6 = (f32[24,256]{1,0:T(8,128)S(1)}, f32[24,256]{1,0:T(8,128)S(1)}, u32[]{:S(2)}, u32[]{:S(2)}) collective-permute-start(f32[24,256]{1,0:T(8,128)S(1)} %pad_maximum_fusion.3), channel_id=1, source_target_pairs={{0,9},{1,8},{2,11},{3,10},{4,13},{5,12},{6,15},{7,14},{8,1},{9,0},... | collective-permute-start | bytes 73736 | tf_op jit(solution)/shard_map/ppermute | solution.py:157
  13.2 1.7 %collective-permute-done.6 = f32[24,256]{1,0:T(8,128)S(1)} collective-permute-done((f32[24,256]{1,0:T(8,128)S(1)}, f32[24,256]{1,0:T(8,128)S(1)}, u32[]{:S(2)}, u32[]{:S(2)}) %collective-permute-start.6) | collective-permute-done | bytes 24608 | tf_op jit(solution)/shard_map/ppermute | solution.py:157
  15.0 2.6 %collective-permute-start.7 = (f32[20,256]{1,0:T(8,128)S(1)}, f32[20,256]{1,0:T(8,128)S(1)}, u32[]{:S(2)}, u32[]{:S(2)}) collective-permute-start(f32[20,256]{1,0:T(8,128)S(1)} %maximum_maximum_fusion), channel_id=1, source_target_pairs={{0,17},{1,16},{2,19},{3,18},{4,21},{5,20},{6,23},{7,22},{8,25},{9,... | collective-permute-start | bytes 61448 | tf_op jit(solution)/shard_map/ppermute | solution.py:157
  17.6 0.2 collective-permute-start.10
  17.8 1.4 %collective-permute-done.7 = f32[20,256]{1,0:T(8,128)S(1)} collective-permute-done((f32[20,256]{1,0:T(8,128)S(1)}, f32[20,256]{1,0:T(8,128)S(1)}, u32[]{:S(2)}, u32[]{:S(2)}) %collective-permute-start.7) | collective-permute-done | bytes 20512 | tf_op jit(solution)/shard_map/ppermute | solution.py:157
  19.2 0.9 %collective-permute-start.8 = (f32[2,256]{1,0:T(2,128)S(1)}, f32[2,256]{1,0:T(2,128)S(1)}, u32[]{:S(2)}, u32[]{:S(2)}) collective-permute-start(f32[2,256]{1,0:T(2,128)S(1)} %get-tuple-element.20), channel_id=1, source_target_pairs={{0,2},{1,3},{2,0},{3,1},{4,7},{5,6},{6,5},{7,4},{8,11},{9,10},{10,... | collective-permute-start | bytes 6152 | tf_op jit(solution)/shard_map/ppermute | solution.py:157
  20.1 0.0 collective-permute-start.9
  20.1 0.0 collective-permute-done.10.refs_3_
  20.1 1.6 %shard_map.63 = f32[1024,256]{1,0:T(8,128)} custom-call(f32[64,128]{1,0:T(8,128)S(1)} %pad_maximum_fusion.1.normed_ref, bf16[128,256]{1,0:T(8,128)(2,1)S(1)} %bitcast.11, bf16[128,256]{1,0:T(8,128)(2,1)S(1)} %collective-permute-done.1.refs_0_.refs_1_, bf16[128,256]{1,0:T(8,128)(2,1)S(1)} %collective-permute-done.other_ref.refs_2_, ...), custom_call_target="tpu_custom_call" | custom-call | flops 268435456 | bytes 294912 | tf_op jit(solution)/shard_map/pallas_call | solution.py:170
  21.7 1.1 %collective-permute-done.8.refs_1_ = f32[2,256]{1,0:T(2,128)S(1)} collective-permute-done((f32[2,256]{1,0:T(2,128)S(1)}, f32[2,256]{1,0:T(2,128)S(1)}, u32[]{:S(2)}, u32[]{:S(2)}) %collective-permute-start.8) | collective-permute-done | bytes 2080 | tf_op jit(solution)/shard_map/ppermute | solution.py:157
  22.8 0.0 collective-permute-done.9.refs_2_
  22.8 0.8 %shard_map.62 = f32[2,512]{1,0:T(2,128)} custom-call(bf16[2,512]{1,0:T(2,128)(2,1)S(1)} %bitcast.14, f32[1,512]{1,0:T(1,128)S(1)} %bitcast.16, f32[2,256]{1,0:T(2,128)S(1)} %get-tuple-element.21.refs_0_, f32[2,256]{1,0:T(2,128)S(1)} %collective-permute-done.8.refs_1_, f32[2,256]{1,0:T(2,128)S(1)} %collective-permute-done.9.refs_2_), custom_call_target="tpu_custom_call" | custom-call | bytes 10240 | tf_op jit(solution)/shard_map/pallas_call | solution.py:170
  (17 shorter events, 0.1 us)
Async XLA Ops:
  0.6 3.3 %copy-start.2 = (bf16[1,2,512]{2,1,0:T(2,128)(2,1)S(1)}, bf16[1,2,512]{2,1,0:T(2,128)(2,1)}, u32[]{:S(2)}) copy-start(bf16[1,2,512]{2,1,0:T(2,128)(2,1)} %param.4) | copy-start | bytes 6148
  0.6 4.5 %collective-permute-start.2 = (bf16[1024,256]{1,0:T(8,128)(2,1)}, bf16[1024,256]{1,0:T(8,128)(2,1)S(1)}, u32[]{:S(2)}, u32[]{:S(2)}) collective-permute-start(bf16[1024,256]{1,0:T(8,128)(2,1)} %bitcast.6), channel_id=1, source_target_pairs={{0,1},{1,0},{2,3},{3,2},{4,5},{5,4},{6,7},{7,6},{8,9},{9,8},{10,11... | collective-permute-start | bytes 1572872 | tf_op jit(solution)/shard_map/ppermute | solution.py:157
  1.2 3.9 %copy-start.3 = (f32[512]{0:T(512)S(1)}, f32[512]{0:T(512)}, u32[]{:S(2)}) copy-start(f32[512]{0:T(512)} %param.5) | copy-start | bytes 6148
  1.2 5.5 %collective-permute-start.1 = (bf16[128,256]{1,0:T(8,128)(2,1)}, bf16[128,256]{1,0:T(8,128)(2,1)S(1)}, u32[]{:S(2)}, u32[]{:S(2)}) collective-permute-start(bf16[128,256]{1,0:T(8,128)(2,1)} %bitcast.8), channel_id=1, source_target_pairs={{0,2},{1,3},{2,0},{3,1},{4,7},{5,6},{6,5},{7,4},{8,11},{9,10},{10,... | collective-permute-start | bytes 196616 | tf_op jit(solution)/shard_map/ppermute | solution.py:157
  3.7 2.9 %collective-permute-start = (bf16[128,256]{1,0:T(8,128)(2,1)}, bf16[128,256]{1,0:T(8,128)(2,1)S(1)}, u32[]{:S(2)}, u32[]{:S(2)}) collective-permute-start(bf16[128,256]{1,0:T(8,128)(2,1)} %bitcast.9), channel_id=1, source_target_pairs={{0,1},{1,0},{2,3},{3,2},{4,5},{5,4},{6,7},{7,6},{8,9},{9,8},{10,11... | collective-permute-start | bytes 196616 | tf_op jit(solution)/shard_map/ppermute | solution.py:157
  3.9 1.2 %collective-permute-start.3 = (bf16[2,512]{1,0:T(2,128)(2,1)S(1)}, bf16[2,512]{1,0:T(2,128)(2,1)S(1)}, u32[]{:S(2)}, u32[]{:S(2)}) collective-permute-start(bf16[2,512]{1,0:T(2,128)(2,1)S(1)} %bitcast.12), channel_id=1, source_target_pairs={{0,1},{1,0},{2,3},{3,2},{4,5},{5,4},{6,7},{7,6},{8,9},{9,8},{10,11... | collective-permute-start | bytes 6152 | tf_op jit(solution)/shard_map/ppermute | solution.py:157
  5.1 1.0 %copy-start = (bf16[128,8,256]{2,1,0:T(8,128)(2,1)S(1)}, bf16[128,8,256]{2,1,0:T(8,128)(2,1)}, u32[]{:S(2)}) copy-start(bf16[128,8,256]{2,1,0:T(8,128)(2,1)} %param.7) | copy-start | bytes 1572868
  5.2 1.5 %copy-start.1 = (bf16[1,16,8,256]{3,2,1,0:T(8,128)(2,1)S(1)}, bf16[1,16,8,256]{3,2,1,0:T(8,128)(2,1)}, u32[]{:S(2)}) copy-start(bf16[1,16,8,256]{3,2,1,0:T(8,128)(2,1)} %param.6) | copy-start | bytes 196612
  5.2 3.1 %collective-permute-start.4 = (f32[4,256]{1,0:T(4,128)S(1)}, f32[4,256]{1,0:T(4,128)S(1)}, u32[]{:S(2)}, u32[]{:S(2)}) collective-permute-start(f32[4,256]{1,0:T(4,128)S(1)} %get-tuple-element.13), channel_id=1, source_target_pairs={{0,3},{1,2},{2,1},{3,0},{4,7},{5,6},{6,5},{7,4},{8,11},{9,10},{10,... | collective-permute-start | bytes 12296 | tf_op jit(solution)/shard_map/ppermute | solution.py:157
  8.3 3.3 %collective-permute-start.5 = (f32[24,256]{1,0:T(8,128)S(1)}, f32[24,256]{1,0:T(8,128)S(1)}, u32[]{:S(2)}, u32[]{:S(2)}) collective-permute-start(f32[24,256]{1,0:T(8,128)S(1)} %pad_maximum_fusion.2), channel_id=1, source_target_pairs={{0,5},{1,4},{2,7},{3,6},{4,1},{5,0},{6,3},{7,2},{8,13},{9,12},{10,... | collective-permute-start | bytes 73736 | tf_op jit(solution)/shard_map/ppermute | solution.py:157
  11.6 3.3 %collective-permute-start.6 = (f32[24,256]{1,0:T(8,128)S(1)}, f32[24,256]{1,0:T(8,128)S(1)}, u32[]{:S(2)}, u32[]{:S(2)}) collective-permute-start(f32[24,256]{1,0:T(8,128)S(1)} %pad_maximum_fusion.3), channel_id=1, source_target_pairs={{0,9},{1,8},{2,11},{3,10},{4,13},{5,12},{6,15},{7,14},{8,1},{9,0},... | collective-permute-start | bytes 73736 | tf_op jit(solution)/shard_map/ppermute | solution.py:157
  15.0 4.2 %collective-permute-start.7 = (f32[20,256]{1,0:T(8,128)S(1)}, f32[20,256]{1,0:T(8,128)S(1)}, u32[]{:S(2)}, u32[]{:S(2)}) collective-permute-start(f32[20,256]{1,0:T(8,128)S(1)} %maximum_maximum_fusion), channel_id=1, source_target_pairs={{0,17},{1,16},{2,19},{3,18},{4,21},{5,20},{6,23},{7,22},{8,25},{9,... | collective-permute-start | bytes 61448 | tf_op jit(solution)/shard_map/ppermute | solution.py:157
  17.6 2.5 %collective-permute-start.10 = (bf16[128,256]{1,0:T(8,128)(2,1)S(1)}, bf16[128,256]{1,0:T(8,128)(2,1)S(1)}, u32[]{:S(2)}, u32[]{:S(2)}) collective-permute-start(bf16[128,256]{1,0:T(8,128)(2,1)S(1)} %collective-permute-done.1.refs_0_.refs_1_), channel_id=1, source_target_pairs={{0,1},{1,0},{2,3},{3,2},{4,5},{5,4},{6,7},{7,6},{8,9},{9,8},{10,11... | collective-permute-start | bytes 196616 | tf_op jit(solution)/shard_map/ppermute | solution.py:157
  19.2 3.6 %collective-permute-start.8 = (f32[2,256]{1,0:T(2,128)S(1)}, f32[2,256]{1,0:T(2,128)S(1)}, u32[]{:S(2)}, u32[]{:S(2)}) collective-permute-start(f32[2,256]{1,0:T(2,128)S(1)} %get-tuple-element.20), channel_id=1, source_target_pairs={{0,2},{1,3},{2,0},{3,1},{4,7},{5,6},{6,5},{7,4},{8,11},{9,10},{10,... | collective-permute-start | bytes 6152 | tf_op jit(solution)/shard_map/ppermute | solution.py:157
  20.1 2.7 %collective-permute-start.9 = (f32[2,256]{1,0:T(2,128)S(1)}, f32[2,256]{1,0:T(2,128)S(1)}, u32[]{:S(2)}, u32[]{:S(2)}) collective-permute-start(f32[2,256]{1,0:T(2,128)S(1)} %get-tuple-element.21.refs_0_), channel_id=1, source_target_pairs={{0,1},{1,0},{2,3},{3,2},{4,5},{5,4},{6,7},{7,6},{8,9},{9,8},{10,11... | collective-permute-start | bytes 6152 | tf_op jit(solution)/shard_map/ppermute | solution.py:157

commit v6 on v5

--- a/solution.py
+++ b/solution.py
@@ -189,7 +189,7 @@
     latent_other = ctx_swap(latent[0], 1)
     gain_row = gain.reshape(1, width)
     block = jax.ShapeDtypeStruct((2 * owned, 2 * rows), F32)
-    normed = list(call(functools.partial(norm_kernel, columns), [block] * columns, latent[0], latent_other, gain_row, flops=4 * 10**8))
+    normed = list(call(functools.partial(norm_kernel, columns), [block] * columns, latent[0], latent_other, gain_row, flops=10**9))
 
     weight_flat = weight.reshape(rows * heads, channels)
     weight_other = ctx_swap(weight_flat, 1)

time: 23.7 us -> 23.4 us (0.987)
  starting transfers between devices: 10.7 us -> 12.3 us
  waiting for transfers between devices: 7.96 us -> 6.38 us
  local copies, waits for them, and re-layouts: 0.66 us -> 0.24 us
    ppermute x11, starting transfers between devices: 10.7 us -> 12.3 us  [swap(): return lax.ppermute(value, ('head', 'ctx'), pairs)]
    ppermute x11, waiting for transfers between devices: 7.96 us -> 6.38 us  [swap(): return lax.ppermute(value, ('head', 'ctx'), pairs)]
    unnamed x8, local copies, waits for them, and re-layouts: 0.62 us -> 0.19 us
  transfers between devices with their start and end apart: 11 -> 11, of which waited for: 7 -> 4; matrix products, arithmetic and copies ran while one was open for 0% -> 0% of each run, Pallas kernels for 11% -> 11%
where the time goes in v6:
time: 23.4 us; the launch traced here: 23.2 us
  starting transfers between devices  12.3 us (53%)
  waiting for transfers between devices  6.38 us (27%)
  Pallas kernels  3.39 us (14%)
  between operations  0.75 us (3%)
  local copies, waits for them, and re-layouts  0.24 us (1%)
    ppermute x11, starting transfers between devices, swap(): return lax.ppermute(value, ('head', 'ctx'), pairs)  12.3 us
    ppermute x11, waiting for transfers between devices, swap(): return lax.ppermute(value, ('head', 'ctx'), pairs)  6.38 us
    pallas_call x5, Pallas kernels, call(): pl.pallas_call(kernel, out_shape=out, scratch_shapes=scratch, compiler_pa...  3.39 us
  transfers between devices with their start and end apart: 11, of which 4 were waited for; matrix products, arithmetic and copies ran while one was open for 0% of the time, Pallas kernels for 11%

profile of v6, /device:TPU:0, one launch (start us, length us, event | category | flops | bytes accessed | tf_op | source)
XLA Modules:
  0.0 23.2 jit_solution(2953093855611524203)
XLA Ops:
  0.6 0.0 copy-start.2
  0.6 0.5 %collective-permute-start.2 = (bf16[1024,256]{1,0:T(8,128)(2,1)}, bf16[1024,256]{1,0:T(8,128)(2,1)S(1)}, u32[]{:S(2)}, u32[]{:S(2)}) collective-permute-start(bf16[1024,256]{1,0:T(8,128)(2,1)} %bitcast.6), channel_id=1, source_target_pairs={{0,1},{1,0},{2,3},{3,2},{4,5},{5,4},{6,7},{7,6},{8,9},{9,8},{10,11... | collective-permute-start | bytes 1572872 | tf_op jit(solution)/shard_map/ppermute | solution.py:157
  1.2 0.2 copy-done.2
  1.3 0.0 copy-start.3
  1.3 0.5 %collective-permute-start.3 = (bf16[2,512]{1,0:T(2,128)(2,1)S(1)}, bf16[2,512]{1,0:T(2,128)(2,1)S(1)}, u32[]{:S(2)}, u32[]{:S(2)}) collective-permute-start(bf16[2,512]{1,0:T(2,128)(2,1)S(1)} %bitcast.12), channel_id=1, source_target_pairs={{0,1},{1,0},{2,3},{3,2},{4,5},{5,4},{6,7},{7,6},{8,9},{9,8},{10,11... | collective-permute-start | bytes 6152 | tf_op jit(solution)/shard_map/ppermute | solution.py:157
  1.8 2.5 %collective-permute-start.1 = (bf16[128,256]{1,0:T(8,128)(2,1)}, bf16[128,256]{1,0:T(8,128)(2,1)S(1)}, u32[]{:S(2)}, u32[]{:S(2)}) collective-permute-start(bf16[128,256]{1,0:T(8,128)(2,1)} %bitcast.8), channel_id=1, source_target_pairs={{0,2},{1,3},{2,0},{3,1},{4,7},{5,6},{6,5},{7,4},{8,11},{9,10},{10,... | collective-permute-start | bytes 196616 | tf_op jit(solution)/shard_map/ppermute | solution.py:157
  4.3 0.2 collective-permute-start
  4.5 0.0 collective-permute-done.3.other_ref
  4.5 0.0 copy-done.3
  4.5 0.0 copy-start
  4.5 0.1 shard_map.59
  4.6 0.0 collective-permute-done.2.other_ref
  4.6 0.0 copy-start.1
  4.6 0.9 %collective-permute-start.4 = (f32[4,256]{1,0:T(4,128)S(1)}, f32[4,256]{1,0:T(4,128)S(1)}, u32[]{:S(2)}, u32[]{:S(2)}) collective-permute-start(f32[4,256]{1,0:T(4,128)S(1)} %get-tuple-element.13), channel_id=1, source_target_pairs={{0,3},{1,2},{2,1},{3,0},{4,7},{5,6},{6,5},{7,4},{8,11},{9,10},{10,... | collective-permute-start | bytes 12296 | tf_op jit(solution)/shard_map/ppermute | solution.py:157
  5.5 0.0 copy-done
  5.5 0.4 %shard_map.60.refs_1_ = bf16[8,256,256]{2,1,0:T(8,128)(2,1)S(1)} custom-call(bf16[1024,256]{1,0:T(8,128)(2,1)S(1)} %bitcast.7, bf16[1024,256]{1,0:T(8,128)(2,1)S(1)} %collective-permute-done.2.other_ref), custom_call_target="tpu_custom_call" | custom-call | bytes 1048576 | tf_op jit(solution)/shard_map/pallas_call | solution.py:170
  6.0 1.2 %collective-permute-done.1.refs_0_.refs_1_ = bf16[128,256]{1,0:T(8,128)(2,1)S(1)} collective-permute-done((bf16[128,256]{1,0:T(8,128)(2,1)}, bf16[128,256]{1,0:T(8,128)(2,1)S(1)}, u32[]{:S(2)}, u32[]{:S(2)}) %collective-permute-start.1) | collective-permute-done | bytes 65568 | tf_op jit(solution)/shard_map/ppermute | solution.py:157
  7.2 0.0 collective-permute-done.other_ref.refs_2_
  7.2 0.0 copy-done.1
  7.2 0.5 %shard_map.61 = f32[32,256]{1,0:T(8,128)S(1)} custom-call(bf16[128,256]{1,0:T(8,128)(2,1)S(1)} %bitcast.10, bf16[128,256]{1,0:T(8,128)(2,1)S(1)} %collective-permute-done.other_ref.refs_2_, bf16[128,256]{1,0:T(8,128)(2,1)S(1)} %collective-permute-done.1.refs_0_.refs_1_, bf16[8,256,256]{2,1,0:T(8,128)(2,1)S(1)} %shard_map.60.refs_1_), custom_call_target="tpu_custom_call" | custom-call | bytes 1245184 | tf_op jit(solution)/shard_map/pallas_call | solution.py:170
  7.8 0.0 collective-permute-done.4
  7.8 1.4 %collective-permute-start.5 = (f32[24,256]{1,0:T(8,128)S(1)}, f32[24,256]{1,0:T(8,128)S(1)}, u32[]{:S(2)}, u32[]{:S(2)}) collective-permute-start(f32[24,256]{1,0:T(8,128)S(1)} %pad_maximum_fusion.2), channel_id=1, source_target_pairs={{0,5},{1,4},{2,7},{3,6},{4,1},{5,0},{6,3},{7,2},{8,13},{9,12},{10,... | collective-permute-start | bytes 73736 | tf_op jit(solution)/shard_map/ppermute | solution.py:157
  9.2 1.9 %collective-permute-done.5 = f32[24,256]{1,0:T(8,128)S(1)} collective-permute-done((f32[24,256]{1,0:T(8,128)S(1)}, f32[24,256]{1,0:T(8,128)S(1)}, u32[]{:S(2)}, u32[]{:S(2)}) %collective-permute-start.5) | collective-permute-done | bytes 24608 | tf_op jit(solution)/shard_map/ppermute | solution.py:157
  11.1 1.5 %collective-permute-start.6 = (f32[24,256]{1,0:T(8,128)S(1)}, f32[24,256]{1,0:T(8,128)S(1)}, u32[]{:S(2)}, u32[]{:S(2)}) collective-permute-start(f32[24,256]{1,0:T(8,128)S(1)} %pad_maximum_fusion.3), channel_id=1, source_target_pairs={{0,9},{1,8},{2,11},{3,10},{4,13},{5,12},{6,15},{7,14},{8,1},{9,0},... | collective-permute-start | bytes 73736 | tf_op jit(solution)/shard_map/ppermute | solution.py:157
  12.6 1.8 %collective-permute-done.6 = f32[24,256]{1,0:T(8,128)S(1)} collective-permute-done((f32[24,256]{1,0:T(8,128)S(1)}, f32[24,256]{1,0:T(8,128)S(1)}, u32[]{:S(2)}, u32[]{:S(2)}) %collective-permute-start.6) | collective-permute-done | bytes 24608 | tf_op jit(solution)/shard_map/ppermute | solution.py:157
  14.5 2.7 %collective-permute-start.7 = (f32[20,256]{1,0:T(8,128)S(1)}, f32[20,256]{1,0:T(8,128)S(1)}, u32[]{:S(2)}, u32[]{:S(2)}) collective-permute-start(f32[20,256]{1,0:T(8,128)S(1)} %maximum_maximum_fusion), channel_id=1, source_target_pairs={{0,17},{1,16},{2,19},{3,18},{4,21},{5,20},{6,23},{7,22},{8,25},{9,... | collective-permute-start | bytes 61448 | tf_op jit(solution)/shard_map/ppermute | solution.py:157
  17.2 0.1 collective-permute-start.10
  17.3 1.4 %collective-permute-done.7 = f32[20,256]{1,0:T(8,128)S(1)} collective-permute-done((f32[20,256]{1,0:T(8,128)S(1)}, f32[20,256]{1,0:T(8,128)S(1)}, u32[]{:S(2)}, u32[]{:S(2)}) %collective-permute-start.7) | collective-permute-done | bytes 20512 | tf_op jit(solution)/shard_map/ppermute | solution.py:157
  18.8 2.0 %collective-permute-start.8 = (f32[2,256]{1,0:T(2,128)S(1)}, f32[2,256]{1,0:T(2,128)S(1)}, u32[]{:S(2)}, u32[]{:S(2)}) collective-permute-start(f32[2,256]{1,0:T(2,128)S(1)} %get-tuple-element.20), channel_id=1, source_target_pairs={{0,2},{1,3},{2,0},{3,1},{4,7},{5,6},{6,5},{7,4},{8,11},{9,10},{10,... | collective-permute-start | bytes 6152 | tf_op jit(solution)/shard_map/ppermute | solution.py:157
  20.8 0.0 collective-permute-start.9
  20.8 0.0 collective-permute-done.10.refs_3_
  20.8 1.6 %shard_map.63 = f32[1024,256]{1,0:T(8,128)} custom-call(f32[64,128]{1,0:T(8,128)S(1)} %pad_maximum_fusion.1.normed_ref, bf16[128,256]{1,0:T(8,128)(2,1)S(1)} %bitcast.11, bf16[128,256]{1,0:T(8,128)(2,1)S(1)} %collective-permute-done.1.refs_0_.refs_1_, bf16[128,256]{1,0:T(8,128)(2,1)S(1)} %collective-permute-done.other_ref.refs_2_, ...), custom_call_target="tpu_custom_call" | custom-call | flops 268435456 | bytes 294912 | tf_op jit(solution)/shard_map/pallas_call | solution.py:170
  22.4 0.0 collective-permute-done.8.refs_1_
  22.4 0.0 collective-permute-done.9.refs_2_
  22.4 0.8 %shard_map.62 = f32[2,512]{1,0:T(2,128)} custom-call(bf16[2,512]{1,0:T(2,128)(2,1)S(1)} %bitcast.14, f32[1,512]{1,0:T(1,128)S(1)} %bitcast.16, f32[2,256]{1,0:T(2,128)S(1)} %get-tuple-element.21.refs_0_, f32[2,256]{1,0:T(2,128)S(1)} %collective-permute-done.8.refs_1_, f32[2,256]{1,0:T(2,128)S(1)} %collective-permute-done.9.refs_2_), custom_call_target="tpu_custom_call" | custom-call | bytes 10240 | tf_op jit(solution)/shard_map/pallas_call | solution.py:170
  (17 shorter events, 0.1 us)
Async XLA Ops:
  0.6 0.7 %copy-start.2 = (bf16[1,2,512]{2,1,0:T(2,128)(2,1)S(1)}, bf16[1,2,512]{2,1,0:T(2,128)(2,1)}, u32[]{:S(2)}) copy-start(bf16[1,2,512]{2,1,0:T(2,128)(2,1)} %param.4) | copy-start | bytes 6148
  0.6 4.0 %collective-permute-start.2 = (bf16[1024,256]{1,0:T(8,128)(2,1)}, bf16[1024,256]{1,0:T(8,128)(2,1)S(1)}, u32[]{:S(2)}, u32[]{:S(2)}) collective-permute-start(bf16[1024,256]{1,0:T(8,128)(2,1)} %bitcast.6), channel_id=1, source_target_pairs={{0,1},{1,0},{2,3},{3,2},{4,5},{5,4},{6,7},{7,6},{8,9},{9,8},{10,11... | collective-permute-start | bytes 1572872 | tf_op jit(solution)/shard_map/ppermute | solution.py:157
  1.3 3.2 %copy-start.3 = (f32[512]{0:T(512)S(1)}, f32[512]{0:T(512)}, u32[]{:S(2)}) copy-start(f32[512]{0:T(512)} %param.5) | copy-start | bytes 6148
  1.3 3.2 %collective-permute-start.3 = (bf16[2,512]{1,0:T(2,128)(2,1)S(1)}, bf16[2,512]{1,0:T(2,128)(2,1)S(1)}, u32[]{:S(2)}, u32[]{:S(2)}) collective-permute-start(bf16[2,512]{1,0:T(2,128)(2,1)S(1)} %bitcast.12), channel_id=1, source_target_pairs={{0,1},{1,0},{2,3},{3,2},{4,5},{5,4},{6,7},{7,6},{8,9},{9,8},{10,11... | collective-permute-start | bytes 6152 | tf_op jit(solution)/shard_map/ppermute | solution.py:157
  1.8 5.5 %collective-permute-start.1 = (bf16[128,256]{1,0:T(8,128)(2,1)}, bf16[128,256]{1,0:T(8,128)(2,1)S(1)}, u32[]{:S(2)}, u32[]{:S(2)}) collective-permute-start(bf16[128,256]{1,0:T(8,128)(2,1)} %bitcast.8), channel_id=1, source_target_pairs={{0,2},{1,3},{2,0},{3,1},{4,7},{5,6},{6,5},{7,4},{8,11},{9,10},{10,... | collective-permute-start | bytes 196616 | tf_op jit(solution)/shard_map/ppermute | solution.py:157
  4.3 3.0 %collective-permute-start = (bf16[128,256]{1,0:T(8,128)(2,1)}, bf16[128,256]{1,0:T(8,128)(2,1)S(1)}, u32[]{:S(2)}, u32[]{:S(2)}) collective-permute-start(bf16[128,256]{1,0:T(8,128)(2,1)} %bitcast.9), channel_id=1, source_target_pairs={{0,1},{1,0},{2,3},{3,2},{4,5},{5,4},{6,7},{7,6},{8,9},{9,8},{10,11... | collective-permute-start | bytes 196616 | tf_op jit(solution)/shard_map/ppermute | solution.py:157
  4.5 1.0 %copy-start = (bf16[128,8,256]{2,1,0:T(8,128)(2,1)S(1)}, bf16[128,8,256]{2,1,0:T(8,128)(2,1)}, u32[]{:S(2)}) copy-start(bf16[128,8,256]{2,1,0:T(8,128)(2,1)} %param.7) | copy-start | bytes 1572868
  4.6 2.6 %copy-start.1 = (bf16[1,16,8,256]{3,2,1,0:T(8,128)(2,1)S(1)}, bf16[1,16,8,256]{3,2,1,0:T(8,128)(2,1)}, u32[]{:S(2)}) copy-start(bf16[1,16,8,256]{3,2,1,0:T(8,128)(2,1)} %param.6) | copy-start | bytes 196612
  4.6 3.2 %collective-permute-start.4 = (f32[4,256]{1,0:T(4,128)S(1)}, f32[4,256]{1,0:T(4,128)S(1)}, u32[]{:S(2)}, u32[]{:S(2)}) collective-permute-start(f32[4,256]{1,0:T(4,128)S(1)} %get-tuple-element.13), channel_id=1, source_target_pairs={{0,3},{1,2},{2,1},{3,0},{4,7},{5,6},{6,5},{7,4},{8,11},{9,10},{10,... | collective-permute-start | bytes 12296 | tf_op jit(solution)/shard_map/ppermute | solution.py:157
  7.8 3.3 %collective-permute-start.5 = (f32[24,256]{1,0:T(8,128)S(1)}, f32[24,256]{1,0:T(8,128)S(1)}, u32[]{:S(2)}, u32[]{:S(2)}) collective-permute-start(f32[24,256]{1,0:T(8,128)S(1)} %pad_maximum_fusion.2), channel_id=1, source_target_pairs={{0,5},{1,4},{2,7},{3,6},{4,1},{5,0},{6,3},{7,2},{8,13},{9,12},{10,... | collective-permute-start | bytes 73736 | tf_op jit(solution)/shard_map/ppermute | solution.py:157
  11.1 3.3 %collective-permute-start.6 = (f32[24,256]{1,0:T(8,128)S(1)}, f32[24,256]{1,0:T(8,128)S(1)}, u32[]{:S(2)}, u32[]{:S(2)}) collective-permute-start(f32[24,256]{1,0:T(8,128)S(1)} %pad_maximum_fusion.3), channel_id=1, source_target_pairs={{0,9},{1,8},{2,11},{3,10},{4,13},{5,12},{6,15},{7,14},{8,1},{9,0},... | collective-permute-start | bytes 73736 | tf_op jit(solution)/shard_map/ppermute | solution.py:157
  14.5 4.2 %collective-permute-start.7 = (f32[20,256]{1,0:T(8,128)S(1)}, f32[20,256]{1,0:T(8,128)S(1)}, u32[]{:S(2)}, u32[]{:S(2)}) collective-permute-start(f32[20,256]{1,0:T(8,128)S(1)} %maximum_maximum_fusion), channel_id=1, source_target_pairs={{0,17},{1,16},{2,19},{3,18},{4,21},{5,20},{6,23},{7,22},{8,25},{9,... | collective-permute-start | bytes 61448 | tf_op jit(solution)/shard_map/ppermute | solution.py:157
  17.2 3.6 %collective-permute-start.10 = (bf16[128,256]{1,0:T(8,128)(2,1)S(1)}, bf16[128,256]{1,0:T(8,128)(2,1)S(1)}, u32[]{:S(2)}, u32[]{:S(2)}) collective-permute-start(bf16[128,256]{1,0:T(8,128)(2,1)S(1)} %collective-permute-done.1.refs_0_.refs_1_), channel_id=1, source_target_pairs={{0,1},{1,0},{2,3},{3,2},{4,5},{5,4},{6,7},{7,6},{8,9},{9,8},{10,11... | collective-permute-start | bytes 196616 | tf_op jit(solution)/shard_map/ppermute | solution.py:157
  18.8 3.6 %collective-permute-start.8 = (f32[2,256]{1,0:T(2,128)S(1)}, f32[2,256]{1,0:T(2,128)S(1)}, u32[]{:S(2)}, u32[]{:S(2)}) collective-permute-start(f32[2,256]{1,0:T(2,128)S(1)} %get-tuple-element.20), channel_id=1, source_target_pairs={{0,2},{1,3},{2,0},{3,1},{4,7},{5,6},{6,5},{7,4},{8,11},{9,10},{10,... | collective-permute-start | bytes 6152 | tf_op jit(solution)/shard_map/ppermute | solution.py:157
  20.8 1.6 %collective-permute-start.9 = (f32[2,256]{1,0:T(2,128)S(1)}, f32[2,256]{1,0:T(2,128)S(1)}, u32[]{:S(2)}, u32[]{:S(2)}) collective-permute-start(f32[2,256]{1,0:T(2,128)S(1)} %get-tuple-element.21.refs_0_), channel_id=1, source_target_pairs={{0,1},{1,0},{2,3},{3,2},{4,5},{5,4},{6,7},{7,6},{8,9},{9,8},{10,11... | collective-permute-start | bytes 6152 | tf_op jit(solution)/shard_map/ppermute | solution.py:157

commit v7 on v6

--- a/solution.py
+++ b/solution.py
@@ -75,10 +75,9 @@
     out_ref[...] = total
 
 
-def norm_kernel(columns, own_ref, other_ref, gain_ref, *out_refs):
-    core, column = lax.axis_index("ctx") & 1, lax.axis_index("ctx") >> 1
-    own, other = own_ref[...].astype(F32), other_ref[...].astype(F32)
-    raw = jnp.concatenate([jnp.where(core == 0, own, other), jnp.where(core == 0, other, own)], axis=0)
+def norm_kernel(columns, latent_ref, gain_ref, *out_refs):
+    column = lax.axis_index("ctx") >> 1
+    raw = latent_ref[...].astype(F32)
     rms = lax.rsqrt(jnp.mean(raw * raw, axis=1, keepdims=True) + 1e-06)
     normed = ((raw * rms) * gain_ref[...]).astype(BF16).astype(F32)
     width = normed.shape[1] // columns
@@ -89,20 +88,23 @@
         ref[...] = block
 
 
-def weight_grad_kernel(head_count, heads, owned, columns, normed_ref, *refs):
+def weight_grad_kernel(head_count, heads, owned, columns, own_ref, other_ref, *refs):
     shard_refs, out_ref, scratch_ref = refs[:-2], refs[-2], refs[-1]
     me = lax.axis_index("head")
     core = lax.axis_index("ctx") & 1
     role = core ^ parity(me, head_count.bit_length() - 1)
     rows = out_ref.shape[0] // heads
     tokens = head_count * owned
-    normed = normed_ref[...].astype(BF16)
+    normed = jnp.concatenate([own_ref[...], other_ref[...]], axis=0).astype(BF16)
     size = columns * tokens * heads
     at, to = iota((normed.shape[0], size), 0), iota((normed.shape[0], size), 1)
     token, j = (to // heads) % tokens, to // (heads * tokens)
+    distance = (token // owned) ^ me
+    turned = parity(distance, head_count.bit_length() - 1) ^ (j & 1)
     cots = []
     for side in range(2):
-        place = (((token // owned) ^ me) * columns + j) * 2 + (jnp.where(j == 0, core, role) ^ side)
+        held = jnp.where(j == 0, core, role) ^ side ^ core ^ turned
+        place = (held * head_count + distance) * columns + j
         spread = one_hot(at == place * owned + token % owned)
         scratch_ref[side] = matmul(normed, spread, 0, 0)
         cots.append(jnp.concatenate([r[...] for r in shard_refs[side * columns : (side + 1) * columns]], axis=0))
@@ -186,10 +188,9 @@
             shards += [ctx_swap(s, mask) for s in shards]
             mask *= 2
         far = shards[1:]
-    latent_other = ctx_swap(latent[0], 1)
     gain_row = gain.reshape(1, width)
-    block = jax.ShapeDtypeStruct((2 * owned, 2 * rows), F32)
-    normed = list(call(functools.partial(norm_kernel, columns), [block] * columns, latent[0], latent_other, gain_row, flops=10**9))
+    block = jax.ShapeDtypeStruct((owned, 2 * rows), F32)
+    normed = list(call(functools.partial(norm_kernel, columns), [block] * columns, latent[0], gain_row, flops=4 * 10**8))
 
     weight_flat = weight.reshape(rows * heads, channels)
     weight_other = ctx_swap(weight_flat, 1)
@@ -205,7 +206,7 @@
     while mask < ctx_count:
         for j in range(columns):
             if j & (mask >> 1):
-                normed[j] = ctx_swap(normed[j], mask | 1)
+                normed[j] = ctx_swap(normed[j], mask | (mask == 2))
         mask *= 2
     normed = jnp.concatenate(normed, axis=0)
 
@@ -221,18 +222,13 @@
     mask = 1
     while mask < head_count:
         half = sums.shape[0] // 2
-        if 2 * mask < head_count:
-            got = head_swap(jnp.concatenate([sums[half:], normed], axis=0), mask)
-            normed = jnp.concatenate([normed, got[half:]], axis=0)
-        else:
-            keep = jnp.where(core == 0, normed[:, :rows], normed[:, rows:])
-            send = jnp.where(core == 0, normed[:, rows:], normed[:, :rows])
-            count = send.shape[0] // 2
-            send = jnp.concatenate([send[:count], send[count:]], axis=1)
-            got = head_swap(jnp.concatenate([sums[half:], send], axis=0), mask)
-            normed = jnp.concatenate([keep, got[half:, :rows], got[half:, rows:]], axis=0)
+        got = head_swap(jnp.concatenate([sums[half:], normed], axis=0), mask)
+        normed = jnp.concatenate([normed, got[half:]], axis=0)
         sums = sums[:half] + got[:half]
         mask *= 2
+
+    normed_own = jnp.where(core == 0, normed[:, :rows], normed[:, rows:])
+    normed_other = ctx_swap(jnp.where(core == 0, normed[:, rows:], normed[:, :rows]), 1)
 
     blocks = [sums[j * owned : (j + 1) * owned] for j in range(columns)]
     mask = ctx_count // 2
@@ -248,7 +244,8 @@
     weight_grad = call(
         functools.partial(weight_grad_kernel, head_count, heads, owned, columns),
         jax.ShapeDtypeStruct((rows * heads, channels), F32),
-        normed,
+        normed_own,
+        normed_other,
         own,
         *far,
         other,
@@ -256,6 +253,7 @@
         scratch=[pltpu.VMEM((2, rows, columns * tokens * heads), F32)],
         flops=2 * rows * heads * channels * ctx_count * tokens * heads,
     )
+    weight_grad, *blocks = lax.optimization_barrier((weight_grad, *blocks))
     latent_gradient = call(
         functools.partial(latent_kernel, head_count, columns),
         jax.ShapeDtypeStruct((owned, width), F32),

time: 23.4 us -> 22.9 us (0.979)
  waiting for transfers between devices: 6.38 us -> 5.76 us
  starting transfers between devices: 12.3 us -> 12.7 us
    ppermute x11, waiting for transfers between devices: 6.38 us -> 5.76 us  [swap(): return lax.ppermute(value, ('head', 'ctx'), pairs)]
    ppermute x11, starting transfers between devices: 12.3 us -> 12.7 us  [swap(): return lax.ppermute(value, ('head', 'ctx'), pairs)]
where the time goes in v7:
time: 22.9 us; the launch traced here: 22.8 us
  starting transfers between devices  12.7 us (55%)
  waiting for transfers between devices  5.76 us (25%)
  Pallas kernels  3.4 us (15%)
  between operations  0.71 us (3%)
    ppermute x11, starting transfers between devices, swap(): return lax.ppermute(value, ('head', 'ctx'), pairs)  12.7 us
    ppermute x11, waiting for transfers between devices, swap(): return lax.ppermute(value, ('head', 'ctx'), pairs)  5.76 us
    pallas_call x5, Pallas kernels, call(): pl.pallas_call(kernel, out_shape=out, scratch_shapes=scratch, compiler_pa...  3.4 us
  transfers between devices with their start and end apart: 11, of which 4 were waited for; matrix products, arithmetic and copies ran while one was open for 0% of the time, Pallas kernels for 11%

profile of v7, /device:TPU:0, one launch (start us, length us, event | category | flops | bytes accessed | tf_op | source)
XLA Modules:
  0.0 22.8 jit_solution(16238898508861379035)
XLA Ops:
  0.6 0.5 %collective-permute-start = (bf16[1024,256]{1,0:T(8,128)(2,1)}, bf16[1024,256]{1,0:T(8,128)(2,1)S(1)}, u32[]{:S(2)}, u32[]{:S(2)}) collective-permute-start(bf16[1024,256]{1,0:T(8,128)(2,1)} %bitcast.6), channel_id=1, source_target_pairs={{0,1},{1,0},{2,3},{3,2},{4,5},{5,4},{6,7},{7,6},{8,9},{9,8},{10,11... | collective-permute-start | bytes 1572872 | tf_op jit(solution)/shard_map/ppermute | solution.py:159
  1.1 0.0 copy-start.3
  1.1 0.0 copy-start.2
  1.2 2.6 %collective-permute-start.3 = (bf16[128,256]{1,0:T(8,128)(2,1)}, bf16[128,256]{1,0:T(8,128)(2,1)S(1)}, u32[]{:S(2)}, u32[]{:S(2)}) collective-permute-start(bf16[128,256]{1,0:T(8,128)(2,1)} %bitcast.8), channel_id=1, source_target_pairs={{0,2},{1,3},{2,0},{3,1},{4,7},{5,6},{6,5},{7,4},{8,11},{9,10},{10,... | collective-permute-start | bytes 196616 | tf_op jit(solution)/shard_map/ppermute | solution.py:159
  3.7 0.2 collective-permute-start.2
  3.9 0.0 copy-done.3
  3.9 0.0 copy-done.2
  3.9 0.0 copy-start
  3.9 0.1 shard_map.59
  4.0 0.0 collective-permute-done.other_ref
  4.0 0.0 copy-start.1
  4.0 1.5 %collective-permute-start.1 = (f32[2,256]{1,0:T(2,128)S(1)}, f32[2,256]{1,0:T(2,128)S(1)}, u32[]{:S(2)}, u32[]{:S(2)}) collective-permute-start(f32[2,256]{1,0:T(2,128)S(1)} %get-tuple-element.14), channel_id=1, source_target_pairs={{0,3},{1,2},{2,1},{3,0},{4,7},{5,6},{6,5},{7,4},{8,11},{9,10},{10,... | collective-permute-start | bytes 6152 | tf_op jit(solution)/shard_map/ppermute | solution.py:159
  5.5 0.0 copy-done
  5.5 0.4 %shard_map.60.refs_1_ = bf16[8,256,256]{2,1,0:T(8,128)(2,1)S(1)} custom-call(bf16[1024,256]{1,0:T(8,128)(2,1)S(1)} %bitcast.7, bf16[1024,256]{1,0:T(8,128)(2,1)S(1)} %collective-permute-done.other_ref), custom_call_target="tpu_custom_call" | custom-call | bytes 1048576 | tf_op jit(solution)/shard_map/pallas_call | solution.py:172
  5.9 0.7 %collective-permute-done.3.refs_0_.refs_1_ = bf16[128,256]{1,0:T(8,128)(2,1)S(1)} collective-permute-done((bf16[128,256]{1,0:T(8,128)(2,1)}, bf16[128,256]{1,0:T(8,128)(2,1)S(1)}, u32[]{:S(2)}, u32[]{:S(2)}) %collective-permute-start.3) | collective-permute-done | bytes 65568 | tf_op jit(solution)/shard_map/ppermute | solution.py:159
  6.6 0.0 collective-permute-done.2.other_ref.refs_2_
  6.6 0.0 copy-done.1
  6.6 0.5 %shard_map.61 = f32[32,256]{1,0:T(8,128)S(1)} custom-call(bf16[128,256]{1,0:T(8,128)(2,1)S(1)} %bitcast.10, bf16[128,256]{1,0:T(8,128)(2,1)S(1)} %collective-permute-done.2.other_ref.refs_2_, bf16[128,256]{1,0:T(8,128)(2,1)S(1)} %collective-permute-done.3.refs_0_.refs_1_, bf16[8,256,256]{2,1,0:T(8,128)(2,1)S(1)} %shard_map.60.refs_1_), custom_call_target="tpu_custom_call" | custom-call | bytes 1245184 | tf_op jit(solution)/shard_map/pallas_call | solution.py:172
  7.2 0.0 collective-permute-done.1
  7.2 1.4 %collective-permute-start.4 = (f32[20,256]{1,0:T(8,128)S(1)}, f32[20,256]{1,0:T(8,128)S(1)}, u32[]{:S(2)}, u32[]{:S(2)}) collective-permute-start(f32[20,256]{1,0:T(8,128)S(1)} %pad_maximum_fusion), channel_id=1, source_target_pairs={{0,5},{1,4},{2,7},{3,6},{4,1},{5,0},{6,3},{7,2},{8,13},{9,12},{10,... | collective-permute-start | bytes 61448 | tf_op jit(solution)/shard_map/ppermute | solution.py:159
  8.6 1.9 %collective-permute-done.4 = f32[20,256]{1,0:T(8,128)S(1)} collective-permute-done((f32[20,256]{1,0:T(8,128)S(1)}, f32[20,256]{1,0:T(8,128)S(1)}, u32[]{:S(2)}, u32[]{:S(2)}) %collective-permute-start.4) | collective-permute-done | bytes 20512 | tf_op jit(solution)/shard_map/ppermute | solution.py:159
  10.5 1.5 %collective-permute-start.5 = (f32[16,256]{1,0:T(8,128)S(1)}, f32[16,256]{1,0:T(8,128)S(1)}, u32[]{:S(2)}, u32[]{:S(2)}) collective-permute-start(f32[16,256]{1,0:T(8,128)S(1)} %pad_maximum_fusion.1), channel_id=1, source_target_pairs={{0,9},{1,8},{2,11},{3,10},{4,13},{5,12},{6,15},{7,14},{8,1},{9,0},... | collective-permute-start | bytes 49160 | tf_op jit(solution)/shard_map/ppermute | solution.py:159
  12.0 1.7 %collective-permute-done.5 = f32[16,256]{1,0:T(8,128)S(1)} collective-permute-done((f32[16,256]{1,0:T(8,128)S(1)}, f32[16,256]{1,0:T(8,128)S(1)}, u32[]{:S(2)}, u32[]{:S(2)}) %collective-permute-start.5) | collective-permute-done | bytes 16416 | tf_op jit(solution)/shard_map/ppermute | solution.py:159
  13.8 0.1 concatenate.23
  13.9 2.6 %collective-permute-start.6 = (f32[20,256]{1,0:T(8,128)S(1)}, f32[20,256]{1,0:T(8,128)S(1)}, u32[]{:S(2)}, u32[]{:S(2)}) collective-permute-start(f32[20,256]{1,0:T(8,128)S(1)} %concatenate.23), channel_id=1, source_target_pairs={{0,17},{1,16},{2,19},{3,18},{4,21},{5,20},{6,23},{7,22},{8,25},{9,... | collective-permute-start | bytes 61448 | tf_op jit(solution)/shard_map/ppermute | solution.py:159
  16.5 0.2 collective-permute-start.8
  16.7 1.4 %collective-permute-done.6 = f32[20,256]{1,0:T(8,128)S(1)} collective-permute-done((f32[20,256]{1,0:T(8,128)S(1)}, f32[20,256]{1,0:T(8,128)S(1)}, u32[]{:S(2)}, u32[]{:S(2)}) %collective-permute-start.6) | collective-permute-done | bytes 20512 | tf_op jit(solution)/shard_map/ppermute | solution.py:159
  18.1 0.3 %collective-permute-start.7 = (f32[32,128]{1,0:T(8,128)S(1)}, f32[32,128]{1,0:T(8,128)S(1)}, u32[]{:S(2)}, u32[]{:S(2)}) collective-permute-start(f32[32,128]{1,0:T(8,128)S(1)} %get-tuple-element.20), channel_id=1, source_target_pairs={{0,1},{1,0},{2,3},{3,2},{4,5},{5,4},{6,7},{7,6},{8,9},{9,8},{10,11... | collective-permute-start | bytes 49160 | tf_op jit(solution)/shard_map/ppermute | solution.py:159
  18.4 1.9 %collective-permute-start.9 = (f32[2,256]{1,0:T(2,128)S(1)}, f32[2,256]{1,0:T(2,128)S(1)}, u32[]{:S(2)}, u32[]{:S(2)}) collective-permute-start(f32[2,256]{1,0:T(2,128)S(1)} %get-tuple-element.24), channel_id=1, source_target_pairs={{0,2},{1,3},{2,0},{3,1},{4,7},{5,6},{6,5},{7,4},{8,11},{9,10},{10,... | collective-permute-start | bytes 6152 | tf_op jit(solution)/shard_map/ppermute | solution.py:159
  20.3 0.1 collective-permute-start.10
  20.4 0.0 collective-permute-done.8.refs_3_
  20.4 0.0 collective-permute-done.7.other_ref
  20.4 1.6 %shard_map.62 = f32[1024,256]{1,0:T(8,128)} custom-call(f32[32,128]{1,0:T(8,128)S(1)} %get-tuple-element.21.own_ref, f32[32,128]{1,0:T(8,128)S(1)} %collective-permute-done.7.other_ref, bf16[128,256]{1,0:T(8,128)(2,1)S(1)} %bitcast.11, bf16[128,256]{1,0:T(8,128)(2,1)S(1)} %collective-permute-done.3.refs_0_.refs_1_, ...), custom_call_target="tpu_custom_call" | custom-call | flops 268435456 | bytes 294912 | tf_op jit(solution)/shard_map/pallas_call | solution.py:172
  22.0 0.0 collective-permute-done.9.refs_1_
  22.0 0.0 collective-permute-done.10.refs_2_
  22.0 0.8 %shard_map.63 = f32[2,512]{1,0:T(2,128)} custom-call(bf16[2,512]{1,0:T(2,128)(2,1)S(1)} %bitcast.13, f32[1,512]{1,0:T(1,128)S(1)} %bitcast.15, f32[2,256]{1,0:T(2,128)S(1)} %get-tuple-element.17.refs_0_, f32[2,256]{1,0:T(2,128)S(1)} %collective-permute-done.9.refs_1_, f32[2,256]{1,0:T(2,128)S(1)} %collective-permute-done.10.refs_2_), custom_call_target="tpu_custom_call" | custom-call | bytes 10240 | tf_op jit(solution)/shard_map/pallas_call | solution.py:172
  (13 shorter events, 0.1 us)
Async XLA Ops:
  0.6 3.4 %collective-permute-start = (bf16[1024,256]{1,0:T(8,128)(2,1)}, bf16[1024,256]{1,0:T(8,128)(2,1)S(1)}, u32[]{:S(2)}, u32[]{:S(2)}) collective-permute-start(bf16[1024,256]{1,0:T(8,128)(2,1)} %bitcast.6), channel_id=1, source_target_pairs={{0,1},{1,0},{2,3},{3,2},{4,5},{5,4},{6,7},{7,6},{8,9},{9,8},{10,11... | collective-permute-start | bytes 1572872 | tf_op jit(solution)/shard_map/ppermute | solution.py:159
  1.1 2.7 %copy-start.3 = (f32[512]{0:T(512)S(1)}, f32[512]{0:T(512)}, u32[]{:S(2)}) copy-start(f32[512]{0:T(512)} %param.5) | copy-start | bytes 6148
  1.1 2.7 %copy-start.2 = (bf16[1,2,512]{2,1,0:T(2,128)(2,1)S(1)}, bf16[1,2,512]{2,1,0:T(2,128)(2,1)}, u32[]{:S(2)}) copy-start(bf16[1,2,512]{2,1,0:T(2,128)(2,1)} %param.4) | copy-start | bytes 6148
  1.2 5.5 %collective-permute-start.3 = (bf16[128,256]{1,0:T(8,128)(2,1)}, bf16[128,256]{1,0:T(8,128)(2,1)S(1)}, u32[]{:S(2)}, u32[]{:S(2)}) collective-permute-start(bf16[128,256]{1,0:T(8,128)(2,1)} %bitcast.8), channel_id=1, source_target_pairs={{0,2},{1,3},{2,0},{3,1},{4,7},{5,6},{6,5},{7,4},{8,11},{9,10},{10,... | collective-permute-start | bytes 196616 | tf_op jit(solution)/shard_map/ppermute | solution.py:159
  3.7 2.9 %collective-permute-start.2 = (bf16[128,256]{1,0:T(8,128)(2,1)}, bf16[128,256]{1,0:T(8,128)(2,1)S(1)}, u32[]{:S(2)}, u32[]{:S(2)}) collective-permute-start(bf16[128,256]{1,0:T(8,128)(2,1)} %bitcast.9), channel_id=1, source_target_pairs={{0,1},{1,0},{2,3},{3,2},{4,5},{5,4},{6,7},{7,6},{8,9},{9,8},{10,11... | collective-permute-start | bytes 196616 | tf_op jit(solution)/shard_map/ppermute | solution.py:159
  3.9 1.6 %copy-start = (bf16[128,8,256]{2,1,0:T(8,128)(2,1)S(1)}, bf16[128,8,256]{2,1,0:T(8,128)(2,1)}, u32[]{:S(2)}) copy-start(bf16[128,8,256]{2,1,0:T(8,128)(2,1)} %param.7) | copy-start | bytes 1572868
  4.0 2.6 %copy-start.1 = (bf16[1,16,8,256]{3,2,1,0:T(8,128)(2,1)S(1)}, bf16[1,16,8,256]{3,2,1,0:T(8,128)(2,1)}, u32[]{:S(2)}) copy-start(bf16[1,16,8,256]{3,2,1,0:T(8,128)(2,1)} %param.6) | copy-start | bytes 196612
  4.0 3.2 %collective-permute-start.1 = (f32[2,256]{1,0:T(2,128)S(1)}, f32[2,256]{1,0:T(2,128)S(1)}, u32[]{:S(2)}, u32[]{:S(2)}) collective-permute-start(f32[2,256]{1,0:T(2,128)S(1)} %get-tuple-element.14), channel_id=1, source_target_pairs={{0,3},{1,2},{2,1},{3,0},{4,7},{5,6},{6,5},{7,4},{8,11},{9,10},{10,... | collective-permute-start | bytes 6152 | tf_op jit(solution)/shard_map/ppermute | solution.py:159
  7.2 3.3 %collective-permute-start.4 = (f32[20,256]{1,0:T(8,128)S(1)}, f32[20,256]{1,0:T(8,128)S(1)}, u32[]{:S(2)}, u32[]{:S(2)}) collective-permute-start(f32[20,256]{1,0:T(8,128)S(1)} %pad_maximum_fusion), channel_id=1, source_target_pairs={{0,5},{1,4},{2,7},{3,6},{4,1},{5,0},{6,3},{7,2},{8,13},{9,12},{10,... | collective-permute-start | bytes 61448 | tf_op jit(solution)/shard_map/ppermute | solution.py:159
  10.5 3.2 %collective-permute-start.5 = (f32[16,256]{1,0:T(8,128)S(1)}, f32[16,256]{1,0:T(8,128)S(1)}, u32[]{:S(2)}, u32[]{:S(2)}) collective-permute-start(f32[16,256]{1,0:T(8,128)S(1)} %pad_maximum_fusion.1), channel_id=1, source_target_pairs={{0,9},{1,8},{2,11},{3,10},{4,13},{5,12},{6,15},{7,14},{8,1},{9,0},... | collective-permute-start | bytes 49160 | tf_op jit(solution)/shard_map/ppermute | solution.py:159
  13.9 4.2 %collective-permute-start.6 = (f32[20,256]{1,0:T(8,128)S(1)}, f32[20,256]{1,0:T(8,128)S(1)}, u32[]{:S(2)}, u32[]{:S(2)}) collective-permute-start(f32[20,256]{1,0:T(8,128)S(1)} %concatenate.23), channel_id=1, source_target_pairs={{0,17},{1,16},{2,19},{3,18},{4,21},{5,20},{6,23},{7,22},{8,25},{9,... | collective-permute-start | bytes 61448 | tf_op jit(solution)/shard_map/ppermute | solution.py:159
  16.5 3.9 %collective-permute-start.8 = (bf16[128,256]{1,0:T(8,128)(2,1)S(1)}, bf16[128,256]{1,0:T(8,128)(2,1)S(1)}, u32[]{:S(2)}, u32[]{:S(2)}) collective-permute-start(bf16[128,256]{1,0:T(8,128)(2,1)S(1)} %collective-permute-done.3.refs_0_.refs_1_), channel_id=1, source_target_pairs={{0,1},{1,0},{2,3},{3,2},{4,5},{5,4},{6,7},{7,6},{8,9},{9,8},{10,11... | collective-permute-start | bytes 196616 | tf_op jit(solution)/shard_map/ppermute | solution.py:159
  18.1 2.2 %collective-permute-start.7 = (f32[32,128]{1,0:T(8,128)S(1)}, f32[32,128]{1,0:T(8,128)S(1)}, u32[]{:S(2)}, u32[]{:S(2)}) collective-permute-start(f32[32,128]{1,0:T(8,128)S(1)} %get-tuple-element.20), channel_id=1, source_target_pairs={{0,1},{1,0},{2,3},{3,2},{4,5},{5,4},{6,7},{7,6},{8,9},{9,8},{10,11... | collective-permute-start | bytes 49160 | tf_op jit(solution)/shard_map/ppermute | solution.py:159
  18.4 3.6 %collective-permute-start.9 = (f32[2,256]{1,0:T(2,128)S(1)}, f32[2,256]{1,0:T(2,128)S(1)}, u32[]{:S(2)}, u32[]{:S(2)}) collective-permute-start(f32[2,256]{1,0:T(2,128)S(1)} %get-tuple-element.24), channel_id=1, source_target_pairs={{0,2},{1,3},{2,0},{3,1},{4,7},{5,6},{6,5},{7,4},{8,11},{9,10},{10,... | collective-permute-start | bytes 6152 | tf_op jit(solution)/shard_map/ppermute | solution.py:159
  20.3 1.7 %collective-permute-start.10 = (f32[2,256]{1,0:T(2,128)S(1)}, f32[2,256]{1,0:T(2,128)S(1)}, u32[]{:S(2)}, u32[]{:S(2)}) collective-permute-start(f32[2,256]{1,0:T(2,128)S(1)} %get-tuple-element.17.refs_0_), channel_id=1, source_target_pairs={{0,1},{1,0},{2,3},{3,2},{4,5},{5,4},{6,7},{7,6},{8,9},{9,8},{10,11... | collective-permute-start | bytes 6152 | tf_op jit(solution)/shard_map/ppermute | solution.py:159

commit v8 on v7

--- a/solution.py
+++ b/solution.py
@@ -31,8 +31,8 @@
     return out
 
 
-def parity(value, count):
-    out = value & 1
+def even_bits(value, count):
+    out = 1 ^ (value & 1)
     for bit in range(1, count):
         out = out ^ ((value >> bit) & 1)
     return out
@@ -59,7 +59,7 @@
     me = lax.axis_index("head")
     bits = head_count.bit_length() - 1
     rows = head_count * owned
-    first = jnp.where(parity(me, bits) == 0, own_ref[...], other_ref[...])
+    first = jnp.where(even_bits(me, bits) == 0, own_ref[...], other_ref[...])
     stacked = jnp.concatenate([first] + [ref[...] for ref in shard_refs], axis=0)
     size = shards * rows * heads
     to, at = iota((size, size), 0), iota((size, size), 1)
@@ -92,7 +92,7 @@
     shard_refs, out_ref, scratch_ref = refs[:-2], refs[-2], refs[-1]
     me = lax.axis_index("head")
     core = lax.axis_index("ctx") & 1
-    role = core ^ parity(me, head_count.bit_length() - 1)
+    role = core ^ even_bits(me, head_count.bit_length() - 1)
     rows = out_ref.shape[0] // heads
     tokens = head_count * owned
     normed = jnp.concatenate([own_ref[...], other_ref[...]], axis=0).astype(BF16)
@@ -100,7 +100,7 @@
     at, to = iota((normed.shape[0], size), 0), iota((normed.shape[0], size), 1)
     token, j = (to // heads) % tokens, to // (heads * tokens)
     distance = (token // owned) ^ me
-    turned = parity(distance, head_count.bit_length() - 1) ^ (j & 1)
+    turned = 1 ^ even_bits(distance, head_count.bit_length() - 1) ^ (j & 1)
     cots = []
     for side in range(2):
         held = jnp.where(j == 0, core, role) ^ side ^ core ^ turned
@@ -123,13 +123,13 @@
 def latent_kernel(head_count, columns, latent_ref, gain_ref, *refs):
     block_refs, other_refs, out_ref = refs[:columns], refs[columns:-1], refs[-1]
     column = lax.axis_index("ctx") >> 1
-    odd = parity(lax.axis_index("head"), head_count.bit_length() - 1)
+    crossed = even_bits(lax.axis_index("head"), head_count.bit_length() - 1)
     raw = latent_ref[...].astype(F32)
     rms = lax.rsqrt(jnp.mean(raw * raw, axis=1, keepdims=True) + 1e-06)
     hat = raw * rms
     relative = [ref[...] for ref in block_refs]
     for j, ref in enumerate(other_refs):
-        relative[2 * j] = jnp.where(odd == 0, relative[2 * j], ref[...])
+        relative[2 * j] = jnp.where(crossed == 0, relative[2 * j], ref[...])
     blocks = []
     for b in range(columns):
         block = relative[0]
@@ -162,7 +162,7 @@
         return swap(value, lambda h, c: (h, c ^ mask))
 
     def role_swap(value, mask):
-        return swap(value, lambda h, c: (h, c ^ mask ^ parity(h, bits)))
+        return swap(value, lambda h, c: (h, c ^ mask ^ even_bits(h, bits)))
 
     def head_swap(value, mask):
         return swap(value, lambda h, c: (h ^ mask, c ^ 1))
@@ -181,7 +181,7 @@
     far = [role_swap(own, 2)]
     other = ctx_swap(own, 1)
     if columns > 2:
-        first = jnp.where(parity(lax.axis_index("head"), bits) == 0, own, other)
+        first = jnp.where(even_bits(lax.axis_index("head"), bits) == 0, own, other)
         shards = [first] + far
         mask = 4
         while mask < ctx_count:

time: 22.9 us -> 22.9 us (level)
  waiting for transfers between devices: 5.76 us -> 4.9 us
  starting transfers between devices: 12.7 us -> 13.5 us
    ppermute x11, waiting for transfers between devices: 5.76 us -> 4.9 us  [swap(): return lax.ppermute(value, ('head', 'ctx'), pairs)]
    ppermute x11, starting transfers between devices: 12.7 us -> 13.5 us  [swap(): return lax.ppermute(value, ('head', 'ctx'), pairs)]
  transfers between devices with their start and end apart: 11 -> 11, of which waited for: 4 -> 5; matrix products, arithmetic and copies ran while one was open for 0% -> 0% of each run, Pallas kernels for 11% -> 12%
where the time goes in v8:
time: 22.9 us; the launch traced here: 22.7 us
  starting transfers between devices  13.5 us (59%)
  waiting for transfers between devices  4.9 us (21%)
  Pallas kernels  3.4 us (15%)
  between operations  0.7 us (3%)
    ppermute x11, starting transfers between devices, swap(): return lax.ppermute(value, ('head', 'ctx'), pairs)  13.5 us
    ppermute x11, waiting for transfers between devices, swap(): return lax.ppermute(value, ('head', 'ctx'), pairs)  4.9 us
    pallas_call x5, Pallas kernels, call(): pl.pallas_call(kernel, out_shape=out, scratch_shapes=scratch, compiler_pa...  3.4 us
  transfers between devices with their start and end apart: 11, of which 5 were waited for; matrix products, arithmetic and copies ran while one was open for 0% of the time, Pallas kernels for 12%

profile of v8, /device:TPU:0, one launch (start us, length us, event | category | flops | bytes accessed | tf_op | source)
XLA Modules:
  0.0 22.7 jit_solution(16370360464035340937)
XLA Ops:
  0.6 0.5 %collective-permute-start = (bf16[1024,256]{1,0:T(8,128)(2,1)}, bf16[1024,256]{1,0:T(8,128)(2,1)S(1)}, u32[]{:S(2)}, u32[]{:S(2)}) collective-permute-start(bf16[1024,256]{1,0:T(8,128)(2,1)} %bitcast.6), channel_id=1, source_target_pairs={{0,1},{1,0},{2,3},{3,2},{4,5},{5,4},{6,7},{7,6},{8,9},{9,8},{10,11... | collective-permute-start | bytes 1572872 | tf_op jit(solution)/shard_map/ppermute | solution.py:159
  1.1 0.0 copy-start.3
  1.1 0.0 copy-start.2
  1.2 2.6 %collective-permute-start.3 = (bf16[128,256]{1,0:T(8,128)(2,1)}, bf16[128,256]{1,0:T(8,128)(2,1)S(1)}, u32[]{:S(2)}, u32[]{:S(2)}) collective-permute-start(bf16[128,256]{1,0:T(8,128)(2,1)} %bitcast.8), channel_id=1, source_target_pairs={{0,3},{1,2},{2,1},{3,0},{4,6},{5,7},{6,4},{7,5},{8,10},{9,11},{10,... | collective-permute-start | bytes 196616 | tf_op jit(solution)/shard_map/ppermute | solution.py:159
  3.8 0.1 collective-permute-start.2
  3.8 0.0 copy-done.3
  3.9 0.0 copy-done.2
  3.9 0.0 copy-start
  3.9 0.1 shard_map.59
  4.0 0.0 collective-permute-done.other_ref
  4.0 0.0 copy-start.1
  4.0 1.5 %collective-permute-start.1 = (f32[2,256]{1,0:T(2,128)S(1)}, f32[2,256]{1,0:T(2,128)S(1)}, u32[]{:S(2)}, u32[]{:S(2)}) collective-permute-start(f32[2,256]{1,0:T(2,128)S(1)} %get-tuple-element.14), channel_id=1, source_target_pairs={{0,3},{1,2},{2,1},{3,0},{4,7},{5,6},{6,5},{7,4},{8,11},{9,10},{10,... | collective-permute-start | bytes 6152 | tf_op jit(solution)/shard_map/ppermute | solution.py:159
  5.5 0.0 copy-done
  5.5 0.4 %shard_map.60.refs_1_ = bf16[8,256,256]{2,1,0:T(8,128)(2,1)S(1)} custom-call(bf16[1024,256]{1,0:T(8,128)(2,1)S(1)} %bitcast.7, bf16[1024,256]{1,0:T(8,128)(2,1)S(1)} %collective-permute-done.other_ref), custom_call_target="tpu_custom_call" | custom-call | bytes 1048576 | tf_op jit(solution)/shard_map/pallas_call | solution.py:172
  5.9 0.4 %collective-permute-done.3.refs_0_.refs_1_ = bf16[128,256]{1,0:T(8,128)(2,1)S(1)} collective-permute-done((bf16[128,256]{1,0:T(8,128)(2,1)}, bf16[128,256]{1,0:T(8,128)(2,1)S(1)}, u32[]{:S(2)}, u32[]{:S(2)}) %collective-permute-start.3) | collective-permute-done | bytes 65568 | tf_op jit(solution)/shard_map/ppermute | solution.py:159
  6.3 0.0 collective-permute-done.2.other_ref.refs_2_
  6.3 0.0 copy-done.1
  6.3 0.5 %shard_map.61 = f32[32,256]{1,0:T(8,128)S(1)} custom-call(bf16[128,256]{1,0:T(8,128)(2,1)S(1)} %bitcast.10, bf16[128,256]{1,0:T(8,128)(2,1)S(1)} %collective-permute-done.2.other_ref.refs_2_, bf16[128,256]{1,0:T(8,128)(2,1)S(1)} %collective-permute-done.3.refs_0_.refs_1_, bf16[8,256,256]{2,1,0:T(8,128)(2,1)S(1)} %shard_map.60.refs_1_), custom_call_target="tpu_custom_call" | custom-call | bytes 1245184 | tf_op jit(solution)/shard_map/pallas_call | solution.py:172
  6.9 0.2 collective-permute-done.1
  7.1 1.5 %collective-permute-start.4 = (f32[20,256]{1,0:T(8,128)S(1)}, f32[20,256]{1,0:T(8,128)S(1)}, u32[]{:S(2)}, u32[]{:S(2)}) collective-permute-start(f32[20,256]{1,0:T(8,128)S(1)} %pad_maximum_fusion), channel_id=1, source_target_pairs={{0,5},{1,4},{2,7},{3,6},{4,1},{5,0},{6,3},{7,2},{8,13},{9,12},{10,... | collective-permute-start | bytes 61448 | tf_op jit(solution)/shard_map/ppermute | solution.py:159
  8.6 1.8 %collective-permute-done.4 = f32[20,256]{1,0:T(8,128)S(1)} collective-permute-done((f32[20,256]{1,0:T(8,128)S(1)}, f32[20,256]{1,0:T(8,128)S(1)}, u32[]{:S(2)}, u32[]{:S(2)}) %collective-permute-start.4) | collective-permute-done | bytes 20512 | tf_op jit(solution)/shard_map/ppermute | solution.py:159
  10.4 1.9 %collective-permute-start.5 = (f32[16,256]{1,0:T(8,128)S(1)}, f32[16,256]{1,0:T(8,128)S(1)}, u32[]{:S(2)}, u32[]{:S(2)}) collective-permute-start(f32[16,256]{1,0:T(8,128)S(1)} %pad_maximum_fusion.1), channel_id=1, source_target_pairs={{0,9},{1,8},{2,11},{3,10},{4,13},{5,12},{6,15},{7,14},{8,1},{9,0},... | collective-permute-start | bytes 49160 | tf_op jit(solution)/shard_map/ppermute | solution.py:159
  12.3 1.4 %collective-permute-done.5 = f32[16,256]{1,0:T(8,128)S(1)} collective-permute-done((f32[16,256]{1,0:T(8,128)S(1)}, f32[16,256]{1,0:T(8,128)S(1)}, u32[]{:S(2)}, u32[]{:S(2)}) %collective-permute-start.5) | collective-permute-done | bytes 16416 | tf_op jit(solution)/shard_map/ppermute | solution.py:159
  13.8 0.1 concatenate.23
  13.9 2.8 %collective-permute-start.6 = (f32[20,256]{1,0:T(8,128)S(1)}, f32[20,256]{1,0:T(8,128)S(1)}, u32[]{:S(2)}, u32[]{:S(2)}) collective-permute-start(f32[20,256]{1,0:T(8,128)S(1)} %concatenate.23), channel_id=1, source_target_pairs={{0,17},{1,16},{2,19},{3,18},{4,21},{5,20},{6,23},{7,22},{8,25},{9,... | collective-permute-start | bytes 61448 | tf_op jit(solution)/shard_map/ppermute | solution.py:159
  16.7 0.4 %collective-permute-start.8 = (bf16[128,256]{1,0:T(8,128)(2,1)S(1)}, bf16[128,256]{1,0:T(8,128)(2,1)S(1)}, u32[]{:S(2)}, u32[]{:S(2)}) collective-permute-start(bf16[128,256]{1,0:T(8,128)(2,1)S(1)} %collective-permute-done.3.refs_0_.refs_1_), channel_id=1, source_target_pairs={{0,1},{1,0},{2,3},{3,2},{4,5},{5,4},{6,7},{7,6},{8,9},{9,8},{10,11... | collective-permute-start | bytes 196616 | tf_op jit(solution)/shard_map/ppermute | solution.py:159
  17.1 1.1 %collective-permute-done.6 = f32[20,256]{1,0:T(8,128)S(1)} collective-permute-done((f32[20,256]{1,0:T(8,128)S(1)}, f32[20,256]{1,0:T(8,128)S(1)}, u32[]{:S(2)}, u32[]{:S(2)}) %collective-permute-start.6) | collective-permute-done | bytes 20512 | tf_op jit(solution)/shard_map/ppermute | solution.py:159
  18.2 0.5 %collective-permute-start.7 = (f32[32,128]{1,0:T(8,128)S(1)}, f32[32,128]{1,0:T(8,128)S(1)}, u32[]{:S(2)}, u32[]{:S(2)}) collective-permute-start(f32[32,128]{1,0:T(8,128)S(1)} %get-tuple-element.20), channel_id=1, source_target_pairs={{0,1},{1,0},{2,3},{3,2},{4,5},{5,4},{6,7},{7,6},{8,9},{9,8},{10,11... | collective-permute-start | bytes 49160 | tf_op jit(solution)/shard_map/ppermute | solution.py:159
  18.7 1.3 %collective-permute-start.9 = (f32[2,256]{1,0:T(2,128)S(1)}, f32[2,256]{1,0:T(2,128)S(1)}, u32[]{:S(2)}, u32[]{:S(2)}) collective-permute-start(f32[2,256]{1,0:T(2,128)S(1)} %get-tuple-element.24), channel_id=1, source_target_pairs={{0,3},{1,2},{2,1},{3,0},{4,6},{5,7},{6,4},{7,5},{8,10},{9,11},{10,... | collective-permute-start | bytes 6152 | tf_op jit(solution)/shard_map/ppermute | solution.py:159
  20.0 0.4 %collective-permute-start.10 = (f32[2,256]{1,0:T(2,128)S(1)}, f32[2,256]{1,0:T(2,128)S(1)}, u32[]{:S(2)}, u32[]{:S(2)}) collective-permute-start(f32[2,256]{1,0:T(2,128)S(1)} %get-tuple-element.17.refs_0_), channel_id=1, source_target_pairs={{0,1},{1,0},{2,3},{3,2},{4,5},{5,4},{6,7},{7,6},{8,9},{9,8},{10,11... | collective-permute-start | bytes 6152 | tf_op jit(solution)/shard_map/ppermute | solution.py:159
  20.3 0.0 collective-permute-done.8.refs_3_
  20.3 0.0 collective-permute-done.7.other_ref
  20.3 1.6 %shard_map.62 = f32[1024,256]{1,0:T(8,128)} custom-call(f32[32,128]{1,0:T(8,128)S(1)} %get-tuple-element.21.own_ref, f32[32,128]{1,0:T(8,128)S(1)} %collective-permute-done.7.other_ref, bf16[128,256]{1,0:T(8,128)(2,1)S(1)} %bitcast.11, bf16[128,256]{1,0:T(8,128)(2,1)S(1)} %collective-permute-done.3.refs_0_.refs_1_, ...), custom_call_target="tpu_custom_call" | custom-call | flops 268435456 | bytes 294912 | tf_op jit(solution)/shard_map/pallas_call | solution.py:172
  21.9 0.0 collective-permute-done.9.refs_1_
  21.9 0.0 collective-permute-done.10.refs_2_
  21.9 0.8 %shard_map.63 = f32[2,512]{1,0:T(2,128)} custom-call(bf16[2,512]{1,0:T(2,128)(2,1)S(1)} %bitcast.13, f32[1,512]{1,0:T(1,128)S(1)} %bitcast.15, f32[2,256]{1,0:T(2,128)S(1)} %get-tuple-element.17.refs_0_, f32[2,256]{1,0:T(2,128)S(1)} %collective-permute-done.9.refs_1_, f32[2,256]{1,0:T(2,128)S(1)} %collective-permute-done.10.refs_2_), custom_call_target="tpu_custom_call" | custom-call | bytes 10240 | tf_op jit(solution)/shard_map/pallas_call | solution.py:172
  (13 shorter events, 0.1 us)
Async XLA Ops:
  0.6 3.3 %collective-permute-start = (bf16[1024,256]{1,0:T(8,128)(2,1)}, bf16[1024,256]{1,0:T(8,128)(2,1)S(1)}, u32[]{:S(2)}, u32[]{:S(2)}) collective-permute-start(bf16[1024,256]{1,0:T(8,128)(2,1)} %bitcast.6), channel_id=1, source_target_pairs={{0,1},{1,0},{2,3},{3,2},{4,5},{5,4},{6,7},{7,6},{8,9},{9,8},{10,11... | collective-permute-start | bytes 1572872 | tf_op jit(solution)/shard_map/ppermute | solution.py:159
  1.1 2.7 %copy-start.3 = (f32[512]{0:T(512)S(1)}, f32[512]{0:T(512)}, u32[]{:S(2)}) copy-start(f32[512]{0:T(512)} %param.5) | copy-start | bytes 6148
  1.1 2.7 %copy-start.2 = (bf16[1,2,512]{2,1,0:T(2,128)(2,1)S(1)}, bf16[1,2,512]{2,1,0:T(2,128)(2,1)}, u32[]{:S(2)}) copy-start(bf16[1,2,512]{2,1,0:T(2,128)(2,1)} %param.4) | copy-start | bytes 6148
  1.2 5.2 %collective-permute-start.3 = (bf16[128,256]{1,0:T(8,128)(2,1)}, bf16[128,256]{1,0:T(8,128)(2,1)S(1)}, u32[]{:S(2)}, u32[]{:S(2)}) collective-permute-start(bf16[128,256]{1,0:T(8,128)(2,1)} %bitcast.8), channel_id=1, source_target_pairs={{0,3},{1,2},{2,1},{3,0},{4,6},{5,7},{6,4},{7,5},{8,10},{9,11},{10,... | collective-permute-start | bytes 196616 | tf_op jit(solution)/shard_map/ppermute | solution.py:159
  3.8 2.6 %collective-permute-start.2 = (bf16[128,256]{1,0:T(8,128)(2,1)}, bf16[128,256]{1,0:T(8,128)(2,1)S(1)}, u32[]{:S(2)}, u32[]{:S(2)}) collective-permute-start(bf16[128,256]{1,0:T(8,128)(2,1)} %bitcast.9), channel_id=1, source_target_pairs={{0,1},{1,0},{2,3},{3,2},{4,5},{5,4},{6,7},{7,6},{8,9},{9,8},{10,11... | collective-permute-start | bytes 196616 | tf_op jit(solution)/shard_map/ppermute | solution.py:159
  3.9 1.6 %copy-start = (bf16[128,8,256]{2,1,0:T(8,128)(2,1)S(1)}, bf16[128,8,256]{2,1,0:T(8,128)(2,1)}, u32[]{:S(2)}) copy-start(bf16[128,8,256]{2,1,0:T(8,128)(2,1)} %param.7) | copy-start | bytes 1572868
  4.0 2.4 %copy-start.1 = (bf16[1,16,8,256]{3,2,1,0:T(8,128)(2,1)S(1)}, bf16[1,16,8,256]{3,2,1,0:T(8,128)(2,1)}, u32[]{:S(2)}) copy-start(bf16[1,16,8,256]{3,2,1,0:T(8,128)(2,1)} %param.6) | copy-start | bytes 196612
  4.0 3.1 %collective-permute-start.1 = (f32[2,256]{1,0:T(2,128)S(1)}, f32[2,256]{1,0:T(2,128)S(1)}, u32[]{:S(2)}, u32[]{:S(2)}) collective-permute-start(f32[2,256]{1,0:T(2,128)S(1)} %get-tuple-element.14), channel_id=1, source_target_pairs={{0,3},{1,2},{2,1},{3,0},{4,7},{5,6},{6,5},{7,4},{8,11},{9,10},{10,... | collective-permute-start | bytes 6152 | tf_op jit(solution)/shard_map/ppermute | solution.py:159
  7.1 3.3 %collective-permute-start.4 = (f32[20,256]{1,0:T(8,128)S(1)}, f32[20,256]{1,0:T(8,128)S(1)}, u32[]{:S(2)}, u32[]{:S(2)}) collective-permute-start(f32[20,256]{1,0:T(8,128)S(1)} %pad_maximum_fusion), channel_id=1, source_target_pairs={{0,5},{1,4},{2,7},{3,6},{4,1},{5,0},{6,3},{7,2},{8,13},{9,12},{10,... | collective-permute-start | bytes 61448 | tf_op jit(solution)/shard_map/ppermute | solution.py:159
  10.4 3.4 %collective-permute-start.5 = (f32[16,256]{1,0:T(8,128)S(1)}, f32[16,256]{1,0:T(8,128)S(1)}, u32[]{:S(2)}, u32[]{:S(2)}) collective-permute-start(f32[16,256]{1,0:T(8,128)S(1)} %pad_maximum_fusion.1), channel_id=1, source_target_pairs={{0,9},{1,8},{2,11},{3,10},{4,13},{5,12},{6,15},{7,14},{8,1},{9,0},... | collective-permute-start | bytes 49160 | tf_op jit(solution)/shard_map/ppermute | solution.py:159
  13.9 4.3 %collective-permute-start.6 = (f32[20,256]{1,0:T(8,128)S(1)}, f32[20,256]{1,0:T(8,128)S(1)}, u32[]{:S(2)}, u32[]{:S(2)}) collective-permute-start(f32[20,256]{1,0:T(8,128)S(1)} %concatenate.23), channel_id=1, source_target_pairs={{0,17},{1,16},{2,19},{3,18},{4,21},{5,20},{6,23},{7,22},{8,25},{9,... | collective-permute-start | bytes 61448 | tf_op jit(solution)/shard_map/ppermute | solution.py:159
  16.7 3.7 %collective-permute-start.8 = (bf16[128,256]{1,0:T(8,128)(2,1)S(1)}, bf16[128,256]{1,0:T(8,128)(2,1)S(1)}, u32[]{:S(2)}, u32[]{:S(2)}) collective-permute-start(bf16[128,256]{1,0:T(8,128)(2,1)S(1)} %collective-permute-done.3.refs_0_.refs_1_), channel_id=1, source_target_pairs={{0,1},{1,0},{2,3},{3,2},{4,5},{5,4},{6,7},{7,6},{8,9},{9,8},{10,11... | collective-permute-start | bytes 196616 | tf_op jit(solution)/shard_map/ppermute | solution.py:159
  18.2 2.1 %collective-permute-start.7 = (f32[32,128]{1,0:T(8,128)S(1)}, f32[32,128]{1,0:T(8,128)S(1)}, u32[]{:S(2)}, u32[]{:S(2)}) collective-permute-start(f32[32,128]{1,0:T(8,128)S(1)} %get-tuple-element.20), channel_id=1, source_target_pairs={{0,1},{1,0},{2,3},{3,2},{4,5},{5,4},{6,7},{7,6},{8,9},{9,8},{10,11... | collective-permute-start | bytes 49160 | tf_op jit(solution)/shard_map/ppermute | solution.py:159
  18.7 3.2 %collective-permute-start.9 = (f32[2,256]{1,0:T(2,128)S(1)}, f32[2,256]{1,0:T(2,128)S(1)}, u32[]{:S(2)}, u32[]{:S(2)}) collective-permute-start(f32[2,256]{1,0:T(2,128)S(1)} %get-tuple-element.24), channel_id=1, source_target_pairs={{0,3},{1,2},{2,1},{3,0},{4,6},{5,7},{6,4},{7,5},{8,10},{9,11},{10,... | collective-permute-start | bytes 6152 | tf_op jit(solution)/shard_map/ppermute | solution.py:159
  20.0 2.0 %collective-permute-start.10 = (f32[2,256]{1,0:T(2,128)S(1)}, f32[2,256]{1,0:T(2,128)S(1)}, u32[]{:S(2)}, u32[]{:S(2)}) collective-permute-start(f32[2,256]{1,0:T(2,128)S(1)} %get-tuple-element.17.refs_0_), channel_id=1, source_target_pairs={{0,1},{1,0},{2,3},{3,2},{4,5},{5,4},{6,7},{7,6},{8,9},{9,8},{10,11... | collective-permute-start | bytes 6152 | tf_op jit(solution)/shard_map/ppermute | solution.py:159

commit v9 on v8

--- a/solution.py
+++ b/solution.py
@@ -24,6 +24,14 @@
     return lax.dot_general(a, b, (((a_axis,), (b_axis,)), ((), ())), preferred_element_type=F32)
 
 
+def whole(value, step):
+    return value >> (step.bit_length() - 1) if step & (step - 1) == 0 else value // step
+
+
+def rest(value, step):
+    return value & (step - 1) if step & (step - 1) == 0 else value % step
+
+
 def reverse_bits(value, count):
     out = 0
     for bit in range(count):
@@ -44,7 +52,7 @@
     group = min(rows, max(256 // heads, 1))
     size = group * heads
     to, at = iota((size, size), 0), iota((size, size), 1)
-    order = one_hot(at == (to % group) * heads + to // group)
+    order = one_hot(at == rest(to, group) * heads + whole(to, group))
     for ref, place in ((own_ref, core), (other_ref, 1 - core)):
         for start in range(0, rows, group):
             moved = matmul(order, ref[pl.ds(start * heads, size), :]).astype(BF16)
@@ -63,10 +71,10 @@
     stacked = jnp.concatenate([first] + [ref[...] for ref in shard_refs], axis=0)
     size = shards * rows * heads
     to, at = iota((size, size), 0), iota((size, size), 1)
-    i, j = to % owned, (to // owned) % shards
-    position = (to // (owned * shards)) % head_count
+    i, j = rest(to, owned), rest(whole(to, owned), shards)
+    position = rest(whole(to, owned * shards), head_count)
     token = (reverse_bits(position, bits) ^ me) * owned + i
-    order = one_hot(at == (j * rows + token) * heads + to // (rows * shards))
+    order = one_hot(at == (j * rows + token) * heads + whole(to, rows * shards))
     moved = matmul(order, stacked).astype(BF16)
     part = rows * shards
     total = matmul(moved[:part], weight_ref[0], 1, 1)
@@ -89,47 +97,53 @@
 
 
 def weight_grad_kernel(head_count, heads, owned, columns, own_ref, other_ref, *refs):
-    shard_refs, out_ref, scratch_ref = refs[:-2], refs[-2], refs[-1]
+    shard_refs, (out_ref, spread_ref, total_ref, sems) = refs[:-4], refs[-4:]
     me = lax.axis_index("head")
     core = lax.axis_index("ctx") & 1
     role = core ^ even_bits(me, head_count.bit_length() - 1)
-    rows = out_ref.shape[0] // heads
+    groups = sems.shape[0]
+    rows = out_ref.shape[0] // heads // groups
     tokens = head_count * owned
     normed = jnp.concatenate([own_ref[...], other_ref[...]], axis=0).astype(BF16)
     size = columns * tokens * heads
-    at, to = iota((normed.shape[0], size), 0), iota((normed.shape[0], size), 1)
-    token, j = (to // heads) % tokens, to // (heads * tokens)
-    distance = (token // owned) ^ me
+    at, to = iota((normed.shape[0], size), 0), iota((1, size), 1)
+    token, j = rest(whole(to, heads), tokens), whole(to, heads * tokens)
+    distance = whole(token, owned) ^ me
     turned = 1 ^ even_bits(distance, head_count.bit_length() - 1) ^ (j & 1)
     cots = []
     for side in range(2):
         held = jnp.where(j == 0, core, role) ^ side ^ core ^ turned
-        place = (held * head_count + distance) * columns + j
-        spread = one_hot(at == place * owned + token % owned)
-        scratch_ref[side] = matmul(normed, spread, 0, 0)
+        place = ((held * head_count + distance) * columns + j) * owned + rest(token, owned)
+        spread_ref[side] = matmul(normed, one_hot(at == place), 0, 0)
         cots.append(jnp.concatenate([r[...] for r in shard_refs[side * columns : (side + 1) * columns]], axis=0))
-    group = min(rows, max(256 // heads, 1))
-    keep = (iota((1, heads, size), 2) % heads) == iota((1, heads, size), 1)
-    for start in range(0, rows, group):
+    keep = rest(iota((1, heads, size), 2), heads) == iota((1, heads, size), 1)
+    copies = []
+    for g in range(groups):
         total = None
         for side in range(2):
-            block = scratch_ref[side, start : start + group, :]
-            left = jnp.where(keep, block[:, None, :], 0.0).reshape(group * heads, size).astype(BF16)
+            block = spread_ref[side, g * rows : (g + 1) * rows, :]
+            left = jnp.where(keep, block[:, None, :], 0.0).reshape(rows * heads, size).astype(BF16)
             part = matmul(left, cots[side])
             total = part if total is None else total + part
-        out_ref[start * heads : (start + group) * heads, :] = total
-
-
-def latent_kernel(head_count, columns, latent_ref, gain_ref, *refs):
-    block_refs, other_refs, out_ref = refs[:columns], refs[columns:-1], refs[-1]
+        place = pl.ds(g * rows * heads, rows * heads)
+        total_ref[place, :] = total
+        copies.append(pltpu.make_async_copy(total_ref.at[place], out_ref.at[place], sems.at[g]))
+        copies[g].start()
+    for copy in copies:
+        copy.wait()
+
+
+def latent_kernel(head_count, columns, latent_ref, gain_ref, other_ref, *refs):
+    block_refs, out_ref = refs[:-1], refs[-1]
     column = lax.axis_index("ctx") >> 1
     crossed = even_bits(lax.axis_index("head"), head_count.bit_length() - 1)
     raw = latent_ref[...].astype(F32)
     rms = lax.rsqrt(jnp.mean(raw * raw, axis=1, keepdims=True) + 1e-06)
     hat = raw * rms
     relative = [ref[...] for ref in block_refs]
-    for j, ref in enumerate(other_refs):
-        relative[2 * j] = jnp.where(crossed == 0, relative[2 * j], ref[...])
+    count = raw.shape[0]
+    for j in range(0, columns, 2):
+        relative[j] = jnp.where(crossed == 0, relative[j], other_ref[j // 2 * count : (j // 2 + 1) * count, :])
     blocks = []
     for b in range(columns):
         block = relative[0]
@@ -167,11 +181,12 @@
     def head_swap(value, mask):
         return swap(value, lambda h, c: (h ^ mask, c ^ 1))
 
-    def call(kernel, out, *args, scratch=(), flops=0):
+    def call(kernel, out, *args, scratch=(), flops=0, place=pltpu.VMEM):
         moved = sum(a.size * a.dtype.itemsize for a in args)
         return pl.pallas_call(
             kernel,
             out_shape=out,
+            out_specs=jax.tree.map(lambda _: pl.BlockSpec(memory_space=place), out),
             scratch_shapes=scratch,
             compiler_params=params,
             cost_estimate=pl.CostEstimate(flops=flops, bytes_accessed=moved, transcendentals=0),
@@ -219,16 +234,22 @@
         chip_weight,
     )
     core = lax.axis_index("ctx") & 1
+    far_other = [ctx_swap(s, 1) for s in far]
     mask = 1
     while mask < head_count:
+        if mask == 2:
+            sums, *far_other = lax.optimization_barrier((sums, *far_other))
         half = sums.shape[0] // 2
-        got = head_swap(jnp.concatenate([sums[half:], normed], axis=0), mask)
-        normed = jnp.concatenate([normed, got[half:]], axis=0)
-        sums = sums[:half] + got[:half]
+        count = normed.shape[0]
+        if half >= count:
+            got = head_swap(jnp.concatenate([sums[half:], normed], axis=0), mask)
+            got_sums, got_normed = got[:half], got[half:]
+        else:
+            got = head_swap(jnp.concatenate([normed, sums[half:]], axis=0), mask)
+            got_normed, got_sums = got[:count], got[count:]
+        normed = jnp.concatenate([normed, got_normed], axis=0)
+        sums = sums[:half] + got_sums
         mask *= 2
-
-    normed_own = jnp.where(core == 0, normed[:, :rows], normed[:, rows:])
-    normed_other = ctx_swap(jnp.where(core == 0, normed[:, rows:], normed[:, :rows]), 1)
 
     blocks = [sums[j * owned : (j + 1) * owned] for j in range(columns)]
     mask = ctx_count // 2
@@ -237,7 +258,12 @@
             if j & (mask >> 1):
                 blocks[j] = ctx_swap(blocks[j], mask)
         mask //= 2
-    kept = [ctx_swap(blocks[j], 1) for j in range(0, columns, 2)]
+    normed_own = jnp.where(core == 0, normed[:, :rows], normed[:, rows:])
+    sent = jnp.where(core == 0, normed[:, rows:], normed[:, :rows])
+    count = sent.shape[0] // 2
+    sent = [sent[:count], sent[count:]]
+    both = ctx_swap(jnp.concatenate([jnp.concatenate(sent, axis=1)] + blocks[::2], axis=0), 1)
+    normed_other = jnp.concatenate([both[:count, :rows], both[:count, rows:]], axis=0)
     for j in range(1, columns, 2):
         blocks[j] = role_swap(blocks[j], 2)
 
@@ -249,9 +275,14 @@
         own,
         *far,
         other,
-        *[ctx_swap(s, 1) for s in far],
-        scratch=[pltpu.VMEM((2, rows, columns * tokens * heads), F32)],
+        *far_other,
+        scratch=[
+            pltpu.VMEM((2, rows, columns * tokens * heads), F32),
+            pltpu.VMEM((rows * heads, channels), F32),
+            pltpu.SemaphoreType.DMA((4 if rows % 32 == 0 else 1,)),
+        ],
         flops=2 * rows * heads * channels * ctx_count * tokens * heads,
+        place=pl.ANY,
     )
     weight_grad, *blocks = lax.optimization_barrier((weight_grad, *blocks))
     latent_gradient = call(
@@ -259,8 +290,8 @@
         jax.ShapeDtypeStruct((owned, width), F32),
         latent[0],
         gain_row,
+        both[count:],
         *blocks,
-        *kept,
     )
     return latent_gradient[None], weight_grad.reshape(weight.shape)
 

time: 22.9 us -> 22.6 us (0.987)
    ppermute x11 -> x10, starting transfers between devices: 13.5 us -> 13.3 us  [swap(): return lax.ppermute(value, ('head', 'ctx'), pairs)]
    ppermute x11 -> x10, waiting for transfers between devices: 4.9 us -> 5 us  [swap(): return lax.ppermute(value, ('head', 'ctx'), pairs)]
  transfers between devices with their start and end apart: 11 -> 10, of which waited for: 5 -> 6; matrix products, arithmetic and copies ran while one was open for 0% -> 0% of each run, Pallas kernels for 12% -> 11%
where the time goes in v9:
time: 22.6 us; the launch traced here: 22.4 us
  starting transfers between devices  13.3 us (59%)
  waiting for transfers between devices  5 us (22%)
  Pallas kernels  3.28 us (15%)
  between operations  0.75 us (3%)
    ppermute x10, starting transfers between devices, swap(): return lax.ppermute(value, ('head', 'ctx'), pairs)  13.3 us
    ppermute x10, waiting for transfers between devices, swap(): return lax.ppermute(value, ('head', 'ctx'), pairs)  5 us
    pallas_call x5, Pallas kernels, call(): pl.pallas_call(kernel, out_shape=out, out_specs=jax.tree.map(lambda _: pl...  3.28 us
  transfers between devices with their start and end apart: 10, of which 6 were waited for; matrix products, arithmetic and copies ran while one was open for 0% of the time, Pallas kernels for 11%

profile of v9, /device:TPU:0, one launch (start us, length us, event | category | flops | bytes accessed | tf_op | source)
XLA Modules:
  0.0 22.4 jit_solution(9505094995946506956)
XLA Ops:
  0.6 0.5 %collective-permute-start = (bf16[1024,256]{1,0:T(8,128)(2,1)}, bf16[1024,256]{1,0:T(8,128)(2,1)S(1)}, u32[]{:S(2)}, u32[]{:S(2)}) collective-permute-start(bf16[1024,256]{1,0:T(8,128)(2,1)} %bitcast.6), channel_id=1, source_target_pairs={{0,1},{1,0},{2,3},{3,2},{4,5},{5,4},{6,7},{7,6},{8,9},{9,8},{10,11... | collective-permute-start | bytes 1572872 | tf_op jit(solution)/shard_map/ppermute | solution.py:173
  1.1 0.0 copy-start.3
  1.1 0.0 copy-start.2
  1.2 2.6 %collective-permute-start.3 = (bf16[128,256]{1,0:T(8,128)(2,1)}, bf16[128,256]{1,0:T(8,128)(2,1)S(1)}, u32[]{:S(2)}, u32[]{:S(2)}) collective-permute-start(bf16[128,256]{1,0:T(8,128)(2,1)} %bitcast.8), channel_id=1, source_target_pairs={{0,3},{1,2},{2,1},{3,0},{4,6},{5,7},{6,4},{7,5},{8,10},{9,11},{10,... | collective-permute-start | bytes 196616 | tf_op jit(solution)/shard_map/ppermute | solution.py:173
  3.8 0.1 collective-permute-start.2
  3.8 0.0 copy-done.3
  3.9 0.0 copy-done.2
  3.9 0.0 copy-start
  3.9 0.1 shard_map.59
  4.0 0.0 collective-permute-done.other_ref
  4.0 0.0 copy-start.1
  4.0 1.5 %collective-permute-start.1 = (f32[2,256]{1,0:T(2,128)S(1)}, f32[2,256]{1,0:T(2,128)S(1)}, u32[]{:S(2)}, u32[]{:S(2)}) collective-permute-start(f32[2,256]{1,0:T(2,128)S(1)} %get-tuple-element.16), channel_id=1, source_target_pairs={{0,3},{1,2},{2,1},{3,0},{4,7},{5,6},{6,5},{7,4},{8,11},{9,10},{10,... | collective-permute-start | bytes 6152 | tf_op jit(solution)/shard_map/ppermute | solution.py:173
  5.5 0.0 copy-done
  5.5 0.4 %shard_map.60.refs_1_ = bf16[8,256,256]{2,1,0:T(8,128)(2,1)S(1)} custom-call(bf16[1024,256]{1,0:T(8,128)(2,1)S(1)} %bitcast.7, bf16[1024,256]{1,0:T(8,128)(2,1)S(1)} %collective-permute-done.other_ref), custom_call_target="tpu_custom_call" | custom-call | bytes 1048576 | tf_op jit(solution)/shard_map/pallas_call | solution.py:186
  5.9 0.4 %collective-permute-done.3.refs_0_.refs_1_ = bf16[128,256]{1,0:T(8,128)(2,1)S(1)} collective-permute-done((bf16[128,256]{1,0:T(8,128)(2,1)}, bf16[128,256]{1,0:T(8,128)(2,1)S(1)}, u32[]{:S(2)}, u32[]{:S(2)}) %collective-permute-start.3) | collective-permute-done | bytes 65568 | tf_op jit(solution)/shard_map/ppermute | solution.py:173
  6.3 0.0 collective-permute-done.2.other_ref.refs_2_
  6.3 0.0 copy-done.1
  6.3 0.5 %shard_map.61 = f32[32,256]{1,0:T(8,128)S(1)} custom-call(bf16[128,256]{1,0:T(8,128)(2,1)S(1)} %bitcast.10, bf16[128,256]{1,0:T(8,128)(2,1)S(1)} %collective-permute-done.2.other_ref.refs_2_, bf16[128,256]{1,0:T(8,128)(2,1)S(1)} %collective-permute-done.3.refs_0_.refs_1_, bf16[8,256,256]{2,1,0:T(8,128)(2,1)S(1)} %shard_map.60.refs_1_), custom_call_target="tpu_custom_call" | custom-call | bytes 1245184 | tf_op jit(solution)/shard_map/pallas_call | solution.py:186
  6.9 0.2 collective-permute-done.1
  7.1 1.5 %collective-permute-start.4 = (f32[20,256]{1,0:T(8,128)S(1)}, f32[20,256]{1,0:T(8,128)S(1)}, u32[]{:S(2)}, u32[]{:S(2)}) collective-permute-start(f32[20,256]{1,0:T(8,128)S(1)} %pad_maximum_fusion), channel_id=1, source_target_pairs={{0,5},{1,4},{2,7},{3,6},{4,1},{5,0},{6,3},{7,2},{8,13},{9,12},{10,... | collective-permute-start | bytes 61448 | tf_op jit(solution)/shard_map/ppermute | solution.py:173
  8.6 0.6 %collective-permute-start.5 = (bf16[128,256]{1,0:T(8,128)(2,1)S(1)}, bf16[128,256]{1,0:T(8,128)(2,1)S(1)}, u32[]{:S(2)}, u32[]{:S(2)}) collective-permute-start(bf16[128,256]{1,0:T(8,128)(2,1)S(1)} %collective-permute-done.3.refs_0_.refs_1_), channel_id=1, source_target_pairs={{0,1},{1,0},{2,3},{3,2},{4,5},{5,4},{6,7},{7,6},{8,9},{9,8},{10,11... | collective-permute-start | bytes 196616 | tf_op jit(solution)/shard_map/ppermute | solution.py:173
  9.1 1.2 %collective-permute-done.4 = f32[20,256]{1,0:T(8,128)S(1)} collective-permute-done((f32[20,256]{1,0:T(8,128)S(1)}, f32[20,256]{1,0:T(8,128)S(1)}, u32[]{:S(2)}, u32[]{:S(2)}) %collective-permute-start.4) | collective-permute-done | bytes 20512 | tf_op jit(solution)/shard_map/ppermute | solution.py:173
  10.3 0.0 collective-permute-done.5.refs_3_
  10.4 1.9 %collective-permute-start.6 = (f32[16,256]{1,0:T(8,128)S(1)}, f32[16,256]{1,0:T(8,128)S(1)}, u32[]{:S(2)}, u32[]{:S(2)}) collective-permute-start(f32[16,256]{1,0:T(8,128)S(1)} %pad_maximum_fusion.2), channel_id=1, source_target_pairs={{0,9},{1,8},{2,11},{3,10},{4,13},{5,12},{6,15},{7,14},{8,1},{9,0},... | collective-permute-start | bytes 49160 | tf_op jit(solution)/shard_map/ppermute | solution.py:173
  12.3 1.4 %collective-permute-done.6 = f32[16,256]{1,0:T(8,128)S(1)} collective-permute-done((f32[16,256]{1,0:T(8,128)S(1)}, f32[16,256]{1,0:T(8,128)S(1)}, u32[]{:S(2)}, u32[]{:S(2)}) %collective-permute-start.6) | collective-permute-done | bytes 16416 | tf_op jit(solution)/shard_map/ppermute | solution.py:173
  13.8 2.8 %collective-permute-start.7 = (f32[20,256]{1,0:T(8,128)S(1)}, f32[20,256]{1,0:T(8,128)S(1)}, u32[]{:S(2)}, u32[]{:S(2)}) collective-permute-start(f32[20,256]{1,0:T(8,128)S(1)} %concatenate.32), channel_id=1, source_target_pairs={{0,17},{1,16},{2,19},{3,18},{4,21},{5,20},{6,23},{7,22},{8,25},{9,... | collective-permute-start | bytes 61448 | tf_op jit(solution)/shard_map/ppermute | solution.py:173
  16.6 1.5 %collective-permute-done.7 = f32[20,256]{1,0:T(8,128)S(1)} collective-permute-done((f32[20,256]{1,0:T(8,128)S(1)}, f32[20,256]{1,0:T(8,128)S(1)}, u32[]{:S(2)}, u32[]{:S(2)}) %collective-permute-start.7) | collective-permute-done | bytes 20512 | tf_op jit(solution)/shard_map/ppermute | solution.py:173
  18.2 0.5 %collective-permute-start.8 = (f32[18,256]{1,0:T(8,128)S(1)}, f32[18,256]{1,0:T(8,128)S(1)}, u32[]{:S(2)}, u32[]{:S(2)}) collective-permute-start(f32[18,256]{1,0:T(8,128)S(1)} %pad_maximum_fusion.1), channel_id=1, source_target_pairs={{0,1},{1,0},{2,3},{3,2},{4,5},{5,4},{6,7},{7,6},{8,9},{9,8},{10,11... | collective-permute-start | bytes 55304 | tf_op jit(solution)/shard_map/ppermute | solution.py:173
  18.7 1.2 %collective-permute-start.9 = (f32[2,256]{1,0:T(2,128)S(1)}, f32[2,256]{1,0:T(2,128)S(1)}, u32[]{:S(2)}, u32[]{:S(2)}) collective-permute-start(f32[2,256]{1,0:T(2,128)S(1)} %get-tuple-element.32), channel_id=1, source_target_pairs={{0,3},{1,2},{2,1},{3,0},{4,6},{5,7},{6,4},{7,5},{8,10},{9,11},{10,... | collective-permute-start | bytes 6152 | tf_op jit(solution)/shard_map/ppermute | solution.py:173
  19.9 0.0 collective-permute-done.8
  19.9 1.5 %shard_map.62 = f32[1024,256]{1,0:T(8,128)} custom-call(f32[32,128]{1,0:T(8,128)S(1)} %get-tuple-element.24.own_ref, f32[32,128]{1,0:T(8,128)S(1)} %pad_maximum_fusion.3.other_ref, bf16[128,256]{1,0:T(8,128)(2,1)S(1)} %bitcast.11, bf16[128,256]{1,0:T(8,128)(2,1)S(1)} %collective-permute-done.3.refs_0_.refs_1_, ...), custom_call_target="tpu_custom_call" | custom-call | flops 268435456 | bytes 294912 | tf_op jit(solution)/shard_map/pallas_call | solution.py:186
  21.4 0.3 %collective-permute-done.9.refs_1_ = f32[2,256]{1,0:T(2,128)S(1)} collective-permute-done((f32[2,256]{1,0:T(2,128)S(1)}, f32[2,256]{1,0:T(2,128)S(1)}, u32[]{:S(2)}, u32[]{:S(2)}) %collective-permute-start.9) | collective-permute-done | bytes 2080 | tf_op jit(solution)/shard_map/ppermute | solution.py:173
  21.7 0.8 %shard_map.63 = f32[2,512]{1,0:T(2,128)} custom-call(bf16[2,512]{1,0:T(2,128)(2,1)S(1)} %bitcast.13, f32[1,512]{1,0:T(1,128)S(1)} %bitcast.15, f32[2,256]{1,0:T(2,128)S(1)} %slice.101.other_ref, f32[2,256]{1,0:T(2,128)S(1)} %get-tuple-element.21.refs_0_, f32[2,256]{1,0:T(2,128)S(1)} %collective-permute-done.9.refs_1_), custom_call_target="tpu_custom_call" | custom-call | bytes 10240 | tf_op jit(solution)/shard_map/pallas_call | solution.py:186
  (19 shorter events, 0.2 us)
Async XLA Ops:
  0.6 3.3 %collective-permute-start = (bf16[1024,256]{1,0:T(8,128)(2,1)}, bf16[1024,256]{1,0:T(8,128)(2,1)S(1)}, u32[]{:S(2)}, u32[]{:S(2)}) collective-permute-start(bf16[1024,256]{1,0:T(8,128)(2,1)} %bitcast.6), channel_id=1, source_target_pairs={{0,1},{1,0},{2,3},{3,2},{4,5},{5,4},{6,7},{7,6},{8,9},{9,8},{10,11... | collective-permute-start | bytes 1572872 | tf_op jit(solution)/shard_map/ppermute | solution.py:173
  1.1 2.7 %copy-start.3 = (f32[512]{0:T(512)S(1)}, f32[512]{0:T(512)}, u32[]{:S(2)}) copy-start(f32[512]{0:T(512)} %param.5) | copy-start | bytes 6148
  1.1 2.7 %copy-start.2 = (bf16[1,2,512]{2,1,0:T(2,128)(2,1)S(1)}, bf16[1,2,512]{2,1,0:T(2,128)(2,1)}, u32[]{:S(2)}) copy-start(bf16[1,2,512]{2,1,0:T(2,128)(2,1)} %param.4) | copy-start | bytes 6148
  1.2 5.2 %collective-permute-start.3 = (bf16[128,256]{1,0:T(8,128)(2,1)}, bf16[128,256]{1,0:T(8,128)(2,1)S(1)}, u32[]{:S(2)}, u32[]{:S(2)}) collective-permute-start(bf16[128,256]{1,0:T(8,128)(2,1)} %bitcast.8), channel_id=1, source_target_pairs={{0,3},{1,2},{2,1},{3,0},{4,6},{5,7},{6,4},{7,5},{8,10},{9,11},{10,... | collective-permute-start | bytes 196616 | tf_op jit(solution)/shard_map/ppermute | solution.py:173
  3.8 2.6 %collective-permute-start.2 = (bf16[128,256]{1,0:T(8,128)(2,1)}, bf16[128,256]{1,0:T(8,128)(2,1)S(1)}, u32[]{:S(2)}, u32[]{:S(2)}) collective-permute-start(bf16[128,256]{1,0:T(8,128)(2,1)} %bitcast.9), channel_id=1, source_target_pairs={{0,1},{1,0},{2,3},{3,2},{4,5},{5,4},{6,7},{7,6},{8,9},{9,8},{10,11... | collective-permute-start | bytes 196616 | tf_op jit(solution)/shard_map/ppermute | solution.py:173
  3.9 1.6 %copy-start = (bf16[128,8,256]{2,1,0:T(8,128)(2,1)S(1)}, bf16[128,8,256]{2,1,0:T(8,128)(2,1)}, u32[]{:S(2)}) copy-start(bf16[128,8,256]{2,1,0:T(8,128)(2,1)} %param.7) | copy-start | bytes 1572868
  4.0 2.4 %copy-start.1 = (bf16[1,16,8,256]{3,2,1,0:T(8,128)(2,1)S(1)}, bf16[1,16,8,256]{3,2,1,0:T(8,128)(2,1)}, u32[]{:S(2)}) copy-start(bf16[1,16,8,256]{3,2,1,0:T(8,128)(2,1)} %param.6) | copy-start | bytes 196612
  4.0 3.1 %collective-permute-start.1 = (f32[2,256]{1,0:T(2,128)S(1)}, f32[2,256]{1,0:T(2,128)S(1)}, u32[]{:S(2)}, u32[]{:S(2)}) collective-permute-start(f32[2,256]{1,0:T(2,128)S(1)} %get-tuple-element.16), channel_id=1, source_target_pairs={{0,3},{1,2},{2,1},{3,0},{4,7},{5,6},{6,5},{7,4},{8,11},{9,10},{10,... | collective-permute-start | bytes 6152 | tf_op jit(solution)/shard_map/ppermute | solution.py:173
  7.1 3.3 %collective-permute-start.4 = (f32[20,256]{1,0:T(8,128)S(1)}, f32[20,256]{1,0:T(8,128)S(1)}, u32[]{:S(2)}, u32[]{:S(2)}) collective-permute-start(f32[20,256]{1,0:T(8,128)S(1)} %pad_maximum_fusion), channel_id=1, source_target_pairs={{0,5},{1,4},{2,7},{3,6},{4,1},{5,0},{6,3},{7,2},{8,13},{9,12},{10,... | collective-permute-start | bytes 61448 | tf_op jit(solution)/shard_map/ppermute | solution.py:173
  8.6 1.8 %collective-permute-start.5 = (bf16[128,256]{1,0:T(8,128)(2,1)S(1)}, bf16[128,256]{1,0:T(8,128)(2,1)S(1)}, u32[]{:S(2)}, u32[]{:S(2)}) collective-permute-start(bf16[128,256]{1,0:T(8,128)(2,1)S(1)} %collective-permute-done.3.refs_0_.refs_1_), channel_id=1, source_target_pairs={{0,1},{1,0},{2,3},{3,2},{4,5},{5,4},{6,7},{7,6},{8,9},{9,8},{10,11... | collective-permute-start | bytes 196616 | tf_op jit(solution)/shard_map/ppermute | solution.py:173
  10.4 3.4 %collective-permute-start.6 = (f32[16,256]{1,0:T(8,128)S(1)}, f32[16,256]{1,0:T(8,128)S(1)}, u32[]{:S(2)}, u32[]{:S(2)}) collective-permute-start(f32[16,256]{1,0:T(8,128)S(1)} %pad_maximum_fusion.2), channel_id=1, source_target_pairs={{0,9},{1,8},{2,11},{3,10},{4,13},{5,12},{6,15},{7,14},{8,1},{9,0},... | collective-permute-start | bytes 49160 | tf_op jit(solution)/shard_map/ppermute | solution.py:173
  13.8 4.3 %collective-permute-start.7 = (f32[20,256]{1,0:T(8,128)S(1)}, f32[20,256]{1,0:T(8,128)S(1)}, u32[]{:S(2)}, u32[]{:S(2)}) collective-permute-start(f32[20,256]{1,0:T(8,128)S(1)} %concatenate.32), channel_id=1, source_target_pairs={{0,17},{1,16},{2,19},{3,18},{4,21},{5,20},{6,23},{7,22},{8,25},{9,... | collective-permute-start | bytes 61448 | tf_op jit(solution)/shard_map/ppermute | solution.py:173
  18.2 1.7 %collective-permute-start.8 = (f32[18,256]{1,0:T(8,128)S(1)}, f32[18,256]{1,0:T(8,128)S(1)}, u32[]{:S(2)}, u32[]{:S(2)}) collective-permute-start(f32[18,256]{1,0:T(8,128)S(1)} %pad_maximum_fusion.1), channel_id=1, source_target_pairs={{0,1},{1,0},{2,3},{3,2},{4,5},{5,4},{6,7},{7,6},{8,9},{9,8},{10,11... | collective-permute-start | bytes 55304 | tf_op jit(solution)/shard_map/ppermute | solution.py:173
  18.7 3.0 %collective-permute-start.9 = (f32[2,256]{1,0:T(2,128)S(1)}, f32[2,256]{1,0:T(2,128)S(1)}, u32[]{:S(2)}, u32[]{:S(2)}) collective-permute-start(f32[2,256]{1,0:T(2,128)S(1)} %get-tuple-element.32), channel_id=1, source_target_pairs={{0,3},{1,2},{2,1},{3,0},{4,6},{5,7},{6,4},{7,5},{8,10},{9,11},{10,... | collective-permute-start | bytes 6152 | tf_op jit(solution)/shard_map/ppermute | solution.py:173

commit v10 on v9

--- a/solution.py
+++ b/solution.py
@@ -46,41 +46,44 @@
     return out
 
 
-def weight_kernel(heads, own_ref, other_ref, out_ref):
-    core = lax.axis_index("ctx") & 1
+def weight_kernel(head_count, heads, owned, shards, own_ref, other_ref, out_ref, order_ref):
     rows = own_ref.shape[0] // heads
     group = min(rows, max(256 // heads, 1))
     size = group * heads
     to, at = iota((size, size), 0), iota((size, size), 1)
     order = one_hot(at == rest(to, group) * heads + whole(to, group))
-    for ref, place in ((own_ref, core), (other_ref, 1 - core)):
+    parts = [[] for _ in range(heads)]
+    for ref in (own_ref, other_ref):
         for start in range(0, rows, group):
-            moved = matmul(order, ref[pl.ds(start * heads, size), :]).astype(BF16)
-            first = pl.multiple_of(place * rows + start, group)
+            moved = matmul(order, ref[pl.ds(start * heads, size), :])
             for h in range(heads):
-                out_ref[h, pl.ds(first, group), :] = moved[h * group : (h + 1) * group, :]
-
-
-def partial_kernel(head_count, heads, owned, own_ref, other_ref, *refs):
-    shard_refs, weight_ref, out_ref = refs[:-2], refs[-2], refs[-1]
-    shards = len(shard_refs) + 1
+                parts[h].append(moved[h * group : (h + 1) * group, :])
+    for h in range(heads):
+        out_ref[h] = jnp.concatenate(parts[h], axis=0).T.astype(BF16)
     me = lax.axis_index("head")
     bits = head_count.bit_length() - 1
-    rows = head_count * owned
-    first = jnp.where(even_bits(me, bits) == 0, own_ref[...], other_ref[...])
-    stacked = jnp.concatenate([first] + [ref[...] for ref in shard_refs], axis=0)
-    size = shards * rows * heads
+    tokens = head_count * owned
+    size = order_ref.shape[0]
     to, at = iota((size, size), 0), iota((size, size), 1)
     i, j = rest(to, owned), rest(whole(to, owned), shards)
     position = rest(whole(to, owned * shards), head_count)
     token = (reverse_bits(position, bits) ^ me) * owned + i
-    order = one_hot(at == (j * rows + token) * heads + whole(to, rows * shards))
-    moved = matmul(order, stacked).astype(BF16)
-    part = rows * shards
-    total = matmul(moved[:part], weight_ref[0], 1, 1)
-    for h in range(1, heads):
-        total += matmul(moved[h * part : (h + 1) * part], weight_ref[h], 1, 1)
-    out_ref[...] = total
+    order_ref[...] = one_hot(at == (j * tokens + token) * heads + whole(to, tokens * shards))
+
+
+def partial_kernel(head_count, order_ref, weight_ref, *refs):
+    shard_refs, (own_ref, other_ref, out_ref) = refs[:-3], refs[-3:]
+    core = lax.axis_index("ctx") & 1
+    crossed = even_bits(lax.axis_index("head"), head_count.bit_length() - 1)
+    first = jnp.where(crossed == 0, own_ref[...], other_ref[...])
+    stacked = jnp.concatenate([first] + [ref[...] for ref in shard_refs], axis=0)
+    moved = matmul(order_ref[...], stacked).astype(BF16)
+    part, rows = out_ref.shape[0], out_ref.shape[1] // 2
+    total = matmul(moved[:part], weight_ref[0])
+    for h in range(1, weight_ref.shape[0]):
+        total += matmul(moved[h * part : (h + 1) * part], weight_ref[h])
+    turned = jnp.concatenate([total[:, rows:], total[:, :rows]], axis=1)
+    out_ref[...] = jnp.where(core == 0, total, turned)
 
 
 def norm_kernel(columns, latent_ref, gain_ref, *out_refs):
@@ -209,10 +212,11 @@
 
     weight_flat = weight.reshape(rows * heads, channels)
     weight_other = ctx_swap(weight_flat, 1)
-    weight_flat, weight_other, *normed = lax.optimization_barrier((weight_flat, weight_other, *normed))
-    chip_weight = call(
-        functools.partial(weight_kernel, heads),
-        jax.ShapeDtypeStruct((heads, 2 * rows, channels), BF16),
+    weight_flat, weight_other, _ = lax.optimization_barrier((weight_flat, weight_other, normed[0]))
+    size = columns * tokens * heads
+    chip_weight, order = call(
+        functools.partial(weight_kernel, head_count, heads, owned, columns),
+        [jax.ShapeDtypeStruct((heads, channels, 2 * rows), BF16), jax.ShapeDtypeStruct((size, size), BF16)],
         weight_flat,
         weight_other,
     )
@@ -226,12 +230,13 @@
     normed = jnp.concatenate(normed, axis=0)
 
     sums = call(
-        functools.partial(partial_kernel, head_count, heads, owned),
+        functools.partial(partial_kernel, head_count),
         jax.ShapeDtypeStruct((head_count * columns * owned, 2 * rows), F32),
+        order,
+        chip_weight,
+        *far,
         own,
         other,
-        *far,
-        chip_weight,
     )
     core = lax.axis_index("ctx") & 1
     far_other = [ctx_swap(s, 1) for s in far]

time: 22.6 us -> 22.5 us (level)
  starting transfers between devices: 13.3 us -> 12.3 us
  local copies, waits for them, and re-layouts: 0.12 us -> 0.46 us
  waiting for transfers between devices: 5 us -> 5.31 us
    ppermute x10, starting transfers between devices: 13.3 us -> 12.3 us  [swap(): return lax.ppermute(value, ('head', 'ctx'), pairs)]
    unnamed x8, local copies, waits for them, and re-layouts: 0.02 us -> 0.34 us
    ppermute x10, waiting for transfers between devices: 5 us -> 5.31 us  [swap(): return lax.ppermute(value, ('head', 'ctx'), pairs)]
  transfers between devices with their start and end apart: 10 -> 10, of which waited for: 6 -> 6; matrix products, arithmetic and copies ran while one was open for 0% -> 0% of each run, Pallas kernels for 11% -> 12%
where the time goes in v10:
time: 22.5 us; the launch traced here: 22.3 us
  starting transfers between devices  12.3 us (55%)
  waiting for transfers between devices  5.31 us (24%)
  Pallas kernels  3.5 us (16%)
  between operations  0.72 us (3%)
  local copies, waits for them, and re-layouts  0.46 us (2%)
    ppermute x10, starting transfers between devices, swap(): return lax.ppermute(value, ('head', 'ctx'), pairs)  12.3 us
    ppermute x10, waiting for transfers between devices, swap(): return lax.ppermute(value, ('head', 'ctx'), pairs)  5.31 us
    pallas_call x5, Pallas kernels, call(): pl.pallas_call(kernel, out_shape=out, out_specs=jax.tree.map(lambda _: pl...  3.5 us
  transfers between devices with their start and end apart: 10, of which 6 were waited for; matrix products, arithmetic and copies ran while one was open for 0% of the time, Pallas kernels for 12%

profile of v10, /device:TPU:0, one launch (start us, length us, event | category | flops | bytes accessed | tf_op | source)
XLA Modules:
  0.0 22.3 jit_solution(17211078326828252832)
XLA Ops:
  0.6 0.5 %collective-permute-start.1 = (bf16[1024,256]{1,0:T(8,128)(2,1)}, bf16[1024,256]{1,0:T(8,128)(2,1)S(1)}, u32[]{:S(2)}, u32[]{:S(2)}) collective-permute-start(bf16[1024,256]{1,0:T(8,128)(2,1)} %bitcast.6), channel_id=1, source_target_pairs={{0,1},{1,0},{2,3},{3,2},{4,5},{5,4},{6,7},{7,6},{8,9},{9,8},{10,11... | collective-permute-start | bytes 1572872 | tf_op jit(solution)/shard_map/ppermute | solution.py:176
  1.1 0.0 copy-start.3
  1.1 0.0 copy-start.2
  1.2 2.6 %collective-permute-start.2 = (bf16[128,256]{1,0:T(8,128)(2,1)}, bf16[128,256]{1,0:T(8,128)(2,1)S(1)}, u32[]{:S(2)}, u32[]{:S(2)}) collective-permute-start(bf16[128,256]{1,0:T(8,128)(2,1)} %bitcast.8), channel_id=1, source_target_pairs={{0,3},{1,2},{2,1},{3,0},{4,6},{5,7},{6,4},{7,5},{8,10},{9,11},{10,... | collective-permute-start | bytes 196616 | tf_op jit(solution)/shard_map/ppermute | solution.py:176
  3.8 0.1 collective-permute-start.3
  3.8 0.0 copy-done.3
  3.9 0.0 copy-done.2
  3.9 0.0 copy-start
  3.9 0.1 shard_map.59
  4.0 0.6 %collective-permute-start = (f32[2,256]{1,0:T(2,128)S(1)}, f32[2,256]{1,0:T(2,128)S(1)}, u32[]{:S(2)}, u32[]{:S(2)}) collective-permute-start(f32[2,256]{1,0:T(2,128)S(1)} %get-tuple-element.14), channel_id=1, source_target_pairs={{0,3},{1,2},{2,1},{3,0},{4,7},{5,6},{6,5},{7,4},{8,11},{9,10},{10,... | collective-permute-start | bytes 6152 | tf_op jit(solution)/shard_map/ppermute | solution.py:176
  4.6 0.0 collective-permute-done.1.other_ref
  4.6 0.3 %copy-done = bf16[128,8,256]{2,1,0:T(8,128)(2,1)S(1)} copy-done((bf16[128,8,256]{2,1,0:T(8,128)(2,1)S(1)}, bf16[128,8,256]{2,1,0:T(8,128)(2,1)}, u32[]{:S(2)}) %copy-start) | copy-done | bytes 524312
  4.9 0.0 copy-start.1
  4.9 0.8 %shard_map.60 = (bf16[8,256,256]{2,1,0:T(8,128)(2,1)S(1)}, bf16[256,256]{1,0:T(8,128)(2,1)S(1)}) custom-call(bf16[1024,256]{1,0:T(8,128)(2,1)S(1)} %bitcast.7, bf16[1024,256]{1,0:T(8,128)(2,1)S(1)} %collective-permute-done.1.other_ref), custom_call_target="tpu_custom_call" | custom-call | bytes 1048576 | tf_op jit(solution)/shard_map/pallas_call | solution.py:189
  5.7 0.7 %collective-permute-done.2.refs_0_.refs_1_ = bf16[128,256]{1,0:T(8,128)(2,1)S(1)} collective-permute-done((bf16[128,256]{1,0:T(8,128)(2,1)}, bf16[128,256]{1,0:T(8,128)(2,1)S(1)}, u32[]{:S(2)}, u32[]{:S(2)}) %collective-permute-start.2) | collective-permute-done | bytes 65568 | tf_op jit(solution)/shard_map/ppermute | solution.py:176
  6.3 0.0 collective-permute-done.3.refs_2_
  6.3 0.0 copy-done.1
  6.3 0.4 %shard_map.61 = f32[32,256]{1,0:T(8,128)S(1)} custom-call(bf16[256,256]{1,0:T(8,128)(2,1)S(1)} %get-tuple-element.17.order_ref, bf16[8,256,256]{2,1,0:T(8,128)(2,1)S(1)} %get-tuple-element.18.weight_ref, bf16[128,256]{1,0:T(8,128)(2,1)S(1)} %collective-permute-done.2.refs_0_.refs_1_, bf16[128,256]{1,0:T(8,128)(2,1)S(1)} %bitcast.10, ...), custom_call_target="tpu_custom_call" | custom-call | bytes 1376256 | tf_op jit(solution)/shard_map/pallas_call | solution.py:189
  6.8 0.2 collective-permute-done
  7.0 1.5 %collective-permute-start.4 = (f32[20,256]{1,0:T(8,128)S(1)}, f32[20,256]{1,0:T(8,128)S(1)}, u32[]{:S(2)}, u32[]{:S(2)}) collective-permute-start(f32[20,256]{1,0:T(8,128)S(1)} %pad_maximum_fusion), channel_id=1, source_target_pairs={{0,5},{1,4},{2,7},{3,6},{4,1},{5,0},{6,3},{7,2},{8,13},{9,12},{10,... | collective-permute-start | bytes 61448 | tf_op jit(solution)/shard_map/ppermute | solution.py:176
  8.5 0.6 %collective-permute-start.5 = (bf16[128,256]{1,0:T(8,128)(2,1)S(1)}, bf16[128,256]{1,0:T(8,128)(2,1)S(1)}, u32[]{:S(2)}, u32[]{:S(2)}) collective-permute-start(bf16[128,256]{1,0:T(8,128)(2,1)S(1)} %collective-permute-done.2.refs_0_.refs_1_), channel_id=1, source_target_pairs={{0,1},{1,0},{2,3},{3,2},{4,5},{5,4},{6,7},{7,6},{8,9},{9,8},{10,11... | collective-permute-start | bytes 196616 | tf_op jit(solution)/shard_map/ppermute | solution.py:176
  9.1 1.2 %collective-permute-done.4 = f32[20,256]{1,0:T(8,128)S(1)} collective-permute-done((f32[20,256]{1,0:T(8,128)S(1)}, f32[20,256]{1,0:T(8,128)S(1)}, u32[]{:S(2)}, u32[]{:S(2)}) %collective-permute-start.4) | collective-permute-done | bytes 20512 | tf_op jit(solution)/shard_map/ppermute | solution.py:176
  10.3 0.0 collective-permute-done.5.refs_3_
  10.3 1.9 %collective-permute-start.6 = (f32[16,256]{1,0:T(8,128)S(1)}, f32[16,256]{1,0:T(8,128)S(1)}, u32[]{:S(2)}, u32[]{:S(2)}) collective-permute-start(f32[16,256]{1,0:T(8,128)S(1)} %pad_maximum_fusion.2), channel_id=1, source_target_pairs={{0,9},{1,8},{2,11},{3,10},{4,13},{5,12},{6,15},{7,14},{8,1},{9,0},... | collective-permute-start | bytes 49160 | tf_op jit(solution)/shard_map/ppermute | solution.py:176
  12.2 1.4 %collective-permute-done.6 = f32[16,256]{1,0:T(8,128)S(1)} collective-permute-done((f32[16,256]{1,0:T(8,128)S(1)}, f32[16,256]{1,0:T(8,128)S(1)}, u32[]{:S(2)}, u32[]{:S(2)}) %collective-permute-start.6) | collective-permute-done | bytes 16416 | tf_op jit(solution)/shard_map/ppermute | solution.py:176
  13.7 2.8 %collective-permute-start.7 = (f32[20,256]{1,0:T(8,128)S(1)}, f32[20,256]{1,0:T(8,128)S(1)}, u32[]{:S(2)}, u32[]{:S(2)}) collective-permute-start(f32[20,256]{1,0:T(8,128)S(1)} %concatenate.32), channel_id=1, source_target_pairs={{0,17},{1,16},{2,19},{3,18},{4,21},{5,20},{6,23},{7,22},{8,25},{9,... | collective-permute-start | bytes 61448 | tf_op jit(solution)/shard_map/ppermute | solution.py:176
  16.5 1.5 %collective-permute-done.7 = f32[20,256]{1,0:T(8,128)S(1)} collective-permute-done((f32[20,256]{1,0:T(8,128)S(1)}, f32[20,256]{1,0:T(8,128)S(1)}, u32[]{:S(2)}, u32[]{:S(2)}) %collective-permute-start.7) | collective-permute-done | bytes 20512 | tf_op jit(solution)/shard_map/ppermute | solution.py:176
  18.1 0.5 %collective-permute-start.8 = (f32[18,256]{1,0:T(8,128)S(1)}, f32[18,256]{1,0:T(8,128)S(1)}, u32[]{:S(2)}, u32[]{:S(2)}) collective-permute-start(f32[18,256]{1,0:T(8,128)S(1)} %pad_maximum_fusion.1), channel_id=1, source_target_pairs={{0,1},{1,0},{2,3},{3,2},{4,5},{5,4},{6,7},{7,6},{8,9},{9,8},{10,11... | collective-permute-start | bytes 55304 | tf_op jit(solution)/shard_map/ppermute | solution.py:176
  18.5 1.3 %collective-permute-start.9 = (f32[2,256]{1,0:T(2,128)S(1)}, f32[2,256]{1,0:T(2,128)S(1)}, u32[]{:S(2)}, u32[]{:S(2)}) collective-permute-start(f32[2,256]{1,0:T(2,128)S(1)} %get-tuple-element.32), channel_id=1, source_target_pairs={{0,3},{1,2},{2,1},{3,0},{4,6},{5,7},{6,4},{7,5},{8,10},{9,11},{10,... | collective-permute-start | bytes 6152 | tf_op jit(solution)/shard_map/ppermute | solution.py:176
  19.8 0.0 collective-permute-done.8
  19.8 1.5 %shard_map.62 = f32[1024,256]{1,0:T(8,128)} custom-call(f32[32,128]{1,0:T(8,128)S(1)} %get-tuple-element.24.own_ref, f32[32,128]{1,0:T(8,128)S(1)} %pad_maximum_fusion.3.other_ref, bf16[128,256]{1,0:T(8,128)(2,1)S(1)} %bitcast.11, bf16[128,256]{1,0:T(8,128)(2,1)S(1)} %collective-permute-done.2.refs_0_.refs_1_, ...), custom_call_target="tpu_custom_call" | custom-call | flops 268435456 | bytes 294912 | tf_op jit(solution)/shard_map/pallas_call | solution.py:189
  21.3 0.3 %collective-permute-done.9.refs_1_ = f32[2,256]{1,0:T(2,128)S(1)} collective-permute-done((f32[2,256]{1,0:T(2,128)S(1)}, f32[2,256]{1,0:T(2,128)S(1)}, u32[]{:S(2)}, u32[]{:S(2)}) %collective-permute-start.9) | collective-permute-done | bytes 2080 | tf_op jit(solution)/shard_map/ppermute | solution.py:176
  21.6 0.8 %shard_map.63 = f32[2,512]{1,0:T(2,128)} custom-call(bf16[2,512]{1,0:T(2,128)(2,1)S(1)} %bitcast.13, f32[1,512]{1,0:T(1,128)S(1)} %bitcast.15, f32[2,256]{1,0:T(2,128)S(1)} %slice.101.other_ref, f32[2,256]{1,0:T(2,128)S(1)} %get-tuple-element.21.refs_0_, f32[2,256]{1,0:T(2,128)S(1)} %collective-permute-done.9.refs_1_), custom_call_target="tpu_custom_call" | custom-call | bytes 10240 | tf_op jit(solution)/shard_map/pallas_call | solution.py:189
  (19 shorter events, 0.2 us)
Async XLA Ops:
  0.6 3.9 %collective-permute-start.1 = (bf16[1024,256]{1,0:T(8,128)(2,1)}, bf16[1024,256]{1,0:T(8,128)(2,1)S(1)}, u32[]{:S(2)}, u32[]{:S(2)}) collective-permute-start(bf16[1024,256]{1,0:T(8,128)(2,1)} %bitcast.6), channel_id=1, source_target_pairs={{0,1},{1,0},{2,3},{3,2},{4,5},{5,4},{6,7},{7,6},{8,9},{9,8},{10,11... | collective-permute-start | bytes 1572872 | tf_op jit(solution)/shard_map/ppermute | solution.py:176
  1.1 2.7 %copy-start.3 = (f32[512]{0:T(512)S(1)}, f32[512]{0:T(512)}, u32[]{:S(2)}) copy-start(f32[512]{0:T(512)} %param.5) | copy-start | bytes 6148
  1.1 2.7 %copy-start.2 = (bf16[1,2,512]{2,1,0:T(2,128)(2,1)S(1)}, bf16[1,2,512]{2,1,0:T(2,128)(2,1)}, u32[]{:S(2)}) copy-start(bf16[1,2,512]{2,1,0:T(2,128)(2,1)} %param.4) | copy-start | bytes 6148
  1.2 5.2 %collective-permute-start.2 = (bf16[128,256]{1,0:T(8,128)(2,1)}, bf16[128,256]{1,0:T(8,128)(2,1)S(1)}, u32[]{:S(2)}, u32[]{:S(2)}) collective-permute-start(bf16[128,256]{1,0:T(8,128)(2,1)} %bitcast.8), channel_id=1, source_target_pairs={{0,3},{1,2},{2,1},{3,0},{4,6},{5,7},{6,4},{7,5},{8,10},{9,11},{10,... | collective-permute-start | bytes 196616 | tf_op jit(solution)/shard_map/ppermute | solution.py:176
  3.8 2.6 %collective-permute-start.3 = (bf16[128,256]{1,0:T(8,128)(2,1)}, bf16[128,256]{1,0:T(8,128)(2,1)S(1)}, u32[]{:S(2)}, u32[]{:S(2)}) collective-permute-start(bf16[128,256]{1,0:T(8,128)(2,1)} %bitcast.9), channel_id=1, source_target_pairs={{0,1},{1,0},{2,3},{3,2},{4,5},{5,4},{6,7},{7,6},{8,9},{9,8},{10,11... | collective-permute-start | bytes 196616 | tf_op jit(solution)/shard_map/ppermute | solution.py:176
  3.9 1.0 %copy-start = (bf16[128,8,256]{2,1,0:T(8,128)(2,1)S(1)}, bf16[128,8,256]{2,1,0:T(8,128)(2,1)}, u32[]{:S(2)}) copy-start(bf16[128,8,256]{2,1,0:T(8,128)(2,1)} %param.7) | copy-start | bytes 1572868
  4.0 3.0 %collective-permute-start = (f32[2,256]{1,0:T(2,128)S(1)}, f32[2,256]{1,0:T(2,128)S(1)}, u32[]{:S(2)}, u32[]{:S(2)}) collective-permute-start(f32[2,256]{1,0:T(2,128)S(1)} %get-tuple-element.14), channel_id=1, source_target_pairs={{0,3},{1,2},{2,1},{3,0},{4,7},{5,6},{6,5},{7,4},{8,11},{9,10},{10,... | collective-permute-start | bytes 6152 | tf_op jit(solution)/shard_map/ppermute | solution.py:176
  4.9 1.4 %copy-start.1 = (bf16[1,16,8,256]{3,2,1,0:T(8,128)(2,1)S(1)}, bf16[1,16,8,256]{3,2,1,0:T(8,128)(2,1)}, u32[]{:S(2)}) copy-start(bf16[1,16,8,256]{3,2,1,0:T(8,128)(2,1)} %param.6) | copy-start | bytes 196612
  7.0 3.3 %collective-permute-start.4 = (f32[20,256]{1,0:T(8,128)S(1)}, f32[20,256]{1,0:T(8,128)S(1)}, u32[]{:S(2)}, u32[]{:S(2)}) collective-permute-start(f32[20,256]{1,0:T(8,128)S(1)} %pad_maximum_fusion), channel_id=1, source_target_pairs={{0,5},{1,4},{2,7},{3,6},{4,1},{5,0},{6,3},{7,2},{8,13},{9,12},{10,... | collective-permute-start | bytes 61448 | tf_op jit(solution)/shard_map/ppermute | solution.py:176
  8.5 1.8 %collective-permute-start.5 = (bf16[128,256]{1,0:T(8,128)(2,1)S(1)}, bf16[128,256]{1,0:T(8,128)(2,1)S(1)}, u32[]{:S(2)}, u32[]{:S(2)}) collective-permute-start(bf16[128,256]{1,0:T(8,128)(2,1)S(1)} %collective-permute-done.2.refs_0_.refs_1_), channel_id=1, source_target_pairs={{0,1},{1,0},{2,3},{3,2},{4,5},{5,4},{6,7},{7,6},{8,9},{9,8},{10,11... | collective-permute-start | bytes 196616 | tf_op jit(solution)/shard_map/ppermute | solution.py:176
  10.3 3.3 %collective-permute-start.6 = (f32[16,256]{1,0:T(8,128)S(1)}, f32[16,256]{1,0:T(8,128)S(1)}, u32[]{:S(2)}, u32[]{:S(2)}) collective-permute-start(f32[16,256]{1,0:T(8,128)S(1)} %pad_maximum_fusion.2), channel_id=1, source_target_pairs={{0,9},{1,8},{2,11},{3,10},{4,13},{5,12},{6,15},{7,14},{8,1},{9,0},... | collective-permute-start | bytes 49160 | tf_op jit(solution)/shard_map/ppermute | solution.py:176
  13.7 4.3 %collective-permute-start.7 = (f32[20,256]{1,0:T(8,128)S(1)}, f32[20,256]{1,0:T(8,128)S(1)}, u32[]{:S(2)}, u32[]{:S(2)}) collective-permute-start(f32[20,256]{1,0:T(8,128)S(1)} %concatenate.32), channel_id=1, source_target_pairs={{0,17},{1,16},{2,19},{3,18},{4,21},{5,20},{6,23},{7,22},{8,25},{9,... | collective-permute-start | bytes 61448 | tf_op jit(solution)/shard_map/ppermute | solution.py:176
  18.1 1.7 %collective-permute-start.8 = (f32[18,256]{1,0:T(8,128)S(1)}, f32[18,256]{1,0:T(8,128)S(1)}, u32[]{:S(2)}, u32[]{:S(2)}) collective-permute-start(f32[18,256]{1,0:T(8,128)S(1)} %pad_maximum_fusion.1), channel_id=1, source_target_pairs={{0,1},{1,0},{2,3},{3,2},{4,5},{5,4},{6,7},{7,6},{8,9},{9,8},{10,11... | collective-permute-start | bytes 55304 | tf_op jit(solution)/shard_map/ppermute | solution.py:176
  18.5 3.0 %collective-permute-start.9 = (f32[2,256]{1,0:T(2,128)S(1)}, f32[2,256]{1,0:T(2,128)S(1)}, u32[]{:S(2)}, u32[]{:S(2)}) collective-permute-start(f32[2,256]{1,0:T(2,128)S(1)} %get-tuple-element.32), channel_id=1, source_target_pairs={{0,3},{1,2},{2,1},{3,0},{4,6},{5,7},{6,4},{7,5},{8,10},{9,11},{10,... | collective-permute-start | bytes 6152 | tf_op jit(solution)/shard_map/ppermute | solution.py:176

commit v11 on v10

--- a/solution.py
+++ b/solution.py
@@ -10,6 +10,9 @@
 
 F32 = jnp.float32
 BF16 = jnp.bfloat16
+
+
+PLANE = ((1, 1), (3, 2), (2, 0))
 
 
 def iota(shape, axis):
@@ -71,19 +74,22 @@
     order_ref[...] = one_hot(at == (j * tokens + token) * heads + whole(to, tokens * shards))
 
 
-def partial_kernel(head_count, order_ref, weight_ref, *refs):
-    shard_refs, (own_ref, other_ref, out_ref) = refs[:-3], refs[-3:]
+def partial_kernel(head_count, count, order_ref, weight_ref, *refs):
+    shard_refs, (own_ref, other_ref), out_refs = refs[: -count - 2], refs[-count - 2 : -count], refs[-count:]
     core = lax.axis_index("ctx") & 1
     crossed = even_bits(lax.axis_index("head"), head_count.bit_length() - 1)
     first = jnp.where(crossed == 0, own_ref[...], other_ref[...])
     stacked = jnp.concatenate([first] + [ref[...] for ref in shard_refs], axis=0)
     moved = matmul(order_ref[...], stacked).astype(BF16)
-    part, rows = out_ref.shape[0], out_ref.shape[1] // 2
+    size, rows = out_refs[0].shape[0], out_refs[0].shape[1] // 2
+    part = count * size
     total = matmul(moved[:part], weight_ref[0])
     for h in range(1, weight_ref.shape[0]):
         total += matmul(moved[h * part : (h + 1) * part], weight_ref[h])
     turned = jnp.concatenate([total[:, rows:], total[:, :rows]], axis=1)
-    out_ref[...] = jnp.where(core == 0, total, turned)
+    total = jnp.where(core == 0, total, turned)
+    for n, ref in enumerate(out_refs):
+        ref[...] = total[n * size : (n + 1) * size]
 
 
 def norm_kernel(columns, latent_ref, gain_ref, *out_refs):
@@ -112,11 +118,12 @@
     at, to = iota((normed.shape[0], size), 0), iota((1, size), 1)
     token, j = rest(whole(to, heads), tokens), whole(to, heads * tokens)
     distance = whole(token, owned) ^ me
+    slot = distance ^ ((distance >> 1) & 1) if head_count >= 4 else distance
     turned = 1 ^ even_bits(distance, head_count.bit_length() - 1) ^ (j & 1)
     cots = []
     for side in range(2):
         held = jnp.where(j == 0, core, role) ^ side ^ core ^ turned
-        place = ((held * head_count + distance) * columns + j) * owned + rest(token, owned)
+        place = ((held * head_count + slot) * columns + j) * owned + rest(token, owned)
         spread_ref[side] = matmul(normed, one_hot(at == place), 0, 0)
         cots.append(jnp.concatenate([r[...] for r in shard_refs[side * columns : (side + 1) * columns]], axis=0))
     keep = rest(iota((1, heads, size), 2), heads) == iota((1, heads, size), 1)
@@ -182,7 +189,7 @@
         return swap(value, lambda h, c: (h, c ^ mask ^ even_bits(h, bits)))
 
     def head_swap(value, mask):
-        return swap(value, lambda h, c: (h ^ mask, c ^ 1))
+        return swap(value, lambda h, c: (h ^ mask, c ^ 1 ^ even_bits(mask, bits)))
 
     def call(kernel, out, *args, scratch=(), flops=0, place=pltpu.VMEM):
         moved = sum(a.size * a.dtype.itemsize for a in args)
@@ -229,9 +236,10 @@
         mask *= 2
     normed = jnp.concatenate(normed, axis=0)
 
-    sums = call(
-        functools.partial(partial_kernel, head_count),
-        jax.ShapeDtypeStruct((head_count * columns * owned, 2 * rows), F32),
+    count = 4 if head_count >= 4 else 1
+    sums, *sent = call(
+        functools.partial(partial_kernel, head_count, count),
+        [jax.ShapeDtypeStruct((head_count * columns * owned // count, 2 * rows), F32)] * count,
         order,
         chip_weight,
         *far,
@@ -241,11 +249,15 @@
     core = lax.axis_index("ctx") & 1
     far_other = [ctx_swap(s, 1) for s in far]
     mask = 1
+    if count == 4:
+        got = {m: head_swap(jnp.concatenate([sent[n], normed], axis=0), m) for m, n in PLANE}
+        half = sums.shape[0]
+        sums = sums + got[1][:half] + got[3][:half] + got[2][:half]
+        sums, *far_other = lax.optimization_barrier((sums, *far_other))
+        normed = jnp.concatenate([normed] + [got[m][half:] for m in (1, 3, 2)], axis=0)
+        mask = 4
     while mask < head_count:
-        if mask == 2:
-            sums, *far_other = lax.optimization_barrier((sums, *far_other))
-        half = sums.shape[0] // 2
-        count = normed.shape[0]
+        half, count = sums.shape[0] // 2, normed.shape[0]
         if half >= count:
             got = head_swap(jnp.concatenate([sums[half:], normed], axis=0), mask)
             got_sums, got_normed = got[:half], got[half:]

time: 22.5 us -> 22 us (0.978)
  starting transfers between devices: 12.3 us -> 11.5 us
  waiting for transfers between devices: 5.31 us -> 5.56 us
    ppermute x10 -> x11, starting transfers between devices: 12.3 us -> 11.5 us  [swap(): return lax.ppermute(value, ('head', 'ctx'), pairs)]
    ppermute x10 -> x11, waiting for transfers between devices: 5.31 us -> 5.56 us  [swap(): return lax.ppermute(value, ('head', 'ctx'), pairs)]
  transfers between devices with their start and end apart: 10 -> 11, of which waited for: 6 -> 5; matrix products, arithmetic and copies ran while one was open for 0% -> 0% of each run, Pallas kernels for 12% -> 12%
where the time goes in v11:
time: 22 us; the launch traced here: 21.8 us
  starting transfers between devices  11.5 us (52%)
  waiting for transfers between devices  5.56 us (25%)
  Pallas kernels  3.5 us (16%)
  between operations  0.71 us (3%)
  local copies, waits for them, and re-layouts  0.47 us (2%)
    ppermute x11, starting transfers between devices, swap(): return lax.ppermute(value, ('head', 'ctx'), pairs)  11.5 us
    ppermute x11, waiting for transfers between devices, swap(): return lax.ppermute(value, ('head', 'ctx'), pairs)  5.56 us
    pallas_call x5, Pallas kernels, call(): pl.pallas_call(kernel, out_shape=out, out_specs=jax.tree.map(lambda _: pl...  3.5 us
  transfers between devices with their start and end apart: 11, of which 5 were waited for; matrix products, arithmetic and copies ran while one was open for 0% of the time, Pallas kernels for 12%

profile of v11, /device:TPU:0, one launch (start us, length us, event | category | flops | bytes accessed | tf_op | source)
XLA Modules:
  0.0 21.8 jit_solution(9508275369590217148)
XLA Ops:
  0.6 0.5 %collective-permute-start.1 = (bf16[1024,256]{1,0:T(8,128)(2,1)}, bf16[1024,256]{1,0:T(8,128)(2,1)S(1)}, u32[]{:S(2)}, u32[]{:S(2)}) collective-permute-start(bf16[1024,256]{1,0:T(8,128)(2,1)} %bitcast.6), channel_id=1, source_target_pairs={{0,1},{1,0},{2,3},{3,2},{4,5},{5,4},{6,7},{7,6},{8,9},{9,8},{10,11... | collective-permute-start | bytes 1572872 | tf_op jit(solution)/shard_map/ppermute | solution.py:183
  1.1 0.0 copy-start.3
  1.1 0.0 copy-start.2
  1.2 2.6 %collective-permute-start.2 = (bf16[128,256]{1,0:T(8,128)(2,1)}, bf16[128,256]{1,0:T(8,128)(2,1)S(1)}, u32[]{:S(2)}, u32[]{:S(2)}) collective-permute-start(bf16[128,256]{1,0:T(8,128)(2,1)} %bitcast.8), channel_id=1, source_target_pairs={{0,3},{1,2},{2,1},{3,0},{4,6},{5,7},{6,4},{7,5},{8,10},{9,11},{10,... | collective-permute-start | bytes 196616 | tf_op jit(solution)/shard_map/ppermute | solution.py:183
  3.8 0.1 collective-permute-start.3
  3.8 0.0 copy-done.3
  3.9 0.0 copy-done.2
  3.9 0.0 copy-start
  3.9 0.1 shard_map.59
  4.0 0.6 %collective-permute-start = (f32[2,256]{1,0:T(2,128)S(1)}, f32[2,256]{1,0:T(2,128)S(1)}, u32[]{:S(2)}, u32[]{:S(2)}) collective-permute-start(f32[2,256]{1,0:T(2,128)S(1)} %get-tuple-element.18), channel_id=1, source_target_pairs={{0,3},{1,2},{2,1},{3,0},{4,7},{5,6},{6,5},{7,4},{8,11},{9,10},{10,... | collective-permute-start | bytes 6152 | tf_op jit(solution)/shard_map/ppermute | solution.py:183
  4.6 0.0 collective-permute-done.1.other_ref
  4.6 0.3 %copy-done = bf16[128,8,256]{2,1,0:T(8,128)(2,1)S(1)} copy-done((bf16[128,8,256]{2,1,0:T(8,128)(2,1)S(1)}, bf16[128,8,256]{2,1,0:T(8,128)(2,1)}, u32[]{:S(2)}) %copy-start) | copy-done | bytes 524312
  4.9 0.0 copy-start.1
  4.9 0.8 %shard_map.60 = (bf16[8,256,256]{2,1,0:T(8,128)(2,1)S(1)}, bf16[256,256]{1,0:T(8,128)(2,1)S(1)}) custom-call(bf16[1024,256]{1,0:T(8,128)(2,1)S(1)} %bitcast.7, bf16[1024,256]{1,0:T(8,128)(2,1)S(1)} %collective-permute-done.1.other_ref), custom_call_target="tpu_custom_call" | custom-call | bytes 1048576 | tf_op jit(solution)/shard_map/pallas_call | solution.py:196
  5.7 0.7 %collective-permute-done.2.refs_0_.refs_1_ = bf16[128,256]{1,0:T(8,128)(2,1)S(1)} collective-permute-done((bf16[128,256]{1,0:T(8,128)(2,1)}, bf16[128,256]{1,0:T(8,128)(2,1)S(1)}, u32[]{:S(2)}, u32[]{:S(2)}) %collective-permute-start.2) | collective-permute-done | bytes 65568 | tf_op jit(solution)/shard_map/ppermute | solution.py:183
  6.3 0.0 collective-permute-done.3.refs_2_
  6.3 0.0 copy-done.1
  6.3 0.4 %shard_map.61 = (f32[8,256]{1,0:T(8,128)S(1)}, f32[8,256]{1,0:T(8,128)S(1)}, f32[8,256]{1,0:T(8,128)S(1)}, f32[8,256]{1,0:T(8,128)S(1)}) custom-call(bf16[256,256]{1,0:T(8,128)(2,1)S(1)} %get-tuple-element.21.order_ref, bf16[8,256,256]{2,1,0:T(8,128)(2,1)S(1)} %get-tuple-element.22.weight_ref, bf16[128,256]{1,0:T(8,128)(2,1)S(1)} %collective-permute-done.2.refs_0_.refs_1_, ...), custom_call_target="tpu_custom_call" | custom-call | bytes 1376256 | tf_op jit(solution)/shard_map/pallas_call | solution.py:196
  6.8 0.2 %collective-permute-done = f32[2,256]{1,0:T(2,128)S(1)} collective-permute-done((f32[2,256]{1,0:T(2,128)S(1)}, f32[2,256]{1,0:T(2,128)S(1)}, u32[]{:S(2)}, u32[]{:S(2)}) %collective-permute-start) | collective-permute-done | bytes 2080 | tf_op jit(solution)/shard_map/ppermute | solution.py:183
  7.0 1.6 %collective-permute-start.4 = (f32[12,256]{1,0:T(8,128)S(1)}, f32[12,256]{1,0:T(8,128)S(1)}, u32[]{:S(2)}, u32[]{:S(2)}) collective-permute-start(f32[12,256]{1,0:T(8,128)S(1)} %get-tuple-element.42), channel_id=1, source_target_pairs={{0,5},{1,4},{2,7},{3,6},{4,1},{5,0},{6,3},{7,2},{8,13},{9,12},{10,... | collective-permute-start | bytes 36872 | tf_op jit(solution)/shard_map/ppermute | solution.py:183
  8.6 1.5 %collective-permute-start.5 = (f32[12,256]{1,0:T(8,128)S(1)}, f32[12,256]{1,0:T(8,128)S(1)}, u32[]{:S(2)}, u32[]{:S(2)}) collective-permute-start(f32[12,256]{1,0:T(8,128)S(1)} %get-tuple-element.41), channel_id=1, source_target_pairs={{0,12},{1,13},{2,14},{3,15},{4,8},{5,9},{6,10},{7,11},{8,4},{9,5},... | collective-permute-start | bytes 36872 | tf_op jit(solution)/shard_map/ppermute | solution.py:183
  10.1 0.0 collective-permute-start.6
  10.1 0.6 %collective-permute-start.7 = (bf16[128,256]{1,0:T(8,128)(2,1)S(1)}, bf16[128,256]{1,0:T(8,128)(2,1)S(1)}, u32[]{:S(2)}, u32[]{:S(2)}) collective-permute-start(bf16[128,256]{1,0:T(8,128)(2,1)S(1)} %collective-permute-done.2.refs_0_.refs_1_), channel_id=1, source_target_pairs={{0,1},{1,0},{2,3},{3,2},{4,5},{5,4},{6,7},{7,6},{8,9},{9,8},{10,11... | collective-permute-start | bytes 196616 | tf_op jit(solution)/shard_map/ppermute | solution.py:183
  10.7 0.0 collective-permute-done.4
  10.7 2.5 %collective-permute-done.5 = f32[12,256]{1,0:T(8,128)S(1)} collective-permute-done((f32[12,256]{1,0:T(8,128)S(1)}, f32[12,256]{1,0:T(8,128)S(1)}, u32[]{:S(2)}, u32[]{:S(2)}) %collective-permute-start.5) | collective-permute-done | bytes 12320 | tf_op jit(solution)/shard_map/ppermute | solution.py:183
  13.2 0.0 collective-permute-done.6
  13.3 0.0 collective-permute-done.7.refs_3_
  13.3 0.1 concatenate.35
  13.4 2.5 %collective-permute-start.8 = (f32[20,256]{1,0:T(8,128)S(1)}, f32[20,256]{1,0:T(8,128)S(1)}, u32[]{:S(2)}, u32[]{:S(2)}) collective-permute-start(f32[20,256]{1,0:T(8,128)S(1)} %concatenate.35), channel_id=1, source_target_pairs={{0,17},{1,16},{2,19},{3,18},{4,21},{5,20},{6,23},{7,22},{8,25},{9,... | collective-permute-start | bytes 61448 | tf_op jit(solution)/shard_map/ppermute | solution.py:183
  15.9 1.7 %collective-permute-done.8 = f32[20,256]{1,0:T(8,128)S(1)} collective-permute-done((f32[20,256]{1,0:T(8,128)S(1)}, f32[20,256]{1,0:T(8,128)S(1)}, u32[]{:S(2)}, u32[]{:S(2)}) %collective-permute-start.8) | collective-permute-done | bytes 20512 | tf_op jit(solution)/shard_map/ppermute | solution.py:183
  17.7 0.3 %collective-permute-start.9 = (f32[18,256]{1,0:T(8,128)S(1)}, f32[18,256]{1,0:T(8,128)S(1)}, u32[]{:S(2)}, u32[]{:S(2)}) collective-permute-start(f32[18,256]{1,0:T(8,128)S(1)} %pad_maximum_fusion.6), channel_id=1, source_target_pairs={{0,1},{1,0},{2,3},{3,2},{4,5},{5,4},{6,7},{7,6},{8,9},{9,8},{10,11... | collective-permute-start | bytes 55304 | tf_op jit(solution)/shard_map/ppermute | solution.py:183
  18.0 1.1 %collective-permute-start.10 = (f32[2,256]{1,0:T(2,128)S(1)}, f32[2,256]{1,0:T(2,128)S(1)}, u32[]{:S(2)}, u32[]{:S(2)}) collective-permute-start(f32[2,256]{1,0:T(2,128)S(1)} %get-tuple-element.38), channel_id=1, source_target_pairs={{0,3},{1,2},{2,1},{3,0},{4,6},{5,7},{6,4},{7,5},{8,10},{9,11},{10,... | collective-permute-start | bytes 6152 | tf_op jit(solution)/shard_map/ppermute | solution.py:183
  19.1 0.0 collective-permute-done.9
  19.1 1.5 %shard_map.62 = f32[1024,256]{1,0:T(8,128)} custom-call(f32[32,128]{1,0:T(8,128)S(1)} %get-tuple-element.32.own_ref, f32[32,128]{1,0:T(8,128)S(1)} %pad_maximum_fusion.7.other_ref, bf16[128,256]{1,0:T(8,128)(2,1)S(1)} %bitcast.11, bf16[128,256]{1,0:T(8,128)(2,1)S(1)} %collective-permute-done.2.refs_0_.refs_1_, ...), custom_call_target="tpu_custom_call" | custom-call | flops 268435456 | bytes 294912 | tf_op jit(solution)/shard_map/pallas_call | solution.py:196
  20.6 0.4 %collective-permute-done.10.refs_1_ = f32[2,256]{1,0:T(2,128)S(1)} collective-permute-done((f32[2,256]{1,0:T(2,128)S(1)}, f32[2,256]{1,0:T(2,128)S(1)}, u32[]{:S(2)}, u32[]{:S(2)}) %collective-permute-start.10) | collective-permute-done | bytes 2080 | tf_op jit(solution)/shard_map/ppermute | solution.py:183
  21.0 0.8 %shard_map.63 = f32[2,512]{1,0:T(2,128)} custom-call(bf16[2,512]{1,0:T(2,128)(2,1)S(1)} %bitcast.13, f32[1,512]{1,0:T(1,128)S(1)} %bitcast.15, f32[2,256]{1,0:T(2,128)S(1)} %slice.91.other_ref, f32[2,256]{1,0:T(2,128)S(1)} %get-tuple-element.29.refs_0_, f32[2,256]{1,0:T(2,128)S(1)} %collective-permute-done.10.refs_1_), custom_call_target="tpu_custom_call" | custom-call | bytes 10240 | tf_op jit(solution)/shard_map/pallas_call | solution.py:196
  (16 shorter events, 0.1 us)
Async XLA Ops:
  0.6 3.9 %collective-permute-start.1 = (bf16[1024,256]{1,0:T(8,128)(2,1)}, bf16[1024,256]{1,0:T(8,128)(2,1)S(1)}, u32[]{:S(2)}, u32[]{:S(2)}) collective-permute-start(bf16[1024,256]{1,0:T(8,128)(2,1)} %bitcast.6), channel_id=1, source_target_pairs={{0,1},{1,0},{2,3},{3,2},{4,5},{5,4},{6,7},{7,6},{8,9},{9,8},{10,11... | collective-permute-start | bytes 1572872 | tf_op jit(solution)/shard_map/ppermute | solution.py:183
  1.1 2.7 %copy-start.3 = (f32[512]{0:T(512)S(1)}, f32[512]{0:T(512)}, u32[]{:S(2)}) copy-start(f32[512]{0:T(512)} %param.5) | copy-start | bytes 6148
  1.1 2.7 %copy-start.2 = (bf16[1,2,512]{2,1,0:T(2,128)(2,1)S(1)}, bf16[1,2,512]{2,1,0:T(2,128)(2,1)}, u32[]{:S(2)}) copy-start(bf16[1,2,512]{2,1,0:T(2,128)(2,1)} %param.4) | copy-start | bytes 6148
  1.2 5.2 %collective-permute-start.2 = (bf16[128,256]{1,0:T(8,128)(2,1)}, bf16[128,256]{1,0:T(8,128)(2,1)S(1)}, u32[]{:S(2)}, u32[]{:S(2)}) collective-permute-start(bf16[128,256]{1,0:T(8,128)(2,1)} %bitcast.8), channel_id=1, source_target_pairs={{0,3},{1,2},{2,1},{3,0},{4,6},{5,7},{6,4},{7,5},{8,10},{9,11},{10,... | collective-permute-start | bytes 196616 | tf_op jit(solution)/shard_map/ppermute | solution.py:183
  3.8 2.6 %collective-permute-start.3 = (bf16[128,256]{1,0:T(8,128)(2,1)}, bf16[128,256]{1,0:T(8,128)(2,1)S(1)}, u32[]{:S(2)}, u32[]{:S(2)}) collective-permute-start(bf16[128,256]{1,0:T(8,128)(2,1)} %bitcast.9), channel_id=1, source_target_pairs={{0,1},{1,0},{2,3},{3,2},{4,5},{5,4},{6,7},{7,6},{8,9},{9,8},{10,11... | collective-permute-start | bytes 196616 | tf_op jit(solution)/shard_map/ppermute | solution.py:183
  3.9 1.0 %copy-start = (bf16[128,8,256]{2,1,0:T(8,128)(2,1)S(1)}, bf16[128,8,256]{2,1,0:T(8,128)(2,1)}, u32[]{:S(2)}) copy-start(bf16[128,8,256]{2,1,0:T(8,128)(2,1)} %param.7) | copy-start | bytes 1572868
  4.0 3.0 %collective-permute-start = (f32[2,256]{1,0:T(2,128)S(1)}, f32[2,256]{1,0:T(2,128)S(1)}, u32[]{:S(2)}, u32[]{:S(2)}) collective-permute-start(f32[2,256]{1,0:T(2,128)S(1)} %get-tuple-element.18), channel_id=1, source_target_pairs={{0,3},{1,2},{2,1},{3,0},{4,7},{5,6},{6,5},{7,4},{8,11},{9,10},{10,... | collective-permute-start | bytes 6152 | tf_op jit(solution)/shard_map/ppermute | solution.py:183
  4.9 1.4 %copy-start.1 = (bf16[1,16,8,256]{3,2,1,0:T(8,128)(2,1)S(1)}, bf16[1,16,8,256]{3,2,1,0:T(8,128)(2,1)}, u32[]{:S(2)}) copy-start(bf16[1,16,8,256]{3,2,1,0:T(8,128)(2,1)} %param.6) | copy-start | bytes 196612
  7.0 3.7 %collective-permute-start.4 = (f32[12,256]{1,0:T(8,128)S(1)}, f32[12,256]{1,0:T(8,128)S(1)}, u32[]{:S(2)}, u32[]{:S(2)}) collective-permute-start(f32[12,256]{1,0:T(8,128)S(1)} %get-tuple-element.42), channel_id=1, source_target_pairs={{0,5},{1,4},{2,7},{3,6},{4,1},{5,0},{6,3},{7,2},{8,13},{9,12},{10,... | collective-permute-start | bytes 36872 | tf_op jit(solution)/shard_map/ppermute | solution.py:183
  8.6 4.6 %collective-permute-start.5 = (f32[12,256]{1,0:T(8,128)S(1)}, f32[12,256]{1,0:T(8,128)S(1)}, u32[]{:S(2)}, u32[]{:S(2)}) collective-permute-start(f32[12,256]{1,0:T(8,128)S(1)} %get-tuple-element.41), channel_id=1, source_target_pairs={{0,12},{1,13},{2,14},{3,15},{4,8},{5,9},{6,10},{7,11},{8,4},{9,5},... | collective-permute-start | bytes 36872 | tf_op jit(solution)/shard_map/ppermute | solution.py:183
  10.1 3.2 %collective-permute-start.6 = (f32[12,256]{1,0:T(8,128)S(1)}, f32[12,256]{1,0:T(8,128)S(1)}, u32[]{:S(2)}, u32[]{:S(2)}) collective-permute-start(f32[12,256]{1,0:T(8,128)S(1)} %get-tuple-element.40), channel_id=1, source_target_pairs={{0,9},{1,8},{2,11},{3,10},{4,13},{5,12},{6,15},{7,14},{8,1},{9,0},... | collective-permute-start | bytes 36872 | tf_op jit(solution)/shard_map/ppermute | solution.py:183
  10.1 3.2 %collective-permute-start.7 = (bf16[128,256]{1,0:T(8,128)(2,1)S(1)}, bf16[128,256]{1,0:T(8,128)(2,1)S(1)}, u32[]{:S(2)}, u32[]{:S(2)}) collective-permute-start(bf16[128,256]{1,0:T(8,128)(2,1)S(1)} %collective-permute-done.2.refs_0_.refs_1_), channel_id=1, source_target_pairs={{0,1},{1,0},{2,3},{3,2},{4,5},{5,4},{6,7},{7,6},{8,9},{9,8},{10,11... | collective-permute-start | bytes 196616 | tf_op jit(solution)/shard_map/ppermute | solution.py:183
  13.4 4.2 %collective-permute-start.8 = (f32[20,256]{1,0:T(8,128)S(1)}, f32[20,256]{1,0:T(8,128)S(1)}, u32[]{:S(2)}, u32[]{:S(2)}) collective-permute-start(f32[20,256]{1,0:T(8,128)S(1)} %concatenate.35), channel_id=1, source_target_pairs={{0,17},{1,16},{2,19},{3,18},{4,21},{5,20},{6,23},{7,22},{8,25},{9,... | collective-permute-start | bytes 61448 | tf_op jit(solution)/shard_map/ppermute | solution.py:183
  17.7 1.5 %collective-permute-start.9 = (f32[18,256]{1,0:T(8,128)S(1)}, f32[18,256]{1,0:T(8,128)S(1)}, u32[]{:S(2)}, u32[]{:S(2)}) collective-permute-start(f32[18,256]{1,0:T(8,128)S(1)} %pad_maximum_fusion.6), channel_id=1, source_target_pairs={{0,1},{1,0},{2,3},{3,2},{4,5},{5,4},{6,7},{7,6},{8,9},{9,8},{10,11... | collective-permute-start | bytes 55304 | tf_op jit(solution)/shard_map/ppermute | solution.py:183
  18.0 3.0 %collective-permute-start.10 = (f32[2,256]{1,0:T(2,128)S(1)}, f32[2,256]{1,0:T(2,128)S(1)}, u32[]{:S(2)}, u32[]{:S(2)}) collective-permute-start(f32[2,256]{1,0:T(2,128)S(1)} %get-tuple-element.38), channel_id=1, source_target_pairs={{0,3},{1,2},{2,1},{3,0},{4,6},{5,7},{6,4},{7,5},{8,10},{9,11},{10,... | collective-permute-start | bytes 6152 | tf_op jit(solution)/shard_map/ppermute | solution.py:183

commit v12 on v11

--- a/solution.py
+++ b/solution.py
@@ -40,6 +40,11 @@
     for bit in range(count):
         out = out | (((value >> bit) & 1) << (count - 1 - bit))
     return out
+
+
+def two_terms(value):
+    high = lax.reduce_precision(value, 8, 7)
+    return [high.astype(BF16), (value - high).astype(BF16)]
 
 
 def even_bits(value, count):
@@ -96,7 +101,7 @@
     column = lax.axis_index("ctx") >> 1
     raw = latent_ref[...].astype(F32)
     rms = lax.rsqrt(jnp.mean(raw * raw, axis=1, keepdims=True) + 1e-06)
-    normed = ((raw * rms) * gain_ref[...]).astype(BF16).astype(F32)
+    normed = ((raw * rms) * gain_ref[...]).astype(BF16)
     width = normed.shape[1] // columns
     for j, ref in enumerate(out_refs):
         block = normed[:, :width]
@@ -214,7 +219,7 @@
             mask *= 2
         far = shards[1:]
     gain_row = gain.reshape(1, width)
-    block = jax.ShapeDtypeStruct((owned, 2 * rows), F32)
+    block = jax.ShapeDtypeStruct((owned, 2 * rows), BF16)
     normed = list(call(functools.partial(norm_kernel, columns), [block] * columns, latent[0], gain_row, flops=4 * 10**8))
 
     weight_flat = weight.reshape(rows * heads, channels)
@@ -250,22 +255,19 @@
     far_other = [ctx_swap(s, 1) for s in far]
     mask = 1
     if count == 4:
-        got = {m: head_swap(jnp.concatenate([sent[n], normed], axis=0), m) for m, n in PLANE}
+        got = {m: head_swap(jnp.concatenate(two_terms(sent[n]) + [normed], axis=0), m) for m, n in PLANE}
         half = sums.shape[0]
-        sums = sums + got[1][:half] + got[3][:half] + got[2][:half]
+        for m in (1, 3, 2):
+            sums = sums + (got[m][:half].astype(F32) + got[m][half : 2 * half].astype(F32))
         sums, *far_other = lax.optimization_barrier((sums, *far_other))
-        normed = jnp.concatenate([normed] + [got[m][half:] for m in (1, 3, 2)], axis=0)
+        normed = jnp.concatenate([normed] + [got[m][2 * half :] for m in (1, 3, 2)], axis=0)
         mask = 4
     while mask < head_count:
         half, count = sums.shape[0] // 2, normed.shape[0]
-        if half >= count:
-            got = head_swap(jnp.concatenate([sums[half:], normed], axis=0), mask)
-            got_sums, got_normed = got[:half], got[half:]
-        else:
-            got = head_swap(jnp.concatenate([normed, sums[half:]], axis=0), mask)
-            got_normed, got_sums = got[:count], got[count:]
-        normed = jnp.concatenate([normed, got_normed], axis=0)
-        sums = sums[:half] + got_sums
+        got = head_swap(jnp.concatenate([normed] + two_terms(sums[half:]), axis=0), mask)
+        normed = jnp.concatenate([normed, got[:count]], axis=0)
+        got = got[count:].astype(F32)
+        sums = sums[:half] + (got[:half] + got[half:])
         mask *= 2
 
     blocks = [sums[j * owned : (j + 1) * owned] for j in range(columns)]

time: 22 us -> 21.8 us (level)
  waiting for transfers between devices: 5.56 us -> 5.3 us
    ppermute x11, waiting for transfers between devices: 5.56 us -> 5.3 us  [swap(): return lax.ppermute(value, ('head', 'ctx'), pairs)]
  transfers between devices with their start and end apart: 11 -> 11, of which waited for: 5 -> 5; matrix products, arithmetic and copies ran while one was open for 0% -> 0% of each run, Pallas kernels for 12% -> 13%
where the time goes in v12:
time: 21.8 us; the launch traced here: 21.6 us
  starting transfers between devices  11.5 us (53%)
  waiting for transfers between devices  5.3 us (24%)
  Pallas kernels  3.5 us (16%)
  between operations  0.74 us (3%)
  local copies, waits for them, and re-layouts  0.49 us (2%)
    ppermute x11, starting transfers between devices, swap(): return lax.ppermute(value, ('head', 'ctx'), pairs)  11.5 us
    ppermute x11, waiting for transfers between devices, swap(): return lax.ppermute(value, ('head', 'ctx'), pairs)  5.3 us
    pallas_call x5, Pallas kernels, call(): pl.pallas_call(kernel, out_shape=out, out_specs=jax.tree.map(lambda _: pl...  3.5 us
  transfers between devices with their start and end apart: 11, of which 5 were waited for; matrix products, arithmetic and copies ran while one was open for 0% of the time, Pallas kernels for 13%

profile of v12, /device:TPU:0, one launch (start us, length us, event | category | flops | bytes accessed | tf_op | source)
XLA Modules:
  0.0 21.6 jit_solution(5165301846851468171)
XLA Ops:
  0.6 0.5 %collective-permute-start.1 = (bf16[1024,256]{1,0:T(8,128)(2,1)}, bf16[1024,256]{1,0:T(8,128)(2,1)S(1)}, u32[]{:S(2)}, u32[]{:S(2)}) collective-permute-start(bf16[1024,256]{1,0:T(8,128)(2,1)} %bitcast.6), channel_id=1, source_target_pairs={{0,1},{1,0},{2,3},{3,2},{4,5},{5,4},{6,7},{7,6},{8,9},{9,8},{10,11... | collective-permute-start | bytes 1572872 | tf_op jit(solution)/shard_map/ppermute | solution.py:188
  1.1 0.0 copy-start.3
  1.1 0.0 copy-start.2
  1.2 2.6 %collective-permute-start.2 = (bf16[128,256]{1,0:T(8,128)(2,1)}, bf16[128,256]{1,0:T(8,128)(2,1)S(1)}, u32[]{:S(2)}, u32[]{:S(2)}) collective-permute-start(bf16[128,256]{1,0:T(8,128)(2,1)} %bitcast.8), channel_id=1, source_target_pairs={{0,3},{1,2},{2,1},{3,0},{4,6},{5,7},{6,4},{7,5},{8,10},{9,11},{10,... | collective-permute-start | bytes 196616 | tf_op jit(solution)/shard_map/ppermute | solution.py:188
  3.8 0.1 collective-permute-start.3
  3.8 0.0 copy-done.3
  3.9 0.0 copy-done.2
  3.9 0.0 copy-start
  3.9 0.1 shard_map.59
  4.0 0.6 %collective-permute-start = (bf16[2,256]{1,0:T(2,128)(2,1)S(1)}, bf16[2,256]{1,0:T(2,128)(2,1)S(1)}, u32[]{:S(2)}, u32[]{:S(2)}) collective-permute-start(bf16[2,256]{1,0:T(2,128)(2,1)S(1)} %get-tuple-element.18), channel_id=1, source_target_pairs={{0,3},{1,2},{2,1},{3,0},{4,7},{5,6},{6,5},{7,4},{8,11},{9,10},{10,... | collective-permute-start | bytes 3080 | tf_op jit(solution)/shard_map/ppermute | solution.py:188
  4.6 0.0 collective-permute-done.1.other_ref
  4.6 0.3 %copy-done = bf16[128,8,256]{2,1,0:T(8,128)(2,1)S(1)} copy-done((bf16[128,8,256]{2,1,0:T(8,128)(2,1)S(1)}, bf16[128,8,256]{2,1,0:T(8,128)(2,1)}, u32[]{:S(2)}) %copy-start) | copy-done | bytes 524312
  4.9 0.0 copy-start.1
  4.9 0.8 %shard_map.60 = (bf16[8,256,256]{2,1,0:T(8,128)(2,1)S(1)}, bf16[256,256]{1,0:T(8,128)(2,1)S(1)}) custom-call(bf16[1024,256]{1,0:T(8,128)(2,1)S(1)} %bitcast.7, bf16[1024,256]{1,0:T(8,128)(2,1)S(1)} %collective-permute-done.1.other_ref), custom_call_target="tpu_custom_call" | custom-call | bytes 1048576 | tf_op jit(solution)/shard_map/pallas_call | solution.py:201
  5.7 0.7 %collective-permute-done.2.refs_0_.refs_1_ = bf16[128,256]{1,0:T(8,128)(2,1)S(1)} collective-permute-done((bf16[128,256]{1,0:T(8,128)(2,1)}, bf16[128,256]{1,0:T(8,128)(2,1)S(1)}, u32[]{:S(2)}, u32[]{:S(2)}) %collective-permute-start.2) | collective-permute-done | bytes 65568 | tf_op jit(solution)/shard_map/ppermute | solution.py:188
  6.3 0.0 collective-permute-done.3.refs_2_
  6.3 0.0 copy-done.1
  6.3 0.4 %shard_map.61 = (f32[8,256]{1,0:T(8,128)S(1)}, f32[8,256]{1,0:T(8,128)S(1)}, f32[8,256]{1,0:T(8,128)S(1)}, f32[8,256]{1,0:T(8,128)S(1)}) custom-call(bf16[256,256]{1,0:T(8,128)(2,1)S(1)} %get-tuple-element.21.order_ref, bf16[8,256,256]{2,1,0:T(8,128)(2,1)S(1)} %get-tuple-element.22.weight_ref, bf16[128,256]{1,0:T(8,128)(2,1)S(1)} %collective-permute-done.2.refs_0_.refs_1_, ...), custom_call_target="tpu_custom_call" | custom-call | bytes 1376256 | tf_op jit(solution)/shard_map/pallas_call | solution.py:201
  6.8 0.2 collective-permute-done
  7.0 1.6 %collective-permute-start.4 = (bf16[20,256]{1,0:T(8,128)(2,1)S(1)}, bf16[20,256]{1,0:T(8,128)(2,1)S(1)}, u32[]{:S(2)}, u32[]{:S(2)}) collective-permute-start(bf16[20,256]{1,0:T(8,128)(2,1)S(1)} %get-tuple-element.50), channel_id=1, source_target_pairs={{0,5},{1,4},{2,7},{3,6},{4,1},{5,0},{6,3},{7,2},{8,13},{9,12},{10,... | collective-permute-start | bytes 30728 | tf_op jit(solution)/shard_map/ppermute | solution.py:188
  8.6 1.5 %collective-permute-start.5 = (bf16[20,256]{1,0:T(8,128)(2,1)S(1)}, bf16[20,256]{1,0:T(8,128)(2,1)S(1)}, u32[]{:S(2)}, u32[]{:S(2)}) collective-permute-start(bf16[20,256]{1,0:T(8,128)(2,1)S(1)} %get-tuple-element.49), channel_id=1, source_target_pairs={{0,12},{1,13},{2,14},{3,15},{4,8},{5,9},{6,10},{7,11},{8,4},{9,5},... | collective-permute-start | bytes 30728 | tf_op jit(solution)/shard_map/ppermute | solution.py:188
  10.1 0.0 collective-permute-start.6
  10.1 0.6 %collective-permute-start.7 = (bf16[128,256]{1,0:T(8,128)(2,1)S(1)}, bf16[128,256]{1,0:T(8,128)(2,1)S(1)}, u32[]{:S(2)}, u32[]{:S(2)}) collective-permute-start(bf16[128,256]{1,0:T(8,128)(2,1)S(1)} %collective-permute-done.2.refs_0_.refs_1_), channel_id=1, source_target_pairs={{0,1},{1,0},{2,3},{3,2},{4,5},{5,4},{6,7},{7,6},{8,9},{9,8},{10,11... | collective-permute-start | bytes 196616 | tf_op jit(solution)/shard_map/ppermute | solution.py:188
  10.7 0.0 collective-permute-done.4
  10.7 2.5 %collective-permute-done.5 = bf16[20,256]{1,0:T(8,128)(2,1)S(1)} collective-permute-done((bf16[20,256]{1,0:T(8,128)(2,1)S(1)}, bf16[20,256]{1,0:T(8,128)(2,1)S(1)}, u32[]{:S(2)}, u32[]{:S(2)}) %collective-permute-start.5) | collective-permute-done | bytes 10272 | tf_op jit(solution)/shard_map/ppermute | solution.py:188
  13.2 0.0 collective-permute-done.6
  13.2 0.0 collective-permute-done.7.refs_3_
  13.3 0.1 concatenate.35
  13.3 2.5 %collective-permute-start.8 = (bf16[24,256]{1,0:T(8,128)(2,1)S(1)}, bf16[24,256]{1,0:T(8,128)(2,1)S(1)}, u32[]{:S(2)}, u32[]{:S(2)}) collective-permute-start(bf16[24,256]{1,0:T(8,128)(2,1)S(1)} %concatenate.35), channel_id=1, source_target_pairs={{0,17},{1,16},{2,19},{3,18},{4,21},{5,20},{6,23},{7,22},{8,25},{9,... | collective-permute-start | bytes 36872 | tf_op jit(solution)/shard_map/ppermute | solution.py:188
  15.8 1.6 %collective-permute-done.8 = bf16[24,256]{1,0:T(8,128)(2,1)S(1)} collective-permute-done((bf16[24,256]{1,0:T(8,128)(2,1)S(1)}, bf16[24,256]{1,0:T(8,128)(2,1)S(1)}, u32[]{:S(2)}, u32[]{:S(2)}) %collective-permute-start.8) | collective-permute-done | bytes 12320 | tf_op jit(solution)/shard_map/ppermute | solution.py:188
  17.5 0.3 %collective-permute-start.9 = (f32[18,256]{1,0:T(8,128)S(1)}, f32[18,256]{1,0:T(8,128)S(1)}, u32[]{:S(2)}, u32[]{:S(2)}) collective-permute-start(f32[18,256]{1,0:T(8,128)S(1)} %pad_maximum_fusion), channel_id=1, source_target_pairs={{0,1},{1,0},{2,3},{3,2},{4,5},{5,4},{6,7},{7,6},{8,9},{9,8},{10,11... | collective-permute-start | bytes 55304 | tf_op jit(solution)/shard_map/ppermute | solution.py:188
  17.8 1.2 %collective-permute-start.10 = (f32[2,256]{1,0:T(2,128)S(1)}, f32[2,256]{1,0:T(2,128)S(1)}, u32[]{:S(2)}, u32[]{:S(2)}) collective-permute-start(f32[2,256]{1,0:T(2,128)S(1)} %get-tuple-element.46), channel_id=1, source_target_pairs={{0,3},{1,2},{2,1},{3,0},{4,6},{5,7},{6,4},{7,5},{8,10},{9,11},{10,... | collective-permute-start | bytes 6152 | tf_op jit(solution)/shard_map/ppermute | solution.py:188
  19.0 0.0 collective-permute-done.9
  19.0 1.5 %shard_map.62 = f32[1024,256]{1,0:T(8,128)} custom-call(bf16[32,128]{1,0:T(8,128)(2,1)S(1)} %get-tuple-element.34.own_ref, f32[32,128]{1,0:T(8,128)S(1)} %pad_maximum_fusion.7.other_ref, bf16[128,256]{1,0:T(8,128)(2,1)S(1)} %bitcast.11, bf16[128,256]{1,0:T(8,128)(2,1)S(1)} %collective-permute-done.2.refs_0_.refs_1_, ...), custom_call_target="tpu_custom_call" | custom-call | flops 268435456 | bytes 286720 | tf_op jit(solution)/shard_map/pallas_call | solution.py:201
  20.5 0.3 %collective-permute-done.10.refs_1_ = f32[2,256]{1,0:T(2,128)S(1)} collective-permute-done((f32[2,256]{1,0:T(2,128)S(1)}, f32[2,256]{1,0:T(2,128)S(1)}, u32[]{:S(2)}, u32[]{:S(2)}) %collective-permute-start.10) | collective-permute-done | bytes 2080 | tf_op jit(solution)/shard_map/ppermute | solution.py:188
  20.9 0.8 %shard_map.63 = f32[2,512]{1,0:T(2,128)} custom-call(bf16[2,512]{1,0:T(2,128)(2,1)S(1)} %bitcast.13, f32[1,512]{1,0:T(1,128)S(1)} %bitcast.15, f32[2,256]{1,0:T(2,128)S(1)} %slice.116.other_ref, f32[2,256]{1,0:T(2,128)S(1)} %get-tuple-element.29.refs_0_, f32[2,256]{1,0:T(2,128)S(1)} %collective-permute-done.10.refs_1_), custom_call_target="tpu_custom_call" | custom-call | bytes 10240 | tf_op jit(solution)/shard_map/pallas_call | solution.py:201
  (20 shorter events, 0.2 us)
Async XLA Ops:
  0.6 3.9 %collective-permute-start.1 = (bf16[1024,256]{1,0:T(8,128)(2,1)}, bf16[1024,256]{1,0:T(8,128)(2,1)S(1)}, u32[]{:S(2)}, u32[]{:S(2)}) collective-permute-start(bf16[1024,256]{1,0:T(8,128)(2,1)} %bitcast.6), channel_id=1, source_target_pairs={{0,1},{1,0},{2,3},{3,2},{4,5},{5,4},{6,7},{7,6},{8,9},{9,8},{10,11... | collective-permute-start | bytes 1572872 | tf_op jit(solution)/shard_map/ppermute | solution.py:188
  1.1 2.7 %copy-start.3 = (f32[512]{0:T(512)S(1)}, f32[512]{0:T(512)}, u32[]{:S(2)}) copy-start(f32[512]{0:T(512)} %param.5) | copy-start | bytes 6148
  1.1 2.7 %copy-start.2 = (bf16[1,2,512]{2,1,0:T(2,128)(2,1)S(1)}, bf16[1,2,512]{2,1,0:T(2,128)(2,1)}, u32[]{:S(2)}) copy-start(bf16[1,2,512]{2,1,0:T(2,128)(2,1)} %param.4) | copy-start | bytes 6148
  1.2 5.2 %collective-permute-start.2 = (bf16[128,256]{1,0:T(8,128)(2,1)}, bf16[128,256]{1,0:T(8,128)(2,1)S(1)}, u32[]{:S(2)}, u32[]{:S(2)}) collective-permute-start(bf16[128,256]{1,0:T(8,128)(2,1)} %bitcast.8), channel_id=1, source_target_pairs={{0,3},{1,2},{2,1},{3,0},{4,6},{5,7},{6,4},{7,5},{8,10},{9,11},{10,... | collective-permute-start | bytes 196616 | tf_op jit(solution)/shard_map/ppermute | solution.py:188
  3.8 2.6 %collective-permute-start.3 = (bf16[128,256]{1,0:T(8,128)(2,1)}, bf16[128,256]{1,0:T(8,128)(2,1)S(1)}, u32[]{:S(2)}, u32[]{:S(2)}) collective-permute-start(bf16[128,256]{1,0:T(8,128)(2,1)} %bitcast.9), channel_id=1, source_target_pairs={{0,1},{1,0},{2,3},{3,2},{4,5},{5,4},{6,7},{7,6},{8,9},{9,8},{10,11... | collective-permute-start | bytes 196616 | tf_op jit(solution)/shard_map/ppermute | solution.py:188
  3.9 1.0 %copy-start = (bf16[128,8,256]{2,1,0:T(8,128)(2,1)S(1)}, bf16[128,8,256]{2,1,0:T(8,128)(2,1)}, u32[]{:S(2)}) copy-start(bf16[128,8,256]{2,1,0:T(8,128)(2,1)} %param.7) | copy-start | bytes 1572868
  4.0 3.0 %collective-permute-start = (bf16[2,256]{1,0:T(2,128)(2,1)S(1)}, bf16[2,256]{1,0:T(2,128)(2,1)S(1)}, u32[]{:S(2)}, u32[]{:S(2)}) collective-permute-start(bf16[2,256]{1,0:T(2,128)(2,1)S(1)} %get-tuple-element.18), channel_id=1, source_target_pairs={{0,3},{1,2},{2,1},{3,0},{4,7},{5,6},{6,5},{7,4},{8,11},{9,10},{10,... | collective-permute-start | bytes 3080 | tf_op jit(solution)/shard_map/ppermute | solution.py:188
  4.9 1.4 %copy-start.1 = (bf16[1,16,8,256]{3,2,1,0:T(8,128)(2,1)S(1)}, bf16[1,16,8,256]{3,2,1,0:T(8,128)(2,1)}, u32[]{:S(2)}) copy-start(bf16[1,16,8,256]{3,2,1,0:T(8,128)(2,1)} %param.6) | copy-start | bytes 196612
  7.0 3.7 %collective-permute-start.4 = (bf16[20,256]{1,0:T(8,128)(2,1)S(1)}, bf16[20,256]{1,0:T(8,128)(2,1)S(1)}, u32[]{:S(2)}, u32[]{:S(2)}) collective-permute-start(bf16[20,256]{1,0:T(8,128)(2,1)S(1)} %get-tuple-element.50), channel_id=1, source_target_pairs={{0,5},{1,4},{2,7},{3,6},{4,1},{5,0},{6,3},{7,2},{8,13},{9,12},{10,... | collective-permute-start | bytes 30728 | tf_op jit(solution)/shard_map/ppermute | solution.py:188
  8.6 4.6 %collective-permute-start.5 = (bf16[20,256]{1,0:T(8,128)(2,1)S(1)}, bf16[20,256]{1,0:T(8,128)(2,1)S(1)}, u32[]{:S(2)}, u32[]{:S(2)}) collective-permute-start(bf16[20,256]{1,0:T(8,128)(2,1)S(1)} %get-tuple-element.49), channel_id=1, source_target_pairs={{0,12},{1,13},{2,14},{3,15},{4,8},{5,9},{6,10},{7,11},{8,4},{9,5},... | collective-permute-start | bytes 30728 | tf_op jit(solution)/shard_map/ppermute | solution.py:188
  10.1 3.1 %collective-permute-start.6 = (bf16[20,256]{1,0:T(8,128)(2,1)S(1)}, bf16[20,256]{1,0:T(8,128)(2,1)S(1)}, u32[]{:S(2)}, u32[]{:S(2)}) collective-permute-start(bf16[20,256]{1,0:T(8,128)(2,1)S(1)} %get-tuple-element.48), channel_id=1, source_target_pairs={{0,9},{1,8},{2,11},{3,10},{4,13},{5,12},{6,15},{7,14},{8,1},{9,0},... | collective-permute-start | bytes 30728 | tf_op jit(solution)/shard_map/ppermute | solution.py:188
  10.1 3.1 %collective-permute-start.7 = (bf16[128,256]{1,0:T(8,128)(2,1)S(1)}, bf16[128,256]{1,0:T(8,128)(2,1)S(1)}, u32[]{:S(2)}, u32[]{:S(2)}) collective-permute-start(bf16[128,256]{1,0:T(8,128)(2,1)S(1)} %collective-permute-done.2.refs_0_.refs_1_), channel_id=1, source_target_pairs={{0,1},{1,0},{2,3},{3,2},{4,5},{5,4},{6,7},{7,6},{8,9},{9,8},{10,11... | collective-permute-start | bytes 196616 | tf_op jit(solution)/shard_map/ppermute | solution.py:188
  13.3 4.1 %collective-permute-start.8 = (bf16[24,256]{1,0:T(8,128)(2,1)S(1)}, bf16[24,256]{1,0:T(8,128)(2,1)S(1)}, u32[]{:S(2)}, u32[]{:S(2)}) collective-permute-start(bf16[24,256]{1,0:T(8,128)(2,1)S(1)} %concatenate.35), channel_id=1, source_target_pairs={{0,17},{1,16},{2,19},{3,18},{4,21},{5,20},{6,23},{7,22},{8,25},{9,... | collective-permute-start | bytes 36872 | tf_op jit(solution)/shard_map/ppermute | solution.py:188
  17.5 1.5 %collective-permute-start.9 = (f32[18,256]{1,0:T(8,128)S(1)}, f32[18,256]{1,0:T(8,128)S(1)}, u32[]{:S(2)}, u32[]{:S(2)}) collective-permute-start(f32[18,256]{1,0:T(8,128)S(1)} %pad_maximum_fusion), channel_id=1, source_target_pairs={{0,1},{1,0},{2,3},{3,2},{4,5},{5,4},{6,7},{7,6},{8,9},{9,8},{10,11... | collective-permute-start | bytes 55304 | tf_op jit(solution)/shard_map/ppermute | solution.py:188
  17.8 3.0 %collective-permute-start.10 = (f32[2,256]{1,0:T(2,128)S(1)}, f32[2,256]{1,0:T(2,128)S(1)}, u32[]{:S(2)}, u32[]{:S(2)}) collective-permute-start(f32[2,256]{1,0:T(2,128)S(1)} %get-tuple-element.46), channel_id=1, source_target_pairs={{0,3},{1,2},{2,1},{3,0},{4,6},{5,7},{6,4},{7,5},{8,10},{9,11},{10,... | collective-permute-start | bytes 6152 | tf_op jit(solution)/shard_map/ppermute | solution.py:188

commit v13 on v12

--- a/solution.py
+++ b/solution.py
@@ -43,8 +43,8 @@
 
 
 def two_terms(value):
-    high = lax.reduce_precision(value, 8, 7)
-    return [high.astype(BF16), (value - high).astype(BF16)]
+    high = value.astype(BF16).astype(F32)
+    return jnp.concatenate([high, (value - high).astype(BF16).astype(F32)], axis=0)
 
 
 def even_bits(value, count):
@@ -93,15 +93,51 @@
         total += matmul(moved[h * part : (h + 1) * part], weight_ref[h])
     turned = jnp.concatenate([total[:, rows:], total[:, :rows]], axis=1)
     total = jnp.where(core == 0, total, turned)
-    for n, ref in enumerate(out_refs):
-        ref[...] = total[n * size : (n + 1) * size]
-
-
-def norm_kernel(columns, latent_ref, gain_ref, *out_refs):
+    out_refs[0][...] = total[:size]
+    for n, ref in enumerate(out_refs[1:]):
+        ref[...] = two_terms(total[(n + 1) * size : (n + 2) * size]).astype(BF16)
+
+
+def merge_kernel(skip, sums_ref, normed_ref, *refs):
+    got_refs, keep_ref, message_ref = refs[:-2], refs[-2], refs[-1]
+    total, rows = merged(skip, sums_ref, normed_ref, got_refs)
+    half = keep_ref.shape[0]
+    keep_ref[...] = total[:half]
+    message_ref[...] = jnp.concatenate([two_terms(total[half:]), rows], axis=0).astype(BF16)
+
+
+def last_merge_kernel(skip, columns, sums_ref, normed_ref, *refs):
+    got_refs, block_refs, own_ref, sent_ref = refs[: -columns - 2], refs[-columns - 2 : -2], refs[-2], refs[-1]
+    total, rows = merged(skip, sums_ref, normed_ref, got_refs)
+    owned = total.shape[0] // columns
+    for j, ref in enumerate(block_refs):
+        ref[...] = total[j * owned : (j + 1) * owned]
+    core = lax.axis_index("ctx") & 1
+    count, width = rows.shape[0] // 2, rows.shape[1] // 2
+    own_ref[...] = jnp.where(core == 0, rows[:, :width], rows[:, width:])
+    sent = jnp.where(core == 0, rows[:, width:], rows[:, :width])
+    sent = jnp.concatenate([sent[:count], sent[count:]], axis=1)
+    sent_ref[...] = jnp.concatenate([sent, total[:owned]], axis=0) if columns == 2 else sent
+
+
+def merged(skip, sums_ref, normed_ref, got_refs):
+    total, half = sums_ref[...], sums_ref.shape[0]
+    rows = [normed_ref[...].astype(F32)[skip:]]
+    for ref in got_refs:
+        got = ref[...].astype(F32)
+        total = total + (got[:half] + got[half : 2 * half])
+        rows.append(got[2 * half :])
+    return total, jnp.concatenate(rows, axis=0)
+
+
+def norm_kernel(columns, latent_ref, gain_ref, rms_ref, hat_ref, *out_refs):
     column = lax.axis_index("ctx") >> 1
     raw = latent_ref[...].astype(F32)
     rms = lax.rsqrt(jnp.mean(raw * raw, axis=1, keepdims=True) + 1e-06)
-    normed = ((raw * rms) * gain_ref[...]).astype(BF16)
+    hat = raw * rms
+    rms_ref[...] = jnp.broadcast_to(rms, raw.shape)
+    hat_ref[...] = hat
+    normed = (hat * gain_ref[...]).astype(BF16)
     width = normed.shape[1] // columns
     for j, ref in enumerate(out_refs):
         block = normed[:, :width]
@@ -118,7 +154,9 @@
     groups = sems.shape[0]
     rows = out_ref.shape[0] // heads // groups
     tokens = head_count * owned
-    normed = jnp.concatenate([own_ref[...], other_ref[...]], axis=0).astype(BF16)
+    count, width = own_ref.shape[0] // 2, own_ref.shape[1]
+    other = other_ref[...]
+    normed = jnp.concatenate([own_ref[...], other[:count, :width], other[:count, width:]], axis=0).astype(BF16)
     size = columns * tokens * heads
     at, to = iota((normed.shape[0], size), 0), iota((1, size), 1)
     token, j = rest(whole(to, heads), tokens), whole(to, heads * tokens)
@@ -148,17 +186,16 @@
         copy.wait()
 
 
-def latent_kernel(head_count, columns, latent_ref, gain_ref, other_ref, *refs):
+def latent_kernel(head_count, columns, rms_ref, hat_ref, gain_ref, other_ref, *refs):
     block_refs, out_ref = refs[:-1], refs[-1]
     column = lax.axis_index("ctx") >> 1
     crossed = even_bits(lax.axis_index("head"), head_count.bit_length() - 1)
-    raw = latent_ref[...].astype(F32)
-    rms = lax.rsqrt(jnp.mean(raw * raw, axis=1, keepdims=True) + 1e-06)
-    hat = raw * rms
     relative = [ref[...] for ref in block_refs]
-    count = raw.shape[0]
+    count = out_ref.shape[0]
+    first = other_ref.shape[0] - count * columns // 2
     for j in range(0, columns, 2):
-        relative[j] = jnp.where(crossed == 0, relative[j], other_ref[j // 2 * count : (j // 2 + 1) * count, :])
+        place = first + j // 2 * count
+        relative[j] = jnp.where(crossed == 0, relative[j], other_ref[place : place + count, :])
     blocks = []
     for b in range(columns):
         block = relative[0]
@@ -166,8 +203,9 @@
             block = jnp.where((column ^ j) == b, relative[j], block)
         blocks.append(block)
     scaled = jnp.concatenate(blocks, axis=1) * gain_ref[...]
+    hat = hat_ref[...]
     inner = jnp.mean(scaled * hat, axis=1, keepdims=True)
-    out_ref[...] = rms * (scaled - hat * inner)
+    out_ref[...] = rms_ref[...] * (scaled - hat * inner)
 
 
 def per_device(head_count, ctx_count, latent, gain, cotangent, weight):
@@ -220,7 +258,10 @@
         far = shards[1:]
     gain_row = gain.reshape(1, width)
     block = jax.ShapeDtypeStruct((owned, 2 * rows), BF16)
-    normed = list(call(functools.partial(norm_kernel, columns), [block] * columns, latent[0], gain_row, flops=4 * 10**8))
+    row = jax.ShapeDtypeStruct((owned, width), F32)
+    rms, hat, *normed = call(
+        functools.partial(norm_kernel, columns), [row] * 2 + [block] * columns, latent[0], gain_row, flops=4 * 10**8
+    )
 
     weight_flat = weight.reshape(rows * heads, channels)
     weight_other = ctx_swap(weight_flat, 1)
@@ -241,48 +282,53 @@
         mask *= 2
     normed = jnp.concatenate(normed, axis=0)
 
-    count = 4 if head_count >= 4 else 1
+    size = head_count * columns * owned // 4
     sums, *sent = call(
-        functools.partial(partial_kernel, head_count, count),
-        [jax.ShapeDtypeStruct((head_count * columns * owned // count, 2 * rows), F32)] * count,
+        functools.partial(partial_kernel, head_count, 4),
+        [jax.ShapeDtypeStruct((size, 2 * rows), F32)] + [jax.ShapeDtypeStruct((2 * size, 2 * rows), BF16)] * 3,
         order,
         chip_weight,
         *far,
         own,
         other,
     )
-    core = lax.axis_index("ctx") & 1
+    sums, *far = lax.optimization_barrier((sums, *far))
     far_other = [ctx_swap(s, 1) for s in far]
-    mask = 1
-    if count == 4:
-        got = {m: head_swap(jnp.concatenate(two_terms(sent[n]) + [normed], axis=0), m) for m, n in PLANE}
-        half = sums.shape[0]
-        for m in (1, 3, 2):
-            sums = sums + (got[m][:half].astype(F32) + got[m][half : 2 * half].astype(F32))
-        sums, *far_other = lax.optimization_barrier((sums, *far_other))
-        normed = jnp.concatenate([normed] + [got[m][2 * half :] for m in (1, 3, 2)], axis=0)
-        mask = 4
+    got = {m: head_swap(jnp.concatenate([sent[n], normed], axis=0), m) for m, n in PLANE}
+    got = [got[m] for m in (1, 3, 2)]
+    skip, count, mask = 0, 4 * normed.shape[0], 4
     while mask < head_count:
-        half, count = sums.shape[0] // 2, normed.shape[0]
-        got = head_swap(jnp.concatenate([normed] + two_terms(sums[half:]), axis=0), mask)
-        normed = jnp.concatenate([normed, got[:count]], axis=0)
-        got = got[count:].astype(F32)
-        sums = sums[:half] + (got[:half] + got[half:])
-        mask *= 2
-
-    blocks = [sums[j * owned : (j + 1) * owned] for j in range(columns)]
+        half = sums.shape[0] // 2
+        sums, normed = call(
+            functools.partial(merge_kernel, skip),
+            [jax.ShapeDtypeStruct((half, 2 * rows), F32), jax.ShapeDtypeStruct((2 * half + count, 2 * rows), BF16)],
+            sums,
+            normed,
+            *got,
+        )
+        if mask == 4:
+            normed, *far_other = lax.optimization_barrier((normed, *far_other))
+        got = [head_swap(normed, mask)]
+        skip, count, mask = 2 * half, 2 * count, 2 * mask
+    short = jax.ShapeDtypeStruct((owned, 2 * rows), F32)
+    kept = owned if columns == 2 else 0
+    *blocks, normed_own, sent = call(
+        functools.partial(last_merge_kernel, skip, columns),
+        [short] * columns
+        + [jax.ShapeDtypeStruct((count, rows), F32), jax.ShapeDtypeStruct((count // 2 + kept, 2 * rows), F32)],
+        sums,
+        normed,
+        *got,
+    )
     mask = ctx_count // 2
     while mask > 2:
         for j in range(columns):
             if j & (mask >> 1):
                 blocks[j] = ctx_swap(blocks[j], mask)
         mask //= 2
-    normed_own = jnp.where(core == 0, normed[:, :rows], normed[:, rows:])
-    sent = jnp.where(core == 0, normed[:, rows:], normed[:, :rows])
-    count = sent.shape[0] // 2
-    sent = [sent[:count], sent[count:]]
-    both = ctx_swap(jnp.concatenate([jnp.concatenate(sent, axis=1)] + blocks[::2], axis=0), 1)
-    normed_other = jnp.concatenate([both[:count, :rows], both[:count, rows:]], axis=0)
+    if columns > 2:
+        sent = jnp.concatenate([sent] + blocks[::2], axis=0)
+    both = ctx_swap(sent, 1)
     for j in range(1, columns, 2):
         blocks[j] = role_swap(blocks[j], 2)
 
@@ -290,7 +336,7 @@
         functools.partial(weight_grad_kernel, head_count, heads, owned, columns),
         jax.ShapeDtypeStruct((rows * heads, channels), F32),
         normed_own,
-        normed_other,
+        both,
         own,
         *far,
         other,
@@ -307,9 +353,10 @@
     latent_gradient = call(
         functools.partial(latent_kernel, head_count, columns),
         jax.ShapeDtypeStruct((owned, width), F32),
-        latent[0],
+        rms,
+        hat,
         gain_row,
-        both[count:],
+        both,
         *blocks,
     )
     return latent_gradient[None], weight_grad.reshape(weight.shape)

time: 21.8 us -> 21.5 us (0.986)
    pallas_call x5 -> x7, Pallas kernels: 3.5 us -> 3.48 us  [call(): pl.pallas_call(kernel, out_shape=out, out_specs=jax.tree.map(lambda _: pl...]
where the time goes in v13:
time: 21.5 us; the launch traced here: 21.3 us
  starting transfers between devices  11.5 us (53%)
  waiting for transfers between devices  5.32 us (25%)
  Pallas kernels  3.48 us (16%)
  between operations  0.68 us (3%)
  local copies, waits for them, and re-layouts  0.34 us (2%)
    ppermute x11, starting transfers between devices, swap(): return lax.ppermute(value, ('head', 'ctx'), pairs)  11.5 us
    ppermute x11, waiting for transfers between devices, swap(): return lax.ppermute(value, ('head', 'ctx'), pairs)  5.32 us
    pallas_call x7, Pallas kernels, call(): pl.pallas_call(kernel, out_shape=out, out_specs=jax.tree.map(lambda _: pl...  3.48 us
  transfers between devices with their start and end apart: 11, of which 5 were waited for; matrix products, arithmetic and copies ran while one was open for 0% of the time, Pallas kernels for 13%

profile of v13, /device:TPU:0, one launch (start us, length us, event | category | flops | bytes accessed | tf_op | source)
XLA Modules:
  0.0 21.3 jit_solution(13950390066308538161)
XLA Ops:
  0.6 0.5 %collective-permute-start = (bf16[1024,256]{1,0:T(8,128)(2,1)}, bf16[1024,256]{1,0:T(8,128)(2,1)S(1)}, u32[]{:S(2)}, u32[]{:S(2)}) collective-permute-start(bf16[1024,256]{1,0:T(8,128)(2,1)} %bitcast.6), channel_id=1, source_target_pairs={{0,1},{1,0},{2,3},{3,2},{4,5},{5,4},{6,7},{7,6},{8,9},{9,8},{10,11... | collective-permute-start | bytes 1572872 | tf_op jit(solution)/shard_map/ppermute | solution.py:226
  1.1 0.0 copy-start.3
  1.1 0.0 copy-start.2
  1.2 2.6 %collective-permute-start.1 = (bf16[128,256]{1,0:T(8,128)(2,1)}, bf16[128,256]{1,0:T(8,128)(2,1)S(1)}, u32[]{:S(2)}, u32[]{:S(2)}) collective-permute-start(bf16[128,256]{1,0:T(8,128)(2,1)} %bitcast.8), channel_id=1, source_target_pairs={{0,3},{1,2},{2,1},{3,0},{4,6},{5,7},{6,4},{7,5},{8,10},{9,11},{10,... | collective-permute-start | bytes 196616 | tf_op jit(solution)/shard_map/ppermute | solution.py:226
  3.8 0.1 collective-permute-start.2
  3.8 0.0 copy-done.3
  3.9 0.0 copy-done.2
  3.9 0.0 copy-start
  3.9 0.1 shard_map.59
  4.0 0.6 %collective-permute-start.3 = (bf16[2,256]{1,0:T(2,128)(2,1)S(1)}, bf16[2,256]{1,0:T(2,128)(2,1)S(1)}, u32[]{:S(2)}, u32[]{:S(2)}) collective-permute-start(bf16[2,256]{1,0:T(2,128)(2,1)S(1)} %get-tuple-element.36), channel_id=1, source_target_pairs={{0,3},{1,2},{2,1},{3,0},{4,7},{5,6},{6,5},{7,4},{8,11},{9,10},{10,... | collective-permute-start | bytes 3080 | tf_op jit(solution)/shard_map/ppermute | solution.py:226
  4.6 0.0 collective-permute-done.other_ref
  4.6 0.3 %copy-done = bf16[128,8,256]{2,1,0:T(8,128)(2,1)S(1)} copy-done((bf16[128,8,256]{2,1,0:T(8,128)(2,1)S(1)}, bf16[128,8,256]{2,1,0:T(8,128)(2,1)}, u32[]{:S(2)}) %copy-start) | copy-done | bytes 524312
  4.9 0.0 copy-start.1
  4.9 0.8 %shard_map.60 = (bf16[8,256,256]{2,1,0:T(8,128)(2,1)S(1)}, bf16[256,256]{1,0:T(8,128)(2,1)S(1)}) custom-call(bf16[1024,256]{1,0:T(8,128)(2,1)S(1)} %bitcast.7, bf16[1024,256]{1,0:T(8,128)(2,1)S(1)} %collective-permute-done.other_ref), custom_call_target="tpu_custom_call" | custom-call | bytes 1048576 | tf_op jit(solution)/shard_map/pallas_call | solution.py:239
  5.7 0.7 %collective-permute-done.1.refs_0_.refs_1_ = bf16[128,256]{1,0:T(8,128)(2,1)S(1)} collective-permute-done((bf16[128,256]{1,0:T(8,128)(2,1)}, bf16[128,256]{1,0:T(8,128)(2,1)S(1)}, u32[]{:S(2)}, u32[]{:S(2)}) %collective-permute-start.1) | collective-permute-done | bytes 65568 | tf_op jit(solution)/shard_map/ppermute | solution.py:226
  6.3 0.0 collective-permute-done.2.refs_2_
  6.3 0.0 copy-done.1
  6.3 0.4 %shard_map.61 = (f32[8,256]{1,0:T(8,128)S(1)}, bf16[16,256]{1,0:T(8,128)(2,1)S(1)}, bf16[16,256]{1,0:T(8,128)(2,1)S(1)}, bf16[16,256]{1,0:T(8,128)(2,1)S(1)}) custom-call(bf16[256,256]{1,0:T(8,128)(2,1)S(1)} %get-tuple-element.32.order_ref, bf16[8,256,256]{2,1,0:T(8,128)(2,1)S(1)} %get-tuple-element.33.weight_ref, ...), custom_call_target="tpu_custom_call" | custom-call | bytes 1376256 | tf_op jit(solution)/shard_map/pallas_call | solution.py:239
  6.8 0.2 collective-permute-done.3
  7.0 1.6 %collective-permute-start.4 = (bf16[20,256]{1,0:T(8,128)(2,1)S(1)}, bf16[20,256]{1,0:T(8,128)(2,1)S(1)}, u32[]{:S(2)}, u32[]{:S(2)}) collective-permute-start(bf16[20,256]{1,0:T(8,128)(2,1)S(1)} %get-tuple-element.54), channel_id=1, source_target_pairs={{0,5},{1,4},{2,7},{3,6},{4,1},{5,0},{6,3},{7,2},{8,13},{9,12},{10,... | collective-permute-start | bytes 30728 | tf_op jit(solution)/shard_map/ppermute | solution.py:226
  8.6 1.5 %collective-permute-start.5 = (bf16[20,256]{1,0:T(8,128)(2,1)S(1)}, bf16[20,256]{1,0:T(8,128)(2,1)S(1)}, u32[]{:S(2)}, u32[]{:S(2)}) collective-permute-start(bf16[20,256]{1,0:T(8,128)(2,1)S(1)} %get-tuple-element.53), channel_id=1, source_target_pairs={{0,12},{1,13},{2,14},{3,15},{4,8},{5,9},{6,10},{7,11},{8,4},{9,5},... | collective-permute-start | bytes 30728 | tf_op jit(solution)/shard_map/ppermute | solution.py:226
  10.1 0.0 collective-permute-start.6
  10.1 0.6 %collective-permute-start.7 = (bf16[128,256]{1,0:T(8,128)(2,1)S(1)}, bf16[128,256]{1,0:T(8,128)(2,1)S(1)}, u32[]{:S(2)}, u32[]{:S(2)}) collective-permute-start(bf16[128,256]{1,0:T(8,128)(2,1)S(1)} %collective-permute-done.1.refs_0_.refs_1_), channel_id=1, source_target_pairs={{0,1},{1,0},{2,3},{3,2},{4,5},{5,4},{6,7},{7,6},{8,9},{9,8},{10,11... | collective-permute-start | bytes 196616 | tf_op jit(solution)/shard_map/ppermute | solution.py:226
  10.7 0.0 collective-permute-done.4.refs_0_
  10.7 2.4 %collective-permute-done.5.refs_1_ = bf16[20,256]{1,0:T(8,128)(2,1)S(1)} collective-permute-done((bf16[20,256]{1,0:T(8,128)(2,1)S(1)}, bf16[20,256]{1,0:T(8,128)(2,1)S(1)}, u32[]{:S(2)}, u32[]{:S(2)}) %collective-permute-start.5) | collective-permute-done | bytes 10272 | tf_op jit(solution)/shard_map/ppermute | solution.py:226
  13.2 0.0 collective-permute-done.6.refs_2_
  13.2 0.0 collective-permute-done.7.refs_3_
  13.2 2.5 %collective-permute-start.8 = (bf16[24,256]{1,0:T(8,128)(2,1)S(1)}, bf16[24,256]{1,0:T(8,128)(2,1)S(1)}, u32[]{:S(2)}, u32[]{:S(2)}) collective-permute-start(bf16[24,256]{1,0:T(8,128)(2,1)S(1)} %get-tuple-element.43.normed_ref), channel_id=1, source_target_pairs={{0,17},{1,16},{2,19},{3,18},{4,21},{5,20},{6,23},{7,22},{8,25},{9,... | collective-permute-start | bytes 36872 | tf_op jit(solution)/shard_map/ppermute | solution.py:226
  15.7 1.6 %collective-permute-done.8.refs_0_ = bf16[24,256]{1,0:T(8,128)(2,1)S(1)} collective-permute-done((bf16[24,256]{1,0:T(8,128)(2,1)S(1)}, bf16[24,256]{1,0:T(8,128)(2,1)S(1)}, u32[]{:S(2)}, u32[]{:S(2)}) %collective-permute-start.8) | collective-permute-done | bytes 12320 | tf_op jit(solution)/shard_map/ppermute | solution.py:226
  17.3 0.3 %collective-permute-start.9 = (f32[18,256]{1,0:T(8,128)S(1)}, f32[18,256]{1,0:T(8,128)S(1)}, u32[]{:S(2)}, u32[]{:S(2)}) collective-permute-start(f32[18,256]{1,0:T(8,128)S(1)} %get-tuple-element.44), channel_id=1, source_target_pairs={{0,1},{1,0},{2,3},{3,2},{4,5},{5,4},{6,7},{7,6},{8,9},{9,8},{10,11... | collective-permute-start | bytes 55304 | tf_op jit(solution)/shard_map/ppermute | solution.py:226
  17.6 1.2 %collective-permute-start.10 = (f32[2,256]{1,0:T(2,128)S(1)}, f32[2,256]{1,0:T(2,128)S(1)}, u32[]{:S(2)}, u32[]{:S(2)}) collective-permute-start(f32[2,256]{1,0:T(2,128)S(1)} %get-tuple-element.48), channel_id=1, source_target_pairs={{0,3},{1,2},{2,1},{3,0},{4,6},{5,7},{6,4},{7,5},{8,10},{9,11},{10,... | collective-permute-start | bytes 6152 | tf_op jit(solution)/shard_map/ppermute | solution.py:226
  18.8 0.0 collective-permute-done.9.other_ref
  18.8 1.5 %shard_map.64 = f32[1024,256]{1,0:T(8,128)} custom-call(f32[32,128]{1,0:T(8,128)S(1)} %get-tuple-element.45.own_ref, f32[18,256]{1,0:T(8,128)S(1)} %collective-permute-done.9.other_ref, bf16[128,256]{1,0:T(8,128)(2,1)S(1)} %bitcast.11, bf16[128,256]{1,0:T(8,128)(2,1)S(1)} %collective-permute-done.1.refs_0_.refs_1_, ...), custom_call_target="tpu_custom_call" | custom-call | flops 268435456 | bytes 296960 | tf_op jit(solution)/shard_map/pallas_call | solution.py:239
  20.3 0.4 %collective-permute-done.10.refs_1_ = f32[2,256]{1,0:T(2,128)S(1)} collective-permute-done((f32[2,256]{1,0:T(2,128)S(1)}, f32[2,256]{1,0:T(2,128)S(1)}, u32[]{:S(2)}, u32[]{:S(2)}) %collective-permute-start.10) | collective-permute-done | bytes 2080 | tf_op jit(solution)/shard_map/ppermute | solution.py:226
  20.6 0.7 %shard_map.65 = f32[2,512]{1,0:T(2,128)} custom-call(f32[2,512]{1,0:T(2,128)S(1)} %get-tuple-element.27.rms_ref, f32[2,512]{1,0:T(2,128)S(1)} %get-tuple-element.28.hat_ref, f32[1,512]{1,0:T(1,128)S(1)} %bitcast.13, f32[18,256]{1,0:T(8,128)S(1)} %collective-permute-done.9.other_ref, f32[2,256]{1,0:T(2,128)S(1)} %get-tuple-element.49.refs_0_, ...), custom_call_target="tpu_custom_call" | custom-call | bytes 32768 | tf_op jit(solution)/shard_map/pallas_call | solution.py:239
  (4 shorter events, 0.0 us)
Async XLA Ops:
  0.6 3.9 %collective-permute-start = (bf16[1024,256]{1,0:T(8,128)(2,1)}, bf16[1024,256]{1,0:T(8,128)(2,1)S(1)}, u32[]{:S(2)}, u32[]{:S(2)}) collective-permute-start(bf16[1024,256]{1,0:T(8,128)(2,1)} %bitcast.6), channel_id=1, source_target_pairs={{0,1},{1,0},{2,3},{3,2},{4,5},{5,4},{6,7},{7,6},{8,9},{9,8},{10,11... | collective-permute-start | bytes 1572872 | tf_op jit(solution)/shard_map/ppermute | solution.py:226
  1.1 2.7 %copy-start.3 = (bf16[1,2,512]{2,1,0:T(2,128)(2,1)S(1)}, bf16[1,2,512]{2,1,0:T(2,128)(2,1)}, u32[]{:S(2)}) copy-start(bf16[1,2,512]{2,1,0:T(2,128)(2,1)} %param.4) | copy-start | bytes 6148
  1.1 2.7 %copy-start.2 = (f32[512]{0:T(512)S(1)}, f32[512]{0:T(512)}, u32[]{:S(2)}) copy-start(f32[512]{0:T(512)} %param.5) | copy-start | bytes 6148
  1.2 5.2 %collective-permute-start.1 = (bf16[128,256]{1,0:T(8,128)(2,1)}, bf16[128,256]{1,0:T(8,128)(2,1)S(1)}, u32[]{:S(2)}, u32[]{:S(2)}) collective-permute-start(bf16[128,256]{1,0:T(8,128)(2,1)} %bitcast.8), channel_id=1, source_target_pairs={{0,3},{1,2},{2,1},{3,0},{4,6},{5,7},{6,4},{7,5},{8,10},{9,11},{10,... | collective-permute-start | bytes 196616 | tf_op jit(solution)/shard_map/ppermute | solution.py:226
  3.8 2.6 %collective-permute-start.2 = (bf16[128,256]{1,0:T(8,128)(2,1)}, bf16[128,256]{1,0:T(8,128)(2,1)S(1)}, u32[]{:S(2)}, u32[]{:S(2)}) collective-permute-start(bf16[128,256]{1,0:T(8,128)(2,1)} %bitcast.9), channel_id=1, source_target_pairs={{0,1},{1,0},{2,3},{3,2},{4,5},{5,4},{6,7},{7,6},{8,9},{9,8},{10,11... | collective-permute-start | bytes 196616 | tf_op jit(solution)/shard_map/ppermute | solution.py:226
  3.9 1.0 %copy-start = (bf16[128,8,256]{2,1,0:T(8,128)(2,1)S(1)}, bf16[128,8,256]{2,1,0:T(8,128)(2,1)}, u32[]{:S(2)}) copy-start(bf16[128,8,256]{2,1,0:T(8,128)(2,1)} %param.7) | copy-start | bytes 1572868
  4.0 3.0 %collective-permute-start.3 = (bf16[2,256]{1,0:T(2,128)(2,1)S(1)}, bf16[2,256]{1,0:T(2,128)(2,1)S(1)}, u32[]{:S(2)}, u32[]{:S(2)}) collective-permute-start(bf16[2,256]{1,0:T(2,128)(2,1)S(1)} %get-tuple-element.36), channel_id=1, source_target_pairs={{0,3},{1,2},{2,1},{3,0},{4,7},{5,6},{6,5},{7,4},{8,11},{9,10},{10,... | collective-permute-start | bytes 3080 | tf_op jit(solution)/shard_map/ppermute | solution.py:226
  4.9 1.4 %copy-start.1 = (bf16[1,16,8,256]{3,2,1,0:T(8,128)(2,1)S(1)}, bf16[1,16,8,256]{3,2,1,0:T(8,128)(2,1)}, u32[]{:S(2)}) copy-start(bf16[1,16,8,256]{3,2,1,0:T(8,128)(2,1)} %param.6) | copy-start | bytes 196612
  7.0 3.7 %collective-permute-start.4 = (bf16[20,256]{1,0:T(8,128)(2,1)S(1)}, bf16[20,256]{1,0:T(8,128)(2,1)S(1)}, u32[]{:S(2)}, u32[]{:S(2)}) collective-permute-start(bf16[20,256]{1,0:T(8,128)(2,1)S(1)} %get-tuple-element.54), channel_id=1, source_target_pairs={{0,5},{1,4},{2,7},{3,6},{4,1},{5,0},{6,3},{7,2},{8,13},{9,12},{10,... | collective-permute-start | bytes 30728 | tf_op jit(solution)/shard_map/ppermute | solution.py:226
  8.6 4.6 %collective-permute-start.5 = (bf16[20,256]{1,0:T(8,128)(2,1)S(1)}, bf16[20,256]{1,0:T(8,128)(2,1)S(1)}, u32[]{:S(2)}, u32[]{:S(2)}) collective-permute-start(bf16[20,256]{1,0:T(8,128)(2,1)S(1)} %get-tuple-element.53), channel_id=1, source_target_pairs={{0,12},{1,13},{2,14},{3,15},{4,8},{5,9},{6,10},{7,11},{8,4},{9,5},... | collective-permute-start | bytes 30728 | tf_op jit(solution)/shard_map/ppermute | solution.py:226
  10.1 3.1 %collective-permute-start.6 = (bf16[20,256]{1,0:T(8,128)(2,1)S(1)}, bf16[20,256]{1,0:T(8,128)(2,1)S(1)}, u32[]{:S(2)}, u32[]{:S(2)}) collective-permute-start(bf16[20,256]{1,0:T(8,128)(2,1)S(1)} %get-tuple-element.52), channel_id=1, source_target_pairs={{0,9},{1,8},{2,11},{3,10},{4,13},{5,12},{6,15},{7,14},{8,1},{9,0},... | collective-permute-start | bytes 30728 | tf_op jit(solution)/shard_map/ppermute | solution.py:226
  10.1 3.1 %collective-permute-start.7 = (bf16[128,256]{1,0:T(8,128)(2,1)S(1)}, bf16[128,256]{1,0:T(8,128)(2,1)S(1)}, u32[]{:S(2)}, u32[]{:S(2)}) collective-permute-start(bf16[128,256]{1,0:T(8,128)(2,1)S(1)} %collective-permute-done.1.refs_0_.refs_1_), channel_id=1, source_target_pairs={{0,1},{1,0},{2,3},{3,2},{4,5},{5,4},{6,7},{7,6},{8,9},{9,8},{10,11... | collective-permute-start | bytes 196616 | tf_op jit(solution)/shard_map/ppermute | solution.py:226
  13.2 4.1 %collective-permute-start.8 = (bf16[24,256]{1,0:T(8,128)(2,1)S(1)}, bf16[24,256]{1,0:T(8,128)(2,1)S(1)}, u32[]{:S(2)}, u32[]{:S(2)}) collective-permute-start(bf16[24,256]{1,0:T(8,128)(2,1)S(1)} %get-tuple-element.43.normed_ref), channel_id=1, source_target_pairs={{0,17},{1,16},{2,19},{3,18},{4,21},{5,20},{6,23},{7,22},{8,25},{9,... | collective-permute-start | bytes 36872 | tf_op jit(solution)/shard_map/ppermute | solution.py:226
  17.3 1.5 %collective-permute-start.9 = (f32[18,256]{1,0:T(8,128)S(1)}, f32[18,256]{1,0:T(8,128)S(1)}, u32[]{:S(2)}, u32[]{:S(2)}) collective-permute-start(f32[18,256]{1,0:T(8,128)S(1)} %get-tuple-element.44), channel_id=1, source_target_pairs={{0,1},{1,0},{2,3},{3,2},{4,5},{5,4},{6,7},{7,6},{8,9},{9,8},{10,11... | collective-permute-start | bytes 55304 | tf_op jit(solution)/shard_map/ppermute | solution.py:226
  17.6 3.0 %collective-permute-start.10 = (f32[2,256]{1,0:T(2,128)S(1)}, f32[2,256]{1,0:T(2,128)S(1)}, u32[]{:S(2)}, u32[]{:S(2)}) collective-permute-start(f32[2,256]{1,0:T(2,128)S(1)} %get-tuple-element.48), channel_id=1, source_target_pairs={{0,3},{1,2},{2,1},{3,0},{4,6},{5,7},{6,4},{7,5},{8,10},{9,11},{10,... | collective-permute-start | bytes 6152 | tf_op jit(solution)/shard_map/ppermute | solution.py:226

commit v14 on v13

--- a/solution.py
+++ b/solution.py
@@ -52,6 +52,10 @@
     for bit in range(1, count):
         out = out ^ ((value >> bit) & 1)
     return out
+
+
+def crossing(head, column, bits):
+    return even_bits(head, bits) ^ (column & 1) ^ 1
 
 
 def weight_kernel(head_count, heads, owned, shards, own_ref, other_ref, out_ref, order_ref):
@@ -82,7 +86,7 @@
 def partial_kernel(head_count, count, order_ref, weight_ref, *refs):
     shard_refs, (own_ref, other_ref), out_refs = refs[: -count - 2], refs[-count - 2 : -count], refs[-count:]
     core = lax.axis_index("ctx") & 1
-    crossed = even_bits(lax.axis_index("head"), head_count.bit_length() - 1)
+    crossed = crossing(lax.axis_index("head"), lax.axis_index("ctx") >> 1, head_count.bit_length() - 1)
     first = jnp.where(crossed == 0, own_ref[...], other_ref[...])
     stacked = jnp.concatenate([first] + [ref[...] for ref in shard_refs], axis=0)
     moved = matmul(order_ref[...], stacked).astype(BF16)
@@ -150,7 +154,7 @@
     shard_refs, (out_ref, spread_ref, total_ref, sems) = refs[:-4], refs[-4:]
     me = lax.axis_index("head")
     core = lax.axis_index("ctx") & 1
-    role = core ^ even_bits(me, head_count.bit_length() - 1)
+    role = core ^ crossing(me, lax.axis_index("ctx") >> 1, head_count.bit_length() - 1)
     groups = sems.shape[0]
     rows = out_ref.shape[0] // heads // groups
     tokens = head_count * owned
@@ -189,7 +193,7 @@
 def latent_kernel(head_count, columns, rms_ref, hat_ref, gain_ref, other_ref, *refs):
     block_refs, out_ref = refs[:-1], refs[-1]
     column = lax.axis_index("ctx") >> 1
-    crossed = even_bits(lax.axis_index("head"), head_count.bit_length() - 1)
+    crossed = crossing(lax.axis_index("head"), lax.axis_index("ctx") >> 1, head_count.bit_length() - 1)
     relative = [ref[...] for ref in block_refs]
     count = out_ref.shape[0]
     first = other_ref.shape[0] - count * columns // 2
@@ -228,8 +232,11 @@
     def ctx_swap(value, mask):
         return swap(value, lambda h, c: (h, c ^ mask))
 
-    def role_swap(value, mask):
-        return swap(value, lambda h, c: (h, c ^ mask ^ even_bits(h, bits)))
+    def to_role(value):
+        return swap(value, lambda h, c: (h, c ^ 2 ^ crossing(h, (c ^ 2) >> 1, bits)))
+
+    def to_owner(value):
+        return swap(value, lambda h, c: (h, c ^ 2 ^ crossing(h, c >> 1, bits)))
 
     def head_swap(value, mask):
         return swap(value, lambda h, c: (h ^ mask, c ^ 1 ^ even_bits(mask, bits)))
@@ -246,10 +253,10 @@
         )(*args)
 
     own = cotangent.reshape(tokens * heads, channels)
-    far = [role_swap(own, 2)]
+    far = [to_role(own)]
     other = ctx_swap(own, 1)
     if columns > 2:
-        first = jnp.where(even_bits(lax.axis_index("head"), bits) == 0, own, other)
+        first = jnp.where(crossing(lax.axis_index("head"), lax.axis_index("ctx") >> 1, bits) == 0, own, other)
         shards = [first] + far
         mask = 4
         while mask < ctx_count:
@@ -330,7 +337,7 @@
         sent = jnp.concatenate([sent] + blocks[::2], axis=0)
     both = ctx_swap(sent, 1)
     for j in range(1, columns, 2):
-        blocks[j] = role_swap(blocks[j], 2)
+        blocks[j] = to_owner(blocks[j])
 
     weight_grad = call(
         functools.partial(weight_grad_kernel, head_count, heads, owned, columns),

time: 21.5 us -> 21.5 us (level)
  transfers between devices with their start and end apart: 11 -> 11, of which waited for: 5 -> 4; matrix products, arithmetic and copies ran while one was open for 0% -> 0% of each run, Pallas kernels for 13% -> 13%
where the time goes in v14:
time: 21.5 us; the launch traced here: 21.3 us
  starting transfers between devices  11.6 us (54%)
  waiting for transfers between devices  5.21 us (24%)
  Pallas kernels  3.48 us (16%)
  between operations  0.69 us (3%)
  local copies, waits for them, and re-layouts  0.32 us (1%)
    ppermute x11, starting transfers between devices, swap(): return lax.ppermute(value, ('head', 'ctx'), pairs)  11.6 us
    ppermute x11, waiting for transfers between devices, swap(): return lax.ppermute(value, ('head', 'ctx'), pairs)  5.21 us
    pallas_call x7, Pallas kernels, call(): pl.pallas_call(kernel, out_shape=out, out_specs=jax.tree.map(lambda _: pl...  3.48 us
  transfers between devices with their start and end apart: 11, of which 4 were waited for; matrix products, arithmetic and copies ran while one was open for 0% of the time, Pallas kernels for 13%

profile of v14, /device:TPU:0, one launch (start us, length us, event | category | flops | bytes accessed | tf_op | source)
XLA Modules:
  0.0 21.3 jit_solution(589470120240187157)
XLA Ops:
  0.6 0.5 %collective-permute-start = (bf16[1024,256]{1,0:T(8,128)(2,1)}, bf16[1024,256]{1,0:T(8,128)(2,1)S(1)}, u32[]{:S(2)}, u32[]{:S(2)}) collective-permute-start(bf16[1024,256]{1,0:T(8,128)(2,1)} %bitcast.6), channel_id=1, source_target_pairs={{0,1},{1,0},{2,3},{3,2},{4,5},{5,4},{6,7},{7,6},{8,9},{9,8},{10,11... | collective-permute-start | bytes 1572872 | tf_op jit(solution)/shard_map/ppermute | solution.py:230
  1.1 0.0 copy-start.3
  1.1 0.0 copy-start.2
  1.2 2.6 %collective-permute-start.1 = (bf16[128,256]{1,0:T(8,128)(2,1)}, bf16[128,256]{1,0:T(8,128)(2,1)S(1)}, u32[]{:S(2)}, u32[]{:S(2)}) collective-permute-start(bf16[128,256]{1,0:T(8,128)(2,1)} %bitcast.8), channel_id=1, source_target_pairs={{0,3},{1,2},{2,0},{3,1},{4,6},{5,7},{6,5},{7,4},{8,10},{9,11},{10,... | collective-permute-start | bytes 196616 | tf_op jit(solution)/shard_map/ppermute | solution.py:230
  3.8 0.1 collective-permute-start.2
  3.8 0.0 copy-done.3
  3.8 0.0 copy-done.2
  3.8 0.0 copy-start
  3.8 0.1 shard_map.59
  3.9 0.6 %collective-permute-start.3 = (bf16[2,256]{1,0:T(2,128)(2,1)S(1)}, bf16[2,256]{1,0:T(2,128)(2,1)S(1)}, u32[]{:S(2)}, u32[]{:S(2)}) collective-permute-start(bf16[2,256]{1,0:T(2,128)(2,1)S(1)} %get-tuple-element.36), channel_id=1, source_target_pairs={{0,3},{1,2},{2,1},{3,0},{4,7},{5,6},{6,5},{7,4},{8,11},{9,10},{10,... | collective-permute-start | bytes 3080 | tf_op jit(solution)/shard_map/ppermute | solution.py:230
  4.6 0.0 collective-permute-done.other_ref
  4.6 0.3 %copy-done = bf16[128,8,256]{2,1,0:T(8,128)(2,1)S(1)} copy-done((bf16[128,8,256]{2,1,0:T(8,128)(2,1)S(1)}, bf16[128,8,256]{2,1,0:T(8,128)(2,1)}, u32[]{:S(2)}) %copy-start) | copy-done | bytes 524312
  4.9 0.0 copy-start.1
  4.9 0.8 %shard_map.60 = (bf16[8,256,256]{2,1,0:T(8,128)(2,1)S(1)}, bf16[256,256]{1,0:T(8,128)(2,1)S(1)}) custom-call(bf16[1024,256]{1,0:T(8,128)(2,1)S(1)} %bitcast.7, bf16[1024,256]{1,0:T(8,128)(2,1)S(1)} %collective-permute-done.other_ref), custom_call_target="tpu_custom_call" | custom-call | bytes 1048576 | tf_op jit(solution)/shard_map/pallas_call | solution.py:246
  5.6 1.0 %collective-permute-done.1.refs_0_.refs_1_ = bf16[128,256]{1,0:T(8,128)(2,1)S(1)} collective-permute-done((bf16[128,256]{1,0:T(8,128)(2,1)}, bf16[128,256]{1,0:T(8,128)(2,1)S(1)}, u32[]{:S(2)}, u32[]{:S(2)}) %collective-permute-start.1) | collective-permute-done | bytes 65568 | tf_op jit(solution)/shard_map/ppermute | solution.py:230
  6.6 0.0 collective-permute-done.2.refs_2_
  6.6 0.0 copy-done.1
  6.6 0.5 %shard_map.61 = (f32[8,256]{1,0:T(8,128)S(1)}, bf16[16,256]{1,0:T(8,128)(2,1)S(1)}, bf16[16,256]{1,0:T(8,128)(2,1)S(1)}, bf16[16,256]{1,0:T(8,128)(2,1)S(1)}) custom-call(bf16[256,256]{1,0:T(8,128)(2,1)S(1)} %get-tuple-element.32.order_ref, bf16[8,256,256]{2,1,0:T(8,128)(2,1)S(1)} %get-tuple-element.33.weight_ref, ...), custom_call_target="tpu_custom_call" | custom-call | bytes 1376256 | tf_op jit(solution)/shard_map/pallas_call | solution.py:246
  7.1 0.0 collective-permute-done.3
  7.1 1.4 %collective-permute-start.4 = (bf16[20,256]{1,0:T(8,128)(2,1)S(1)}, bf16[20,256]{1,0:T(8,128)(2,1)S(1)}, u32[]{:S(2)}, u32[]{:S(2)}) collective-permute-start(bf16[20,256]{1,0:T(8,128)(2,1)S(1)} %get-tuple-element.54), channel_id=1, source_target_pairs={{0,5},{1,4},{2,7},{3,6},{4,1},{5,0},{6,3},{7,2},{8,13},{9,12},{10,... | collective-permute-start | bytes 30728 | tf_op jit(solution)/shard_map/ppermute | solution.py:230
  8.6 1.5 %collective-permute-start.5 = (bf16[20,256]{1,0:T(8,128)(2,1)S(1)}, bf16[20,256]{1,0:T(8,128)(2,1)S(1)}, u32[]{:S(2)}, u32[]{:S(2)}) collective-permute-start(bf16[20,256]{1,0:T(8,128)(2,1)S(1)} %get-tuple-element.53), channel_id=1, source_target_pairs={{0,12},{1,13},{2,14},{3,15},{4,8},{5,9},{6,10},{7,11},{8,4},{9,5},... | collective-permute-start | bytes 30728 | tf_op jit(solution)/shard_map/ppermute | solution.py:230
  10.1 0.2 collective-permute-start.6
  10.3 0.4 %collective-permute-start.7 = (bf16[128,256]{1,0:T(8,128)(2,1)S(1)}, bf16[128,256]{1,0:T(8,128)(2,1)S(1)}, u32[]{:S(2)}, u32[]{:S(2)}) collective-permute-start(bf16[128,256]{1,0:T(8,128)(2,1)S(1)} %collective-permute-done.1.refs_0_.refs_1_), channel_id=1, source_target_pairs={{0,1},{1,0},{2,3},{3,2},{4,5},{5,4},{6,7},{7,6},{8,9},{9,8},{10,11... | collective-permute-start | bytes 196616 | tf_op jit(solution)/shard_map/ppermute | solution.py:230
  10.7 0.0 collective-permute-done.4.refs_0_
  10.7 2.4 %collective-permute-done.5.refs_1_ = bf16[20,256]{1,0:T(8,128)(2,1)S(1)} collective-permute-done((bf16[20,256]{1,0:T(8,128)(2,1)S(1)}, bf16[20,256]{1,0:T(8,128)(2,1)S(1)}, u32[]{:S(2)}, u32[]{:S(2)}) %collective-permute-start.5) | collective-permute-done | bytes 10272 | tf_op jit(solution)/shard_map/ppermute | solution.py:230
  13.1 0.1 collective-permute-done.6.refs_2_
  13.3 0.0 collective-permute-done.7.refs_3_
  13.3 2.4 %collective-permute-start.8 = (bf16[24,256]{1,0:T(8,128)(2,1)S(1)}, bf16[24,256]{1,0:T(8,128)(2,1)S(1)}, u32[]{:S(2)}, u32[]{:S(2)}) collective-permute-start(bf16[24,256]{1,0:T(8,128)(2,1)S(1)} %get-tuple-element.43.normed_ref), channel_id=1, source_target_pairs={{0,17},{1,16},{2,19},{3,18},{4,21},{5,20},{6,23},{7,22},{8,25},{9,... | collective-permute-start | bytes 36872 | tf_op jit(solution)/shard_map/ppermute | solution.py:230
  15.7 1.7 %collective-permute-done.8.refs_0_ = bf16[24,256]{1,0:T(8,128)(2,1)S(1)} collective-permute-done((bf16[24,256]{1,0:T(8,128)(2,1)S(1)}, bf16[24,256]{1,0:T(8,128)(2,1)S(1)}, u32[]{:S(2)}, u32[]{:S(2)}) %collective-permute-start.8) | collective-permute-done | bytes 12320 | tf_op jit(solution)/shard_map/ppermute | solution.py:230
  17.4 0.2 collective-permute-start.9
  17.6 1.6 %collective-permute-start.10 = (f32[2,256]{1,0:T(2,128)S(1)}, f32[2,256]{1,0:T(2,128)S(1)}, u32[]{:S(2)}, u32[]{:S(2)}) collective-permute-start(f32[2,256]{1,0:T(2,128)S(1)} %get-tuple-element.48), channel_id=1, source_target_pairs={{0,2},{1,3},{2,1},{3,0},{4,7},{5,6},{6,4},{7,5},{8,11},{9,10},{10,... | collective-permute-start | bytes 6152 | tf_op jit(solution)/shard_map/ppermute | solution.py:230
  19.1 0.0 collective-permute-done.9.other_ref
  19.1 1.4 %shard_map.64 = f32[1024,256]{1,0:T(8,128)} custom-call(f32[32,128]{1,0:T(8,128)S(1)} %get-tuple-element.45.own_ref, f32[18,256]{1,0:T(8,128)S(1)} %collective-permute-done.9.other_ref, bf16[128,256]{1,0:T(8,128)(2,1)S(1)} %bitcast.11, bf16[128,256]{1,0:T(8,128)(2,1)S(1)} %collective-permute-done.1.refs_0_.refs_1_, ...), custom_call_target="tpu_custom_call" | custom-call | flops 268435456 | bytes 296960 | tf_op jit(solution)/shard_map/pallas_call | solution.py:246
  20.6 0.0 collective-permute-done.10.refs_1_
  20.6 0.7 %shard_map.65 = f32[2,512]{1,0:T(2,128)} custom-call(f32[2,512]{1,0:T(2,128)S(1)} %get-tuple-element.27.rms_ref, f32[2,512]{1,0:T(2,128)S(1)} %get-tuple-element.28.hat_ref, f32[1,512]{1,0:T(1,128)S(1)} %bitcast.13, f32[18,256]{1,0:T(8,128)S(1)} %collective-permute-done.9.other_ref, f32[2,256]{1,0:T(2,128)S(1)} %get-tuple-element.49.refs_0_, ...), custom_call_target="tpu_custom_call" | custom-call | bytes 32768 | tf_op jit(solution)/shard_map/pallas_call | solution.py:246
  (4 shorter events, 0.0 us)
Async XLA Ops:
  0.6 3.9 %collective-permute-start = (bf16[1024,256]{1,0:T(8,128)(2,1)}, bf16[1024,256]{1,0:T(8,128)(2,1)S(1)}, u32[]{:S(2)}, u32[]{:S(2)}) collective-permute-start(bf16[1024,256]{1,0:T(8,128)(2,1)} %bitcast.6), channel_id=1, source_target_pairs={{0,1},{1,0},{2,3},{3,2},{4,5},{5,4},{6,7},{7,6},{8,9},{9,8},{10,11... | collective-permute-start | bytes 1572872 | tf_op jit(solution)/shard_map/ppermute | solution.py:230
  1.1 2.7 %copy-start.3 = (bf16[1,2,512]{2,1,0:T(2,128)(2,1)S(1)}, bf16[1,2,512]{2,1,0:T(2,128)(2,1)}, u32[]{:S(2)}) copy-start(bf16[1,2,512]{2,1,0:T(2,128)(2,1)} %param.4) | copy-start | bytes 6148
  1.1 2.7 %copy-start.2 = (f32[512]{0:T(512)S(1)}, f32[512]{0:T(512)}, u32[]{:S(2)}) copy-start(f32[512]{0:T(512)} %param.5) | copy-start | bytes 6148
  1.2 5.5 %collective-permute-start.1 = (bf16[128,256]{1,0:T(8,128)(2,1)}, bf16[128,256]{1,0:T(8,128)(2,1)S(1)}, u32[]{:S(2)}, u32[]{:S(2)}) collective-permute-start(bf16[128,256]{1,0:T(8,128)(2,1)} %bitcast.8), channel_id=1, source_target_pairs={{0,3},{1,2},{2,0},{3,1},{4,6},{5,7},{6,5},{7,4},{8,10},{9,11},{10,... | collective-permute-start | bytes 196616 | tf_op jit(solution)/shard_map/ppermute | solution.py:230
  3.8 2.8 %collective-permute-start.2 = (bf16[128,256]{1,0:T(8,128)(2,1)}, bf16[128,256]{1,0:T(8,128)(2,1)S(1)}, u32[]{:S(2)}, u32[]{:S(2)}) collective-permute-start(bf16[128,256]{1,0:T(8,128)(2,1)} %bitcast.9), channel_id=1, source_target_pairs={{0,1},{1,0},{2,3},{3,2},{4,5},{5,4},{6,7},{7,6},{8,9},{9,8},{10,11... | collective-permute-start | bytes 196616 | tf_op jit(solution)/shard_map/ppermute | solution.py:230
  3.8 1.0 %copy-start = (bf16[128,8,256]{2,1,0:T(8,128)(2,1)S(1)}, bf16[128,8,256]{2,1,0:T(8,128)(2,1)}, u32[]{:S(2)}) copy-start(bf16[128,8,256]{2,1,0:T(8,128)(2,1)} %param.7) | copy-start | bytes 1572868
  3.9 3.1 %collective-permute-start.3 = (bf16[2,256]{1,0:T(2,128)(2,1)S(1)}, bf16[2,256]{1,0:T(2,128)(2,1)S(1)}, u32[]{:S(2)}, u32[]{:S(2)}) collective-permute-start(bf16[2,256]{1,0:T(2,128)(2,1)S(1)} %get-tuple-element.36), channel_id=1, source_target_pairs={{0,3},{1,2},{2,1},{3,0},{4,7},{5,6},{6,5},{7,4},{8,11},{9,10},{10,... | collective-permute-start | bytes 3080 | tf_op jit(solution)/shard_map/ppermute | solution.py:230
  4.9 1.7 %copy-start.1 = (bf16[1,16,8,256]{3,2,1,0:T(8,128)(2,1)S(1)}, bf16[1,16,8,256]{3,2,1,0:T(8,128)(2,1)}, u32[]{:S(2)}) copy-start(bf16[1,16,8,256]{3,2,1,0:T(8,128)(2,1)} %param.6) | copy-start | bytes 196612
  7.1 3.6 %collective-permute-start.4 = (bf16[20,256]{1,0:T(8,128)(2,1)S(1)}, bf16[20,256]{1,0:T(8,128)(2,1)S(1)}, u32[]{:S(2)}, u32[]{:S(2)}) collective-permute-start(bf16[20,256]{1,0:T(8,128)(2,1)S(1)} %get-tuple-element.54), channel_id=1, source_target_pairs={{0,5},{1,4},{2,7},{3,6},{4,1},{5,0},{6,3},{7,2},{8,13},{9,12},{10,... | collective-permute-start | bytes 30728 | tf_op jit(solution)/shard_map/ppermute | solution.py:230
  8.6 4.6 %collective-permute-start.5 = (bf16[20,256]{1,0:T(8,128)(2,1)S(1)}, bf16[20,256]{1,0:T(8,128)(2,1)S(1)}, u32[]{:S(2)}, u32[]{:S(2)}) collective-permute-start(bf16[20,256]{1,0:T(8,128)(2,1)S(1)} %get-tuple-element.53), channel_id=1, source_target_pairs={{0,12},{1,13},{2,14},{3,15},{4,8},{5,9},{6,10},{7,11},{8,4},{9,5},... | collective-permute-start | bytes 30728 | tf_op jit(solution)/shard_map/ppermute | solution.py:230
  10.1 3.2 %collective-permute-start.6 = (bf16[20,256]{1,0:T(8,128)(2,1)S(1)}, bf16[20,256]{1,0:T(8,128)(2,1)S(1)}, u32[]{:S(2)}, u32[]{:S(2)}) collective-permute-start(bf16[20,256]{1,0:T(8,128)(2,1)S(1)} %get-tuple-element.52), channel_id=1, source_target_pairs={{0,9},{1,8},{2,11},{3,10},{4,13},{5,12},{6,15},{7,14},{8,1},{9,0},... | collective-permute-start | bytes 30728 | tf_op jit(solution)/shard_map/ppermute | solution.py:230
  10.3 3.0 %collective-permute-start.7 = (bf16[128,256]{1,0:T(8,128)(2,1)S(1)}, bf16[128,256]{1,0:T(8,128)(2,1)S(1)}, u32[]{:S(2)}, u32[]{:S(2)}) collective-permute-start(bf16[128,256]{1,0:T(8,128)(2,1)S(1)} %collective-permute-done.1.refs_0_.refs_1_), channel_id=1, source_target_pairs={{0,1},{1,0},{2,3},{3,2},{4,5},{5,4},{6,7},{7,6},{8,9},{9,8},{10,11... | collective-permute-start | bytes 196616 | tf_op jit(solution)/shard_map/ppermute | solution.py:230
  13.3 4.1 %collective-permute-start.8 = (bf16[24,256]{1,0:T(8,128)(2,1)S(1)}, bf16[24,256]{1,0:T(8,128)(2,1)S(1)}, u32[]{:S(2)}, u32[]{:S(2)}) collective-permute-start(bf16[24,256]{1,0:T(8,128)(2,1)S(1)} %get-tuple-element.43.normed_ref), channel_id=1, source_target_pairs={{0,17},{1,16},{2,19},{3,18},{4,21},{5,20},{6,23},{7,22},{8,25},{9,... | collective-permute-start | bytes 36872 | tf_op jit(solution)/shard_map/ppermute | solution.py:230
  17.4 1.7 %collective-permute-start.9 = (f32[18,256]{1,0:T(8,128)S(1)}, f32[18,256]{1,0:T(8,128)S(1)}, u32[]{:S(2)}, u32[]{:S(2)}) collective-permute-start(f32[18,256]{1,0:T(8,128)S(1)} %get-tuple-element.44), channel_id=1, source_target_pairs={{0,1},{1,0},{2,3},{3,2},{4,5},{5,4},{6,7},{7,6},{8,9},{9,8},{10,11... | collective-permute-start | bytes 55304 | tf_op jit(solution)/shard_map/ppermute | solution.py:230
  17.6 3.0 %collective-permute-start.10 = (f32[2,256]{1,0:T(2,128)S(1)}, f32[2,256]{1,0:T(2,128)S(1)}, u32[]{:S(2)}, u32[]{:S(2)}) collective-permute-start(f32[2,256]{1,0:T(2,128)S(1)} %get-tuple-element.48), channel_id=1, source_target_pairs={{0,2},{1,3},{2,1},{3,0},{4,7},{5,6},{6,4},{7,5},{8,11},{9,10},{10,... | collective-permute-start | bytes 6152 | tf_op jit(solution)/shard_map/ppermute | solution.py:230

commit v15 on v14

--- a/solution.py
+++ b/solution.py
@@ -58,7 +58,7 @@
     return even_bits(head, bits) ^ (column & 1) ^ 1
 
 
-def weight_kernel(head_count, heads, owned, shards, own_ref, other_ref, out_ref, order_ref):
+def weight_kernel(head_count, heads, owned, shards, own_ref, other_ref, out_ref, order_ref, place_ref):
     rows = own_ref.shape[0] // heads
     group = min(rows, max(256 // heads, 1))
     size = group * heads
@@ -81,6 +81,18 @@
     position = rest(whole(to, owned * shards), head_count)
     token = (reverse_bits(position, bits) ^ me) * owned + i
     order_ref[...] = one_hot(at == (j * tokens + token) * heads + whole(to, tokens * shards))
+    core = lax.axis_index("ctx") & 1
+    role = core ^ crossing(me, lax.axis_index("ctx") >> 1, bits)
+    size = place_ref.shape[2]
+    at, to = iota(place_ref.shape[1:], 0), iota((1, size), 1)
+    token, j = rest(whole(to, heads), tokens), whole(to, heads * tokens)
+    distance = whole(token, owned) ^ me
+    slot = distance ^ ((distance >> 1) & 1) if head_count >= 4 else distance
+    turned = 1 ^ even_bits(distance, bits) ^ (j & 1)
+    for side in range(2):
+        held = jnp.where(j == 0, core, role) ^ side ^ core ^ turned
+        place = ((held * head_count + slot) * shards + j) * owned + rest(token, owned)
+        place_ref[side] = one_hot(at == place)
 
 
 def partial_kernel(head_count, count, order_ref, weight_ref, *refs):
@@ -150,28 +162,17 @@
         ref[...] = block
 
 
-def weight_grad_kernel(head_count, heads, owned, columns, own_ref, other_ref, *refs):
+def weight_grad_kernel(heads, columns, place_ref, own_ref, other_ref, *refs):
     shard_refs, (out_ref, spread_ref, total_ref, sems) = refs[:-4], refs[-4:]
-    me = lax.axis_index("head")
-    core = lax.axis_index("ctx") & 1
-    role = core ^ crossing(me, lax.axis_index("ctx") >> 1, head_count.bit_length() - 1)
     groups = sems.shape[0]
     rows = out_ref.shape[0] // heads // groups
-    tokens = head_count * owned
     count, width = own_ref.shape[0] // 2, own_ref.shape[1]
     other = other_ref[...]
     normed = jnp.concatenate([own_ref[...], other[:count, :width], other[:count, width:]], axis=0).astype(BF16)
-    size = columns * tokens * heads
-    at, to = iota((normed.shape[0], size), 0), iota((1, size), 1)
-    token, j = rest(whole(to, heads), tokens), whole(to, heads * tokens)
-    distance = whole(token, owned) ^ me
-    slot = distance ^ ((distance >> 1) & 1) if head_count >= 4 else distance
-    turned = 1 ^ even_bits(distance, head_count.bit_length() - 1) ^ (j & 1)
+    size = place_ref.shape[2]
     cots = []
     for side in range(2):
-        held = jnp.where(j == 0, core, role) ^ side ^ core ^ turned
-        place = ((held * head_count + slot) * columns + j) * owned + rest(token, owned)
-        spread_ref[side] = matmul(normed, one_hot(at == place), 0, 0)
+        spread_ref[side] = matmul(normed, place_ref[side], 0, 0)
         cots.append(jnp.concatenate([r[...] for r in shard_refs[side * columns : (side + 1) * columns]], axis=0))
     keep = rest(iota((1, heads, size), 2), heads) == iota((1, heads, size), 1)
     copies = []
@@ -274,9 +275,13 @@
     weight_other = ctx_swap(weight_flat, 1)
     weight_flat, weight_other, _ = lax.optimization_barrier((weight_flat, weight_other, normed[0]))
     size = columns * tokens * heads
-    chip_weight, order = call(
+    chip_weight, order, place = call(
         functools.partial(weight_kernel, head_count, heads, owned, columns),
-        [jax.ShapeDtypeStruct((heads, channels, 2 * rows), BF16), jax.ShapeDtypeStruct((size, size), BF16)],
+        [
+            jax.ShapeDtypeStruct((heads, channels, 2 * rows), BF16),
+            jax.ShapeDtypeStruct((size, size), BF16),
+            jax.ShapeDtypeStruct((2, ctx_count * tokens, size), BF16),
+        ],
         weight_flat,
         weight_other,
     )
@@ -340,8 +345,9 @@
         blocks[j] = to_owner(blocks[j])
 
     weight_grad = call(
-        functools.partial(weight_grad_kernel, head_count, heads, owned, columns),
+        functools.partial(weight_grad_kernel, heads, columns),
         jax.ShapeDtypeStruct((rows * heads, channels), F32),
+        place,
         normed_own,
         both,
         own,

time: 21.5 us -> 21.5 us (level)
  no operation moved by 1% of the time
where the time goes in v15:
time: 21.5 us; the launch traced here: 21.3 us
  starting transfers between devices  11.6 us (54%)
  waiting for transfers between devices  5.2 us (24%)
  Pallas kernels  3.5 us (16%)
  between operations  0.69 us (3%)
  local copies, waits for them, and re-layouts  0.32 us (1%)
    ppermute x11, starting transfers between devices, swap(): return lax.ppermute(value, ('head', 'ctx'), pairs)  11.6 us
    ppermute x11, waiting for transfers between devices, swap(): return lax.ppermute(value, ('head', 'ctx'), pairs)  5.2 us
    pallas_call x7, Pallas kernels, call(): pl.pallas_call(kernel, out_shape=out, out_specs=jax.tree.map(lambda _: pl...  3.5 us
  transfers between devices with their start and end apart: 11, of which 4 were waited for; matrix products, arithmetic and copies ran while one was open for 0% of the time, Pallas kernels for 13%

profile of v15, /device:TPU:0, one launch (start us, length us, event | category | flops | bytes accessed | tf_op | source)
XLA Modules:
  0.0 21.3 jit_solution(1280932453504992617)
XLA Ops:
  0.6 0.5 %collective-permute-start = (bf16[1024,256]{1,0:T(8,128)(2,1)}, bf16[1024,256]{1,0:T(8,128)(2,1)S(1)}, u32[]{:S(2)}, u32[]{:S(2)}) collective-permute-start(bf16[1024,256]{1,0:T(8,128)(2,1)} %bitcast.6), channel_id=1, source_target_pairs={{0,1},{1,0},{2,3},{3,2},{4,5},{5,4},{6,7},{7,6},{8,9},{9,8},{10,11... | collective-permute-start | bytes 1572872 | tf_op jit(solution)/shard_map/ppermute | solution.py:231
  1.1 0.0 copy-start.3
  1.1 0.0 copy-start.2
  1.2 2.6 %collective-permute-start.1 = (bf16[128,256]{1,0:T(8,128)(2,1)}, bf16[128,256]{1,0:T(8,128)(2,1)S(1)}, u32[]{:S(2)}, u32[]{:S(2)}) collective-permute-start(bf16[128,256]{1,0:T(8,128)(2,1)} %bitcast.8), channel_id=1, source_target_pairs={{0,3},{1,2},{2,0},{3,1},{4,6},{5,7},{6,5},{7,4},{8,10},{9,11},{10,... | collective-permute-start | bytes 196616 | tf_op jit(solution)/shard_map/ppermute | solution.py:231
  3.8 0.1 collective-permute-start.2
  3.8 0.0 copy-done.3
  3.8 0.0 copy-done.2
  3.8 0.0 copy-start
  3.8 0.1 shard_map.59
  3.9 0.6 %collective-permute-start.3 = (bf16[2,256]{1,0:T(2,128)(2,1)S(1)}, bf16[2,256]{1,0:T(2,128)(2,1)S(1)}, u32[]{:S(2)}, u32[]{:S(2)}) collective-permute-start(bf16[2,256]{1,0:T(2,128)(2,1)S(1)} %get-tuple-element.37), channel_id=1, source_target_pairs={{0,3},{1,2},{2,1},{3,0},{4,7},{5,6},{6,5},{7,4},{8,11},{9,10},{10,... | collective-permute-start | bytes 3080 | tf_op jit(solution)/shard_map/ppermute | solution.py:231
  4.6 0.0 collective-permute-done.other_ref
  4.6 0.3 %copy-done = bf16[128,8,256]{2,1,0:T(8,128)(2,1)S(1)} copy-done((bf16[128,8,256]{2,1,0:T(8,128)(2,1)S(1)}, bf16[128,8,256]{2,1,0:T(8,128)(2,1)}, u32[]{:S(2)}) %copy-start) | copy-done | bytes 524312
  4.9 0.0 copy-start.1
  4.9 0.8 %shard_map.60 = (bf16[8,256,256]{2,1,0:T(8,128)(2,1)S(1)}, bf16[256,256]{1,0:T(8,128)(2,1)S(1)}, bf16[2,64,256]{2,1,0:T(8,128)(2,1)S(1)}) custom-call(bf16[1024,256]{1,0:T(8,128)(2,1)S(1)} %bitcast.7, bf16[1024,256]{1,0:T(8,128)(2,1)S(1)} %collective-permute-done.other_ref), custom_call_target="tpu_custom_call" | custom-call | bytes 1048576 | tf_op jit(solution)/shard_map/pallas_call | solution.py:247
  5.7 1.0 %collective-permute-done.1.refs_0_.refs_1_ = bf16[128,256]{1,0:T(8,128)(2,1)S(1)} collective-permute-done((bf16[128,256]{1,0:T(8,128)(2,1)}, bf16[128,256]{1,0:T(8,128)(2,1)S(1)}, u32[]{:S(2)}, u32[]{:S(2)}) %collective-permute-start.1) | collective-permute-done | bytes 65568 | tf_op jit(solution)/shard_map/ppermute | solution.py:231
  6.6 0.0 collective-permute-done.2.refs_2_
  6.6 0.0 copy-done.1
  6.6 0.4 %shard_map.61 = (f32[8,256]{1,0:T(8,128)S(1)}, bf16[16,256]{1,0:T(8,128)(2,1)S(1)}, bf16[16,256]{1,0:T(8,128)(2,1)S(1)}, bf16[16,256]{1,0:T(8,128)(2,1)S(1)}) custom-call(bf16[256,256]{1,0:T(8,128)(2,1)S(1)} %get-tuple-element.33.order_ref, bf16[8,256,256]{2,1,0:T(8,128)(2,1)S(1)} %get-tuple-element.34.weight_ref, ...), custom_call_target="tpu_custom_call" | custom-call | bytes 1376256 | tf_op jit(solution)/shard_map/pallas_call | solution.py:247
  7.1 0.0 collective-permute-done.3
  7.1 1.4 %collective-permute-start.4 = (bf16[20,256]{1,0:T(8,128)(2,1)S(1)}, bf16[20,256]{1,0:T(8,128)(2,1)S(1)}, u32[]{:S(2)}, u32[]{:S(2)}) collective-permute-start(bf16[20,256]{1,0:T(8,128)(2,1)S(1)} %get-tuple-element.56), channel_id=1, source_target_pairs={{0,5},{1,4},{2,7},{3,6},{4,1},{5,0},{6,3},{7,2},{8,13},{9,12},{10,... | collective-permute-start | bytes 30728 | tf_op jit(solution)/shard_map/ppermute | solution.py:231
  8.6 1.5 %collective-permute-start.5 = (bf16[20,256]{1,0:T(8,128)(2,1)S(1)}, bf16[20,256]{1,0:T(8,128)(2,1)S(1)}, u32[]{:S(2)}, u32[]{:S(2)}) collective-permute-start(bf16[20,256]{1,0:T(8,128)(2,1)S(1)} %get-tuple-element.55), channel_id=1, source_target_pairs={{0,12},{1,13},{2,14},{3,15},{4,8},{5,9},{6,10},{7,11},{8,4},{9,5},... | collective-permute-start | bytes 30728 | tf_op jit(solution)/shard_map/ppermute | solution.py:231
  10.1 0.2 collective-permute-start.6
  10.3 0.4 %collective-permute-start.7 = (bf16[128,256]{1,0:T(8,128)(2,1)S(1)}, bf16[128,256]{1,0:T(8,128)(2,1)S(1)}, u32[]{:S(2)}, u32[]{:S(2)}) collective-permute-start(bf16[128,256]{1,0:T(8,128)(2,1)S(1)} %collective-permute-done.1.refs_0_.refs_1_), channel_id=1, source_target_pairs={{0,1},{1,0},{2,3},{3,2},{4,5},{5,4},{6,7},{7,6},{8,9},{9,8},{10,11... | collective-permute-start | bytes 196616 | tf_op jit(solution)/shard_map/ppermute | solution.py:231
  10.7 0.0 collective-permute-done.4.refs_0_
  10.7 2.4 %collective-permute-done.5.refs_1_ = bf16[20,256]{1,0:T(8,128)(2,1)S(1)} collective-permute-done((bf16[20,256]{1,0:T(8,128)(2,1)S(1)}, bf16[20,256]{1,0:T(8,128)(2,1)S(1)}, u32[]{:S(2)}, u32[]{:S(2)}) %collective-permute-start.5) | collective-permute-done | bytes 10272 | tf_op jit(solution)/shard_map/ppermute | solution.py:231
  13.1 0.1 collective-permute-done.6.refs_2_
  13.3 0.0 collective-permute-done.7.refs_3_
  13.3 2.4 %collective-permute-start.8 = (bf16[24,256]{1,0:T(8,128)(2,1)S(1)}, bf16[24,256]{1,0:T(8,128)(2,1)S(1)}, u32[]{:S(2)}, u32[]{:S(2)}) collective-permute-start(bf16[24,256]{1,0:T(8,128)(2,1)S(1)} %get-tuple-element.44.normed_ref), channel_id=1, source_target_pairs={{0,17},{1,16},{2,19},{3,18},{4,21},{5,20},{6,23},{7,22},{8,25},{9,... | collective-permute-start | bytes 36872 | tf_op jit(solution)/shard_map/ppermute | solution.py:231
  15.7 1.7 %collective-permute-done.8.refs_0_ = bf16[24,256]{1,0:T(8,128)(2,1)S(1)} collective-permute-done((bf16[24,256]{1,0:T(8,128)(2,1)S(1)}, bf16[24,256]{1,0:T(8,128)(2,1)S(1)}, u32[]{:S(2)}, u32[]{:S(2)}) %collective-permute-start.8) | collective-permute-done | bytes 12320 | tf_op jit(solution)/shard_map/ppermute | solution.py:231
  17.4 0.2 collective-permute-start.9
  17.6 1.6 %collective-permute-start.10 = (f32[2,256]{1,0:T(2,128)S(1)}, f32[2,256]{1,0:T(2,128)S(1)}, u32[]{:S(2)}, u32[]{:S(2)}) collective-permute-start(f32[2,256]{1,0:T(2,128)S(1)} %get-tuple-element.50), channel_id=1, source_target_pairs={{0,2},{1,3},{2,1},{3,0},{4,7},{5,6},{6,4},{7,5},{8,11},{9,10},{10,... | collective-permute-start | bytes 6152 | tf_op jit(solution)/shard_map/ppermute | solution.py:231
  19.1 0.0 collective-permute-done.9.other_ref
  19.1 1.5 %shard_map.64 = f32[1024,256]{1,0:T(8,128)} custom-call(bf16[2,64,256]{2,1,0:T(8,128)(2,1)S(1)} %get-tuple-element.46.place_ref, f32[32,128]{1,0:T(8,128)S(1)} %get-tuple-element.47.own_ref, f32[18,256]{1,0:T(8,128)S(1)} %collective-permute-done.9.other_ref, bf16[128,256]{1,0:T(8,128)(2,1)S(1)} %bitcast.11, ...), custom_call_target="tpu_custom_call" | custom-call | flops 268435456 | bytes 362496 | tf_op jit(solution)/shard_map/pallas_call | solution.py:247
  20.6 0.0 collective-permute-done.10.refs_1_
  20.6 0.7 %shard_map.65 = f32[2,512]{1,0:T(2,128)} custom-call(f32[2,512]{1,0:T(2,128)S(1)} %get-tuple-element.28.rms_ref, f32[2,512]{1,0:T(2,128)S(1)} %get-tuple-element.29.hat_ref, f32[1,512]{1,0:T(1,128)S(1)} %bitcast.13, f32[18,256]{1,0:T(8,128)S(1)} %collective-permute-done.9.other_ref, f32[2,256]{1,0:T(2,128)S(1)} %get-tuple-element.51.refs_0_, ...), custom_call_target="tpu_custom_call" | custom-call | bytes 32768 | tf_op jit(solution)/shard_map/pallas_call | solution.py:247
  (4 shorter events, 0.0 us)
Async XLA Ops:
  0.6 3.9 %collective-permute-start = (bf16[1024,256]{1,0:T(8,128)(2,1)}, bf16[1024,256]{1,0:T(8,128)(2,1)S(1)}, u32[]{:S(2)}, u32[]{:S(2)}) collective-permute-start(bf16[1024,256]{1,0:T(8,128)(2,1)} %bitcast.6), channel_id=1, source_target_pairs={{0,1},{1,0},{2,3},{3,2},{4,5},{5,4},{6,7},{7,6},{8,9},{9,8},{10,11... | collective-permute-start | bytes 1572872 | tf_op jit(solution)/shard_map/ppermute | solution.py:231
  1.1 2.7 %copy-start.3 = (bf16[1,2,512]{2,1,0:T(2,128)(2,1)S(1)}, bf16[1,2,512]{2,1,0:T(2,128)(2,1)}, u32[]{:S(2)}) copy-start(bf16[1,2,512]{2,1,0:T(2,128)(2,1)} %param.4) | copy-start | bytes 6148
  1.1 2.7 %copy-start.2 = (f32[512]{0:T(512)S(1)}, f32[512]{0:T(512)}, u32[]{:S(2)}) copy-start(f32[512]{0:T(512)} %param.5) | copy-start | bytes 6148
  1.2 5.5 %collective-permute-start.1 = (bf16[128,256]{1,0:T(8,128)(2,1)}, bf16[128,256]{1,0:T(8,128)(2,1)S(1)}, u32[]{:S(2)}, u32[]{:S(2)}) collective-permute-start(bf16[128,256]{1,0:T(8,128)(2,1)} %bitcast.8), channel_id=1, source_target_pairs={{0,3},{1,2},{2,0},{3,1},{4,6},{5,7},{6,5},{7,4},{8,10},{9,11},{10,... | collective-permute-start | bytes 196616 | tf_op jit(solution)/shard_map/ppermute | solution.py:231
  3.8 2.8 %collective-permute-start.2 = (bf16[128,256]{1,0:T(8,128)(2,1)}, bf16[128,256]{1,0:T(8,128)(2,1)S(1)}, u32[]{:S(2)}, u32[]{:S(2)}) collective-permute-start(bf16[128,256]{1,0:T(8,128)(2,1)} %bitcast.9), channel_id=1, source_target_pairs={{0,1},{1,0},{2,3},{3,2},{4,5},{5,4},{6,7},{7,6},{8,9},{9,8},{10,11... | collective-permute-start | bytes 196616 | tf_op jit(solution)/shard_map/ppermute | solution.py:231
  3.8 1.0 %copy-start = (bf16[128,8,256]{2,1,0:T(8,128)(2,1)S(1)}, bf16[128,8,256]{2,1,0:T(8,128)(2,1)}, u32[]{:S(2)}) copy-start(bf16[128,8,256]{2,1,0:T(8,128)(2,1)} %param.7) | copy-start | bytes 1572868
  3.9 3.1 %collective-permute-start.3 = (bf16[2,256]{1,0:T(2,128)(2,1)S(1)}, bf16[2,256]{1,0:T(2,128)(2,1)S(1)}, u32[]{:S(2)}, u32[]{:S(2)}) collective-permute-start(bf16[2,256]{1,0:T(2,128)(2,1)S(1)} %get-tuple-element.37), channel_id=1, source_target_pairs={{0,3},{1,2},{2,1},{3,0},{4,7},{5,6},{6,5},{7,4},{8,11},{9,10},{10,... | collective-permute-start | bytes 3080 | tf_op jit(solution)/shard_map/ppermute | solution.py:231
  4.9 1.7 %copy-start.1 = (bf16[1,16,8,256]{3,2,1,0:T(8,128)(2,1)S(1)}, bf16[1,16,8,256]{3,2,1,0:T(8,128)(2,1)}, u32[]{:S(2)}) copy-start(bf16[1,16,8,256]{3,2,1,0:T(8,128)(2,1)} %param.6) | copy-start | bytes 196612
  7.1 3.6 %collective-permute-start.4 = (bf16[20,256]{1,0:T(8,128)(2,1)S(1)}, bf16[20,256]{1,0:T(8,128)(2,1)S(1)}, u32[]{:S(2)}, u32[]{:S(2)}) collective-permute-start(bf16[20,256]{1,0:T(8,128)(2,1)S(1)} %get-tuple-element.56), channel_id=1, source_target_pairs={{0,5},{1,4},{2,7},{3,6},{4,1},{5,0},{6,3},{7,2},{8,13},{9,12},{10,... | collective-permute-start | bytes 30728 | tf_op jit(solution)/shard_map/ppermute | solution.py:231
  8.6 4.6 %collective-permute-start.5 = (bf16[20,256]{1,0:T(8,128)(2,1)S(1)}, bf16[20,256]{1,0:T(8,128)(2,1)S(1)}, u32[]{:S(2)}, u32[]{:S(2)}) collective-permute-start(bf16[20,256]{1,0:T(8,128)(2,1)S(1)} %get-tuple-element.55), channel_id=1, source_target_pairs={{0,12},{1,13},{2,14},{3,15},{4,8},{5,9},{6,10},{7,11},{8,4},{9,5},... | collective-permute-start | bytes 30728 | tf_op jit(solution)/shard_map/ppermute | solution.py:231
  10.1 3.2 %collective-permute-start.6 = (bf16[20,256]{1,0:T(8,128)(2,1)S(1)}, bf16[20,256]{1,0:T(8,128)(2,1)S(1)}, u32[]{:S(2)}, u32[]{:S(2)}) collective-permute-start(bf16[20,256]{1,0:T(8,128)(2,1)S(1)} %get-tuple-element.54), channel_id=1, source_target_pairs={{0,9},{1,8},{2,11},{3,10},{4,13},{5,12},{6,15},{7,14},{8,1},{9,0},... | collective-permute-start | bytes 30728 | tf_op jit(solution)/shard_map/ppermute | solution.py:231
  10.3 3.0 %collective-permute-start.7 = (bf16[128,256]{1,0:T(8,128)(2,1)S(1)}, bf16[128,256]{1,0:T(8,128)(2,1)S(1)}, u32[]{:S(2)}, u32[]{:S(2)}) collective-permute-start(bf16[128,256]{1,0:T(8,128)(2,1)S(1)} %collective-permute-done.1.refs_0_.refs_1_), channel_id=1, source_target_pairs={{0,1},{1,0},{2,3},{3,2},{4,5},{5,4},{6,7},{7,6},{8,9},{9,8},{10,11... | collective-permute-start | bytes 196616 | tf_op jit(solution)/shard_map/ppermute | solution.py:231
  13.3 4.1 %collective-permute-start.8 = (bf16[24,256]{1,0:T(8,128)(2,1)S(1)}, bf16[24,256]{1,0:T(8,128)(2,1)S(1)}, u32[]{:S(2)}, u32[]{:S(2)}) collective-permute-start(bf16[24,256]{1,0:T(8,128)(2,1)S(1)} %get-tuple-element.44.normed_ref), channel_id=1, source_target_pairs={{0,17},{1,16},{2,19},{3,18},{4,21},{5,20},{6,23},{7,22},{8,25},{9,... | collective-permute-start | bytes 36872 | tf_op jit(solution)/shard_map/ppermute | solution.py:231
  17.4 1.7 %collective-permute-start.9 = (f32[18,256]{1,0:T(8,128)S(1)}, f32[18,256]{1,0:T(8,128)S(1)}, u32[]{:S(2)}, u32[]{:S(2)}) collective-permute-start(f32[18,256]{1,0:T(8,128)S(1)} %get-tuple-element.45), channel_id=1, source_target_pairs={{0,1},{1,0},{2,3},{3,2},{4,5},{5,4},{6,7},{7,6},{8,9},{9,8},{10,11... | collective-permute-start | bytes 55304 | tf_op jit(solution)/shard_map/ppermute | solution.py:231
  17.6 3.0 %collective-permute-start.10 = (f32[2,256]{1,0:T(2,128)S(1)}, f32[2,256]{1,0:T(2,128)S(1)}, u32[]{:S(2)}, u32[]{:S(2)}) collective-permute-start(f32[2,256]{1,0:T(2,128)S(1)} %get-tuple-element.50), channel_id=1, source_target_pairs={{0,2},{1,3},{2,1},{3,0},{4,7},{5,6},{6,4},{7,5},{8,11},{9,10},{10,... | collective-permute-start | bytes 6152 | tf_op jit(solution)/shard_map/ppermute | solution.py:231

commit v16 on v14

--- a/solution.py
+++ b/solution.py
@@ -174,14 +174,14 @@
         spread_ref[side] = matmul(normed, one_hot(at == place), 0, 0)
         cots.append(jnp.concatenate([r[...] for r in shard_refs[side * columns : (side + 1) * columns]], axis=0))
     keep = rest(iota((1, heads, size), 2), heads) == iota((1, heads, size), 1)
+    both_cots = jnp.concatenate(cots, axis=0)
     copies = []
     for g in range(groups):
-        total = None
+        lefts = []
         for side in range(2):
             block = spread_ref[side, g * rows : (g + 1) * rows, :]
-            left = jnp.where(keep, block[:, None, :], 0.0).reshape(rows * heads, size).astype(BF16)
-            part = matmul(left, cots[side])
-            total = part if total is None else total + part
+            lefts.append(jnp.where(keep, block[:, None, :], 0.0).reshape(rows * heads, size).astype(BF16))
+        total = matmul(jnp.concatenate(lefts, axis=1), both_cots)
         place = pl.ds(g * rows * heads, rows * heads)
         total_ref[place, :] = total
         copies.append(pltpu.make_async_copy(total_ref.at[place], out_ref.at[place], sems.at[g]))

time: 21.5 us -> 21.5 us (level)
  no operation moved by 1% of the time
where the time goes in v16:
time: 21.5 us; the launch traced here: 21.3 us
  starting transfers between devices  11.6 us (54%)
  waiting for transfers between devices  5.21 us (24%)
  Pallas kernels  3.48 us (16%)
  between operations  0.69 us (3%)
  local copies, waits for them, and re-layouts  0.32 us (1%)
    ppermute x11, starting transfers between devices, swap(): return lax.ppermute(value, ('head', 'ctx'), pairs)  11.6 us
    ppermute x11, waiting for transfers between devices, swap(): return lax.ppermute(value, ('head', 'ctx'), pairs)  5.21 us
    pallas_call x7, Pallas kernels, call(): pl.pallas_call(kernel, out_shape=out, out_specs=jax.tree.map(lambda _: pl...  3.48 us
  transfers between devices with their start and end apart: 11, of which 4 were waited for; matrix products, arithmetic and copies ran while one was open for 0% of the time, Pallas kernels for 13%

profile of v16, /device:TPU:0, one launch (start us, length us, event | category | flops | bytes accessed | tf_op | source)
XLA Modules:
  0.0 21.3 jit_solution(4987098735565000392)
XLA Ops:
  0.6 0.5 %collective-permute-start = (bf16[1024,256]{1,0:T(8,128)(2,1)}, bf16[1024,256]{1,0:T(8,128)(2,1)S(1)}, u32[]{:S(2)}, u32[]{:S(2)}) collective-permute-start(bf16[1024,256]{1,0:T(8,128)(2,1)} %bitcast.6), channel_id=1, source_target_pairs={{0,1},{1,0},{2,3},{3,2},{4,5},{5,4},{6,7},{7,6},{8,9},{9,8},{10,11... | collective-permute-start | bytes 1572872 | tf_op jit(solution)/shard_map/ppermute | solution.py:230
  1.1 0.0 copy-start.3
  1.1 0.0 copy-start.2
  1.2 2.6 %collective-permute-start.1 = (bf16[128,256]{1,0:T(8,128)(2,1)}, bf16[128,256]{1,0:T(8,128)(2,1)S(1)}, u32[]{:S(2)}, u32[]{:S(2)}) collective-permute-start(bf16[128,256]{1,0:T(8,128)(2,1)} %bitcast.8), channel_id=1, source_target_pairs={{0,3},{1,2},{2,0},{3,1},{4,6},{5,7},{6,5},{7,4},{8,10},{9,11},{10,... | collective-permute-start | bytes 196616 | tf_op jit(solution)/shard_map/ppermute | solution.py:230
  3.8 0.1 collective-permute-start.2
  3.8 0.0 copy-done.3
  3.8 0.0 copy-done.2
  3.8 0.0 copy-start
  3.8 0.1 shard_map.59
  3.9 0.6 %collective-permute-start.3 = (bf16[2,256]{1,0:T(2,128)(2,1)S(1)}, bf16[2,256]{1,0:T(2,128)(2,1)S(1)}, u32[]{:S(2)}, u32[]{:S(2)}) collective-permute-start(bf16[2,256]{1,0:T(2,128)(2,1)S(1)} %get-tuple-element.36), channel_id=1, source_target_pairs={{0,3},{1,2},{2,1},{3,0},{4,7},{5,6},{6,5},{7,4},{8,11},{9,10},{10,... | collective-permute-start | bytes 3080 | tf_op jit(solution)/shard_map/ppermute | solution.py:230
  4.6 0.0 collective-permute-done.other_ref
  4.6 0.3 %copy-done = bf16[128,8,256]{2,1,0:T(8,128)(2,1)S(1)} copy-done((bf16[128,8,256]{2,1,0:T(8,128)(2,1)S(1)}, bf16[128,8,256]{2,1,0:T(8,128)(2,1)}, u32[]{:S(2)}) %copy-start) | copy-done | bytes 524312
  4.9 0.0 copy-start.1
  4.9 0.8 %shard_map.60 = (bf16[8,256,256]{2,1,0:T(8,128)(2,1)S(1)}, bf16[256,256]{1,0:T(8,128)(2,1)S(1)}) custom-call(bf16[1024,256]{1,0:T(8,128)(2,1)S(1)} %bitcast.7, bf16[1024,256]{1,0:T(8,128)(2,1)S(1)} %collective-permute-done.other_ref), custom_call_target="tpu_custom_call" | custom-call | bytes 1048576 | tf_op jit(solution)/shard_map/pallas_call | solution.py:246
  5.6 1.0 %collective-permute-done.1.refs_0_.refs_1_ = bf16[128,256]{1,0:T(8,128)(2,1)S(1)} collective-permute-done((bf16[128,256]{1,0:T(8,128)(2,1)}, bf16[128,256]{1,0:T(8,128)(2,1)S(1)}, u32[]{:S(2)}, u32[]{:S(2)}) %collective-permute-start.1) | collective-permute-done | bytes 65568 | tf_op jit(solution)/shard_map/ppermute | solution.py:230
  6.6 0.0 collective-permute-done.2.refs_2_
  6.6 0.0 copy-done.1
  6.6 0.5 %shard_map.61 = (f32[8,256]{1,0:T(8,128)S(1)}, bf16[16,256]{1,0:T(8,128)(2,1)S(1)}, bf16[16,256]{1,0:T(8,128)(2,1)S(1)}, bf16[16,256]{1,0:T(8,128)(2,1)S(1)}) custom-call(bf16[256,256]{1,0:T(8,128)(2,1)S(1)} %get-tuple-element.32.order_ref, bf16[8,256,256]{2,1,0:T(8,128)(2,1)S(1)} %get-tuple-element.33.weight_ref, ...), custom_call_target="tpu_custom_call" | custom-call | bytes 1376256 | tf_op jit(solution)/shard_map/pallas_call | solution.py:246
  7.1 0.0 collective-permute-done.3
  7.1 1.4 %collective-permute-start.4 = (bf16[20,256]{1,0:T(8,128)(2,1)S(1)}, bf16[20,256]{1,0:T(8,128)(2,1)S(1)}, u32[]{:S(2)}, u32[]{:S(2)}) collective-permute-start(bf16[20,256]{1,0:T(8,128)(2,1)S(1)} %get-tuple-element.54), channel_id=1, source_target_pairs={{0,5},{1,4},{2,7},{3,6},{4,1},{5,0},{6,3},{7,2},{8,13},{9,12},{10,... | collective-permute-start | bytes 30728 | tf_op jit(solution)/shard_map/ppermute | solution.py:230
  8.6 1.5 %collective-permute-start.5 = (bf16[20,256]{1,0:T(8,128)(2,1)S(1)}, bf16[20,256]{1,0:T(8,128)(2,1)S(1)}, u32[]{:S(2)}, u32[]{:S(2)}) collective-permute-start(bf16[20,256]{1,0:T(8,128)(2,1)S(1)} %get-tuple-element.53), channel_id=1, source_target_pairs={{0,12},{1,13},{2,14},{3,15},{4,8},{5,9},{6,10},{7,11},{8,4},{9,5},... | collective-permute-start | bytes 30728 | tf_op jit(solution)/shard_map/ppermute | solution.py:230
  10.1 0.2 collective-permute-start.6
  10.3 0.4 %collective-permute-start.7 = (bf16[128,256]{1,0:T(8,128)(2,1)S(1)}, bf16[128,256]{1,0:T(8,128)(2,1)S(1)}, u32[]{:S(2)}, u32[]{:S(2)}) collective-permute-start(bf16[128,256]{1,0:T(8,128)(2,1)S(1)} %collective-permute-done.1.refs_0_.refs_1_), channel_id=1, source_target_pairs={{0,1},{1,0},{2,3},{3,2},{4,5},{5,4},{6,7},{7,6},{8,9},{9,8},{10,11... | collective-permute-start | bytes 196616 | tf_op jit(solution)/shard_map/ppermute | solution.py:230
  10.7 0.0 collective-permute-done.4.refs_0_
  10.7 2.4 %collective-permute-done.5.refs_1_ = bf16[20,256]{1,0:T(8,128)(2,1)S(1)} collective-permute-done((bf16[20,256]{1,0:T(8,128)(2,1)S(1)}, bf16[20,256]{1,0:T(8,128)(2,1)S(1)}, u32[]{:S(2)}, u32[]{:S(2)}) %collective-permute-start.5) | collective-permute-done | bytes 10272 | tf_op jit(solution)/shard_map/ppermute | solution.py:230
  13.1 0.1 collective-permute-done.6.refs_2_
  13.3 0.0 collective-permute-done.7.refs_3_
  13.3 2.4 %collective-permute-start.8 = (bf16[24,256]{1,0:T(8,128)(2,1)S(1)}, bf16[24,256]{1,0:T(8,128)(2,1)S(1)}, u32[]{:S(2)}, u32[]{:S(2)}) collective-permute-start(bf16[24,256]{1,0:T(8,128)(2,1)S(1)} %get-tuple-element.43.normed_ref), channel_id=1, source_target_pairs={{0,17},{1,16},{2,19},{3,18},{4,21},{5,20},{6,23},{7,22},{8,25},{9,... | collective-permute-start | bytes 36872 | tf_op jit(solution)/shard_map/ppermute | solution.py:230
  15.7 1.7 %collective-permute-done.8.refs_0_ = bf16[24,256]{1,0:T(8,128)(2,1)S(1)} collective-permute-done((bf16[24,256]{1,0:T(8,128)(2,1)S(1)}, bf16[24,256]{1,0:T(8,128)(2,1)S(1)}, u32[]{:S(2)}, u32[]{:S(2)}) %collective-permute-start.8) | collective-permute-done | bytes 12320 | tf_op jit(solution)/shard_map/ppermute | solution.py:230
  17.4 0.2 collective-permute-start.9
  17.6 1.6 %collective-permute-start.10 = (f32[2,256]{1,0:T(2,128)S(1)}, f32[2,256]{1,0:T(2,128)S(1)}, u32[]{:S(2)}, u32[]{:S(2)}) collective-permute-start(f32[2,256]{1,0:T(2,128)S(1)} %get-tuple-element.48), channel_id=1, source_target_pairs={{0,2},{1,3},{2,1},{3,0},{4,7},{5,6},{6,4},{7,5},{8,11},{9,10},{10,... | collective-permute-start | bytes 6152 | tf_op jit(solution)/shard_map/ppermute | solution.py:230
  19.1 0.0 collective-permute-done.9.other_ref
  19.1 1.4 %shard_map.64 = f32[1024,256]{1,0:T(8,128)} custom-call(f32[32,128]{1,0:T(8,128)S(1)} %get-tuple-element.45.own_ref, f32[18,256]{1,0:T(8,128)S(1)} %collective-permute-done.9.other_ref, bf16[128,256]{1,0:T(8,128)(2,1)S(1)} %bitcast.11, bf16[128,256]{1,0:T(8,128)(2,1)S(1)} %collective-permute-done.1.refs_0_.refs_1_, ...), custom_call_target="tpu_custom_call" | custom-call | flops 268435456 | bytes 296960 | tf_op jit(solution)/shard_map/pallas_call | solution.py:246
  20.6 0.0 collective-permute-done.10.refs_1_
  20.6 0.7 %shard_map.65 = f32[2,512]{1,0:T(2,128)} custom-call(f32[2,512]{1,0:T(2,128)S(1)} %get-tuple-element.27.rms_ref, f32[2,512]{1,0:T(2,128)S(1)} %get-tuple-element.28.hat_ref, f32[1,512]{1,0:T(1,128)S(1)} %bitcast.13, f32[18,256]{1,0:T(8,128)S(1)} %collective-permute-done.9.other_ref, f32[2,256]{1,0:T(2,128)S(1)} %get-tuple-element.49.refs_0_, ...), custom_call_target="tpu_custom_call" | custom-call | bytes 32768 | tf_op jit(solution)/shard_map/pallas_call | solution.py:246
  (4 shorter events, 0.0 us)
Async XLA Ops:
  0.6 3.9 %collective-permute-start = (bf16[1024,256]{1,0:T(8,128)(2,1)}, bf16[1024,256]{1,0:T(8,128)(2,1)S(1)}, u32[]{:S(2)}, u32[]{:S(2)}) collective-permute-start(bf16[1024,256]{1,0:T(8,128)(2,1)} %bitcast.6), channel_id=1, source_target_pairs={{0,1},{1,0},{2,3},{3,2},{4,5},{5,4},{6,7},{7,6},{8,9},{9,8},{10,11... | collective-permute-start | bytes 1572872 | tf_op jit(solution)/shard_map/ppermute | solution.py:230
  1.1 2.7 %copy-start.3 = (bf16[1,2,512]{2,1,0:T(2,128)(2,1)S(1)}, bf16[1,2,512]{2,1,0:T(2,128)(2,1)}, u32[]{:S(2)}) copy-start(bf16[1,2,512]{2,1,0:T(2,128)(2,1)} %param.4) | copy-start | bytes 6148
  1.1 2.7 %copy-start.2 = (f32[512]{0:T(512)S(1)}, f32[512]{0:T(512)}, u32[]{:S(2)}) copy-start(f32[512]{0:T(512)} %param.5) | copy-start | bytes 6148
  1.2 5.5 %collective-permute-start.1 = (bf16[128,256]{1,0:T(8,128)(2,1)}, bf16[128,256]{1,0:T(8,128)(2,1)S(1)}, u32[]{:S(2)}, u32[]{:S(2)}) collective-permute-start(bf16[128,256]{1,0:T(8,128)(2,1)} %bitcast.8), channel_id=1, source_target_pairs={{0,3},{1,2},{2,0},{3,1},{4,6},{5,7},{6,5},{7,4},{8,10},{9,11},{10,... | collective-permute-start | bytes 196616 | tf_op jit(solution)/shard_map/ppermute | solution.py:230
  3.8 2.8 %collective-permute-start.2 = (bf16[128,256]{1,0:T(8,128)(2,1)}, bf16[128,256]{1,0:T(8,128)(2,1)S(1)}, u32[]{:S(2)}, u32[]{:S(2)}) collective-permute-start(bf16[128,256]{1,0:T(8,128)(2,1)} %bitcast.9), channel_id=1, source_target_pairs={{0,1},{1,0},{2,3},{3,2},{4,5},{5,4},{6,7},{7,6},{8,9},{9,8},{10,11... | collective-permute-start | bytes 196616 | tf_op jit(solution)/shard_map/ppermute | solution.py:230
  3.8 1.0 %copy-start = (bf16[128,8,256]{2,1,0:T(8,128)(2,1)S(1)}, bf16[128,8,256]{2,1,0:T(8,128)(2,1)}, u32[]{:S(2)}) copy-start(bf16[128,8,256]{2,1,0:T(8,128)(2,1)} %param.7) | copy-start | bytes 1572868
  3.9 3.1 %collective-permute-start.3 = (bf16[2,256]{1,0:T(2,128)(2,1)S(1)}, bf16[2,256]{1,0:T(2,128)(2,1)S(1)}, u32[]{:S(2)}, u32[]{:S(2)}) collective-permute-start(bf16[2,256]{1,0:T(2,128)(2,1)S(1)} %get-tuple-element.36), channel_id=1, source_target_pairs={{0,3},{1,2},{2,1},{3,0},{4,7},{5,6},{6,5},{7,4},{8,11},{9,10},{10,... | collective-permute-start | bytes 3080 | tf_op jit(solution)/shard_map/ppermute | solution.py:230
  4.9 1.7 %copy-start.1 = (bf16[1,16,8,256]{3,2,1,0:T(8,128)(2,1)S(1)}, bf16[1,16,8,256]{3,2,1,0:T(8,128)(2,1)}, u32[]{:S(2)}) copy-start(bf16[1,16,8,256]{3,2,1,0:T(8,128)(2,1)} %param.6) | copy-start | bytes 196612
  7.1 3.6 %collective-permute-start.4 = (bf16[20,256]{1,0:T(8,128)(2,1)S(1)}, bf16[20,256]{1,0:T(8,128)(2,1)S(1)}, u32[]{:S(2)}, u32[]{:S(2)}) collective-permute-start(bf16[20,256]{1,0:T(8,128)(2,1)S(1)} %get-tuple-element.54), channel_id=1, source_target_pairs={{0,5},{1,4},{2,7},{3,6},{4,1},{5,0},{6,3},{7,2},{8,13},{9,12},{10,... | collective-permute-start | bytes 30728 | tf_op jit(solution)/shard_map/ppermute | solution.py:230
  8.6 4.6 %collective-permute-start.5 = (bf16[20,256]{1,0:T(8,128)(2,1)S(1)}, bf16[20,256]{1,0:T(8,128)(2,1)S(1)}, u32[]{:S(2)}, u32[]{:S(2)}) collective-permute-start(bf16[20,256]{1,0:T(8,128)(2,1)S(1)} %get-tuple-element.53), channel_id=1, source_target_pairs={{0,12},{1,13},{2,14},{3,15},{4,8},{5,9},{6,10},{7,11},{8,4},{9,5},... | collective-permute-start | bytes 30728 | tf_op jit(solution)/shard_map/ppermute | solution.py:230
  10.1 3.2 %collective-permute-start.6 = (bf16[20,256]{1,0:T(8,128)(2,1)S(1)}, bf16[20,256]{1,0:T(8,128)(2,1)S(1)}, u32[]{:S(2)}, u32[]{:S(2)}) collective-permute-start(bf16[20,256]{1,0:T(8,128)(2,1)S(1)} %get-tuple-element.52), channel_id=1, source_target_pairs={{0,9},{1,8},{2,11},{3,10},{4,13},{5,12},{6,15},{7,14},{8,1},{9,0},... | collective-permute-start | bytes 30728 | tf_op jit(solution)/shard_map/ppermute | solution.py:230
  10.3 3.0 %collective-permute-start.7 = (bf16[128,256]{1,0:T(8,128)(2,1)S(1)}, bf16[128,256]{1,0:T(8,128)(2,1)S(1)}, u32[]{:S(2)}, u32[]{:S(2)}) collective-permute-start(bf16[128,256]{1,0:T(8,128)(2,1)S(1)} %collective-permute-done.1.refs_0_.refs_1_), channel_id=1, source_target_pairs={{0,1},{1,0},{2,3},{3,2},{4,5},{5,4},{6,7},{7,6},{8,9},{9,8},{10,11... | collective-permute-start | bytes 196616 | tf_op jit(solution)/shard_map/ppermute | solution.py:230
  13.3 4.1 %collective-permute-start.8 = (bf16[24,256]{1,0:T(8,128)(2,1)S(1)}, bf16[24,256]{1,0:T(8,128)(2,1)S(1)}, u32[]{:S(2)}, u32[]{:S(2)}) collective-permute-start(bf16[24,256]{1,0:T(8,128)(2,1)S(1)} %get-tuple-element.43.normed_ref), channel_id=1, source_target_pairs={{0,17},{1,16},{2,19},{3,18},{4,21},{5,20},{6,23},{7,22},{8,25},{9,... | collective-permute-start | bytes 36872 | tf_op jit(solution)/shard_map/ppermute | solution.py:230
  17.4 1.7 %collective-permute-start.9 = (f32[18,256]{1,0:T(8,128)S(1)}, f32[18,256]{1,0:T(8,128)S(1)}, u32[]{:S(2)}, u32[]{:S(2)}) collective-permute-start(f32[18,256]{1,0:T(8,128)S(1)} %get-tuple-element.44), channel_id=1, source_target_pairs={{0,1},{1,0},{2,3},{3,2},{4,5},{5,4},{6,7},{7,6},{8,9},{9,8},{10,11... | collective-permute-start | bytes 55304 | tf_op jit(solution)/shard_map/ppermute | solution.py:230
  17.6 3.0 %collective-permute-start.10 = (f32[2,256]{1,0:T(2,128)S(1)}, f32[2,256]{1,0:T(2,128)S(1)}, u32[]{:S(2)}, u32[]{:S(2)}) collective-permute-start(f32[2,256]{1,0:T(2,128)S(1)} %get-tuple-element.48), channel_id=1, source_target_pairs={{0,2},{1,3},{2,1},{3,0},{4,7},{5,6},{6,4},{7,5},{8,11},{9,10},{10,... | collective-permute-start | bytes 6152 | tf_op jit(solution)/shard_map/ppermute | solution.py:230

commit v17 on v14

--- a/solution.py
+++ b/solution.py
@@ -92,9 +92,9 @@
     moved = matmul(order_ref[...], stacked).astype(BF16)
     size, rows = out_refs[0].shape[0], out_refs[0].shape[1] // 2
     part = count * size
-    total = matmul(moved[:part], weight_ref[0])
-    for h in range(1, weight_ref.shape[0]):
-        total += matmul(moved[h * part : (h + 1) * part], weight_ref[h])
+    heads, channels, width = weight_ref.shape
+    left = jnp.concatenate([moved[h * part : (h + 1) * part] for h in range(heads)], axis=1)
+    total = matmul(left, weight_ref[...].reshape(heads * channels, width))
     turned = jnp.concatenate([total[:, rows:], total[:, :rows]], axis=1)
     total = jnp.where(core == 0, total, turned)
     out_refs[0][...] = total[:size]

time: 21.5 us -> 21.5 us (level)
  no operation moved by 1% of the time
where the time goes in v17:
time: 21.5 us; the launch traced here: 21.3 us
  starting transfers between devices  11.6 us (54%)
  waiting for transfers between devices  5.19 us (24%)
  Pallas kernels  3.5 us (16%)
  between operations  0.69 us (3%)
  local copies, waits for them, and re-layouts  0.32 us (1%)
    ppermute x11, starting transfers between devices, swap(): return lax.ppermute(value, ('head', 'ctx'), pairs)  11.6 us
    ppermute x11, waiting for transfers between devices, swap(): return lax.ppermute(value, ('head', 'ctx'), pairs)  5.19 us
    pallas_call x7, Pallas kernels, call(): pl.pallas_call(kernel, out_shape=out, out_specs=jax.tree.map(lambda _: pl...  3.5 us
  transfers between devices with their start and end apart: 11, of which 4 were waited for; matrix products, arithmetic and copies ran while one was open for 0% of the time, Pallas kernels for 13%

profile of v17, /device:TPU:0, one launch (start us, length us, event | category | flops | bytes accessed | tf_op | source)
XLA Modules:
  0.0 21.3 jit_solution(4003063948144778178)
XLA Ops:
  0.6 0.5 %collective-permute-start = (bf16[1024,256]{1,0:T(8,128)(2,1)}, bf16[1024,256]{1,0:T(8,128)(2,1)S(1)}, u32[]{:S(2)}, u32[]{:S(2)}) collective-permute-start(bf16[1024,256]{1,0:T(8,128)(2,1)} %bitcast.6), channel_id=1, source_target_pairs={{0,1},{1,0},{2,3},{3,2},{4,5},{5,4},{6,7},{7,6},{8,9},{9,8},{10,11... | collective-permute-start | bytes 1572872 | tf_op jit(solution)/shard_map/ppermute | solution.py:230
  1.1 0.0 copy-start.3
  1.1 0.0 copy-start.2
  1.2 2.6 %collective-permute-start.1 = (bf16[128,256]{1,0:T(8,128)(2,1)}, bf16[128,256]{1,0:T(8,128)(2,1)S(1)}, u32[]{:S(2)}, u32[]{:S(2)}) collective-permute-start(bf16[128,256]{1,0:T(8,128)(2,1)} %bitcast.8), channel_id=1, source_target_pairs={{0,3},{1,2},{2,0},{3,1},{4,6},{5,7},{6,5},{7,4},{8,10},{9,11},{10,... | collective-permute-start | bytes 196616 | tf_op jit(solution)/shard_map/ppermute | solution.py:230
  3.8 0.1 collective-permute-start.2
  3.8 0.0 copy-done.3
  3.8 0.0 copy-done.2
  3.8 0.0 copy-start
  3.8 0.1 shard_map.59
  3.9 0.6 %collective-permute-start.3 = (bf16[2,256]{1,0:T(2,128)(2,1)S(1)}, bf16[2,256]{1,0:T(2,128)(2,1)S(1)}, u32[]{:S(2)}, u32[]{:S(2)}) collective-permute-start(bf16[2,256]{1,0:T(2,128)(2,1)S(1)} %get-tuple-element.36), channel_id=1, source_target_pairs={{0,3},{1,2},{2,1},{3,0},{4,7},{5,6},{6,5},{7,4},{8,11},{9,10},{10,... | collective-permute-start | bytes 3080 | tf_op jit(solution)/shard_map/ppermute | solution.py:230
  4.6 0.0 collective-permute-done.other_ref
  4.6 0.3 %copy-done = bf16[128,8,256]{2,1,0:T(8,128)(2,1)S(1)} copy-done((bf16[128,8,256]{2,1,0:T(8,128)(2,1)S(1)}, bf16[128,8,256]{2,1,0:T(8,128)(2,1)}, u32[]{:S(2)}) %copy-start) | copy-done | bytes 524312
  4.9 0.0 copy-start.1
  4.9 0.8 %shard_map.60 = (bf16[8,256,256]{2,1,0:T(8,128)(2,1)S(1)}, bf16[256,256]{1,0:T(8,128)(2,1)S(1)}) custom-call(bf16[1024,256]{1,0:T(8,128)(2,1)S(1)} %bitcast.7, bf16[1024,256]{1,0:T(8,128)(2,1)S(1)} %collective-permute-done.other_ref), custom_call_target="tpu_custom_call" | custom-call | bytes 1048576 | tf_op jit(solution)/shard_map/pallas_call | solution.py:246
  5.6 1.0 %collective-permute-done.1.refs_0_.refs_1_ = bf16[128,256]{1,0:T(8,128)(2,1)S(1)} collective-permute-done((bf16[128,256]{1,0:T(8,128)(2,1)}, bf16[128,256]{1,0:T(8,128)(2,1)S(1)}, u32[]{:S(2)}, u32[]{:S(2)}) %collective-permute-start.1) | collective-permute-done | bytes 65568 | tf_op jit(solution)/shard_map/ppermute | solution.py:230
  6.6 0.0 collective-permute-done.2.refs_2_
  6.6 0.0 copy-done.1
  6.6 0.5 %shard_map.61 = (f32[8,256]{1,0:T(8,128)S(1)}, bf16[16,256]{1,0:T(8,128)(2,1)S(1)}, bf16[16,256]{1,0:T(8,128)(2,1)S(1)}, bf16[16,256]{1,0:T(8,128)(2,1)S(1)}) custom-call(bf16[256,256]{1,0:T(8,128)(2,1)S(1)} %get-tuple-element.32.order_ref, bf16[8,256,256]{2,1,0:T(8,128)(2,1)S(1)} %get-tuple-element.33.weight_ref, ...), custom_call_target="tpu_custom_call" | custom-call | bytes 1376256 | tf_op jit(solution)/shard_map/pallas_call | solution.py:246
  7.1 0.0 collective-permute-done.3
  7.1 1.4 %collective-permute-start.4 = (bf16[20,256]{1,0:T(8,128)(2,1)S(1)}, bf16[20,256]{1,0:T(8,128)(2,1)S(1)}, u32[]{:S(2)}, u32[]{:S(2)}) collective-permute-start(bf16[20,256]{1,0:T(8,128)(2,1)S(1)} %get-tuple-element.54), channel_id=1, source_target_pairs={{0,5},{1,4},{2,7},{3,6},{4,1},{5,0},{6,3},{7,2},{8,13},{9,12},{10,... | collective-permute-start | bytes 30728 | tf_op jit(solution)/shard_map/ppermute | solution.py:230
  8.6 1.5 %collective-permute-start.5 = (bf16[20,256]{1,0:T(8,128)(2,1)S(1)}, bf16[20,256]{1,0:T(8,128)(2,1)S(1)}, u32[]{:S(2)}, u32[]{:S(2)}) collective-permute-start(bf16[20,256]{1,0:T(8,128)(2,1)S(1)} %get-tuple-element.53), channel_id=1, source_target_pairs={{0,12},{1,13},{2,14},{3,15},{4,8},{5,9},{6,10},{7,11},{8,4},{9,5},... | collective-permute-start | bytes 30728 | tf_op jit(solution)/shard_map/ppermute | solution.py:230
  10.1 0.2 collective-permute-start.6
  10.3 0.4 %collective-permute-start.7 = (bf16[128,256]{1,0:T(8,128)(2,1)S(1)}, bf16[128,256]{1,0:T(8,128)(2,1)S(1)}, u32[]{:S(2)}, u32[]{:S(2)}) collective-permute-start(bf16[128,256]{1,0:T(8,128)(2,1)S(1)} %collective-permute-done.1.refs_0_.refs_1_), channel_id=1, source_target_pairs={{0,1},{1,0},{2,3},{3,2},{4,5},{5,4},{6,7},{7,6},{8,9},{9,8},{10,11... | collective-permute-start | bytes 196616 | tf_op jit(solution)/shard_map/ppermute | solution.py:230
  10.7 0.0 collective-permute-done.4.refs_0_
  10.7 2.4 %collective-permute-done.5.refs_1_ = bf16[20,256]{1,0:T(8,128)(2,1)S(1)} collective-permute-done((bf16[20,256]{1,0:T(8,128)(2,1)S(1)}, bf16[20,256]{1,0:T(8,128)(2,1)S(1)}, u32[]{:S(2)}, u32[]{:S(2)}) %collective-permute-start.5) | collective-permute-done | bytes 10272 | tf_op jit(solution)/shard_map/ppermute | solution.py:230
  13.1 0.1 collective-permute-done.6.refs_2_
  13.3 0.0 collective-permute-done.7.refs_3_
  13.3 2.4 %collective-permute-start.8 = (bf16[24,256]{1,0:T(8,128)(2,1)S(1)}, bf16[24,256]{1,0:T(8,128)(2,1)S(1)}, u32[]{:S(2)}, u32[]{:S(2)}) collective-permute-start(bf16[24,256]{1,0:T(8,128)(2,1)S(1)} %get-tuple-element.43.normed_ref), channel_id=1, source_target_pairs={{0,17},{1,16},{2,19},{3,18},{4,21},{5,20},{6,23},{7,22},{8,25},{9,... | collective-permute-start | bytes 36872 | tf_op jit(solution)/shard_map/ppermute | solution.py:230
  15.7 1.6 %collective-permute-done.8.refs_0_ = bf16[24,256]{1,0:T(8,128)(2,1)S(1)} collective-permute-done((bf16[24,256]{1,0:T(8,128)(2,1)S(1)}, bf16[24,256]{1,0:T(8,128)(2,1)S(1)}, u32[]{:S(2)}, u32[]{:S(2)}) %collective-permute-start.8) | collective-permute-done | bytes 12320 | tf_op jit(solution)/shard_map/ppermute | solution.py:230
  17.4 0.2 collective-permute-start.9
  17.6 1.6 %collective-permute-start.10 = (f32[2,256]{1,0:T(2,128)S(1)}, f32[2,256]{1,0:T(2,128)S(1)}, u32[]{:S(2)}, u32[]{:S(2)}) collective-permute-start(f32[2,256]{1,0:T(2,128)S(1)} %get-tuple-element.48), channel_id=1, source_target_pairs={{0,2},{1,3},{2,1},{3,0},{4,7},{5,6},{6,4},{7,5},{8,11},{9,10},{10,... | collective-permute-start | bytes 6152 | tf_op jit(solution)/shard_map/ppermute | solution.py:230
  19.1 0.0 collective-permute-done.9.other_ref
  19.1 1.4 %shard_map.64 = f32[1024,256]{1,0:T(8,128)} custom-call(f32[32,128]{1,0:T(8,128)S(1)} %get-tuple-element.45.own_ref, f32[18,256]{1,0:T(8,128)S(1)} %collective-permute-done.9.other_ref, bf16[128,256]{1,0:T(8,128)(2,1)S(1)} %bitcast.11, bf16[128,256]{1,0:T(8,128)(2,1)S(1)} %collective-permute-done.1.refs_0_.refs_1_, ...), custom_call_target="tpu_custom_call" | custom-call | flops 268435456 | bytes 296960 | tf_op jit(solution)/shard_map/pallas_call | solution.py:246
  20.6 0.0 collective-permute-done.10.refs_1_
  20.6 0.7 %shard_map.65 = f32[2,512]{1,0:T(2,128)} custom-call(f32[2,512]{1,0:T(2,128)S(1)} %get-tuple-element.27.rms_ref, f32[2,512]{1,0:T(2,128)S(1)} %get-tuple-element.28.hat_ref, f32[1,512]{1,0:T(1,128)S(1)} %bitcast.13, f32[18,256]{1,0:T(8,128)S(1)} %collective-permute-done.9.other_ref, f32[2,256]{1,0:T(2,128)S(1)} %get-tuple-element.49.refs_0_, ...), custom_call_target="tpu_custom_call" | custom-call | bytes 32768 | tf_op jit(solution)/shard_map/pallas_call | solution.py:246
  (4 shorter events, 0.0 us)
Async XLA Ops:
  0.6 3.9 %collective-permute-start = (bf16[1024,256]{1,0:T(8,128)(2,1)}, bf16[1024,256]{1,0:T(8,128)(2,1)S(1)}, u32[]{:S(2)}, u32[]{:S(2)}) collective-permute-start(bf16[1024,256]{1,0:T(8,128)(2,1)} %bitcast.6), channel_id=1, source_target_pairs={{0,1},{1,0},{2,3},{3,2},{4,5},{5,4},{6,7},{7,6},{8,9},{9,8},{10,11... | collective-permute-start | bytes 1572872 | tf_op jit(solution)/shard_map/ppermute | solution.py:230
  1.1 2.7 %copy-start.3 = (bf16[1,2,512]{2,1,0:T(2,128)(2,1)S(1)}, bf16[1,2,512]{2,1,0:T(2,128)(2,1)}, u32[]{:S(2)}) copy-start(bf16[1,2,512]{2,1,0:T(2,128)(2,1)} %param.4) | copy-start | bytes 6148
  1.1 2.7 %copy-start.2 = (f32[512]{0:T(512)S(1)}, f32[512]{0:T(512)}, u32[]{:S(2)}) copy-start(f32[512]{0:T(512)} %param.5) | copy-start | bytes 6148
  1.2 5.5 %collective-permute-start.1 = (bf16[128,256]{1,0:T(8,128)(2,1)}, bf16[128,256]{1,0:T(8,128)(2,1)S(1)}, u32[]{:S(2)}, u32[]{:S(2)}) collective-permute-start(bf16[128,256]{1,0:T(8,128)(2,1)} %bitcast.8), channel_id=1, source_target_pairs={{0,3},{1,2},{2,0},{3,1},{4,6},{5,7},{6,5},{7,4},{8,10},{9,11},{10,... | collective-permute-start | bytes 196616 | tf_op jit(solution)/shard_map/ppermute | solution.py:230
  3.8 2.8 %collective-permute-start.2 = (bf16[128,256]{1,0:T(8,128)(2,1)}, bf16[128,256]{1,0:T(8,128)(2,1)S(1)}, u32[]{:S(2)}, u32[]{:S(2)}) collective-permute-start(bf16[128,256]{1,0:T(8,128)(2,1)} %bitcast.9), channel_id=1, source_target_pairs={{0,1},{1,0},{2,3},{3,2},{4,5},{5,4},{6,7},{7,6},{8,9},{9,8},{10,11... | collective-permute-start | bytes 196616 | tf_op jit(solution)/shard_map/ppermute | solution.py:230
  3.8 1.0 %copy-start = (bf16[128,8,256]{2,1,0:T(8,128)(2,1)S(1)}, bf16[128,8,256]{2,1,0:T(8,128)(2,1)}, u32[]{:S(2)}) copy-start(bf16[128,8,256]{2,1,0:T(8,128)(2,1)} %param.7) | copy-start | bytes 1572868
  3.9 3.1 %collective-permute-start.3 = (bf16[2,256]{1,0:T(2,128)(2,1)S(1)}, bf16[2,256]{1,0:T(2,128)(2,1)S(1)}, u32[]{:S(2)}, u32[]{:S(2)}) collective-permute-start(bf16[2,256]{1,0:T(2,128)(2,1)S(1)} %get-tuple-element.36), channel_id=1, source_target_pairs={{0,3},{1,2},{2,1},{3,0},{4,7},{5,6},{6,5},{7,4},{8,11},{9,10},{10,... | collective-permute-start | bytes 3080 | tf_op jit(solution)/shard_map/ppermute | solution.py:230
  4.9 1.7 %copy-start.1 = (bf16[1,16,8,256]{3,2,1,0:T(8,128)(2,1)S(1)}, bf16[1,16,8,256]{3,2,1,0:T(8,128)(2,1)}, u32[]{:S(2)}) copy-start(bf16[1,16,8,256]{3,2,1,0:T(8,128)(2,1)} %param.6) | copy-start | bytes 196612
  7.1 3.6 %collective-permute-start.4 = (bf16[20,256]{1,0:T(8,128)(2,1)S(1)}, bf16[20,256]{1,0:T(8,128)(2,1)S(1)}, u32[]{:S(2)}, u32[]{:S(2)}) collective-permute-start(bf16[20,256]{1,0:T(8,128)(2,1)S(1)} %get-tuple-element.54), channel_id=1, source_target_pairs={{0,5},{1,4},{2,7},{3,6},{4,1},{5,0},{6,3},{7,2},{8,13},{9,12},{10,... | collective-permute-start | bytes 30728 | tf_op jit(solution)/shard_map/ppermute | solution.py:230
  8.6 4.6 %collective-permute-start.5 = (bf16[20,256]{1,0:T(8,128)(2,1)S(1)}, bf16[20,256]{1,0:T(8,128)(2,1)S(1)}, u32[]{:S(2)}, u32[]{:S(2)}) collective-permute-start(bf16[20,256]{1,0:T(8,128)(2,1)S(1)} %get-tuple-element.53), channel_id=1, source_target_pairs={{0,12},{1,13},{2,14},{3,15},{4,8},{5,9},{6,10},{7,11},{8,4},{9,5},... | collective-permute-start | bytes 30728 | tf_op jit(solution)/shard_map/ppermute | solution.py:230
  10.1 3.2 %collective-permute-start.6 = (bf16[20,256]{1,0:T(8,128)(2,1)S(1)}, bf16[20,256]{1,0:T(8,128)(2,1)S(1)}, u32[]{:S(2)}, u32[]{:S(2)}) collective-permute-start(bf16[20,256]{1,0:T(8,128)(2,1)S(1)} %get-tuple-element.52), channel_id=1, source_target_pairs={{0,9},{1,8},{2,11},{3,10},{4,13},{5,12},{6,15},{7,14},{8,1},{9,0},... | collective-permute-start | bytes 30728 | tf_op jit(solution)/shard_map/ppermute | solution.py:230
  10.3 3.0 %collective-permute-start.7 = (bf16[128,256]{1,0:T(8,128)(2,1)S(1)}, bf16[128,256]{1,0:T(8,128)(2,1)S(1)}, u32[]{:S(2)}, u32[]{:S(2)}) collective-permute-start(bf16[128,256]{1,0:T(8,128)(2,1)S(1)} %collective-permute-done.1.refs_0_.refs_1_), channel_id=1, source_target_pairs={{0,1},{1,0},{2,3},{3,2},{4,5},{5,4},{6,7},{7,6},{8,9},{9,8},{10,11... | collective-permute-start | bytes 196616 | tf_op jit(solution)/shard_map/ppermute | solution.py:230
  13.3 4.1 %collective-permute-start.8 = (bf16[24,256]{1,0:T(8,128)(2,1)S(1)}, bf16[24,256]{1,0:T(8,128)(2,1)S(1)}, u32[]{:S(2)}, u32[]{:S(2)}) collective-permute-start(bf16[24,256]{1,0:T(8,128)(2,1)S(1)} %get-tuple-element.43.normed_ref), channel_id=1, source_target_pairs={{0,17},{1,16},{2,19},{3,18},{4,21},{5,20},{6,23},{7,22},{8,25},{9,... | collective-permute-start | bytes 36872 | tf_op jit(solution)/shard_map/ppermute | solution.py:230
  17.4 1.8 %collective-permute-start.9 = (f32[18,256]{1,0:T(8,128)S(1)}, f32[18,256]{1,0:T(8,128)S(1)}, u32[]{:S(2)}, u32[]{:S(2)}) collective-permute-start(f32[18,256]{1,0:T(8,128)S(1)} %get-tuple-element.44), channel_id=1, source_target_pairs={{0,1},{1,0},{2,3},{3,2},{4,5},{5,4},{6,7},{7,6},{8,9},{9,8},{10,11... | collective-permute-start | bytes 55304 | tf_op jit(solution)/shard_map/ppermute | solution.py:230
  17.6 3.0 %collective-permute-start.10 = (f32[2,256]{1,0:T(2,128)S(1)}, f32[2,256]{1,0:T(2,128)S(1)}, u32[]{:S(2)}, u32[]{:S(2)}) collective-permute-start(f32[2,256]{1,0:T(2,128)S(1)} %get-tuple-element.48), channel_id=1, source_target_pairs={{0,2},{1,3},{2,1},{3,0},{4,7},{5,6},{6,4},{7,5},{8,11},{9,10},{10,... | collective-permute-start | bytes 6152 | tf_op jit(solution)/shard_map/ppermute | solution.py:230

commit v18 on v16

--- a/solution.py
+++ b/solution.py
@@ -92,9 +92,9 @@
     moved = matmul(order_ref[...], stacked).astype(BF16)
     size, rows = out_refs[0].shape[0], out_refs[0].shape[1] // 2
     part = count * size
-    total = matmul(moved[:part], weight_ref[0])
-    for h in range(1, weight_ref.shape[0]):
-        total += matmul(moved[h * part : (h + 1) * part], weight_ref[h])
+    heads, channels, width = weight_ref.shape
+    left = jnp.concatenate([moved[h * part : (h + 1) * part] for h in range(heads)], axis=1)
+    total = matmul(left, weight_ref[...].reshape(heads * channels, width))
     turned = jnp.concatenate([total[:, rows:], total[:, :rows]], axis=1)
     total = jnp.where(core == 0, total, turned)
     out_refs[0][...] = total[:size]

time: 21.5 us -> 21.5 us (level)
  no operation moved by 1% of the time
where the time goes in v18:
time: 21.5 us; the launch traced here: 21.3 us
  starting transfers between devices  11.6 us (54%)
  waiting for transfers between devices  5.19 us (24%)
  Pallas kernels  3.49 us (16%)
  between operations  0.69 us (3%)
  local copies, waits for them, and re-layouts  0.32 us (1%)
    ppermute x11, starting transfers between devices, swap(): return lax.ppermute(value, ('head', 'ctx'), pairs)  11.6 us
    ppermute x11, waiting for transfers between devices, swap(): return lax.ppermute(value, ('head', 'ctx'), pairs)  5.19 us
    pallas_call x7, Pallas kernels, call(): pl.pallas_call(kernel, out_shape=out, out_specs=jax.tree.map(lambda _: pl...  3.49 us
  transfers between devices with their start and end apart: 11, of which 4 were waited for; matrix products, arithmetic and copies ran while one was open for 0% of the time, Pallas kernels for 13%

profile of v18, /device:TPU:0, one launch (start us, length us, event | category | flops | bytes accessed | tf_op | source)
XLA Modules:
  0.0 21.3 jit_solution(1594856103143601234)
XLA Ops:
  0.6 0.5 %collective-permute-start = (bf16[1024,256]{1,0:T(8,128)(2,1)}, bf16[1024,256]{1,0:T(8,128)(2,1)S(1)}, u32[]{:S(2)}, u32[]{:S(2)}) collective-permute-start(bf16[1024,256]{1,0:T(8,128)(2,1)} %bitcast.6), channel_id=1, source_target_pairs={{0,1},{1,0},{2,3},{3,2},{4,5},{5,4},{6,7},{7,6},{8,9},{9,8},{10,11... | collective-permute-start | bytes 1572872 | tf_op jit(solution)/shard_map/ppermute | solution.py:230
  1.1 0.0 copy-start.3
  1.1 0.0 copy-start.2
  1.2 2.6 %collective-permute-start.1 = (bf16[128,256]{1,0:T(8,128)(2,1)}, bf16[128,256]{1,0:T(8,128)(2,1)S(1)}, u32[]{:S(2)}, u32[]{:S(2)}) collective-permute-start(bf16[128,256]{1,0:T(8,128)(2,1)} %bitcast.8), channel_id=1, source_target_pairs={{0,3},{1,2},{2,0},{3,1},{4,6},{5,7},{6,5},{7,4},{8,10},{9,11},{10,... | collective-permute-start | bytes 196616 | tf_op jit(solution)/shard_map/ppermute | solution.py:230
  3.8 0.1 collective-permute-start.2
  3.8 0.0 copy-done.3
  3.8 0.0 copy-done.2
  3.8 0.0 copy-start
  3.8 0.1 shard_map.59
  3.9 0.6 %collective-permute-start.3 = (bf16[2,256]{1,0:T(2,128)(2,1)S(1)}, bf16[2,256]{1,0:T(2,128)(2,1)S(1)}, u32[]{:S(2)}, u32[]{:S(2)}) collective-permute-start(bf16[2,256]{1,0:T(2,128)(2,1)S(1)} %get-tuple-element.36), channel_id=1, source_target_pairs={{0,3},{1,2},{2,1},{3,0},{4,7},{5,6},{6,5},{7,4},{8,11},{9,10},{10,... | collective-permute-start | bytes 3080 | tf_op jit(solution)/shard_map/ppermute | solution.py:230
  4.6 0.0 collective-permute-done.other_ref
  4.6 0.3 %copy-done = bf16[128,8,256]{2,1,0:T(8,128)(2,1)S(1)} copy-done((bf16[128,8,256]{2,1,0:T(8,128)(2,1)S(1)}, bf16[128,8,256]{2,1,0:T(8,128)(2,1)}, u32[]{:S(2)}) %copy-start) | copy-done | bytes 524312
  4.9 0.0 copy-start.1
  4.9 0.8 %shard_map.60 = (bf16[8,256,256]{2,1,0:T(8,128)(2,1)S(1)}, bf16[256,256]{1,0:T(8,128)(2,1)S(1)}) custom-call(bf16[1024,256]{1,0:T(8,128)(2,1)S(1)} %bitcast.7, bf16[1024,256]{1,0:T(8,128)(2,1)S(1)} %collective-permute-done.other_ref), custom_call_target="tpu_custom_call" | custom-call | bytes 1048576 | tf_op jit(solution)/shard_map/pallas_call | solution.py:246
  5.6 1.0 %collective-permute-done.1.refs_0_.refs_1_ = bf16[128,256]{1,0:T(8,128)(2,1)S(1)} collective-permute-done((bf16[128,256]{1,0:T(8,128)(2,1)}, bf16[128,256]{1,0:T(8,128)(2,1)S(1)}, u32[]{:S(2)}, u32[]{:S(2)}) %collective-permute-start.1) | collective-permute-done | bytes 65568 | tf_op jit(solution)/shard_map/ppermute | solution.py:230
  6.6 0.0 collective-permute-done.2.refs_2_
  6.6 0.0 copy-done.1
  6.6 0.5 %shard_map.61 = (f32[8,256]{1,0:T(8,128)S(1)}, bf16[16,256]{1,0:T(8,128)(2,1)S(1)}, bf16[16,256]{1,0:T(8,128)(2,1)S(1)}, bf16[16,256]{1,0:T(8,128)(2,1)S(1)}) custom-call(bf16[256,256]{1,0:T(8,128)(2,1)S(1)} %get-tuple-element.32.order_ref, bf16[8,256,256]{2,1,0:T(8,128)(2,1)S(1)} %get-tuple-element.33.weight_ref, ...), custom_call_target="tpu_custom_call" | custom-call | bytes 1376256 | tf_op jit(solution)/shard_map/pallas_call | solution.py:246
  7.1 0.0 collective-permute-done.3
  7.1 1.4 %collective-permute-start.4 = (bf16[20,256]{1,0:T(8,128)(2,1)S(1)}, bf16[20,256]{1,0:T(8,128)(2,1)S(1)}, u32[]{:S(2)}, u32[]{:S(2)}) collective-permute-start(bf16[20,256]{1,0:T(8,128)(2,1)S(1)} %get-tuple-element.54), channel_id=1, source_target_pairs={{0,5},{1,4},{2,7},{3,6},{4,1},{5,0},{6,3},{7,2},{8,13},{9,12},{10,... | collective-permute-start | bytes 30728 | tf_op jit(solution)/shard_map/ppermute | solution.py:230
  8.6 1.5 %collective-permute-start.5 = (bf16[20,256]{1,0:T(8,128)(2,1)S(1)}, bf16[20,256]{1,0:T(8,128)(2,1)S(1)}, u32[]{:S(2)}, u32[]{:S(2)}) collective-permute-start(bf16[20,256]{1,0:T(8,128)(2,1)S(1)} %get-tuple-element.53), channel_id=1, source_target_pairs={{0,12},{1,13},{2,14},{3,15},{4,8},{5,9},{6,10},{7,11},{8,4},{9,5},... | collective-permute-start | bytes 30728 | tf_op jit(solution)/shard_map/ppermute | solution.py:230
  10.1 0.2 collective-permute-start.6
  10.3 0.4 %collective-permute-start.7 = (bf16[128,256]{1,0:T(8,128)(2,1)S(1)}, bf16[128,256]{1,0:T(8,128)(2,1)S(1)}, u32[]{:S(2)}, u32[]{:S(2)}) collective-permute-start(bf16[128,256]{1,0:T(8,128)(2,1)S(1)} %collective-permute-done.1.refs_0_.refs_1_), channel_id=1, source_target_pairs={{0,1},{1,0},{2,3},{3,2},{4,5},{5,4},{6,7},{7,6},{8,9},{9,8},{10,11... | collective-permute-start | bytes 196616 | tf_op jit(solution)/shard_map/ppermute | solution.py:230
  10.7 0.0 collective-permute-done.4.refs_0_
  10.7 2.4 %collective-permute-done.5.refs_1_ = bf16[20,256]{1,0:T(8,128)(2,1)S(1)} collective-permute-done((bf16[20,256]{1,0:T(8,128)(2,1)S(1)}, bf16[20,256]{1,0:T(8,128)(2,1)S(1)}, u32[]{:S(2)}, u32[]{:S(2)}) %collective-permute-start.5) | collective-permute-done | bytes 10272 | tf_op jit(solution)/shard_map/ppermute | solution.py:230
  13.1 0.1 collective-permute-done.6.refs_2_
  13.3 0.0 collective-permute-done.7.refs_3_
  13.3 2.4 %collective-permute-start.8 = (bf16[24,256]{1,0:T(8,128)(2,1)S(1)}, bf16[24,256]{1,0:T(8,128)(2,1)S(1)}, u32[]{:S(2)}, u32[]{:S(2)}) collective-permute-start(bf16[24,256]{1,0:T(8,128)(2,1)S(1)} %get-tuple-element.43.normed_ref), channel_id=1, source_target_pairs={{0,17},{1,16},{2,19},{3,18},{4,21},{5,20},{6,23},{7,22},{8,25},{9,... | collective-permute-start | bytes 36872 | tf_op jit(solution)/shard_map/ppermute | solution.py:230
  15.7 1.6 %collective-permute-done.8.refs_0_ = bf16[24,256]{1,0:T(8,128)(2,1)S(1)} collective-permute-done((bf16[24,256]{1,0:T(8,128)(2,1)S(1)}, bf16[24,256]{1,0:T(8,128)(2,1)S(1)}, u32[]{:S(2)}, u32[]{:S(2)}) %collective-permute-start.8) | collective-permute-done | bytes 12320 | tf_op jit(solution)/shard_map/ppermute | solution.py:230
  17.4 0.2 collective-permute-start.9
  17.6 1.6 %collective-permute-start.10 = (f32[2,256]{1,0:T(2,128)S(1)}, f32[2,256]{1,0:T(2,128)S(1)}, u32[]{:S(2)}, u32[]{:S(2)}) collective-permute-start(f32[2,256]{1,0:T(2,128)S(1)} %get-tuple-element.48), channel_id=1, source_target_pairs={{0,2},{1,3},{2,1},{3,0},{4,7},{5,6},{6,4},{7,5},{8,11},{9,10},{10,... | collective-permute-start | bytes 6152 | tf_op jit(solution)/shard_map/ppermute | solution.py:230
  19.1 0.0 collective-permute-done.9.other_ref
  19.1 1.4 %shard_map.64 = f32[1024,256]{1,0:T(8,128)} custom-call(f32[32,128]{1,0:T(8,128)S(1)} %get-tuple-element.45.own_ref, f32[18,256]{1,0:T(8,128)S(1)} %collective-permute-done.9.other_ref, bf16[128,256]{1,0:T(8,128)(2,1)S(1)} %bitcast.11, bf16[128,256]{1,0:T(8,128)(2,1)S(1)} %collective-permute-done.1.refs_0_.refs_1_, ...), custom_call_target="tpu_custom_call" | custom-call | flops 268435456 | bytes 296960 | tf_op jit(solution)/shard_map/pallas_call | solution.py:246
  20.6 0.0 collective-permute-done.10.refs_1_
  20.6 0.7 %shard_map.65 = f32[2,512]{1,0:T(2,128)} custom-call(f32[2,512]{1,0:T(2,128)S(1)} %get-tuple-element.27.rms_ref, f32[2,512]{1,0:T(2,128)S(1)} %get-tuple-element.28.hat_ref, f32[1,512]{1,0:T(1,128)S(1)} %bitcast.13, f32[18,256]{1,0:T(8,128)S(1)} %collective-permute-done.9.other_ref, f32[2,256]{1,0:T(2,128)S(1)} %get-tuple-element.49.refs_0_, ...), custom_call_target="tpu_custom_call" | custom-call | bytes 32768 | tf_op jit(solution)/shard_map/pallas_call | solution.py:246
  (4 shorter events, 0.0 us)
Async XLA Ops:
  0.6 3.9 %collective-permute-start = (bf16[1024,256]{1,0:T(8,128)(2,1)}, bf16[1024,256]{1,0:T(8,128)(2,1)S(1)}, u32[]{:S(2)}, u32[]{:S(2)}) collective-permute-start(bf16[1024,256]{1,0:T(8,128)(2,1)} %bitcast.6), channel_id=1, source_target_pairs={{0,1},{1,0},{2,3},{3,2},{4,5},{5,4},{6,7},{7,6},{8,9},{9,8},{10,11... | collective-permute-start | bytes 1572872 | tf_op jit(solution)/shard_map/ppermute | solution.py:230
  1.1 2.7 %copy-start.3 = (bf16[1,2,512]{2,1,0:T(2,128)(2,1)S(1)}, bf16[1,2,512]{2,1,0:T(2,128)(2,1)}, u32[]{:S(2)}) copy-start(bf16[1,2,512]{2,1,0:T(2,128)(2,1)} %param.4) | copy-start | bytes 6148
  1.1 2.7 %copy-start.2 = (f32[512]{0:T(512)S(1)}, f32[512]{0:T(512)}, u32[]{:S(2)}) copy-start(f32[512]{0:T(512)} %param.5) | copy-start | bytes 6148
  1.2 5.5 %collective-permute-start.1 = (bf16[128,256]{1,0:T(8,128)(2,1)}, bf16[128,256]{1,0:T(8,128)(2,1)S(1)}, u32[]{:S(2)}, u32[]{:S(2)}) collective-permute-start(bf16[128,256]{1,0:T(8,128)(2,1)} %bitcast.8), channel_id=1, source_target_pairs={{0,3},{1,2},{2,0},{3,1},{4,6},{5,7},{6,5},{7,4},{8,10},{9,11},{10,... | collective-permute-start | bytes 196616 | tf_op jit(solution)/shard_map/ppermute | solution.py:230
  3.8 2.8 %collective-permute-start.2 = (bf16[128,256]{1,0:T(8,128)(2,1)}, bf16[128,256]{1,0:T(8,128)(2,1)S(1)}, u32[]{:S(2)}, u32[]{:S(2)}) collective-permute-start(bf16[128,256]{1,0:T(8,128)(2,1)} %bitcast.9), channel_id=1, source_target_pairs={{0,1},{1,0},{2,3},{3,2},{4,5},{5,4},{6,7},{7,6},{8,9},{9,8},{10,11... | collective-permute-start | bytes 196616 | tf_op jit(solution)/shard_map/ppermute | solution.py:230
  3.8 1.0 %copy-start = (bf16[128,8,256]{2,1,0:T(8,128)(2,1)S(1)}, bf16[128,8,256]{2,1,0:T(8,128)(2,1)}, u32[]{:S(2)}) copy-start(bf16[128,8,256]{2,1,0:T(8,128)(2,1)} %param.7) | copy-start | bytes 1572868
  3.9 3.1 %collective-permute-start.3 = (bf16[2,256]{1,0:T(2,128)(2,1)S(1)}, bf16[2,256]{1,0:T(2,128)(2,1)S(1)}, u32[]{:S(2)}, u32[]{:S(2)}) collective-permute-start(bf16[2,256]{1,0:T(2,128)(2,1)S(1)} %get-tuple-element.36), channel_id=1, source_target_pairs={{0,3},{1,2},{2,1},{3,0},{4,7},{5,6},{6,5},{7,4},{8,11},{9,10},{10,... | collective-permute-start | bytes 3080 | tf_op jit(solution)/shard_map/ppermute | solution.py:230
  4.9 1.7 %copy-start.1 = (bf16[1,16,8,256]{3,2,1,0:T(8,128)(2,1)S(1)}, bf16[1,16,8,256]{3,2,1,0:T(8,128)(2,1)}, u32[]{:S(2)}) copy-start(bf16[1,16,8,256]{3,2,1,0:T(8,128)(2,1)} %param.6) | copy-start | bytes 196612
  7.1 3.6 %collective-permute-start.4 = (bf16[20,256]{1,0:T(8,128)(2,1)S(1)}, bf16[20,256]{1,0:T(8,128)(2,1)S(1)}, u32[]{:S(2)}, u32[]{:S(2)}) collective-permute-start(bf16[20,256]{1,0:T(8,128)(2,1)S(1)} %get-tuple-element.54), channel_id=1, source_target_pairs={{0,5},{1,4},{2,7},{3,6},{4,1},{5,0},{6,3},{7,2},{8,13},{9,12},{10,... | collective-permute-start | bytes 30728 | tf_op jit(solution)/shard_map/ppermute | solution.py:230
  8.6 4.6 %collective-permute-start.5 = (bf16[20,256]{1,0:T(8,128)(2,1)S(1)}, bf16[20,256]{1,0:T(8,128)(2,1)S(1)}, u32[]{:S(2)}, u32[]{:S(2)}) collective-permute-start(bf16[20,256]{1,0:T(8,128)(2,1)S(1)} %get-tuple-element.53), channel_id=1, source_target_pairs={{0,12},{1,13},{2,14},{3,15},{4,8},{5,9},{6,10},{7,11},{8,4},{9,5},... | collective-permute-start | bytes 30728 | tf_op jit(solution)/shard_map/ppermute | solution.py:230
  10.1 3.2 %collective-permute-start.6 = (bf16[20,256]{1,0:T(8,128)(2,1)S(1)}, bf16[20,256]{1,0:T(8,128)(2,1)S(1)}, u32[]{:S(2)}, u32[]{:S(2)}) collective-permute-start(bf16[20,256]{1,0:T(8,128)(2,1)S(1)} %get-tuple-element.52), channel_id=1, source_target_pairs={{0,9},{1,8},{2,11},{3,10},{4,13},{5,12},{6,15},{7,14},{8,1},{9,0},... | collective-permute-start | bytes 30728 | tf_op jit(solution)/shard_map/ppermute | solution.py:230
  10.3 3.0 %collective-permute-start.7 = (bf16[128,256]{1,0:T(8,128)(2,1)S(1)}, bf16[128,256]{1,0:T(8,128)(2,1)S(1)}, u32[]{:S(2)}, u32[]{:S(2)}) collective-permute-start(bf16[128,256]{1,0:T(8,128)(2,1)S(1)} %collective-permute-done.1.refs_0_.refs_1_), channel_id=1, source_target_pairs={{0,1},{1,0},{2,3},{3,2},{4,5},{5,4},{6,7},{7,6},{8,9},{9,8},{10,11... | collective-permute-start | bytes 196616 | tf_op jit(solution)/shard_map/ppermute | solution.py:230
  13.3 4.1 %collective-permute-start.8 = (bf16[24,256]{1,0:T(8,128)(2,1)S(1)}, bf16[24,256]{1,0:T(8,128)(2,1)S(1)}, u32[]{:S(2)}, u32[]{:S(2)}) collective-permute-start(bf16[24,256]{1,0:T(8,128)(2,1)S(1)} %get-tuple-element.43.normed_ref), channel_id=1, source_target_pairs={{0,17},{1,16},{2,19},{3,18},{4,21},{5,20},{6,23},{7,22},{8,25},{9,... | collective-permute-start | bytes 36872 | tf_op jit(solution)/shard_map/ppermute | solution.py:230
  17.4 1.8 %collective-permute-start.9 = (f32[18,256]{1,0:T(8,128)S(1)}, f32[18,256]{1,0:T(8,128)S(1)}, u32[]{:S(2)}, u32[]{:S(2)}) collective-permute-start(f32[18,256]{1,0:T(8,128)S(1)} %get-tuple-element.44), channel_id=1, source_target_pairs={{0,1},{1,0},{2,3},{3,2},{4,5},{5,4},{6,7},{7,6},{8,9},{9,8},{10,11... | collective-permute-start | bytes 55304 | tf_op jit(solution)/shard_map/ppermute | solution.py:230
  17.6 3.0 %collective-permute-start.10 = (f32[2,256]{1,0:T(2,128)S(1)}, f32[2,256]{1,0:T(2,128)S(1)}, u32[]{:S(2)}, u32[]{:S(2)}) collective-permute-start(f32[2,256]{1,0:T(2,128)S(1)} %get-tuple-element.48), channel_id=1, source_target_pairs={{0,2},{1,3},{2,1},{3,0},{4,7},{5,6},{6,4},{7,5},{8,11},{9,10},{10,... | collective-permute-start | bytes 6152 | tf_op jit(solution)/shard_map/ppermute | solution.py:230

commit v19 on v14

--- a/solution.py
+++ b/solution.py
@@ -351,7 +351,7 @@
         scratch=[
             pltpu.VMEM((2, rows, columns * tokens * heads), F32),
             pltpu.VMEM((rows * heads, channels), F32),
-            pltpu.SemaphoreType.DMA((4 if rows % 32 == 0 else 1,)),
+            pltpu.SemaphoreType.DMA((8 if rows % 64 == 0 else 1,)),
         ],
         flops=2 * rows * heads * channels * ctx_count * tokens * heads,
         place=pl.ANY,

time: 21.5 us -> 21.5 us (level)
  transfers between devices with their start and end apart: 11 -> 11, of which waited for: 4 -> 5; matrix products, arithmetic and copies ran while one was open for 0% -> 0% of each run, Pallas kernels for 13% -> 13%
where the time goes in v19:
time: 21.5 us; the launch traced here: 21.3 us
  starting transfers between devices  11.6 us (54%)
  waiting for transfers between devices  5.25 us (24%)
  Pallas kernels  3.44 us (16%)
  between operations  0.69 us (3%)
  local copies, waits for them, and re-layouts  0.32 us (1%)
    ppermute x11, starting transfers between devices, swap(): return lax.ppermute(value, ('head', 'ctx'), pairs)  11.6 us
    ppermute x11, waiting for transfers between devices, swap(): return lax.ppermute(value, ('head', 'ctx'), pairs)  5.25 us
    pallas_call x7, Pallas kernels, call(): pl.pallas_call(kernel, out_shape=out, out_specs=jax.tree.map(lambda _: pl...  3.44 us
  transfers between devices with their start and end apart: 11, of which 5 were waited for; matrix products, arithmetic and copies ran while one was open for 0% of the time, Pallas kernels for 13%

profile of v19, /device:TPU:0, one launch (start us, length us, event | category | flops | bytes accessed | tf_op | source)
XLA Modules:
  0.0 21.3 jit_solution(9296296296899715941)
XLA Ops:
  0.6 0.5 %collective-permute-start = (bf16[1024,256]{1,0:T(8,128)(2,1)}, bf16[1024,256]{1,0:T(8,128)(2,1)S(1)}, u32[]{:S(2)}, u32[]{:S(2)}) collective-permute-start(bf16[1024,256]{1,0:T(8,128)(2,1)} %bitcast.6), channel_id=1, source_target_pairs={{0,1},{1,0},{2,3},{3,2},{4,5},{5,4},{6,7},{7,6},{8,9},{9,8},{10,11... | collective-permute-start | bytes 1572872 | tf_op jit(solution)/shard_map/ppermute | solution.py:230
  1.1 0.0 copy-start.3
  1.1 0.0 copy-start.2
  1.2 2.6 %collective-permute-start.1 = (bf16[128,256]{1,0:T(8,128)(2,1)}, bf16[128,256]{1,0:T(8,128)(2,1)S(1)}, u32[]{:S(2)}, u32[]{:S(2)}) collective-permute-start(bf16[128,256]{1,0:T(8,128)(2,1)} %bitcast.8), channel_id=1, source_target_pairs={{0,3},{1,2},{2,0},{3,1},{4,6},{5,7},{6,5},{7,4},{8,10},{9,11},{10,... | collective-permute-start | bytes 196616 | tf_op jit(solution)/shard_map/ppermute | solution.py:230
  3.8 0.1 collective-permute-start.2
  3.8 0.0 copy-done.3
  3.8 0.0 copy-done.2
  3.8 0.0 copy-start
  3.8 0.1 shard_map.59
  3.9 0.6 %collective-permute-start.3 = (bf16[2,256]{1,0:T(2,128)(2,1)S(1)}, bf16[2,256]{1,0:T(2,128)(2,1)S(1)}, u32[]{:S(2)}, u32[]{:S(2)}) collective-permute-start(bf16[2,256]{1,0:T(2,128)(2,1)S(1)} %get-tuple-element.36), channel_id=1, source_target_pairs={{0,3},{1,2},{2,1},{3,0},{4,7},{5,6},{6,5},{7,4},{8,11},{9,10},{10,... | collective-permute-start | bytes 3080 | tf_op jit(solution)/shard_map/ppermute | solution.py:230
  4.6 0.0 collective-permute-done.other_ref
  4.6 0.3 %copy-done = bf16[128,8,256]{2,1,0:T(8,128)(2,1)S(1)} copy-done((bf16[128,8,256]{2,1,0:T(8,128)(2,1)S(1)}, bf16[128,8,256]{2,1,0:T(8,128)(2,1)}, u32[]{:S(2)}) %copy-start) | copy-done | bytes 524312
  4.9 0.0 copy-start.1
  4.9 0.8 %shard_map.60 = (bf16[8,256,256]{2,1,0:T(8,128)(2,1)S(1)}, bf16[256,256]{1,0:T(8,128)(2,1)S(1)}) custom-call(bf16[1024,256]{1,0:T(8,128)(2,1)S(1)} %bitcast.7, bf16[1024,256]{1,0:T(8,128)(2,1)S(1)} %collective-permute-done.other_ref), custom_call_target="tpu_custom_call" | custom-call | bytes 1048576 | tf_op jit(solution)/shard_map/pallas_call | solution.py:246
  5.6 1.0 %collective-permute-done.1.refs_0_.refs_1_ = bf16[128,256]{1,0:T(8,128)(2,1)S(1)} collective-permute-done((bf16[128,256]{1,0:T(8,128)(2,1)}, bf16[128,256]{1,0:T(8,128)(2,1)S(1)}, u32[]{:S(2)}, u32[]{:S(2)}) %collective-permute-start.1) | collective-permute-done | bytes 65568 | tf_op jit(solution)/shard_map/ppermute | solution.py:230
  6.6 0.0 collective-permute-done.2.refs_2_
  6.6 0.0 copy-done.1
  6.6 0.5 %shard_map.61 = (f32[8,256]{1,0:T(8,128)S(1)}, bf16[16,256]{1,0:T(8,128)(2,1)S(1)}, bf16[16,256]{1,0:T(8,128)(2,1)S(1)}, bf16[16,256]{1,0:T(8,128)(2,1)S(1)}) custom-call(bf16[256,256]{1,0:T(8,128)(2,1)S(1)} %get-tuple-element.32.order_ref, bf16[8,256,256]{2,1,0:T(8,128)(2,1)S(1)} %get-tuple-element.33.weight_ref, ...), custom_call_target="tpu_custom_call" | custom-call | bytes 1376256 | tf_op jit(solution)/shard_map/pallas_call | solution.py:246
  7.1 0.0 collective-permute-done.3
  7.1 1.4 %collective-permute-start.4 = (bf16[20,256]{1,0:T(8,128)(2,1)S(1)}, bf16[20,256]{1,0:T(8,128)(2,1)S(1)}, u32[]{:S(2)}, u32[]{:S(2)}) collective-permute-start(bf16[20,256]{1,0:T(8,128)(2,1)S(1)} %get-tuple-element.54), channel_id=1, source_target_pairs={{0,5},{1,4},{2,7},{3,6},{4,1},{5,0},{6,3},{7,2},{8,13},{9,12},{10,... | collective-permute-start | bytes 30728 | tf_op jit(solution)/shard_map/ppermute | solution.py:230
  8.6 1.5 %collective-permute-start.5 = (bf16[20,256]{1,0:T(8,128)(2,1)S(1)}, bf16[20,256]{1,0:T(8,128)(2,1)S(1)}, u32[]{:S(2)}, u32[]{:S(2)}) collective-permute-start(bf16[20,256]{1,0:T(8,128)(2,1)S(1)} %get-tuple-element.53), channel_id=1, source_target_pairs={{0,12},{1,13},{2,14},{3,15},{4,8},{5,9},{6,10},{7,11},{8,4},{9,5},... | collective-permute-start | bytes 30728 | tf_op jit(solution)/shard_map/ppermute | solution.py:230
  10.1 0.2 collective-permute-start.6
  10.3 0.4 %collective-permute-start.7 = (bf16[128,256]{1,0:T(8,128)(2,1)S(1)}, bf16[128,256]{1,0:T(8,128)(2,1)S(1)}, u32[]{:S(2)}, u32[]{:S(2)}) collective-permute-start(bf16[128,256]{1,0:T(8,128)(2,1)S(1)} %collective-permute-done.1.refs_0_.refs_1_), channel_id=1, source_target_pairs={{0,1},{1,0},{2,3},{3,2},{4,5},{5,4},{6,7},{7,6},{8,9},{9,8},{10,11... | collective-permute-start | bytes 196616 | tf_op jit(solution)/shard_map/ppermute | solution.py:230
  10.7 0.0 collective-permute-done.4.refs_0_
  10.7 2.4 %collective-permute-done.5.refs_1_ = bf16[20,256]{1,0:T(8,128)(2,1)S(1)} collective-permute-done((bf16[20,256]{1,0:T(8,128)(2,1)S(1)}, bf16[20,256]{1,0:T(8,128)(2,1)S(1)}, u32[]{:S(2)}, u32[]{:S(2)}) %collective-permute-start.5) | collective-permute-done | bytes 10272 | tf_op jit(solution)/shard_map/ppermute | solution.py:230
  13.1 0.1 collective-permute-done.6.refs_2_
  13.3 0.0 collective-permute-done.7.refs_3_
  13.3 2.4 %collective-permute-start.8 = (bf16[24,256]{1,0:T(8,128)(2,1)S(1)}, bf16[24,256]{1,0:T(8,128)(2,1)S(1)}, u32[]{:S(2)}, u32[]{:S(2)}) collective-permute-start(bf16[24,256]{1,0:T(8,128)(2,1)S(1)} %get-tuple-element.43.normed_ref), channel_id=1, source_target_pairs={{0,17},{1,16},{2,19},{3,18},{4,21},{5,20},{6,23},{7,22},{8,25},{9,... | collective-permute-start | bytes 36872 | tf_op jit(solution)/shard_map/ppermute | solution.py:230
  15.7 1.7 %collective-permute-done.8.refs_0_ = bf16[24,256]{1,0:T(8,128)(2,1)S(1)} collective-permute-done((bf16[24,256]{1,0:T(8,128)(2,1)S(1)}, bf16[24,256]{1,0:T(8,128)(2,1)S(1)}, u32[]{:S(2)}, u32[]{:S(2)}) %collective-permute-start.8) | collective-permute-done | bytes 12320 | tf_op jit(solution)/shard_map/ppermute | solution.py:230
  17.4 0.2 collective-permute-start.9
  17.6 1.6 %collective-permute-start.10 = (f32[2,256]{1,0:T(2,128)S(1)}, f32[2,256]{1,0:T(2,128)S(1)}, u32[]{:S(2)}, u32[]{:S(2)}) collective-permute-start(f32[2,256]{1,0:T(2,128)S(1)} %get-tuple-element.48), channel_id=1, source_target_pairs={{0,2},{1,3},{2,1},{3,0},{4,7},{5,6},{6,4},{7,5},{8,11},{9,10},{10,... | collective-permute-start | bytes 6152 | tf_op jit(solution)/shard_map/ppermute | solution.py:230
  19.1 0.0 collective-permute-done.9.other_ref
  19.1 1.4 %shard_map.64 = f32[1024,256]{1,0:T(8,128)} custom-call(f32[32,128]{1,0:T(8,128)S(1)} %get-tuple-element.45.own_ref, f32[18,256]{1,0:T(8,128)S(1)} %collective-permute-done.9.other_ref, bf16[128,256]{1,0:T(8,128)(2,1)S(1)} %bitcast.11, bf16[128,256]{1,0:T(8,128)(2,1)S(1)} %collective-permute-done.1.refs_0_.refs_1_, ...), custom_call_target="tpu_custom_call" | custom-call | flops 268435456 | bytes 296960 | tf_op jit(solution)/shard_map/pallas_call | solution.py:246
  20.6 0.1 collective-permute-done.10.refs_1_
  20.6 0.7 %shard_map.65 = f32[2,512]{1,0:T(2,128)} custom-call(f32[2,512]{1,0:T(2,128)S(1)} %get-tuple-element.27.rms_ref, f32[2,512]{1,0:T(2,128)S(1)} %get-tuple-element.28.hat_ref, f32[1,512]{1,0:T(1,128)S(1)} %bitcast.13, f32[18,256]{1,0:T(8,128)S(1)} %collective-permute-done.9.other_ref, f32[2,256]{1,0:T(2,128)S(1)} %get-tuple-element.49.refs_0_, ...), custom_call_target="tpu_custom_call" | custom-call | bytes 32768 | tf_op jit(solution)/shard_map/pallas_call | solution.py:246
  (4 shorter events, 0.0 us)
Async XLA Ops:
  0.6 3.9 %collective-permute-start = (bf16[1024,256]{1,0:T(8,128)(2,1)}, bf16[1024,256]{1,0:T(8,128)(2,1)S(1)}, u32[]{:S(2)}, u32[]{:S(2)}) collective-permute-start(bf16[1024,256]{1,0:T(8,128)(2,1)} %bitcast.6), channel_id=1, source_target_pairs={{0,1},{1,0},{2,3},{3,2},{4,5},{5,4},{6,7},{7,6},{8,9},{9,8},{10,11... | collective-permute-start | bytes 1572872 | tf_op jit(solution)/shard_map/ppermute | solution.py:230
  1.1 2.7 %copy-start.3 = (bf16[1,2,512]{2,1,0:T(2,128)(2,1)S(1)}, bf16[1,2,512]{2,1,0:T(2,128)(2,1)}, u32[]{:S(2)}) copy-start(bf16[1,2,512]{2,1,0:T(2,128)(2,1)} %param.4) | copy-start | bytes 6148
  1.1 2.7 %copy-start.2 = (f32[512]{0:T(512)S(1)}, f32[512]{0:T(512)}, u32[]{:S(2)}) copy-start(f32[512]{0:T(512)} %param.5) | copy-start | bytes 6148
  1.2 5.5 %collective-permute-start.1 = (bf16[128,256]{1,0:T(8,128)(2,1)}, bf16[128,256]{1,0:T(8,128)(2,1)S(1)}, u32[]{:S(2)}, u32[]{:S(2)}) collective-permute-start(bf16[128,256]{1,0:T(8,128)(2,1)} %bitcast.8), channel_id=1, source_target_pairs={{0,3},{1,2},{2,0},{3,1},{4,6},{5,7},{6,5},{7,4},{8,10},{9,11},{10,... | collective-permute-start | bytes 196616 | tf_op jit(solution)/shard_map/ppermute | solution.py:230
  3.8 2.8 %collective-permute-start.2 = (bf16[128,256]{1,0:T(8,128)(2,1)}, bf16[128,256]{1,0:T(8,128)(2,1)S(1)}, u32[]{:S(2)}, u32[]{:S(2)}) collective-permute-start(bf16[128,256]{1,0:T(8,128)(2,1)} %bitcast.9), channel_id=1, source_target_pairs={{0,1},{1,0},{2,3},{3,2},{4,5},{5,4},{6,7},{7,6},{8,9},{9,8},{10,11... | collective-permute-start | bytes 196616 | tf_op jit(solution)/shard_map/ppermute | solution.py:230
  3.8 1.0 %copy-start = (bf16[128,8,256]{2,1,0:T(8,128)(2,1)S(1)}, bf16[128,8,256]{2,1,0:T(8,128)(2,1)}, u32[]{:S(2)}) copy-start(bf16[128,8,256]{2,1,0:T(8,128)(2,1)} %param.7) | copy-start | bytes 1572868
  3.9 3.1 %collective-permute-start.3 = (bf16[2,256]{1,0:T(2,128)(2,1)S(1)}, bf16[2,256]{1,0:T(2,128)(2,1)S(1)}, u32[]{:S(2)}, u32[]{:S(2)}) collective-permute-start(bf16[2,256]{1,0:T(2,128)(2,1)S(1)} %get-tuple-element.36), channel_id=1, source_target_pairs={{0,3},{1,2},{2,1},{3,0},{4,7},{5,6},{6,5},{7,4},{8,11},{9,10},{10,... | collective-permute-start | bytes 3080 | tf_op jit(solution)/shard_map/ppermute | solution.py:230
  4.9 1.7 %copy-start.1 = (bf16[1,16,8,256]{3,2,1,0:T(8,128)(2,1)S(1)}, bf16[1,16,8,256]{3,2,1,0:T(8,128)(2,1)}, u32[]{:S(2)}) copy-start(bf16[1,16,8,256]{3,2,1,0:T(8,128)(2,1)} %param.6) | copy-start | bytes 196612
  7.1 3.6 %collective-permute-start.4 = (bf16[20,256]{1,0:T(8,128)(2,1)S(1)}, bf16[20,256]{1,0:T(8,128)(2,1)S(1)}, u32[]{:S(2)}, u32[]{:S(2)}) collective-permute-start(bf16[20,256]{1,0:T(8,128)(2,1)S(1)} %get-tuple-element.54), channel_id=1, source_target_pairs={{0,5},{1,4},{2,7},{3,6},{4,1},{5,0},{6,3},{7,2},{8,13},{9,12},{10,... | collective-permute-start | bytes 30728 | tf_op jit(solution)/shard_map/ppermute | solution.py:230
  8.6 4.6 %collective-permute-start.5 = (bf16[20,256]{1,0:T(8,128)(2,1)S(1)}, bf16[20,256]{1,0:T(8,128)(2,1)S(1)}, u32[]{:S(2)}, u32[]{:S(2)}) collective-permute-start(bf16[20,256]{1,0:T(8,128)(2,1)S(1)} %get-tuple-element.53), channel_id=1, source_target_pairs={{0,12},{1,13},{2,14},{3,15},{4,8},{5,9},{6,10},{7,11},{8,4},{9,5},... | collective-permute-start | bytes 30728 | tf_op jit(solution)/shard_map/ppermute | solution.py:230
  10.1 3.2 %collective-permute-start.6 = (bf16[20,256]{1,0:T(8,128)(2,1)S(1)}, bf16[20,256]{1,0:T(8,128)(2,1)S(1)}, u32[]{:S(2)}, u32[]{:S(2)}) collective-permute-start(bf16[20,256]{1,0:T(8,128)(2,1)S(1)} %get-tuple-element.52), channel_id=1, source_target_pairs={{0,9},{1,8},{2,11},{3,10},{4,13},{5,12},{6,15},{7,14},{8,1},{9,0},... | collective-permute-start | bytes 30728 | tf_op jit(solution)/shard_map/ppermute | solution.py:230
  10.3 3.0 %collective-permute-start.7 = (bf16[128,256]{1,0:T(8,128)(2,1)S(1)}, bf16[128,256]{1,0:T(8,128)(2,1)S(1)}, u32[]{:S(2)}, u32[]{:S(2)}) collective-permute-start(bf16[128,256]{1,0:T(8,128)(2,1)S(1)} %collective-permute-done.1.refs_0_.refs_1_), channel_id=1, source_target_pairs={{0,1},{1,0},{2,3},{3,2},{4,5},{5,4},{6,7},{7,6},{8,9},{9,8},{10,11... | collective-permute-start | bytes 196616 | tf_op jit(solution)/shard_map/ppermute | solution.py:230
  13.3 4.1 %collective-permute-start.8 = (bf16[24,256]{1,0:T(8,128)(2,1)S(1)}, bf16[24,256]{1,0:T(8,128)(2,1)S(1)}, u32[]{:S(2)}, u32[]{:S(2)}) collective-permute-start(bf16[24,256]{1,0:T(8,128)(2,1)S(1)} %get-tuple-element.43.normed_ref), channel_id=1, source_target_pairs={{0,17},{1,16},{2,19},{3,18},{4,21},{5,20},{6,23},{7,22},{8,25},{9,... | collective-permute-start | bytes 36872 | tf_op jit(solution)/shard_map/ppermute | solution.py:230
  17.4 1.7 %collective-permute-start.9 = (f32[18,256]{1,0:T(8,128)S(1)}, f32[18,256]{1,0:T(8,128)S(1)}, u32[]{:S(2)}, u32[]{:S(2)}) collective-permute-start(f32[18,256]{1,0:T(8,128)S(1)} %get-tuple-element.44), channel_id=1, source_target_pairs={{0,1},{1,0},{2,3},{3,2},{4,5},{5,4},{6,7},{7,6},{8,9},{9,8},{10,11... | collective-permute-start | bytes 55304 | tf_op jit(solution)/shard_map/ppermute | solution.py:230
  17.6 3.0 %collective-permute-start.10 = (f32[2,256]{1,0:T(2,128)S(1)}, f32[2,256]{1,0:T(2,128)S(1)}, u32[]{:S(2)}, u32[]{:S(2)}) collective-permute-start(f32[2,256]{1,0:T(2,128)S(1)} %get-tuple-element.48), channel_id=1, source_target_pairs={{0,2},{1,3},{2,1},{3,0},{4,7},{5,6},{6,4},{7,5},{8,11},{9,10},{10,... | collective-permute-start | bytes 6152 | tf_op jit(solution)/shard_map/ppermute | solution.py:230
